TPU v7x, 512 devices: a whole 4x8x8 slice. The times are simulated.
512 devices in a mesh: pb: 32 (over x, y_lo, core), ka: 16 (over y_hi, z).
Axes of the slice: x: 4, y: 8 (y_hi: 2, y_lo: 4; y = y_hi * 4 + y_lo), z: 8, core: 2. Of those that a mesh axis runs over, the one named last changes fastest.
Arguments:
- query_states: bfloat16 [65536, 512], P(('pb', 'ka')), may hold values from -128 to 128
- out_grad: bfloat16 [65536, 512], P(('pb', 'ka')), may hold values from -192 to 192
- forward_out: bfloat16 [65536, 512], P(('pb', 'ka')), may hold values from -6 to 6
- key_states: bfloat16 [65536, 128], P(('ka', 'pb')), may hold values from -8 to 8
- value_states: bfloat16 [65536, 128], P(('ka', 'pb')), may hold values from -6 to 6
- block_mask: int32 [512, 512], P('pb', 'ka'), may hold values from 0 to 1, as said below
Outputs:
- query_grad: bfloat16 [65536, 512], P(('pb', 'ka'))
- key_grad: bfloat16 [65536, 128], P(('ka', 'pb'))
- value_grad: bfloat16 [65536, 128], P(('ka', 'pb'))
Inputs may be any that keep to these rules, and one draw needn't show every extreme that they name: `block_mask`: the tiles of one index of pb and one index of ka (16 query tiles by 32 key tiles) hold at most 32 ones, exactly 32 for some such group; every diagonal tile is 1.
All inputs are finite; a program needn't handle non-finite values.
Results may differ from a plain program's by a relative error of at most 0.015.
Values may be sent and summed in bfloat16 or wider, within the bound.
No kernel may reach another device: no remote copies, remote signals or barrier semaphores. Data moves between devices by JAX's collectives and lax.ppermute only.
A program may use at most 64 MiB of HBM per device.

v0:
```python
import math

import jax
import jax.numpy as jnp
from jax import lax
from jax.sharding import Mesh
from jax.sharding import PartitionSpec as P

TILE = 128
HD = 128
HQ = 4
KA = ("ka_0", "ka_1")
PB_KA = ("pb", "ka_0", "ka_1")
KA_PB = ("ka_0", "ka_1", "pb")


NEG_START = -1e30


def sent_together(arrays, axis, dim, along):
    both = jnp.concatenate(arrays, axis=along)
    filled, at, done = (lax.all_gather(both, axis, axis=dim, tiled=True), 0, [])
    for a in arrays:
        done.append(lax.slice_in_dim(filled, at, at + a.shape[along], axis=along))
        at += a.shape[along]
    return tuple(done)


def from_everyone(value, axis):
    peers = lax.axis_size(axis)
    return lax.all_to_all(
        jnp.broadcast_to(value[None], (peers, *value.shape)), axis, 0, 0, tiled=True
    )


def all_in_one(value, axis):
    leaves = jax.tree.leaves(value)
    turns = sorted(range(len(leaves)), key=lambda k: -leaves[k].size)
    width = (1, *leaves[turns[0]].shape)[-1]
    lines = [
        jnp.pad(leaves[k].reshape(-1), (0, -leaves[k].size % width)).reshape(-1, width)
        for k in turns
    ]
    both, at, found = (from_everyone(jnp.concatenate(lines), axis), 0, {})
    for k, line in zip(turns, lines):
        section = both[:, at : at + len(line)].reshape(len(both), -1)
        found[k] = section[:, : leaves[k].size].reshape(-1, *leaves[k].shape)
        at += len(line)
    numbers = iter(range(len(leaves)))
    return jax.tree.map(lambda _: found[next(numbers)], value)


def folded_in_pairs(pieces, combine):
    while len(jax.tree.leaves(pieces)[0]) > 1:
        pieces = jax.vmap(combine)(
            *(jax.tree.map(lambda part: part[side::2], pieces) for side in (0, 1))
        )
    return jax.tree.map(lambda part: part[0], pieces)


def merged(value, axis, combine):
    pieces = all_in_one(value, axis)
    return folded_in_pairs(pieces, combine)


def own_block(pieces, axes, turns):
    inside = pieces.shape[1:]
    pieces = pieces.reshape(*(lax.axis_size(a) for a in axes), *inside)
    pieces = jnp.moveaxis(pieces, turns, range(len(axes))).reshape(-1, *inside)
    for k in turns:
        pieces = lax.psum_scatter(pieces, axes[k], scatter_dimension=0, tiled=True)
    return pieces[0]


def in_blocks(value, dim, peers):
    lengths = value.shape
    pieces = value.reshape(*lengths[:dim], peers, lengths[dim] // peers, *lengths[dim + 1 :])
    return jnp.moveaxis(pieces, dim, 0)


def summed_rows(value, axes, turns, dim):
    peers = lax.axis_size(axes)
    return own_block(in_blocks(value, dim, peers), axes, turns)


def sum_at_owner(value, axis, dim):
    pieces = in_blocks(value, dim, lax.axis_size(axis))
    arrived = lax.all_to_all(pieces, axis, split_axis=0, concat_axis=0, tiled=True)
    return arrived.astype(jnp.float32).sum(axis=0)


def side_by_side(arrays, axis, dim, along):
    ends, at = ([], 0)
    for a in arrays[:-1]:
        at += a.shape[along]
        ends.append(at)
    both = jnp.concatenate(arrays, axis=along)
    return tuple(jnp.split(sum_at_owner(both, axis, dim), ends, axis=along))


def dot_nt(left, right):
    return lax.dot_general(
        left, right, (((1,), (1,)), ((), ())), preferred_element_type=jnp.float32
    )


def dot_tn(left, right):
    return lax.dot_general(
        left, right, (((0,), (0,)), ((), ())), preferred_element_type=jnp.float32
    )


def add_into(total, piece, row_start):
    current = lax.dynamic_slice_in_dim(total, row_start, piece.shape[0], 0)
    return lax.dynamic_update_slice_in_dim(total, current + piece, row_start, 0)


def list_pairs(tile_mask):
    flat = tile_mask.reshape(-1)
    number = flat.shape[0]
    ranked = (1 - flat) * number + jnp.arange(number, dtype=jnp.int32)
    pair_order = jnp.argsort(ranked, stable=True)
    return (pair_order, jnp.sum(flat))


def row_delta(grad_rows, out_rows):
    product = grad_rows.astype(jnp.float32) * out_rows.astype(jnp.float32)
    return jnp.sum(product.reshape(product.shape[0], HQ, HD), axis=2).astype(jnp.bfloat16)


def tile_rows(block, row_tile):
    piece = lax.dynamic_slice_in_dim(block, row_tile * TILE, TILE, 0)
    return piece.reshape(TILE * HQ, HD)


def combine_stats(first_part, second_part):
    larger = jnp.maximum(first_part[0], second_part[0])
    total = first_part[1] * jnp.exp(first_part[0] - larger) + second_part[1] * jnp.exp(
        second_part[0] - larger
    )
    return (larger, total)


def stats_pass(query_block, task_item, carried, score_scale):
    key_block, value_block, pair_order, pair_count, task_tiles = task_item
    row_count = TILE * HQ

    def stats_visit(slot_index, current):
        row_max, row_sum = current
        pair_index = pair_order[slot_index]
        row_tile = pair_index // task_tiles
        col_tile = pair_index % task_tiles
        query_tile = tile_rows(query_block, row_tile)
        key_tile = lax.dynamic_slice_in_dim(key_block, col_tile * TILE, TILE, 0)
        scores = dot_nt(query_tile, key_tile) * score_scale
        row_start = row_tile * row_count
        old_max = lax.dynamic_slice_in_dim(row_max, row_start, row_count, 0)
        old_sum = lax.dynamic_slice_in_dim(row_sum, row_start, row_count, 0)
        new_max = jnp.maximum(old_max, jnp.max(scores, axis=1))
        new_sum = old_sum * jnp.exp(old_max - new_max) + jnp.sum(
            jnp.exp(scores - new_max[:, None]), axis=1
        )
        row_max = lax.dynamic_update_slice_in_dim(row_max, new_max, row_start, 0)
        row_sum = lax.dynamic_update_slice_in_dim(row_sum, new_sum, row_start, 0)
        return (row_max, row_sum)

    return lax.fori_loop(jnp.int32(0), pair_count, stats_visit, carried)


def grad_pass(query_block, grad_block, delta_rows, log_total, task_item, query_acc, score_scale):
    key_block, value_block, pair_order, pair_count, task_tiles = task_item
    row_count = TILE * HQ
    key_acc = jnp.zeros(key_block.shape, jnp.float32)
    value_acc = jnp.zeros(value_block.shape, jnp.float32)

    def grad_visit(slot_index, current):
        query_part, key_part, value_part = current
        pair_index = pair_order[slot_index]
        row_tile = pair_index // task_tiles
        col_tile = pair_index % task_tiles
        query_tile = tile_rows(query_block, row_tile)
        grad_tile = tile_rows(grad_block, row_tile)
        col_start = col_tile * TILE
        key_tile = lax.dynamic_slice_in_dim(key_block, col_start, TILE, 0)
        value_tile = lax.dynamic_slice_in_dim(value_block, col_start, TILE, 0)
        row_start = row_tile * row_count
        scores = dot_nt(query_tile, key_tile) * score_scale
        total_rows = lax.dynamic_slice_in_dim(log_total, row_start, row_count, 0)
        delta_part = lax.dynamic_slice_in_dim(delta_rows, row_start, row_count, 0)
        probs = jnp.exp(scores - total_rows[:, None])
        probs_half = probs.astype(jnp.bfloat16)
        grad_probs = dot_nt(grad_tile, value_tile)
        grad_scores = (probs * (grad_probs - delta_part[:, None])).astype(jnp.bfloat16)
        query_part = add_into(
            query_part,
            jnp.dot(grad_scores, key_tile, preferred_element_type=jnp.float32),
            row_start,
        )
        key_part = add_into(key_part, dot_tn(grad_scores, query_tile), col_start)
        value_part = add_into(value_part, dot_tn(probs_half, grad_tile), col_start)
        return (query_part, key_part, value_part)

    return lax.fori_loop(jnp.int32(0), pair_count, grad_visit, (query_acc, key_acc, value_acc))


def body(query_states, out_grad, forward_out, key_states, value_states, block_mask):
    score_scale = 1.0 / math.sqrt(HD)
    key_tiles = block_mask.shape[1]
    local_delta = row_delta(out_grad, forward_out)
    query_block, grad_block, delta_half = sent_together(
        (query_states, out_grad, local_delta), KA, 0, 1
    )
    delta_rows = delta_half.astype(jnp.float32).reshape(-1)
    key_block, value_block = sent_together((key_states, value_states), "pb", 0, 1)
    pair_order, pair_count = list_pairs(block_mask)
    task_list = (key_block, value_block, pair_order, pair_count, key_tiles)
    row_count = query_block.shape[0] * HQ
    statistics = (
        jnp.full((row_count,), NEG_START, jnp.float32),
        jnp.zeros((row_count,), jnp.float32),
    )
    statistics = stats_pass(query_block, task_list, statistics, score_scale)
    row_max, row_sum = merged(statistics, KA, combine_stats)
    log_total = row_max + jnp.log(row_sum)
    query_acc = jnp.zeros((row_count, HD), jnp.float32)
    query_acc, key_acc, value_acc = grad_pass(
        query_block, grad_block, delta_rows, log_total, task_list, query_acc, score_scale
    )
    key_results = (key_acc, value_acc)
    key_acc, value_acc = key_results
    query_sum = summed_rows(
        query_acc.reshape(query_block.shape[0], HQ * HD).astype(jnp.bfloat16), KA, (1, 0), 0
    ).astype(jnp.float32)
    key_sum, value_sum = side_by_side(
        (key_acc.astype(jnp.bfloat16), value_acc.astype(jnp.bfloat16)), "pb", 0, 1
    )
    query_grad = (query_sum * score_scale).astype(jnp.bfloat16)
    key_grad = (key_sum * score_scale).astype(jnp.bfloat16)
    value_grad = value_sum.astype(jnp.bfloat16)
    return (query_grad, key_grad, value_grad)


def solution(mesh):
    torus = Mesh(mesh.devices.reshape(mesh.shape["pb"], 2, 8), ("pb", "ka_0", "ka_1"))
    return jax.shard_map(
        body,
        mesh=torus,
        in_specs=(
            P(PB_KA, None),
            P(PB_KA, None),
            P(PB_KA, None),
            P(KA_PB, None),
            P(KA_PB, None),
            P("pb", KA),
        ),
        out_specs=(P(PB_KA, None), P(KA_PB, None), P(KA_PB, None)),
        check_vma=False,
    )
```

profile of v0, /device:TPU:1, one launch (start us, length us, event | category | flops | bytes accessed | tf_op | source)
XLA Modules:
  0.0 861.2 jit_solution(12352415155189757291)
XLA Ops:
  12.5 3.8 sort.17
  16.3 63.1 %all-gather.5.cloned.1.call-done = bf16[4096,256]{1,0:T(8,128)(2,1)} async-done(((bf16[128,256]{1,0:T(8,128)(2,1)}), bf16[4096,256]{1,0:T(8,128)(2,1)}) %all-gather.5.cloned.1.call-update) | async-done | bytes 2097168 | tf_op jit(solution)/shard_map/all_gather | solution.py:22
  79.4 2.6 fusion.23
  82.0 133.8 %all-gather.3.cloned.1.call-done = bf16[2048,1028]{1,0:T(8,128)(2,1)} async-done(((bf16[128,1028]{1,0:T(8,128)(2,1)}), bf16[2048,1028]{1,0:T(8,128)(2,1)}) %all-gather.3.cloned.1.call-update) | async-done | bytes 4210704 | tf_op jit(solution)/shard_map/all_gather | solution.py:22
  215.8 3.9 fusion.22
  219.7 103.7 %while.30 = (s32[]{:T(128)}, f32[8192]{0:T(1024)S(1)}, f32[8192]{0:T(1024)S(1)}, s32[]{:T(128)}, s32[512]{0:T(512)S(1)}, /*index=5*/bf16[2048,512]{1,0:T(8,128)(...) while((s32[]{:T(128)}, f32[8192]{0:T(1024)S(1)}, ...), condition=%wide.region_6.7_spmd, body=%wide.region_3.6_spmd.sunk | while | flops 17040420 | bytes 1368624 | solution.py:167
  325.2 48.7 %all-to-all-start = ((f32[16,2,8192]{2,1,0:T(2,128)}), f32[16,2,8192]{2,1,0:T(2,128)S(1)}, u32[]{:S(2)}, u32[]{:S(2)}) async-start(f32[16,2,8192]{2,1,0:T(2,128)} %broadcast_in_dim.21), calls=%async_computation | async-start | bytes 2097152 | tf_op jit(solution)/shard_map/all_to_all | solution.py:31
  374.0 2.1 slice_convert_fusion
  377.9 11.7 %all-to-all-done = f32[16,2,8192]{2,1,0:T(2,128)S(1)} async-done(((f32[16,2,8192]{2,1,0:T(2,128)}), f32[16,2,8192]{2,1,0:T(2,128)S(1)}, u32[]{:S(2)}, u32[]{:S(2)}) %all-to-all-start) | async-done | bytes 1048608 | tf_op jit(solution)/shard_map/all_to_all | solution.py:31
  403.0 2.2 broadcast_in_dim.9
  405.2 241.3 %while.31 = (s32[]{:T(128)}, f32[8192,128]{1,0:T(8,128)}, f32[4096,128]{1,0:T(8,128)}, f32[4096,128]{1,0:T(8,128)S(1)}, s32[]{:T(128)}, /*index=5*/s32[512]{0:T(...) while((s32[]{:T(128)}, f32[8192,128]{1,0:T(8,128)}, ...), condition=%wide.region_8.9_spmd, body=%wide.region_7.8_spmd.sunk | while | flops 84377632 | bytes 3650156 | solution.py:203
  436.2 1.8 fusion.65
  479.9 1.8 fusion.65
  490.8 1.9 fusion.65
  501.8 1.8 fusion.65
  534.6 1.8 fusion.65
  556.5 1.9 fusion.65
  589.3 1.9 fusion.65
  649.8 2.6 convert_element_type.56
  652.4 3.1 copy.12
  658.3 131.1 %all-to-all-start.1 = ((bf16[32,128,256]{2,1,0:T(8,128)(2,1)}), bf16[32,128,256]{2,1,0:T(8,128)(2,1)S(1)}, u32[]{:S(2)}, u32[]{:S(2)}) async-start(bf16[32,128,256]{2,1,0:T(8,128)(2,1)} %bitcast.40), calls=%async_computation.3 | async-start | bytes 4194304 | tf_op jit(solution)/shard_map/all_to_all | solution.py:88
  789.5 32.3 %reduce-scatter.3.cloned.1.call-done = bf16[2,128,512]{2,1,0:T(8,128)(2,1)} async-done(((bf16[16,128,512]{2,1,0:T(8,128)(2,1)}), bf16[2,128,512]{2,1,0:T(8,128)(2,1)}) %reduce-scatter.3.cloned.1.call-update) | async-done | bytes 262160 | tf_op jit(solution)/shard_map/reduce_scatter | solution.py:71
  821.8 17.5 %all-to-all-done.1 = bf16[32,128,256]{2,1,0:T(8,128)(2,1)S(1)} async-done(((bf16[32,128,256]{2,1,0:T(8,128)(2,1)}), bf16[32,128,256]{2,1,0:T(8,128)(2,1)S(1)}, u32[]{:S(2)}, u32[]{:S(2)}) %all-to-all-start.1) | async-done | bytes 2097184 | tf_op jit(solution)/shard_map/all_to_all | solution.py:88
  840.9 12.2 %reduce-scatter.5.cloned.1.call-done = bf16[1,128,512]{2,1,0:T(8,128)(2,1)} async-done(((bf16[2,128,512]{2,1,0:T(8,128)(2,1)}), bf16[1,128,512]{2,1,0:T(8,128)(2,1)}) %reduce-scatter.5.cloned.1.call-update) | async-done | bytes 131088 | tf_op jit(solution)/shard_map/reduce_scatter | solution.py:71
  (495 shorter events, 215.6 us)
Async XLA Ops:
  7.2 4.6 copy-start.5
  7.2 72.2 %all-gather.5.cloned.1.call-start = ((), (), s32[]{:S(2)}) async-start(), calls=%async_computation.5 | async-start | bytes 2162688 | tf_op jit(solution)/shard_map/all_gather | solution.py:22
  8.7 207.2 %all-gather.3.cloned.1.call-start = ((), (), s32[]{:S(2)}) async-start(), calls=%async_computation.4 | async-start | bytes 5013504 | tf_op jit(solution)/shard_map/all_gather | solution.py:22
  323.4 1.9 copy-start.4
  323.4 52.7 %copy-start.2 = (bf16[2048,512]{1,0:T(8,128)(2,1)}, bf16[2048,512]{1,0:T(8,128)(2,1)S(1)}, u32[]{:S(2)}) copy-start(bf16[2048,512]{1,0:T(8,128)(2,1)S(1)} %get-tuple-element.585) | copy-start | bytes 6291460
  325.2 64.4 %all-to-all-start = ((f32[16,2,8192]{2,1,0:T(2,128)}), f32[16,2,8192]{2,1,0:T(2,128)S(1)}, u32[]{:S(2)}, u32[]{:S(2)}) async-start(f32[16,2,8192]{2,1,0:T(2,128)} %broadcast_in_dim.21), calls=%async_computation | async-start | bytes 2097152 | tf_op jit(solution)/shard_map/all_to_all | solution.py:31
  373.9 447.8 %reduce-scatter.3.cloned.1.call-start = ((), (), s32[]{:S(2)}) async-start(), calls=%async_computation.6 | async-start | bytes 2359296 | tf_op jit(solution)/shard_map/reduce_scatter | solution.py:71
  646.5 1.6 copy-start.1
  646.5 3.1 copy-start
  655.6 1.2 copy-start.3
  658.3 181.0 %all-to-all-start.1 = ((bf16[32,128,256]{2,1,0:T(8,128)(2,1)}), bf16[32,128,256]{2,1,0:T(8,128)(2,1)S(1)}, u32[]{:S(2)}, u32[]{:S(2)}) async-start(bf16[32,128,256]{2,1,0:T(8,128)(2,1)} %bitcast.40), calls=%async_computation.3 | async-start | bytes 4194304 | tf_op jit(solution)/shard_map/all_to_all | solution.py:88
  789.5 63.6 %reduce-scatter.5.cloned.1.call-start = ((), (), s32[]{:S(2)}) async-start(), calls=%async_computation.7 | async-start | bytes 393216 | tf_op jit(solution)/shard_map/reduce_scatter | solution.py:71
Sparse Core Ops, SparseCore 0:
  10.7 68.5 all-gather.4
  82.5 133.2 all-gather.2
  655.7 166.0 reduce-scatter.2
  824.4 28.6 reduce-scatter.4
where the time goes:
time: 872 us; the launch traced here: 861 us
  waiting for transfers between devices  271 us (31%)
  starting transfers between devices  180 us (21%)
  loops' own time  148 us (17%)
  matrix products  130 us (15%)
  local copies, waits for them, and re-layouts  92 us (11%)
  other arithmetic  26.7 us (3%)
  between operations  14 us (2%)
    all_gather x2, waiting for transfers between devices, sent_together(): filled, at, done = (lax.all_gather(both, axis, axis=dim, tiled=True), 0, [])  197 us
    all_to_all x1, starting transfers between devices, sum_at_owner(): lax.all_to_all(pieces, axis, split_axis=0, concat_axis=0, tiled=True)  131 us
    another operation x1, loops' own time, grad_pass(): lax.fori_loop(jnp.int32(0), pair_count, grad_visit, (query_acc, key_acc,...  74 us
    another operation x1, loops' own time, stats_pass(): return lax.fori_loop(jnp.int32(0), pair_count, stats_visit, carried)  73.9 us
    all_to_all x1, starting transfers between devices, from_everyone(): lax.all_to_all(jnp.broadcast_to(value[None], (peers, *value.shape)), axis...  48.7 us
    dot_general x66, matrix products, dot_nt(): lax.dot_general(left, right, (((1,), (1,)), ((), ())), preferred_element_...  46.7 us
    reduce_scatter x2, waiting for transfers between devices, own_block(): pieces = lax.psum_scatter(pieces, axes[k], scatter_dimension=0, tiled=True)  44.4 us
    dot_general x44, matrix products, dot_tn(): lax.dot_general(left, right, (((0,), (0,)), ((), ())), preferred_element_...  42.7 us
  transfers between devices with their start and end apart: 6, of which 6 were waited for; matrix products, arithmetic and copies ran while one was open for 2% of the time, Pallas kernels for 0%

commit v1 on v0

v1 whole, which is shorter than its diff:
```python
import math

import jax
import jax.numpy as jnp
from jax import lax
from jax.experimental import pallas as pl
from jax.experimental.pallas import tpu as pltpu
from jax.sharding import Mesh
from jax.sharding import PartitionSpec as P

TILE = 128
HD = 128
HQ = 4
ROWS = TILE * HQ
NQ = 16
NK = 32
QPAD = 272
LOW = -1e30
SCALE = 1.0 / math.sqrt(HD)
LOG2E = 1.0 / math.log(2.0)
Y = ("yl", "yh")
VMEM_LIMIT = 56 * 1024 * 1024


def dot(a, b, dims):
    return lax.dot_general(a, b, (dims, ((), ())), preferred_element_type=jnp.float32)


def heads(ref, r, first):
    return jnp.concatenate(
        [ref[r, first : first + TILE, h * HD : (h + 1) * HD] for h in range(HQ)], axis=0
    )


def stats_kernel(pairs_ref, count_ref, q_ref, kv_ref, out_ref, m_ref, l_ref):
    m_ref[...] = jnp.full(m_ref.shape, LOW, jnp.float32)
    l_ref[...] = jnp.zeros(l_ref.shape, jnp.float32)

    def visit(s, carry):
        pair = pairs_ref[s]
        r = pair // NK
        j = pair % NK
        scores = dot(kv_ref[j, :, :HD], heads(q_ref, r, 0), ((1,), (1,))) * (SCALE * LOG2E)
        old = m_ref[r]
        new = jnp.maximum(old, jnp.max(scores, axis=0, keepdims=True))
        m_ref[r] = new
        l_ref[r] = l_ref[r] * jnp.exp2(old - new) + jnp.sum(
            jnp.exp2(scores - new), axis=0, keepdims=True
        )
        return carry

    lax.fori_loop(0, count_ref[0], visit, 0)
    total = l_ref[...]
    out_ref[...] = jnp.where(
        total > 0.0, m_ref[...] + jnp.log2(jnp.maximum(total, 1e-30)), LOW
    )


def grad_kernel(pairs_ref, count_ref, q_ref, kv_ref, total_ref, dq_ref, dkv_ref, dq_acc, dkv_acc):
    dq_acc[...] = jnp.zeros(dq_acc.shape, jnp.float32)
    dkv_acc[...] = jnp.zeros(dkv_acc.shape, jnp.float32)

    def visit(s, carry):
        pair = pairs_ref[s]
        r = pair // NK
        j = pair % NK
        k = kv_ref[j, :, :HD]
        v = kv_ref[j, :, HD:]
        q = heads(q_ref, r, 0)
        g = heads(q_ref, r, TILE)
        delta = q_ref[r, 2 * TILE : 2 * TILE + 16, :].astype(jnp.float32)[0:1, :]
        scores = dot(k, q, ((1,), (1,))) * (SCALE * LOG2E)
        probs = jnp.exp2(scores - total_ref[r])
        grad_probs = dot(v, g, ((1,), (1,)))
        grad_scores = (probs * (grad_probs - delta)).astype(jnp.bfloat16)
        dq_acc[r] += dot(k, grad_scores, ((0,), (0,)))
        dkv_acc[j, :, :HD] += dot(grad_scores, q, ((1,), (0,)))
        dkv_acc[j, :, HD:] += dot(probs.astype(jnp.bfloat16), g, ((1,), (0,)))
        return carry

    lax.fori_loop(0, count_ref[0], visit, 0)
    dq_ref[...] = dq_acc[...].astype(jnp.bfloat16)
    dkv_ref[...] = dkv_acc[...].astype(jnp.bfloat16)


def vmem():
    return pl.BlockSpec(memory_space=pltpu.VMEM)


def smem():
    return pl.BlockSpec(memory_space=pltpu.SMEM)


def call_stats(pairs, count, q, kv):
    return pl.pallas_call(
        stats_kernel,
        out_shape=jax.ShapeDtypeStruct((NQ, 1, ROWS), jnp.float32),
        in_specs=[smem(), smem(), vmem(), vmem()],
        out_specs=vmem(),
        scratch_shapes=[
            pltpu.VMEM((NQ, 1, ROWS), jnp.float32),
            pltpu.VMEM((NQ, 1, ROWS), jnp.float32),
        ],
        compiler_params=pltpu.CompilerParams(vmem_limit_bytes=VMEM_LIMIT),
        name="row_statistics",
    )(pairs, count, q, kv)


def call_grad(pairs, count, q, kv, total):
    return pl.pallas_call(
        grad_kernel,
        out_shape=(
            jax.ShapeDtypeStruct((NQ, HD, ROWS), jnp.bfloat16),
            jax.ShapeDtypeStruct((NK, TILE, 2 * HD), jnp.bfloat16),
        ),
        in_specs=[smem(), smem(), vmem(), vmem(), vmem()],
        out_specs=(vmem(), vmem()),
        scratch_shapes=[
            pltpu.VMEM((NQ, HD, ROWS), jnp.float32),
            pltpu.VMEM((NK, TILE, 2 * HD), jnp.float32),
        ],
        compiler_params=pltpu.CompilerParams(vmem_limit_bytes=VMEM_LIMIT),
        name="gradients",
    )(pairs, count, q, kv, total)


def to_everyone(value, axis):
    peers = lax.axis_size(axis)
    return lax.all_to_all(
        jnp.broadcast_to(value[None], (peers, *value.shape)), axis, 0, 0, tiled=True
    )


def swap_cores(value):
    return lax.ppermute(value, "c", [(0, 1), (1, 0)])


def list_pairs(tile_mask):
    flat = tile_mask.reshape(-1) > 0
    number = flat.shape[0]
    place = jnp.arange(number, dtype=jnp.int32)
    ones = flat.astype(jnp.int32)
    before = jnp.sum(
        jnp.where(place[None, :] < place[:, None], ones[None, :], 0), axis=1
    )
    here = (before[None, :] == place[:, None]) & flat[None, :]
    return jnp.sum(jnp.where(here, place[None, :], 0), axis=1), jnp.sum(ones)[None]


def body(query_states, out_grad, forward_out, key_states, value_states, block_mask):
    core = lax.axis_index("c")
    y_hi = lax.axis_index("yh")
    y_lo = lax.axis_index("yl")
    product = out_grad.astype(jnp.float32) * forward_out.astype(jnp.float32)
    delta = jnp.sum(product.reshape(TILE, HQ, HD), axis=2).astype(jnp.bfloat16)
    delta_rows = jnp.pad(delta.T.reshape(1, ROWS), ((0, 15), (0, 0)))
    q_own = jnp.concatenate([query_states, out_grad, delta_rows], axis=0)
    q_all = lax.all_gather(q_own, ("c", "z"), axis=0, tiled=False)

    mask_rows = jnp.pad(block_mask.astype(jnp.bfloat16).reshape(2, 2 * HD), ((0, 6), (0, 0)))
    kv_own = jnp.concatenate(
        [jnp.concatenate([key_states, value_states], axis=1), mask_rows], axis=0
    )
    kv_y = to_everyone(kv_own, Y)
    kv_all = to_everyone(kv_y[:, :TILE], "x").reshape(NK, TILE, 2 * HD)

    mine = lax.dynamic_slice_in_dim(kv_y[:, TILE : TILE + 2], y_lo * 2, 2, 0)
    mine = mine.reshape(2, 16, 32)
    other = swap_cores(mine)
    first = jnp.where(core == 0, mine, other)
    second = jnp.where(core == 0, other, mine)
    both = jnp.stack([first, second])
    both = lax.dynamic_slice_in_dim(both, y_hi * 8, 8, 2)
    both = both.reshape(2, 2, 8, 16, 2)
    both = jnp.where(core == 0, both[..., 0], both[..., 1])
    mask = both.transpose(0, 2, 3, 1).reshape(NQ, NK)
    pairs, count = list_pairs(mask)

    part = call_stats(pairs, count, q_all, kv_all)
    parts = to_everyone(part.reshape(NQ * ROWS // HD, HD), ("c", "z"))
    top = jnp.max(parts, axis=0)
    total = top + jnp.log2(jnp.sum(jnp.exp2(parts - top[None]), axis=0))
    total = total.reshape(NQ, 1, ROWS)
    dq, dkv = call_grad(pairs, count, q_all, kv_all, total)

    dq = dq.reshape(2, 8, HD, ROWS)
    kept = jnp.where(core == 0, dq[0], dq[1])
    sent = jnp.where(core == 0, dq[1], dq[0])
    got = swap_cores(sent)
    chip = (kept.astype(jnp.float32) + got.astype(jnp.float32)).astype(jnp.bfloat16)
    dq_own = lax.psum_scatter(chip, "z", scatter_dimension=0, tiled=True)[0]
    dq_own = (dq_own.astype(jnp.float32) * SCALE).astype(jnp.bfloat16)
    query_grad = dq_own.reshape(HD, HQ, TILE).transpose(2, 1, 0).reshape(TILE, HQ * HD)

    over_x = lax.all_to_all(dkv.reshape(4, 8 * TILE, 2 * HD), "x", 0, 0, tiled=True)
    over_x = over_x.astype(jnp.float32).sum(axis=0).astype(jnp.bfloat16)
    over_y = lax.all_to_all(over_x.reshape(8, TILE, 2 * HD), Y, 0, 0, tiled=True)
    sums = over_y.astype(jnp.float32).sum(axis=0)
    key_grad = (sums[:, :HD] * SCALE).astype(jnp.bfloat16)
    value_grad = sums[:, HD:].astype(jnp.bfloat16)
    return query_grad, key_grad, value_grad


def solution(mesh):
    torus = Mesh(mesh.devices.reshape(4, 4, 2, 2, 8), ("x", "yl", "c", "yh", "z"))
    queries = P(("x", "yl", "c", "yh", "z"), None)
    keys = P(("yh", "z", "x", "yl", "c"), None)
    return jax.shard_map(
        body,
        mesh=torus,
        in_specs=(queries, queries, queries, keys, keys, P(("x", "yl", "c"), ("yh", "z"))),
        out_specs=(queries, keys, keys),
        check_vma=False,
    )
```

time: 872 us -> 185 us (0.21)
  the two profiles are of different devices: /device:TPU:1 before, /device:TPU:328 now
where the time goes in v1:
time: 185 us; the launch traced here: 184 us
  blocking collectives  65.6 us (35%)
  waiting for transfers between devices  45.8 us (25%)
  starting transfers between devices  24 us (13%)
  Pallas kernels  15 us (8%)
  between operations  14.2 us (8%)
  other arithmetic  13.4 us (7%)
  local copies, waits for them, and re-layouts  6.22 us (3%)
    all_to_all x2, blocking collectives, to_everyone(): lax.all_to_all(jnp.broadcast_to(value[None], (peers, *value.shape)), axis...  47.3 us
    all_to_all x1, waiting for transfers between devices, body(): lax.all_to_all(dkv.reshape(4, 8 * TILE, 2 * HD), 'x', 0, 0, tiled=True)  24 us
    all_to_all x1, waiting for transfers between devices, to_everyone(): lax.all_to_all(jnp.broadcast_to(value[None], (peers, *value.shape)), axis...  20.7 us
    all_to_all x1, blocking collectives, body(): lax.all_to_all(over_x.reshape(8, TILE, 2 * HD), Y, 0, 0, tiled=True)  18.3 us
    all_to_all x1, starting transfers between devices, body(): lax.all_to_all(dkv.reshape(4, 8 * TILE, 2 * HD), 'x', 0, 0, tiled=True)  15.9 us
    pallas_call x1, Pallas kernels, call_grad(): pl.pallas_call(grad_kernel, out_shape=(jax.ShapeDtypeStruct((NQ, HD, ROWS...  9.18 us
    pallas_call x1, Pallas kernels, call_stats(): pl.pallas_call(stats_kernel, out_shape=jax.ShapeDtypeStruct((NQ, 1, ROWS)...  5.86 us
    all_to_all x1, starting transfers between devices, to_everyone(): lax.all_to_all(jnp.broadcast_to(value[None], (peers, *value.shape)), axis...  4.29 us
  transfers between devices with their start and end apart: 6, of which 3 were waited for; matrix products, arithmetic and copies ran while one was open for 5% of the time, Pallas kernels for 0%

profile of v1, /device:TPU:328, one launch (start us, length us, event | category | flops | bytes accessed | tf_op | source)
XLA Modules:
  0.0 184.3 jit_solution(6712600635613696139)
XLA Ops:
  7.2 1.0 convert_multiply_fusion
  8.7 1.7 fusion.2
  10.6 24.0 %all_to_all.25 = bf16[8,136,256]{2,1,0:T(8,128)(2,1)S(1)} all-to-all(bf16[8,136,256]{2,1,0:T(8,128)(2,1)S(1)} %broadcast_in_dim.26), channel_id=1, replica_groups=mesh['x'=4,'yl'=4,'c'=2,'yh'=2,'z'=8] {'yl','yh'}, dimensions={0} | all-to-all | bytes 1114112 | tf_op jit(solution)/shard_map/all_to_all | solution.py:129
  34.7 1.6 broadcast_in_dim.50
  36.2 4.3 %all-to-all-start.1 = ((bf16[4,8,128,256]{3,2,1,0:T(8,128)(2,1)}), bf16[4,8,128,256]{3,2,1,0:T(8,128)(2,1)S(1)}, u32[]{:S(2)}, u32[]{:S(2)}) async-start(bf16[4,8,128,256]{3,2,1,0:T(8,128)(2,1)} %broadcast_in_dim.50), calls=%async_computation.1 | async-start | bytes 4194304 | tf_op jit(solution)/shard_map/all_to_all | solution.py:129
  40.7 1.9 %collective-permute-start = (bf16[2,16,32]{2,1,0:T(8,128)(2,1)S(1)}, bf16[2,16,32]{2,1,0:T(8,128)(2,1)S(1)}, u32[]{:S(2)}, u32[]{:S(2)}) collective-permute-start(bf16[2,16,32]{2,1,0:T(8,128)(2,1)S(1)} %reshape.96), channel_id=1, source_target_pairs={{0,16},{16,0},{1,17},{17,1},{2,18},{18,2},{3,19},{19,3},{4,20},{20... | collective-permute-start | bytes 6152 | tf_op jit(solution)/shard_map/ppermute | solution.py:135
  42.6 1.1 collective-permute-done
  43.8 0.7 convert_reduce_fusion.1
  45.2 0.9 select_reduce_fusion.pairs_ref
  46.0 20.7 %all-to-all-done.1 = bf16[4,8,128,256]{3,2,1,0:T(8,128)(2,1)S(1)} async-done(((bf16[4,8,128,256]{3,2,1,0:T(8,128)(2,1)}), bf16[4,8,128,256]{3,2,1,0:T(8,128)(2,1)S(1)}, u32[]{:S(2)}, u32[]{:S(2)}) %all-to-all-start.1) | async-done | bytes 2097184 | tf_op jit(solution)/shard_map/all_to_all | solution.py:129
  66.7 1.4 copy-done
  68.1 5.9 %row_statistics.1 = f32[16,1,512]{2,1,0:T(1,128)} custom-call(s32[512]{0:T(512)} %select_reduce_fusion.pairs_ref, s32[1]{0:T(128)} %bitcast.6.count_ref, bf16[16,272,512]{2,1,0:T(8,128)(2,1)} %bitcast.32, bf16[32,128,256]{2,1,0:T(8,128)(2,1)} %bitcast.30), custom_call_target="tpu_custom_call" | custom-call | tf_op jit(solution)/shard_map/row_statistics/pallas_call | solution.py:95
  73.9 0.8 broadcast_in_dim.52
  74.7 23.3 %all_to_all.26 = f32[16,64,128]{2,1,0:T(8,128)S(1)} all-to-all(f32[16,64,128]{2,1,0:T(8,128)S(1)} %broadcast_in_dim.52), channel_id=1, replica_groups=mesh['x'=4,'yl'=4,'c'=2,'yh'=2,'z'=8] {'c','z'}, dimensions={0} | all-to-all | bytes 1048576 | tf_op jit(solution)/shard_map/all_to_all | solution.py:129
  98.8 9.2 %gradients.1 = (bf16[16,128,512]{2,1,0:T(8,128)(2,1)}, bf16[32,128,256]{2,1,0:T(8,128)(2,1)}) custom-call(s32[512]{0:T(512)} %select_reduce_fusion.pairs_ref, s32[1]{0:T(128)} %bitcast.6.count_ref, bf16[16,272,512]{2,1,0:T(8,128)(2,1)} %bitcast.33, bf16[32,128,256]{2,1,0:T(8,128)(2,1)} %bitcast.31, f32[16,1,512]{2,1,0:T(1,128)} %bitcast.39), custom_call_target="tpu_custom_call" | custom-call | tf_op jit(solution)/shard_map/gradients/pallas_call | solution.py:110
  108.0 2.6 %broadcast_select_fusion = bf16[8,128,512]{2,1,0:T(8,128)(2,1)} fusion(pred[]{:T(512)S(6)} %eq.6, bf16[16,128,512]{2,1,0:T(8,128)(2,1)} %get-tuple-element.5), kind=kLoop, calls=%fused_computation.7 | loop fusion | flops 524288 | bytes 3145729 | tf_op jit(solution)/shard_map/jit(_where)/select_n | solution.py:188
  110.6 1.9 %collective-permute-start.1 = (bf16[8,128,512]{2,1,0:T(8,128)(2,1)}, bf16[8,128,512]{2,1,0:T(8,128)(2,1)S(1)}, u32[]{:S(2)}, u32[]{:S(2)}) collective-permute-start(bf16[8,128,512]{2,1,0:T(8,128)(2,1)} %broadcast_select_fusion), channel_id=1, source_target_pairs={{0,16},{16,0},{1,17},{17,1},{2,18},{18,2},{3,19},{19,3},{4,20},{20... | collective-permute-start | bytes 3145736 | tf_op jit(solution)/shard_map/ppermute | solution.py:135
  112.5 15.9 %all-to-all-start.3 = ((bf16[4,1024,256]{2,1,0:T(8,128)(2,1)}), bf16[4,1024,256]{2,1,0:T(8,128)(2,1)S(1)}, u32[]{:S(2)}, u32[]{:S(2)}) async-start(bf16[4,1024,256]{2,1,0:T(8,128)(2,1)} %bitcast.34), calls=%async_computation.4 | async-start | bytes 4194304 | tf_op jit(solution)/shard_map/all_to_all | solution.py:195
  128.4 3.0 %add_convert_fusion = bf16[8,128,512]{2,1,0:T(8,128)(2,1)} fusion(bf16[8,128,512]{2,1,0:T(8,128)(2,1)S(1)} %collective-permute-done.1, pred[]{:T(512)S(6)} %eq.6, bf16[16,128,512]{2,1,0:T(8,128)(2,1)} %get-tuple-element.5), kind=kLoop, calls=%fused_computation | loop fusion | flops 2621440 | bytes 4194305 | tf_op jit(solution)/shard_map/convert_element_type | solution.py:190
  131.4 24.0 %all-to-all-done.3 = bf16[4,1024,256]{2,1,0:T(8,128)(2,1)S(1)} async-done(((bf16[4,1024,256]{2,1,0:T(8,128)(2,1)}), bf16[4,1024,256]{2,1,0:T(8,128)(2,1)S(1)}, u32[]{:S(2)}, u32[]{:S(2)}) %all-to-all-start.3) | async-done | bytes 2097184 | tf_op jit(solution)/shard_map/all_to_all | solution.py:195
  155.4 0.6 reduce_sum.71
  156.0 18.3 %all_to_all.27 = bf16[8,128,256]{2,1,0:T(8,128)(2,1)S(1)} all-to-all(bf16[8,128,256]{2,1,0:T(8,128)(2,1)S(1)} %bitcast.35), channel_id=1, replica_groups=mesh['x'=4,'yl'=4,'c'=2,'yh'=2,'z'=8] {'yl','yh'}, dimensions={0} | all-to-all | bytes 1048576 | tf_op jit(solution)/shard_map/all_to_all | solution.py:197
  175.7 0.9 multiply_convert_fusion
  176.8 0.7 copy.36
  (41 shorter events, 3.7 us)
Async XLA Ops:
  7.2 3.2 %copy-start.3 = (s32[16,32]{1,0:T(8,128)S(1)}, s32[16,32]{1,0:T(8,128)}, u32[]{:S(2)}) copy-start(s32[16,32]{1,0:T(8,128)} %param.11) | copy-start | bytes 6148
  7.2 3.3 %copy-start.1 = (bf16[128,128]{1,0:T(8,128)(2,1)S(1)}, bf16[128,128]{1,0:T(8,128)(2,1)}, u32[]{:S(2)}) copy-start(bf16[128,128]{1,0:T(8,128)(2,1)} %param.10) | copy-start | bytes 98308
  7.2 3.3 %copy-start.2 = (bf16[128,128]{1,0:T(8,128)(2,1)S(1)}, bf16[128,128]{1,0:T(8,128)(2,1)}, u32[]{:S(2)}) copy-start(bf16[128,128]{1,0:T(8,128)(2,1)} %param.9) | copy-start | bytes 98308
  7.2 59.5 %all-gather.3.cloned.1.call-start = ((), (), s32[]{:S(2)}) async-start(), calls=%async_computation.7 | async-start | bytes 4734976 | tf_op jit(solution)/shard_map/all_gather | solution.py:158
  36.2 30.4 %all-to-all-start.1 = ((bf16[4,8,128,256]{3,2,1,0:T(8,128)(2,1)}), bf16[4,8,128,256]{3,2,1,0:T(8,128)(2,1)S(1)}, u32[]{:S(2)}, u32[]{:S(2)}) async-start(bf16[4,8,128,256]{3,2,1,0:T(8,128)(2,1)} %broadcast_in_dim.50), calls=%async_computation.1 | async-start | bytes 4194304 | tf_op jit(solution)/shard_map/all_to_all | solution.py:129
  40.7 3.1 %collective-permute-start = (bf16[2,16,32]{2,1,0:T(8,128)(2,1)S(1)}, bf16[2,16,32]{2,1,0:T(8,128)(2,1)S(1)}, u32[]{:S(2)}, u32[]{:S(2)}) collective-permute-start(bf16[2,16,32]{2,1,0:T(8,128)(2,1)S(1)} %reshape.96), channel_id=1, source_target_pairs={{0,16},{16,0},{1,17},{17,1},{2,18},{18,2},{3,19},{19,3},{4,20},{20... | collective-permute-start | bytes 6152 | tf_op jit(solution)/shard_map/ppermute | solution.py:135
  66.7 1.4 copy-start
  110.6 17.8 %collective-permute-start.1 = (bf16[8,128,512]{2,1,0:T(8,128)(2,1)}, bf16[8,128,512]{2,1,0:T(8,128)(2,1)S(1)}, u32[]{:S(2)}, u32[]{:S(2)}) collective-permute-start(bf16[8,128,512]{2,1,0:T(8,128)(2,1)} %broadcast_select_fusion), channel_id=1, source_target_pairs={{0,16},{16,0},{1,17},{17,1},{2,18},{18,2},{3,19},{19,3},{4,20},{20... | collective-permute-start | bytes 3145736 | tf_op jit(solution)/shard_map/ppermute | solution.py:135
  112.5 42.9 %all-to-all-start.3 = ((bf16[4,1024,256]{2,1,0:T(8,128)(2,1)}), bf16[4,1024,256]{2,1,0:T(8,128)(2,1)S(1)}, u32[]{:S(2)}, u32[]{:S(2)}) async-start(bf16[4,1024,256]{2,1,0:T(8,128)(2,1)} %bitcast.34), calls=%async_computation.4 | async-start | bytes 4194304 | tf_op jit(solution)/shard_map/all_to_all | solution.py:195
  128.4 47.3 %reduce-scatter.2.cloned.1.call-start = ((), (), s32[]{:S(2)}) async-start(), calls=%async_computation.6 | async-start | bytes 1179648 | tf_op jit(solution)/shard_map/reduce_scatter | solution.py:191
Sparse Core Ops, SparseCore 0:
  10.5 43.8 all-gather.2
  132.0 36.5 reduce-scatter.1

commit v2 on v1

v2 whole, which is shorter than its diff:
```python
import math

import jax
import jax.numpy as jnp
from jax import lax
from jax.experimental import pallas as pl
from jax.experimental.pallas import tpu as pltpu
from jax.sharding import Mesh
from jax.sharding import PartitionSpec as P

TILE = 128
HD = 128
HQ = 4
ROWS = TILE * HQ
NQ = 16
NK = 32
QPAD = 272
LOW = -1e30
SCALE = 1.0 / math.sqrt(HD)
LOG2E = 1.0 / math.log(2.0)
Y = ("yl", "yh")
STEP = 4


def dot(a, b, dims):
    return lax.dot_general(a, b, (dims, ((), ())), preferred_element_type=jnp.float32)


def heads(ref, r, first):
    return jnp.concatenate(
        [ref[r, first : first + TILE, h * HD : (h + 1) * HD] for h in range(HQ)], axis=0
    )


def unpack(pairs_ref, s):
    pair = pairs_ref[s]
    r, j = pair >> 6, pair & 63
    return r, j, jnp.minimum(r, NQ - 1), jnp.minimum(j, NK - 1)


def blocks_of(count_ref, per_step):
    return (count_ref[0] + (per_step - 1)) // per_step


def stats_kernel(pairs_ref, count_ref, q_hbm, kv_hbm, out_ref, q_ref, k_ref, m_ref, l_ref, sems):
    copies = (
        pltpu.make_async_copy(q_hbm.at[:, pl.ds(0, TILE), :], q_ref, sems.at[0]),
        pltpu.make_async_copy(kv_hbm.at[:, :, pl.ds(0, HD)], k_ref, sems.at[1]),
    )
    for copy in copies:
        copy.start()
    m_ref[...] = jnp.full(m_ref.shape, LOW, jnp.float32)
    l_ref[...] = jnp.zeros(l_ref.shape, jnp.float32)
    for copy in copies:
        copy.wait()

    def visit(i, carry):
        found = []
        for u in range(STEP):
            r, _, rq, jk = unpack(pairs_ref, i * STEP + u)
            scores = dot(k_ref[jk], heads(q_ref, rq, 0), ((1,), (1,))) * (SCALE * LOG2E)
            top = jnp.max(scores, axis=0, keepdims=True)
            found.append((r, top, jnp.sum(jnp.exp2(scores - top), axis=0, keepdims=True)))
        for r, top, total in found:
            old = m_ref[r]
            new = jnp.maximum(old, top)
            m_ref[r] = new
            l_ref[r] = l_ref[r] * jnp.exp2(old - new) + total * jnp.exp2(top - new)
        return carry

    lax.fori_loop(0, blocks_of(count_ref, STEP), visit, 0)
    total = l_ref[...][:NQ]
    out_ref[...] = jnp.where(
        total > 0.0, m_ref[...][:NQ] + jnp.log2(jnp.maximum(total, 1e-30)), LOW
    )


def weights_of(q_ref, kv_ref, total_ref, rq, jk):
    scores = dot(kv_ref[jk, :, :HD], heads(q_ref, rq, 0), ((1,), (1,))) * (SCALE * LOG2E)
    probs = jnp.exp2(scores - total_ref[rq])
    grad_probs = dot(kv_ref[jk, :, HD:], heads(q_ref, rq, TILE), ((1,), (1,)))
    delta = q_ref[rq, 2 * TILE : 2 * TILE + 16, :].astype(jnp.float32)[0:1, :]
    return probs, (probs * (grad_probs - delta)).astype(jnp.bfloat16)


def load(q_hbm, kv_hbm, total_hbm, q_ref, kv_ref, total_ref, sems):
    copies = (
        pltpu.make_async_copy(q_hbm, q_ref, sems.at[0]),
        pltpu.make_async_copy(kv_hbm, kv_ref, sems.at[1]),
        pltpu.make_async_copy(total_hbm, total_ref, sems.at[2]),
    )
    for copy in copies:
        copy.start()
    return copies


def query_kernel(
    pairs_ref, count_ref, core_ref, q_hbm, kv_hbm, total_hbm, out_ref,
    q_ref, kv_ref, total_ref, acc, ds_ref, sems,
):
    copies = load(q_hbm, kv_hbm, total_hbm, q_ref, kv_ref, total_ref, sems)
    acc[...] = jnp.zeros(acc.shape, jnp.float32)
    for copy in copies:
        copy.wait()

    def visit(i, carry):
        where = [unpack(pairs_ref, i * STEP + u) for u in range(STEP)]
        for u, (_, _, rq, jk) in enumerate(where):
            ds_ref[u] = weights_of(q_ref, kv_ref, total_ref, rq, jk)[1]
        parts = [dot(kv_ref[w[3], :, :HD], ds_ref[u], ((0,), (0,))) for u, w in enumerate(where)]
        for (r, _, _, _), part in zip(where, parts):
            acc[r] += part
        return carry

    lax.fori_loop(0, blocks_of(count_ref, STEP), visit, 0)
    core = core_ref[0]
    for r in range(NQ):
        out_ref[(r // 8) ^ core, r % 8] = acc[r].astype(jnp.bfloat16)


def key_kernel(
    pairs_ref, count_ref, q_hbm, kv_hbm, total_hbm, out_ref,
    q_ref, kv_ref, total_ref, acc, p_ref, ds_ref, sems,
):
    copies = load(q_hbm, kv_hbm, total_hbm, q_ref, kv_ref, total_ref, sems)
    acc[...] = jnp.zeros(acc.shape, jnp.float32)
    for copy in copies:
        copy.wait()

    def visit(i, carry):
        where = [unpack(pairs_ref, i * STEP + u) for u in range(STEP)]
        for u, (_, _, rq, jk) in enumerate(where):
            probs, grad_scores = weights_of(q_ref, kv_ref, total_ref, rq, jk)
            p_ref[u] = probs.astype(jnp.bfloat16)
            ds_ref[u] = grad_scores
        parts = [
            (
                dot(ds_ref[u], heads(q_ref, w[2], 0), ((1,), (0,))),
                dot(p_ref[u], heads(q_ref, w[2], TILE), ((1,), (0,))),
            )
            for u, w in enumerate(where)
        ]
        for (_, j, _, _), (of_key, of_value) in zip(where, parts):
            acc[j, :, :HD] += of_key
            acc[j, :, HD:] += of_value
        return carry

    lax.fori_loop(0, blocks_of(count_ref, STEP), visit, 0)
    out_ref[...] = acc[:NK].astype(jnp.bfloat16)


def vmem():
    return pl.BlockSpec(memory_space=pltpu.VMEM)


def smem():
    return pl.BlockSpec(memory_space=pltpu.SMEM)


def anywhere():
    return pl.BlockSpec(memory_space=pl.ANY)


def params(mib):
    return pltpu.CompilerParams(vmem_limit_bytes=mib * 1024 * 1024)


def loaded():
    return [
        pltpu.VMEM((NQ, QPAD, ROWS), jnp.bfloat16),
        pltpu.VMEM((NK, TILE, 2 * HD), jnp.bfloat16),
        pltpu.VMEM((NQ, 1, ROWS), jnp.float32),
    ]


def call_stats(pairs, count, q, kv):
    return pl.pallas_call(
        stats_kernel,
        out_shape=jax.ShapeDtypeStruct((NQ, 1, ROWS), jnp.float32),
        in_specs=[smem(), smem(), anywhere(), anywhere()],
        out_specs=vmem(),
        scratch_shapes=[
            pltpu.VMEM((NQ, TILE, ROWS), jnp.bfloat16),
            pltpu.VMEM((NK, TILE, HD), jnp.bfloat16),
            pltpu.VMEM((NQ + 1, 1, ROWS), jnp.float32),
            pltpu.VMEM((NQ + 1, 1, ROWS), jnp.float32),
            pltpu.SemaphoreType.DMA((2,)),
        ],
        compiler_params=params(60),
        cost_estimate=pl.CostEstimate(
            flops=10_000_000_000, bytes_accessed=4 << 20, transcendentals=0
        ),
        name="row_statistics",
    )(pairs, count, q, kv)


def call_query(pairs, count, core, q, kv, total):
    return pl.pallas_call(
        query_kernel,
        out_shape=jax.ShapeDtypeStruct((2, NQ // 2, HD, ROWS), jnp.bfloat16),
        in_specs=[smem(), smem(), smem(), anywhere(), anywhere(), anywhere()],
        out_specs=vmem(),
        scratch_shapes=loaded()
        + [
            pltpu.VMEM((NQ + 1, HD, ROWS), jnp.float32),
            pltpu.VMEM((STEP, TILE, ROWS), jnp.bfloat16),
            pltpu.SemaphoreType.DMA((3,)),
        ],
        compiler_params=params(60),
        cost_estimate=pl.CostEstimate(
            flops=10_000_000_000, bytes_accessed=8 << 20, transcendentals=0
        ),
        name="query_gradient",
    )(pairs, count, core, q, kv, total)


def call_key(pairs, count, q, kv, total):
    return pl.pallas_call(
        key_kernel,
        out_shape=jax.ShapeDtypeStruct((NK, TILE, 2 * HD), jnp.bfloat16),
        in_specs=[smem(), smem(), anywhere(), anywhere(), anywhere()],
        out_specs=vmem(),
        scratch_shapes=loaded()
        + [
            pltpu.VMEM((NK + 1, TILE, 2 * HD), jnp.float32),
            pltpu.VMEM((STEP, TILE, ROWS), jnp.bfloat16),
            pltpu.VMEM((STEP, TILE, ROWS), jnp.bfloat16),
            pltpu.SemaphoreType.DMA((3,)),
        ],
        compiler_params=params(60),
        cost_estimate=pl.CostEstimate(
            flops=10_000_000_000, bytes_accessed=8 << 20, transcendentals=0
        ),
        name="key_gradient",
    )(pairs, count, q, kv, total)


def to_everyone(value, axis):
    peers = lax.axis_size(axis)
    return lax.all_to_all(
        jnp.broadcast_to(value[None], (peers, *value.shape)), axis, 0, 0, tiled=True
    )


def swap_cores(value):
    return lax.ppermute(value, "c", [(0, 1), (1, 0)])


def list_pairs(tile_mask):
    flat = tile_mask.reshape(-1) > 0
    number = flat.shape[0]
    place = jnp.arange(number, dtype=jnp.int32)
    ones = flat.astype(jnp.int32)
    before = jnp.sum(
        jnp.where(place[None, :] < place[:, None], ones[None, :], 0), axis=1
    )
    here = (before[None, :] == place[:, None]) & flat[None, :]
    spare = jnp.where(place < jnp.sum(ones), 0, NQ * 64 + NK)
    code = place // NK * 64 + place % NK
    pairs = jnp.sum(jnp.where(here, code[None, :], 0), axis=1) + spare
    return jnp.pad(pairs, (0, STEP), constant_values=NQ * 64 + NK), jnp.sum(ones)[None]


def body(query_states, out_grad, forward_out, key_states, value_states, block_mask):
    core = lax.axis_index("c")
    y_hi = lax.axis_index("yh")
    y_lo = lax.axis_index("yl")
    product = out_grad.astype(jnp.float32) * forward_out.astype(jnp.float32)
    delta = jnp.sum(product.reshape(TILE, HQ, HD), axis=2).astype(jnp.bfloat16)
    delta_rows = jnp.pad(delta.T.reshape(1, ROWS), ((0, 15), (0, 0)))
    q_own = jnp.concatenate([query_states, out_grad, delta_rows], axis=0)
    q_all = lax.all_gather(q_own, ("c", "z"), axis=0, tiled=False)

    mask_rows = jnp.pad(block_mask.astype(jnp.bfloat16).reshape(2, 2 * HD), ((0, 6), (0, 0)))
    kv_own = jnp.concatenate(
        [jnp.concatenate([key_states, value_states], axis=1), mask_rows], axis=0
    )
    kv_y = to_everyone(kv_own, Y)
    kv_all = to_everyone(kv_y[:, :TILE], "x").reshape(NK, TILE, 2 * HD)

    mine = lax.dynamic_slice_in_dim(kv_y[:, TILE : TILE + 2], y_lo * 2, 2, 0)
    mine = mine.reshape(2, 16, 32)
    other = swap_cores(mine)
    first = jnp.where(core == 0, mine, other)
    second = jnp.where(core == 0, other, mine)
    both = jnp.stack([first, second])
    both = lax.dynamic_slice_in_dim(both, y_hi * 8, 8, 2)
    both = both.reshape(2, 2, 8, 16, 2)
    both = jnp.where(core == 0, both[..., 0], both[..., 1])
    mask = both.transpose(0, 2, 3, 1).reshape(NQ, NK)
    pairs, count = list_pairs(mask)

    part = call_stats(pairs, count, q_all, kv_all)
    parts = to_everyone(part.reshape(NQ * ROWS // HD, HD), ("c", "z"))
    dq = call_query(pairs, count, core[None], q_all, kv_all, part)
    kept, got = dq[0], swap_cores(dq[1])

    top = jnp.max(parts, axis=0)
    total = top + jnp.log2(jnp.sum(jnp.exp2(parts - top[None]), axis=0))
    dkv = call_key(pairs, count, q_all, kv_all, total.reshape(NQ, 1, ROWS))

    own_part = lax.dynamic_index_in_dim(parts, core * 8 + lax.axis_index("z"), 0, False)
    far_part = lax.dynamic_index_in_dim(parts, (1 - core) * 8 + lax.axis_index("z"), 0, False)
    own_w, far_w = (
        lax.dynamic_slice_in_dim(jnp.exp2(p - total), core * 32, 32, 0).reshape(8, 1, ROWS)
        for p in (own_part, far_part)
    )
    chip = (kept.astype(jnp.float32) * own_w + got.astype(jnp.float32) * far_w).astype(
        jnp.bfloat16
    )
    dq_own = lax.psum_scatter(chip, "z", scatter_dimension=0, tiled=True)[0]
    dq_own = (dq_own.astype(jnp.float32) * SCALE).astype(jnp.bfloat16)
    query_grad = dq_own.reshape(HD, HQ, TILE).transpose(2, 1, 0).reshape(TILE, HQ * HD)

    over_x = lax.all_to_all(dkv.reshape(4, 8 * TILE, 2 * HD), "x", 0, 0, tiled=True)
    over_x = over_x.astype(jnp.float32).sum(axis=0).astype(jnp.bfloat16)
    over_y = lax.all_to_all(over_x.reshape(8, TILE, 2 * HD), Y, 0, 0, tiled=True)
    sums = over_y.astype(jnp.float32).sum(axis=0)
    key_grad = (sums[:, :HD] * SCALE).astype(jnp.bfloat16)
    value_grad = sums[:, HD:].astype(jnp.bfloat16)
    return query_grad, key_grad, value_grad


def solution(mesh):
    torus = Mesh(mesh.devices.reshape(4, 4, 2, 2, 8), ("x", "yl", "c", "yh", "z"))
    queries = P(("x", "yl", "c", "yh", "z"), None)
    keys = P(("yh", "z", "x", "yl", "c"), None)
    return jax.shard_map(
        body,
        mesh=torus,
        in_specs=(queries, queries, queries, keys, keys, P(("x", "yl", "c"), ("yh", "z"))),
        out_specs=(queries, keys, keys),
        check_vma=False,
    )
```

time: 185 us -> 171 us (0.924)
  the two profiles are of different devices: /device:TPU:328 before, /device:TPU:2 now
where the time goes in v2:
time: 171 us; the launch traced here: 170 us
  waiting for transfers between devices  59.7 us (35%)
  starting transfers between devices  29.9 us (17%)
  blocking collectives  24.2 us (14%)
  Pallas kernels  20.9 us (12%)
  between operations  14.3 us (8%)
  local copies, waits for them, and re-layouts  10.5 us (6%)
  other arithmetic  10.5 us (6%)
    all_to_all x1, blocking collectives, to_everyone(): lax.all_to_all(jnp.broadcast_to(value[None], (peers, *value.shape)), axis...  24.2 us
    all_to_all x1, waiting for transfers between devices, body(): lax.all_to_all(dkv.reshape(4, 8 * TILE, 2 * HD), 'x', 0, 0, tiled=True)  22.2 us
    all_to_all x2, waiting for transfers between devices, to_everyone(): lax.all_to_all(jnp.broadcast_to(value[None], (peers, *value.shape)), axis...  20.8 us
    all_to_all x2, starting transfers between devices, to_everyone(): lax.all_to_all(jnp.broadcast_to(value[None], (peers, *value.shape)), axis...  16.6 us
    reduce_scatter x1, waiting for transfers between devices, body(): dq_own = lax.psum_scatter(chip, 'z', scatter_dimension=0, tiled=True)[0]  15.6 us
    pallas_call x1, Pallas kernels, call_key(): pl.pallas_call(key_kernel, out_shape=jax.ShapeDtypeStruct((NK, TILE, 2 *...  8.03 us
    pallas_call x1, Pallas kernels, call_query(): pl.pallas_call(query_kernel, out_shape=jax.ShapeDtypeStruct((2, NQ // 2,...  7.64 us
    pallas_call x1, Pallas kernels, call_stats(): pl.pallas_call(stats_kernel, out_shape=jax.ShapeDtypeStruct((NQ, 1, ROWS)...  5.22 us
  transfers between devices with their start and end apart: 8, of which 5 were waited for; matrix products, arithmetic and copies ran while one was open for 8% of the time, Pallas kernels for 9%

profile of v2, /device:TPU:2, one launch (start us, length us, event | category | flops | bytes accessed | tf_op | source)
XLA Modules:
  0.0 169.9 jit_solution(8895101263749398504)
XLA Ops:
  7.2 1.0 convert_multiply_fusion.1
  8.7 1.7 %fusion.4 = bf16[272,512]{1,0:T(8,128)(2,1)} fusion(bf16[1,512]{1,0:T(2,128)(2,1)S(1)} %bitcast.54, bf16[128,512]{1,0:T(8,128)(2,1)} %param.7, bf16[128,512]{1,0:T(8,128)(2,1)} %param.6), kind=kLoop, calls=%fused_computation.14 | loop fusion | flops 1114112 | bytes 541696 | tf_op jit(solution)/shard_map/concatenate | solution.py:271
  10.6 24.2 %all_to_all.25 = bf16[8,136,256]{2,1,0:T(8,128)(2,1)S(1)} all-to-all(bf16[8,136,256]{2,1,0:T(8,128)(2,1)S(1)} %broadcast_in_dim.57), channel_id=1, replica_groups=mesh['x'=4,'yl'=4,'c'=2,'yh'=2,'z'=8] {'yl','yh'}, dimensions={0} | all-to-all | bytes 1114112 | tf_op jit(solution)/shard_map/all_to_all | solution.py:240
  34.8 1.6 broadcast_in_dim.64
  36.4 4.8 %all-to-all-start.1 = ((bf16[4,8,128,256]{3,2,1,0:T(8,128)(2,1)}), bf16[4,8,128,256]{3,2,1,0:T(8,128)(2,1)S(1)}, u32[]{:S(2)}, u32[]{:S(2)}) async-start(bf16[4,8,128,256]{3,2,1,0:T(8,128)(2,1)} %broadcast_in_dim.64), calls=%async_computation.1 | async-start | bytes 4194304 | tf_op jit(solution)/shard_map/all_to_all | solution.py:240
  41.3 1.9 %collective-permute-start = (bf16[2,16,32]{2,1,0:T(8,128)(2,1)S(1)}, bf16[2,16,32]{2,1,0:T(8,128)(2,1)S(1)}, u32[]{:S(2)}, u32[]{:S(2)}) collective-permute-start(bf16[2,16,32]{2,1,0:T(8,128)(2,1)S(1)} %reshape.119), channel_id=1, source_target_pairs={{0,16},{16,0},{1,17},{17,1},{2,18},{18,2},{3,19},{19,3},{4,20},{20... | collective-permute-start | bytes 6152 | tf_op jit(solution)/shard_map/ppermute | solution.py:246
  43.2 1.1 collective-permute-done
  47.4 16.9 %all-to-all-done.1 = bf16[4,8,128,256]{3,2,1,0:T(8,128)(2,1)S(1)} async-done(((bf16[4,8,128,256]{3,2,1,0:T(8,128)(2,1)}), bf16[4,8,128,256]{3,2,1,0:T(8,128)(2,1)S(1)}, u32[]{:S(2)}, u32[]{:S(2)}) %all-to-all-start.1) | async-done | bytes 2097184 | tf_op jit(solution)/shard_map/all_to_all | solution.py:240
  64.3 1.3 copy-done
  65.7 5.2 %row_statistics.1.total_hbm = f32[16,1,512]{2,1,0:T(1,128)} custom-call(s32[516]{0:T(1024)} %pad.13.pairs_ref, s32[1]{0:T(128)} %bitcast.6.count_ref, bf16[16,272,512]{2,1,0:T(8,128)(2,1)} %bitcast.56, bf16[32,128,256]{2,1,0:T(8,128)(2,1)} %bitcast.42), custom_call_target="tpu_custom_call" | custom-call | flops 10000000000 | bytes 4194304 | tf_op jit(solution)/shard_map/row_statistics/pallas_call | solution.py:177
  70.9 1.6 broadcast_in_dim.66
  72.6 11.8 %all-to-all-start.2 = ((f32[16,64,128]{2,1,0:T(8,128)}), f32[16,64,128]{2,1,0:T(8,128)S(1)}, u32[]{:S(2)}, u32[]{:S(2)}) async-start(f32[16,64,128]{2,1,0:T(8,128)} %broadcast_in_dim.66), calls=%async_computation.2 | async-start | bytes 1048576 | tf_op jit(solution)/shard_map/all_to_all | solution.py:240
  84.3 7.6 %query_gradient.1 = bf16[2,8,128,512]{3,2,1,0:T(8,128)(2,1)} custom-call(s32[516]{0:T(1024)} %pad.13.pairs_ref, s32[1]{0:T(128)} %bitcast.6.count_ref, s32[1]{0:T(128)} %bitcast.7.core_ref, bf16[16,272,512]{2,1,0:T(8,128)(2,1)} %bitcast.57, bf16[32,128,256]{2,1,0:T(8,128)(2,1)} %bitcast.43, f32[16,1,512]{2,1,0:T(1,128)} %row_statistics.1.total_hbm), custom_call_target="tpu_custom_call" | custom-call | flops 10000000000 | bytes 8388608 | tf_op jit(solution)/shard_map/query_gradient/pallas_call | solution.py:198
  92.0 2.3 %slice_bitcast_fusion = bf16[8,128,512]{2,1,0:T(8,128)(2,1)} fusion(bf16[2,8,128,512]{3,2,1,0:T(8,128)(2,1)} %query_gradient.1), kind=kLoop, calls=%fused_computation.3 | loop fusion | bytes 2097152 | tf_op jit(solution)/shard_map/squeeze | solution.py:296
  94.3 1.9 %collective-permute-start.1 = (bf16[8,128,512]{2,1,0:T(8,128)(2,1)}, bf16[8,128,512]{2,1,0:T(8,128)(2,1)S(1)}, u32[]{:S(2)}, u32[]{:S(2)}) collective-permute-start(bf16[8,128,512]{2,1,0:T(8,128)(2,1)} %slice_bitcast_fusion), channel_id=1, source_target_pairs={{0,16},{16,0},{1,17},{17,1},{2,18},{18,2},{3,19},{19,3},{4,20},{20... | collective-permute-start | bytes 3145736 | tf_op jit(solution)/shard_map/ppermute | solution.py:246
  96.2 3.8 %all-to-all-done.2 = f32[16,64,128]{2,1,0:T(8,128)S(1)} async-done(((f32[16,64,128]{2,1,0:T(8,128)}), f32[16,64,128]{2,1,0:T(8,128)S(1)}, u32[]{:S(2)}, u32[]{:S(2)}) %all-to-all-start.2) | async-done | bytes 524320 | tf_op jit(solution)/shard_map/all_to_all | solution.py:240
  100.8 8.0 %key_gradient.1 = bf16[32,128,256]{2,1,0:T(8,128)(2,1)} custom-call(s32[516]{0:T(1024)} %pad.13.pairs_ref, s32[1]{0:T(128)} %bitcast.6.count_ref, bf16[16,272,512]{2,1,0:T(8,128)(2,1)} %bitcast.58, bf16[32,128,256]{2,1,0:T(8,128)(2,1)} %bitcast.44, f32[16,1,512]{2,1,0:T(1,128)} %bitcast.52), custom_call_target="tpu_custom_call" | custom-call | flops 10000000000 | bytes 8388608 | tf_op jit(solution)/shard_map/key_gradient/pallas_call | solution.py:218
  108.8 5.1 %all-to-all-start.3 = ((bf16[4,1024,256]{2,1,0:T(8,128)(2,1)}), bf16[4,1024,256]{2,1,0:T(8,128)(2,1)S(1)}, u32[]{:S(2)}, u32[]{:S(2)}) async-start(bf16[4,1024,256]{2,1,0:T(8,128)(2,1)} %bitcast.45), calls=%async_computation.4 | async-start | bytes 4194304 | tf_op jit(solution)/shard_map/all_to_all | solution.py:315
  114.0 2.6 %fusion.1 = bf16[8,128,512]{2,1,0:T(8,128)(2,1)} fusion(bf16[8,128,512]{2,1,0:T(8,128)(2,1)S(1)} %collective-permute-done.1, bf16[2,8,128,512]{3,2,1,0:T(8,128)(2,1)} %query_gradient.1, f32[8,512]{1,0:T(8,128)S(1)} %mul.74, f32[8,512]{1,0:T(8,128)S(1)} %mul.70), kind=kLoop, calls=%fused_computation.2 | loop fusion | flops 3145728 | bytes 3178496 | tf_op jit(solution)/shard_map/convert_element_type | solution.py:308
  116.6 22.2 %all-to-all-done.3 = bf16[4,1024,256]{2,1,0:T(8,128)(2,1)S(1)} async-done(((bf16[4,1024,256]{2,1,0:T(8,128)(2,1)}), bf16[4,1024,256]{2,1,0:T(8,128)(2,1)S(1)}, u32[]{:S(2)}, u32[]{:S(2)}) %all-to-all-start.3) | async-done | bytes 2097184 | tf_op jit(solution)/shard_map/all_to_all | solution.py:315
  138.8 1.3 reduce_sum.75
  140.1 4.3 %all-to-all-start.4 = ((bf16[8,128,256]{2,1,0:T(8,128)(2,1)}), bf16[8,128,256]{2,1,0:T(8,128)(2,1)S(1)}, u32[]{:S(2)}, u32[]{:S(2)}) async-start(bf16[8,128,256]{2,1,0:T(8,128)(2,1)} %bitcast.19), calls=%async_computation.5 | async-start | bytes 1048576 | tf_op jit(solution)/shard_map/all_to_all | solution.py:317
  144.3 15.6 %reduce-scatter.2.cloned.1.call-done = bf16[1,128,512]{2,1,0:T(8,128)(2,1)} async-done(((bf16[8,128,512]{2,1,0:T(8,128)(2,1)}), bf16[1,128,512]{2,1,0:T(8,128)(2,1)}) %reduce-scatter.2.cloned.1.call-update) | async-done | bytes 131088 | tf_op jit(solution)/shard_map/reduce_scatter | solution.py:311
  159.9 0.9 multiply_convert_fusion
  (53 shorter events, 6.7 us)
Async XLA Ops:
  7.2 3.2 %copy-start.4 = (s32[16,32]{1,0:T(8,128)S(1)}, s32[16,32]{1,0:T(8,128)}, u32[]{:S(2)}) copy-start(s32[16,32]{1,0:T(8,128)} %param.11) | copy-start | bytes 6148
  7.2 3.3 %copy-start.2 = (bf16[128,128]{1,0:T(8,128)(2,1)S(1)}, bf16[128,128]{1,0:T(8,128)(2,1)}, u32[]{:S(2)}) copy-start(bf16[128,128]{1,0:T(8,128)(2,1)} %param.10) | copy-start | bytes 98308
  7.2 3.3 %copy-start.3 = (bf16[128,128]{1,0:T(8,128)(2,1)S(1)}, bf16[128,128]{1,0:T(8,128)(2,1)}, u32[]{:S(2)}) copy-start(bf16[128,128]{1,0:T(8,128)(2,1)} %param.9) | copy-start | bytes 98308
  7.2 57.1 %all-gather.3.cloned.1.call-start = ((), (), s32[]{:S(2)}) async-start(), calls=%async_computation.7 | async-start | bytes 4734976 | tf_op jit(solution)/shard_map/all_gather | solution.py:272
  36.4 28.0 %all-to-all-start.1 = ((bf16[4,8,128,256]{3,2,1,0:T(8,128)(2,1)}), bf16[4,8,128,256]{3,2,1,0:T(8,128)(2,1)S(1)}, u32[]{:S(2)}, u32[]{:S(2)}) async-start(bf16[4,8,128,256]{3,2,1,0:T(8,128)(2,1)} %broadcast_in_dim.64), calls=%async_computation.1 | async-start | bytes 4194304 | tf_op jit(solution)/shard_map/all_to_all | solution.py:240
  41.3 3.1 %collective-permute-start = (bf16[2,16,32]{2,1,0:T(8,128)(2,1)S(1)}, bf16[2,16,32]{2,1,0:T(8,128)(2,1)S(1)}, u32[]{:S(2)}, u32[]{:S(2)}) collective-permute-start(bf16[2,16,32]{2,1,0:T(8,128)(2,1)S(1)} %reshape.119), channel_id=1, source_target_pairs={{0,16},{16,0},{1,17},{17,1},{2,18},{18,2},{3,19},{19,3},{4,20},{20... | collective-permute-start | bytes 6152 | tf_op jit(solution)/shard_map/ppermute | solution.py:246
  64.3 1.3 copy-start
  72.6 27.5 %all-to-all-start.2 = ((f32[16,64,128]{2,1,0:T(8,128)}), f32[16,64,128]{2,1,0:T(8,128)S(1)}, u32[]{:S(2)}, u32[]{:S(2)}) async-start(f32[16,64,128]{2,1,0:T(8,128)} %broadcast_in_dim.66), calls=%async_computation.2 | async-start | bytes 1048576 | tf_op jit(solution)/shard_map/all_to_all | solution.py:240
  94.3 19.7 %collective-permute-start.1 = (bf16[8,128,512]{2,1,0:T(8,128)(2,1)}, bf16[8,128,512]{2,1,0:T(8,128)(2,1)S(1)}, u32[]{:S(2)}, u32[]{:S(2)}) collective-permute-start(bf16[8,128,512]{2,1,0:T(8,128)(2,1)} %slice_bitcast_fusion), channel_id=1, source_target_pairs={{0,16},{16,0},{1,17},{17,1},{2,18},{18,2},{3,19},{19,3},{4,20},{20... | collective-permute-start | bytes 3145736 | tf_op jit(solution)/shard_map/ppermute | solution.py:246
  100.2 0.6 copy-start.1
  108.8 30.0 %all-to-all-start.3 = ((bf16[4,1024,256]{2,1,0:T(8,128)(2,1)}), bf16[4,1024,256]{2,1,0:T(8,128)(2,1)S(1)}, u32[]{:S(2)}, u32[]{:S(2)}) async-start(bf16[4,1024,256]{2,1,0:T(8,128)(2,1)} %bitcast.45), calls=%async_computation.4 | async-start | bytes 4194304 | tf_op jit(solution)/shard_map/all_to_all | solution.py:315
  114.0 46.0 %reduce-scatter.2.cloned.1.call-start = ((), (), s32[]{:S(2)}) async-start(), calls=%async_computation.6 | async-start | bytes 1179648 | tf_op jit(solution)/shard_map/reduce_scatter | solution.py:311
  140.1 21.7 %all-to-all-start.4 = ((bf16[8,128,256]{2,1,0:T(8,128)(2,1)}), bf16[8,128,256]{2,1,0:T(8,128)(2,1)S(1)}, u32[]{:S(2)}, u32[]{:S(2)}) async-start(bf16[8,128,256]{2,1,0:T(8,128)(2,1)} %bitcast.19), calls=%async_computation.5 | async-start | bytes 1048576 | tf_op jit(solution)/shard_map/all_to_all | solution.py:317
Sparse Core Ops, SparseCore 0:
  10.5 50.5 all-gather.2
  117.6 42.2 reduce-scatter.1

commit v3 on v2

--- a/solution.py
+++ b/solution.py
@@ -14,6 +14,8 @@
 ROWS = TILE * HQ
 NQ = 16
 NK = 32
+NY = 8
+NZ = 8
 QPAD = 272
 LOW = -1e30
 SCALE = 1.0 / math.sqrt(HD)
@@ -42,11 +44,15 @@
     return (count_ref[0] + (per_step - 1)) // per_step
 
 
-def stats_kernel(pairs_ref, count_ref, q_hbm, kv_hbm, out_ref, q_ref, k_ref, m_ref, l_ref, sems):
-    copies = (
-        pltpu.make_async_copy(q_hbm.at[:, pl.ds(0, TILE), :], q_ref, sems.at[0]),
-        pltpu.make_async_copy(kv_hbm.at[:, :, pl.ds(0, HD)], k_ref, sems.at[1]),
-    )
+def stats_kernel(
+    pairs_ref, count_ref, q_hbm, kv0, kv1, kv2, kv3, out_ref, q_ref, k_ref, m_ref, l_ref, sems
+):
+    copies = [pltpu.make_async_copy(q_hbm.at[:, pl.ds(0, TILE), :], q_ref, sems.at[0])]
+    for n, piece in enumerate((kv0, kv1, kv2, kv3)):
+        source = piece.at[:, pl.ds(0, TILE), pl.ds(0, HD)]
+        copies.append(
+            pltpu.make_async_copy(source, k_ref.at[pl.ds(n * NY, NY)], sems.at[n + 1])
+        )
     for copy in copies:
         copy.start()
     m_ref[...] = jnp.full(m_ref.shape, LOW, jnp.float32)
@@ -83,22 +89,23 @@
     return probs, (probs * (grad_probs - delta)).astype(jnp.bfloat16)
 
 
-def load(q_hbm, kv_hbm, total_hbm, q_ref, kv_ref, total_ref, sems):
-    copies = (
-        pltpu.make_async_copy(q_hbm, q_ref, sems.at[0]),
-        pltpu.make_async_copy(kv_hbm, kv_ref, sems.at[1]),
-        pltpu.make_async_copy(total_hbm, total_ref, sems.at[2]),
-    )
+def load(q_hbm, pieces, q_ref, kv_ref, sems):
+    copies = [pltpu.make_async_copy(q_hbm, q_ref, sems.at[0])]
+    for n, piece in enumerate(pieces):
+        source = piece.at[:, pl.ds(0, TILE), :]
+        copies.append(
+            pltpu.make_async_copy(source, kv_ref.at[pl.ds(n * NY, NY)], sems.at[n + 1])
+        )
     for copy in copies:
         copy.start()
     return copies
 
 
 def query_kernel(
-    pairs_ref, count_ref, core_ref, q_hbm, kv_hbm, total_hbm, out_ref,
-    q_ref, kv_ref, total_ref, acc, ds_ref, sems,
+    pairs_ref, count_ref, core_ref, q_hbm, kv0, kv1, kv2, kv3, total_ref, kept_ref, sent_ref,
+    q_ref, kv_ref, acc, ds_ref, sems,
 ):
-    copies = load(q_hbm, kv_hbm, total_hbm, q_ref, kv_ref, total_ref, sems)
+    copies = load(q_hbm, (kv0, kv1, kv2, kv3), q_ref, kv_ref, sems)
     acc[...] = jnp.zeros(acc.shape, jnp.float32)
     for copy in copies:
         copy.wait()
@@ -113,17 +120,36 @@
         return carry
 
     lax.fori_loop(0, blocks_of(count_ref, STEP), visit, 0)
-    core = core_ref[0]
-    for r in range(NQ):
-        out_ref[(r // 8) ^ core, r % 8] = acc[r].astype(jnp.bfloat16)
+    mine = core_ref[0] * NZ
+    for n in range(NZ):
+        kept_ref[n] = acc[mine + n].astype(jnp.bfloat16)
+        sent_ref[n] = acc[NZ - mine + n].astype(jnp.bfloat16)
 
 
 def key_kernel(
-    pairs_ref, count_ref, q_hbm, kv_hbm, total_hbm, out_ref,
-    q_ref, kv_ref, total_ref, acc, p_ref, ds_ref, sems,
+    pairs_ref, count_ref, core_ref, q_hbm, kv0, kv1, kv2, kv3, total_ref, own_ref, far_ref,
+    kept_hbm, got_hbm, chip_hbm, out0, out1, out2, out3,
+    q_ref, kv_ref, acc, p_ref, ds_ref, kept_ref, got_ref, chip_ref, sems,
 ):
-    copies = load(q_hbm, kv_hbm, total_hbm, q_ref, kv_ref, total_ref, sems)
+    two = (
+        pltpu.make_async_copy(kept_hbm, kept_ref, sems.at[5]),
+        pltpu.make_async_copy(got_hbm, got_ref, sems.at[6]),
+    )
+    for copy in two:
+        copy.start()
+    copies = load(q_hbm, (kv0, kv1, kv2, kv3), q_ref, kv_ref, sems)
     acc[...] = jnp.zeros(acc.shape, jnp.float32)
+    for copy in two:
+        copy.wait()
+    for n in range(NZ):
+        r = core_ref[0] * NZ + n
+        own = jnp.exp2(own_ref[r] - total_ref[r])
+        far = jnp.exp2(far_ref[r] - total_ref[r])
+        chip_ref[n] = (
+            kept_ref[n].astype(jnp.float32) * own + got_ref[n].astype(jnp.float32) * far
+        ).astype(jnp.bfloat16)
+    leave = pltpu.make_async_copy(chip_ref, chip_hbm, sems.at[7])
+    leave.start()
     for copy in copies:
         copy.wait()
 
@@ -146,7 +172,9 @@
         return carry
 
     lax.fori_loop(0, blocks_of(count_ref, STEP), visit, 0)
-    out_ref[...] = acc[:NK].astype(jnp.bfloat16)
+    for n, out_ref in enumerate((out0, out1, out2, out3)):
+        out_ref[...] = acc[n * NY : (n + 1) * NY].astype(jnp.bfloat16)
+    leave.wait()
 
 
 def vmem():
@@ -161,15 +189,18 @@
     return pl.BlockSpec(memory_space=pl.ANY)
 
 
-def params(mib):
-    return pltpu.CompilerParams(vmem_limit_bytes=mib * 1024 * 1024)
+def params():
+    return pltpu.CompilerParams(vmem_limit_bytes=60 * 1024 * 1024)
+
+
+def cost(mib):
+    return pl.CostEstimate(flops=10_000_000_000, bytes_accessed=mib << 20, transcendentals=0)
 
 
 def loaded():
     return [
         pltpu.VMEM((NQ, QPAD, ROWS), jnp.bfloat16),
         pltpu.VMEM((NK, TILE, 2 * HD), jnp.bfloat16),
-        pltpu.VMEM((NQ, 1, ROWS), jnp.float32),
     ]
 
 
@@ -177,62 +208,62 @@
     return pl.pallas_call(
         stats_kernel,
         out_shape=jax.ShapeDtypeStruct((NQ, 1, ROWS), jnp.float32),
-        in_specs=[smem(), smem(), anywhere(), anywhere()],
+        in_specs=[smem(), smem()] + [anywhere()] * 5,
         out_specs=vmem(),
         scratch_shapes=[
             pltpu.VMEM((NQ, TILE, ROWS), jnp.bfloat16),
             pltpu.VMEM((NK, TILE, HD), jnp.bfloat16),
             pltpu.VMEM((NQ + 1, 1, ROWS), jnp.float32),
             pltpu.VMEM((NQ + 1, 1, ROWS), jnp.float32),
-            pltpu.SemaphoreType.DMA((2,)),
+            pltpu.SemaphoreType.DMA((5,)),
         ],
-        compiler_params=params(60),
-        cost_estimate=pl.CostEstimate(
-            flops=10_000_000_000, bytes_accessed=4 << 20, transcendentals=0
-        ),
+        compiler_params=params(),
+        cost_estimate=cost(4),
         name="row_statistics",
-    )(pairs, count, q, kv)
-
-
-def call_query(pairs, count, core, q, kv, total):
+    )(pairs, count, q, *kv)
+
+
+def call_query(pairs, count, core, q, kv, part):
+    half = jax.ShapeDtypeStruct((NZ, HD, ROWS), jnp.bfloat16)
     return pl.pallas_call(
         query_kernel,
-        out_shape=jax.ShapeDtypeStruct((2, NQ // 2, HD, ROWS), jnp.bfloat16),
-        in_specs=[smem(), smem(), smem(), anywhere(), anywhere(), anywhere()],
-        out_specs=vmem(),
+        out_shape=(half, half),
+        in_specs=[smem()] * 3 + [anywhere()] * 5 + [vmem()],
+        out_specs=(vmem(), vmem()),
         scratch_shapes=loaded()
         + [
             pltpu.VMEM((NQ + 1, HD, ROWS), jnp.float32),
             pltpu.VMEM((STEP, TILE, ROWS), jnp.bfloat16),
-            pltpu.SemaphoreType.DMA((3,)),
+            pltpu.SemaphoreType.DMA((5,)),
         ],
-        compiler_params=params(60),
-        cost_estimate=pl.CostEstimate(
-            flops=10_000_000_000, bytes_accessed=8 << 20, transcendentals=0
-        ),
+        compiler_params=params(),
+        cost_estimate=cost(8),
         name="query_gradient",
-    )(pairs, count, core, q, kv, total)
-
-
-def call_key(pairs, count, q, kv, total):
+    )(pairs, count, core, q, *kv, part)
+
+
+def call_key(pairs, count, core, q, kv, total, own, far, kept, got):
+    quarter = jax.ShapeDtypeStruct((NY, TILE, 2 * HD), jnp.bfloat16)
+    half = pltpu.VMEM((NZ, HD, ROWS), jnp.bfloat16)
     return pl.pallas_call(
         key_kernel,
-        out_shape=jax.ShapeDtypeStruct((NK, TILE, 2 * HD), jnp.bfloat16),
-        in_specs=[smem(), smem(), anywhere(), anywhere(), anywhere()],
-        out_specs=vmem(),
+        out_shape=(jax.ShapeDtypeStruct((NZ, HD, ROWS), jnp.bfloat16),) + (quarter,) * 4,
+        in_specs=[smem()] * 3 + [anywhere()] * 5 + [vmem()] * 3 + [anywhere()] * 2,
+        out_specs=(anywhere(),) + (vmem(),) * 4,
         scratch_shapes=loaded()
         + [
             pltpu.VMEM((NK + 1, TILE, 2 * HD), jnp.float32),
             pltpu.VMEM((STEP, TILE, ROWS), jnp.bfloat16),
             pltpu.VMEM((STEP, TILE, ROWS), jnp.bfloat16),
-            pltpu.SemaphoreType.DMA((3,)),
+            half,
+            half,
+            half,
+            pltpu.SemaphoreType.DMA((8,)),
         ],
-        compiler_params=params(60),
-        cost_estimate=pl.CostEstimate(
-            flops=10_000_000_000, bytes_accessed=8 << 20, transcendentals=0
-        ),
+        compiler_params=params(),
+        cost_estimate=cost(8),
         name="key_gradient",
-    )(pairs, count, q, kv, total)
+    )(pairs, count, core, q, *kv, total, own, far, kept, got)
 
 
 def to_everyone(value, axis):
@@ -240,6 +271,10 @@
     return lax.all_to_all(
         jnp.broadcast_to(value[None], (peers, *value.shape)), axis, 0, 0, tiled=True
     )
+
+
+def along_x(value, by):
+    return lax.ppermute(value, "x", [(n, (n + by) % 4) for n in range(4)])
 
 
 def swap_cores(value):
@@ -271,12 +306,12 @@
     q_own = jnp.concatenate([query_states, out_grad, delta_rows], axis=0)
     q_all = lax.all_gather(q_own, ("c", "z"), axis=0, tiled=False)
 
-    mask_rows = jnp.pad(block_mask.astype(jnp.bfloat16).reshape(2, 2 * HD), ((0, 6), (0, 0)))
+    mask_rows = jnp.pad(block_mask.astype(jnp.bfloat16).reshape(2, 2 * HD), ((0, 14), (0, 0)))
     kv_own = jnp.concatenate(
         [jnp.concatenate([key_states, value_states], axis=1), mask_rows], axis=0
     )
     kv_y = to_everyone(kv_own, Y)
-    kv_all = to_everyone(kv_y[:, :TILE], "x").reshape(NK, TILE, 2 * HD)
+    kv_all = (kv_y, along_x(kv_y, 1), along_x(kv_y, -1), along_x(kv_y, 2))
 
     mine = lax.dynamic_slice_in_dim(kv_y[:, TILE : TILE + 2], y_lo * 2, 2, 0)
     mine = mine.reshape(2, 16, 32)
@@ -287,34 +322,32 @@
     both = lax.dynamic_slice_in_dim(both, y_hi * 8, 8, 2)
     both = both.reshape(2, 2, 8, 16, 2)
     both = jnp.where(core == 0, both[..., 0], both[..., 1])
-    mask = both.transpose(0, 2, 3, 1).reshape(NQ, NK)
+    mask = both.transpose(0, 2, 3, 1).reshape(NQ, 4, NY)
+    turned = lax.dynamic_slice_in_dim(jnp.concatenate([mask, mask], 1), lax.axis_index("x"), 4, 1)
+    mask = jnp.concatenate([turned[:, :1], turned[:, 3:], turned[:, 1:3]], axis=1).reshape(NQ, NK)
     pairs, count = list_pairs(mask)
 
     part = call_stats(pairs, count, q_all, kv_all)
     parts = to_everyone(part.reshape(NQ * ROWS // HD, HD), ("c", "z"))
-    dq = call_query(pairs, count, core[None], q_all, kv_all, part)
-    kept, got = dq[0], swap_cores(dq[1])
+    kept, sent = call_query(pairs, count, core[None], q_all, kv_all, part)
+    got = swap_cores(sent)
 
     top = jnp.max(parts, axis=0)
     total = top + jnp.log2(jnp.sum(jnp.exp2(parts - top[None]), axis=0))
-    dkv = call_key(pairs, count, q_all, kv_all, total.reshape(NQ, 1, ROWS))
-
-    own_part = lax.dynamic_index_in_dim(parts, core * 8 + lax.axis_index("z"), 0, False)
-    far_part = lax.dynamic_index_in_dim(parts, (1 - core) * 8 + lax.axis_index("z"), 0, False)
-    own_w, far_w = (
-        lax.dynamic_slice_in_dim(jnp.exp2(p - total), core * 32, 32, 0).reshape(8, 1, ROWS)
-        for p in (own_part, far_part)
-    )
-    chip = (kept.astype(jnp.float32) * own_w + got.astype(jnp.float32) * far_w).astype(
-        jnp.bfloat16
-    )
+    total = total.reshape(NQ, 1, ROWS)
+    far = lax.dynamic_index_in_dim(parts, (1 - core) * NZ + lax.axis_index("z"), 0, False)
+    far = far.reshape(NQ, 1, ROWS)
+    chip, here, back, ahead, across = call_key(
+        pairs, count, core[None], q_all, kv_all, total, part, far, kept, got
+    )
+
     dq_own = lax.psum_scatter(chip, "z", scatter_dimension=0, tiled=True)[0]
     dq_own = (dq_own.astype(jnp.float32) * SCALE).astype(jnp.bfloat16)
     query_grad = dq_own.reshape(HD, HQ, TILE).transpose(2, 1, 0).reshape(TILE, HQ * HD)
 
-    over_x = lax.all_to_all(dkv.reshape(4, 8 * TILE, 2 * HD), "x", 0, 0, tiled=True)
-    over_x = over_x.astype(jnp.float32).sum(axis=0).astype(jnp.bfloat16)
-    over_y = lax.all_to_all(over_x.reshape(8, TILE, 2 * HD), Y, 0, 0, tiled=True)
+    over_x = (here, along_x(across, 2), along_x(back, -1), along_x(ahead, 1))
+    over_x = sum(p.astype(jnp.float32) for p in over_x).astype(jnp.bfloat16)
+    over_y = lax.all_to_all(over_x, Y, 0, 0, tiled=True)
     sums = over_y.astype(jnp.float32).sum(axis=0)
     key_grad = (sums[:, :HD] * SCALE).astype(jnp.bfloat16)
     value_grad = sums[:, HD:].astype(jnp.bfloat16)

time: 171 us -> 180 us (1.053)
  the two profiles are of different devices: /device:TPU:2 before, /device:TPU:75 now
where the time goes in v3:
time: 180 us; the launch traced here: 179 us
  waiting for transfers between devices  59.8 us (33%)
  starting transfers between devices  35.4 us (20%)
  Pallas kernels  32.7 us (18%)
  blocking collectives  19 us (11%)
  between operations  14.3 us (8%)
  other arithmetic  10.1 us (6%)
  local copies, waits for them, and re-layouts  8.12 us (5%)
    ppermute x6, waiting for transfers between devices, along_x(): return lax.ppermute(value, 'x', [(n, (n + by) % 4) for n in range(4)])  40.5 us
    all_to_all x2, waiting for transfers between devices, to_everyone(): lax.all_to_all(jnp.broadcast_to(value[None], (peers, *value.shape)), axis...  19.2 us
    all_to_all x1, blocking collectives, body(): over_y = lax.all_to_all(over_x, Y, 0, 0, tiled=True)  19 us
    ppermute x6, starting transfers between devices, along_x(): return lax.ppermute(value, 'x', [(n, (n + by) % 4) for n in range(4)])  16.2 us
    all_to_all x2, starting transfers between devices, to_everyone(): lax.all_to_all(jnp.broadcast_to(value[None], (peers, *value.shape)), axis...  14.7 us
    pallas_call x1, Pallas kernels, call_key(): pl.pallas_call(key_kernel, out_shape=(jax.ShapeDtypeStruct((NZ, HD, ROWS)...  13.4 us
    pallas_call x1, Pallas kernels, call_query(): pl.pallas_call(query_kernel, out_shape=(half, half), in_specs=[smem()] *...  11.3 us
    pallas_call x1, Pallas kernels, call_stats(): pl.pallas_call(stats_kernel, out_shape=jax.ShapeDtypeStruct((NQ, 1, ROWS)...  8.04 us
  transfers between devices with their start and end apart: 12, of which 6 were waited for; matrix products, arithmetic and copies ran while one was open for 5% of the time, Pallas kernels for 6%

profile of v3, /device:TPU:75, one launch (start us, length us, event | category | flops | bytes accessed | tf_op | source)
XLA Modules:
  0.0 179.4 jit_solution(16250365643283008487)
XLA Ops:
  7.2 1.0 convert_multiply_fusion
  8.6 1.7 fusion.2
  12.8 7.0 %all-to-all-start = ((bf16[8,144,256]{2,1,0:T(8,128)(2,1)}), bf16[8,144,256]{2,1,0:T(8,128)(2,1)S(1)}, u32[]{:S(2)}, u32[]{:S(2)}) async-start(bf16[8,144,256]{2,1,0:T(8,128)(2,1)} %broadcast_in_dim.52), calls=%async_computation | async-start | bytes 1179648 | tf_op jit(solution)/shard_map/all_to_all | solution.py:271
  19.8 17.3 %all-to-all-done.kv0 = bf16[8,144,256]{2,1,0:T(8,128)(2,1)S(1)} async-done(((bf16[8,144,256]{2,1,0:T(8,128)(2,1)}), bf16[8,144,256]{2,1,0:T(8,128)(2,1)S(1)}, u32[]{:S(2)}, u32[]{:S(2)}) %all-to-all-start) | async-done | bytes 589856 | tf_op jit(solution)/shard_map/all_to_all | solution.py:271
  37.2 2.5 %collective-permute-start = (bf16[2,16,32]{2,1,0:T(8,128)(2,1)S(1)}, bf16[2,16,32]{2,1,0:T(8,128)(2,1)S(1)}, u32[]{:S(2)}, u32[]{:S(2)}) collective-permute-start(bf16[2,16,32]{2,1,0:T(8,128)(2,1)S(1)} %reshape.105), channel_id=1, source_target_pairs={{0,16},{16,0},{1,17},{17,1},{2,18},{18,2},{3,19},{19,3},{4,20},{20... | collective-permute-start | bytes 6152 | tf_op jit(solution)/shard_map/ppermute | solution.py:281
  39.7 3.8 %collective-permute-start.3 = (bf16[8,144,256]{2,1,0:T(8,128)(2,1)S(1)}, bf16[8,144,256]{2,1,0:T(8,128)(2,1)S(1)}, u32[]{:S(2)}, u32[]{:S(2)}) collective-permute-start(bf16[8,144,256]{2,1,0:T(8,128)(2,1)S(1)} %all-to-all-done.kv0), channel_id=1, source_target_pairs={{0,256},{128,384},{256,0},{384,128},{1,257},{129,385},{257,1},{385... | collective-permute-start | bytes 1769480 | tf_op jit(solution)/shard_map/ppermute | solution.py:277
  43.5 3.1 %collective-permute-start.2 = (bf16[8,144,256]{2,1,0:T(8,128)(2,1)S(1)}, bf16[8,144,256]{2,1,0:T(8,128)(2,1)S(1)}, u32[]{:S(2)}, u32[]{:S(2)}) collective-permute-start(bf16[8,144,256]{2,1,0:T(8,128)(2,1)S(1)} %all-to-all-done.kv0), channel_id=1, source_target_pairs={{0,384},{128,0},{256,128},{384,256},{1,385},{129,1},{257,129},{385... | collective-permute-start | bytes 1769480 | tf_op jit(solution)/shard_map/ppermute | solution.py:277
  46.6 2.2 %collective-permute-start.1 = (bf16[8,144,256]{2,1,0:T(8,128)(2,1)S(1)}, bf16[8,144,256]{2,1,0:T(8,128)(2,1)S(1)}, u32[]{:S(2)}, u32[]{:S(2)}) collective-permute-start(bf16[8,144,256]{2,1,0:T(8,128)(2,1)S(1)} %all-to-all-done.kv0), channel_id=1, source_target_pairs={{0,128},{128,256},{256,384},{384,0},{1,129},{129,257},{257,385},{3... | collective-permute-start | bytes 1769480 | tf_op jit(solution)/shard_map/ppermute | solution.py:277
  52.0 6.2 %collective-permute-done.3.kv3 = bf16[8,144,256]{2,1,0:T(8,128)(2,1)S(1)} collective-permute-done((bf16[8,144,256]{2,1,0:T(8,128)(2,1)S(1)}, bf16[8,144,256]{2,1,0:T(8,128)(2,1)S(1)}, u32[]{:S(2)}, u32[]{:S(2)}) %collective-permute-start.3) | collective-permute-done | bytes 589856 | tf_op jit(solution)/shard_map/ppermute | solution.py:277
  58.1 12.9 %collective-permute-done.2.kv2 = bf16[8,144,256]{2,1,0:T(8,128)(2,1)S(1)} collective-permute-done((bf16[8,144,256]{2,1,0:T(8,128)(2,1)S(1)}, bf16[8,144,256]{2,1,0:T(8,128)(2,1)S(1)}, u32[]{:S(2)}, u32[]{:S(2)}) %collective-permute-start.2) | collective-permute-done | bytes 589856 | tf_op jit(solution)/shard_map/ppermute | solution.py:277
  72.1 8.0 %row_statistics.1.total_ref.own_ref = f32[16,1,512]{2,1,0:T(1,128)} custom-call(s32[516]{0:T(1024)} %pad.13.pairs_ref, s32[1]{0:T(128)} %bitcast.5.count_ref, bf16[16,272,512]{2,1,0:T(8,128)(2,1)} %bitcast.40, bf16[8,144,256]{2,1,0:T(8,128)(2,1)} %copy-done, bf16[8,144,256]{2,1,0:T(8,128)(2,1)} %copy-done.4, bf16[8,144,256]{2,1,0:T(8,128)(2,1)} %copy-done.3, ...), custom_call_target="tpu_custom_call" | custom-call | flops 10000000000 | bytes 4194304 | tf_op jit(solution)/shard_map/row_statistics/pallas_call | solution.py:208
  80.2 1.6 broadcast_in_dim.60
  81.8 7.7 %all-to-all-start.1 = ((f32[16,64,128]{2,1,0:T(8,128)}), f32[16,64,128]{2,1,0:T(8,128)S(1)}, u32[]{:S(2)}, u32[]{:S(2)}) async-start(f32[16,64,128]{2,1,0:T(8,128)} %broadcast_in_dim.60), calls=%async_computation.1 | async-start | bytes 1048576 | tf_op jit(solution)/shard_map/all_to_all | solution.py:271
  89.6 11.3 %query_gradient.1 = (bf16[8,128,512]{2,1,0:T(8,128)(2,1)}, bf16[8,128,512]{2,1,0:T(8,128)(2,1)}) custom-call(s32[516]{0:T(1024)} %pad.13.pairs_ref, s32[1]{0:T(128)} %bitcast.5.count_ref, s32[1]{0:T(128)} %bitcast.6.core_ref, bf16[16,272,512]{2,1,0:T(8,128)(2,1)} %bitcast.41, bf16[8,144,256]{2,1,0:T(8,128)(2,1)} %copy-done, bf16[8,144,256]{2,1,0:T(8,128)(2,1)} %copy-done.4, ...), custom_call_target="tpu_custom_call" | custom-call | flops 10000000000 | bytes 8388608 | tf_op jit(solution)/shard_map/query_gradient/pallas_call | solution.py:228
  100.9 1.9 %collective-permute-start.4 = (bf16[8,128,512]{2,1,0:T(8,128)(2,1)}, bf16[8,128,512]{2,1,0:T(8,128)(2,1)S(1)}, u32[]{:S(2)}, u32[]{:S(2)}) collective-permute-start(bf16[8,128,512]{2,1,0:T(8,128)(2,1)} %get-tuple-element.11), channel_id=1, source_target_pairs={{0,16},{16,0},{1,17},{17,1},{2,18},{18,2},{3,19},{19,3},{4,20},{20... | collective-permute-start | bytes 3145736 | tf_op jit(solution)/shard_map/ppermute | solution.py:281
  102.8 1.9 %all-to-all-done.1 = f32[16,64,128]{2,1,0:T(8,128)S(1)} async-done(((f32[16,64,128]{2,1,0:T(8,128)}), f32[16,64,128]{2,1,0:T(8,128)S(1)}, u32[]{:S(2)}, u32[]{:S(2)}) %all-to-all-start.1) | async-done | bytes 524320 | tf_op jit(solution)/shard_map/all_to_all | solution.py:271
  107.1 13.4 %key_gradient.1 = (bf16[8,128,512]{2,1,0:T(8,128)(2,1)}, bf16[8,128,256]{2,1,0:T(8,128)(2,1)}, bf16[8,128,256]{2,1,0:T(8,128)(2,1)}, bf16[8,128,256]{2,1,0:T(8,128)(2,1)}, bf16[8,128,256]{2,1,0:T(8,128)(2,1)}) custom-call(s32[516]{0:T(1024)} %pad.13.pairs_ref, s32[1]{0:T(128)} %bitcast.5.count_ref, s32[1]{0:T(128)} %bitcast.6.core_ref, ...), custom_call_target="tpu_custom_call" | custom-call | flops 10000000000 | bytes 8388608 | tf_op jit(solution)/shard_map/key_gradient/pallas_call | solution.py:248
  120.5 1.9 %collective-permute-start.5 = (bf16[8,128,256]{2,1,0:T(8,128)(2,1)}, bf16[8,128,256]{2,1,0:T(8,128)(2,1)S(1)}, u32[]{:S(2)}, u32[]{:S(2)}) collective-permute-start(bf16[8,128,256]{2,1,0:T(8,128)(2,1)} %get-tuple-element.14), channel_id=1, source_target_pairs={{0,256},{128,384},{256,0},{384,128},{1,257},{129,385},{257,1},{385... | collective-permute-start | bytes 1572872 | tf_op jit(solution)/shard_map/ppermute | solution.py:277
  122.4 3.3 %collective-permute-start.6 = (bf16[8,128,256]{2,1,0:T(8,128)(2,1)}, bf16[8,128,256]{2,1,0:T(8,128)(2,1)S(1)}, u32[]{:S(2)}, u32[]{:S(2)}) collective-permute-start(bf16[8,128,256]{2,1,0:T(8,128)(2,1)} %get-tuple-element.15), channel_id=1, source_target_pairs={{0,384},{128,0},{256,128},{384,256},{1,385},{129,1},{257,129},{385... | collective-permute-start | bytes 1572872 | tf_op jit(solution)/shard_map/ppermute | solution.py:277
  125.7 2.0 %collective-permute-start.7 = (bf16[8,128,256]{2,1,0:T(8,128)(2,1)}, bf16[8,128,256]{2,1,0:T(8,128)(2,1)S(1)}, u32[]{:S(2)}, u32[]{:S(2)}) collective-permute-start(bf16[8,128,256]{2,1,0:T(8,128)(2,1)} %get-tuple-element.16), channel_id=1, source_target_pairs={{0,128},{128,256},{256,384},{384,0},{1,129},{129,257},{257,385},{3... | collective-permute-start | bytes 1572872 | tf_op jit(solution)/shard_map/ppermute | solution.py:277
  127.7 10.1 %collective-permute-done.5 = bf16[8,128,256]{2,1,0:T(8,128)(2,1)S(1)} collective-permute-done((bf16[8,128,256]{2,1,0:T(8,128)(2,1)}, bf16[8,128,256]{2,1,0:T(8,128)(2,1)S(1)}, u32[]{:S(2)}, u32[]{:S(2)}) %collective-permute-start.5) | collective-permute-done | bytes 524320 | tf_op jit(solution)/shard_map/ppermute | solution.py:277
  137.8 11.3 %collective-permute-done.6 = bf16[8,128,256]{2,1,0:T(8,128)(2,1)S(1)} collective-permute-done((bf16[8,128,256]{2,1,0:T(8,128)(2,1)}, bf16[8,128,256]{2,1,0:T(8,128)(2,1)S(1)}, u32[]{:S(2)}, u32[]{:S(2)}) %collective-permute-start.6) | collective-permute-done | bytes 524320 | tf_op jit(solution)/shard_map/ppermute | solution.py:277
  149.1 1.3 add_convert_fusion
  150.4 19.0 %all_to_all.15 = bf16[8,128,256]{2,1,0:T(8,128)(2,1)S(1)} all-to-all(bf16[8,128,256]{2,1,0:T(8,128)(2,1)S(1)} %add_convert_fusion), channel_id=1, replica_groups=mesh['x'=4,'yl'=4,'c'=2,'yh'=2,'z'=8] {'yl','yh'}, dimensions={0} | all-to-all | bytes 1048576 | tf_op jit(solution)/shard_map/all_to_all | solution.py:350
  (61 shorter events, 12.7 us)
Async XLA Ops:
  7.2 63.9 %all-gather.3.cloned.1.call-start = ((), (), s32[]{:S(2)}) async-start(), calls=%async_computation.5 | async-start | bytes 4734976 | tf_op jit(solution)/shard_map/all_gather | solution.py:307
  12.8 24.3 %all-to-all-start = ((bf16[8,144,256]{2,1,0:T(8,128)(2,1)}), bf16[8,144,256]{2,1,0:T(8,128)(2,1)S(1)}, u32[]{:S(2)}, u32[]{:S(2)}) async-start(bf16[8,144,256]{2,1,0:T(8,128)(2,1)} %broadcast_in_dim.52), calls=%async_computation | async-start | bytes 1179648 | tf_op jit(solution)/shard_map/all_to_all | solution.py:271
  37.1 34.0 %copy-start = (bf16[8,144,256]{2,1,0:T(8,128)(2,1)}, bf16[8,144,256]{2,1,0:T(8,128)(2,1)S(1)}, u32[]{:S(2)}) copy-start(bf16[8,144,256]{2,1,0:T(8,128)(2,1)S(1)} %all-to-all-done.kv0) | copy-start | bytes 1769476
  37.2 11.6 %collective-permute-start = (bf16[2,16,32]{2,1,0:T(8,128)(2,1)S(1)}, bf16[2,16,32]{2,1,0:T(8,128)(2,1)S(1)}, u32[]{:S(2)}, u32[]{:S(2)}) collective-permute-start(bf16[2,16,32]{2,1,0:T(8,128)(2,1)S(1)} %reshape.105), channel_id=1, source_target_pairs={{0,16},{16,0},{1,17},{17,1},{2,18},{18,2},{3,19},{19,3},{4,20},{20... | collective-permute-start | bytes 6152 | tf_op jit(solution)/shard_map/ppermute | solution.py:281
  39.7 18.4 %collective-permute-start.3 = (bf16[8,144,256]{2,1,0:T(8,128)(2,1)S(1)}, bf16[8,144,256]{2,1,0:T(8,128)(2,1)S(1)}, u32[]{:S(2)}, u32[]{:S(2)}) collective-permute-start(bf16[8,144,256]{2,1,0:T(8,128)(2,1)S(1)} %all-to-all-done.kv0), channel_id=1, source_target_pairs={{0,256},{128,384},{256,0},{384,128},{1,257},{129,385},{257,1},{385... | collective-permute-start | bytes 1769480 | tf_op jit(solution)/shard_map/ppermute | solution.py:277
  43.5 27.6 %collective-permute-start.2 = (bf16[8,144,256]{2,1,0:T(8,128)(2,1)S(1)}, bf16[8,144,256]{2,1,0:T(8,128)(2,1)S(1)}, u32[]{:S(2)}, u32[]{:S(2)}) collective-permute-start(bf16[8,144,256]{2,1,0:T(8,128)(2,1)S(1)} %all-to-all-done.kv0), channel_id=1, source_target_pairs={{0,384},{128,0},{256,128},{384,256},{1,385},{129,1},{257,129},{385... | collective-permute-start | bytes 1769480 | tf_op jit(solution)/shard_map/ppermute | solution.py:277
  46.6 24.5 %collective-permute-start.1 = (bf16[8,144,256]{2,1,0:T(8,128)(2,1)S(1)}, bf16[8,144,256]{2,1,0:T(8,128)(2,1)S(1)}, u32[]{:S(2)}, u32[]{:S(2)}) collective-permute-start(bf16[8,144,256]{2,1,0:T(8,128)(2,1)S(1)} %all-to-all-done.kv0), channel_id=1, source_target_pairs={{0,128},{128,256},{256,384},{384,0},{1,129},{129,257},{257,385},{3... | collective-permute-start | bytes 1769480 | tf_op jit(solution)/shard_map/ppermute | solution.py:277
  58.1 13.0 %copy-start.2 = (bf16[8,144,256]{2,1,0:T(8,128)(2,1)}, bf16[8,144,256]{2,1,0:T(8,128)(2,1)S(1)}, u32[]{:S(2)}) copy-start(bf16[8,144,256]{2,1,0:T(8,128)(2,1)S(1)} %collective-permute-done.3.kv3) | copy-start | bytes 1769476
  71.0 0.9 copy-start.3
  71.1 1.1 copy-start.4
  81.8 22.9 %all-to-all-start.1 = ((f32[16,64,128]{2,1,0:T(8,128)}), f32[16,64,128]{2,1,0:T(8,128)S(1)}, u32[]{:S(2)}, u32[]{:S(2)}) async-start(f32[16,64,128]{2,1,0:T(8,128)} %broadcast_in_dim.60), calls=%async_computation.1 | async-start | bytes 1048576 | tf_op jit(solution)/shard_map/all_to_all | solution.py:271
  89.5 81.2 %reduce-scatter.2.cloned.1.call-start = ((), (), s32[]{:S(2)}) async-start(), calls=%async_computation.4 | async-start | bytes 1179648 | tf_op jit(solution)/shard_map/reduce_scatter | solution.py:344
  100.9 5.2 %collective-permute-start.4 = (bf16[8,128,512]{2,1,0:T(8,128)(2,1)}, bf16[8,128,512]{2,1,0:T(8,128)(2,1)S(1)}, u32[]{:S(2)}, u32[]{:S(2)}) collective-permute-start(bf16[8,128,512]{2,1,0:T(8,128)(2,1)} %get-tuple-element.11), channel_id=1, source_target_pairs={{0,16},{16,0},{1,17},{17,1},{2,18},{18,2},{3,19},{19,3},{4,20},{20... | collective-permute-start | bytes 3145736 | tf_op jit(solution)/shard_map/ppermute | solution.py:281
  106.1 1.0 copy-start.1
  120.5 17.3 %collective-permute-start.5 = (bf16[8,128,256]{2,1,0:T(8,128)(2,1)}, bf16[8,128,256]{2,1,0:T(8,128)(2,1)S(1)}, u32[]{:S(2)}, u32[]{:S(2)}) collective-permute-start(bf16[8,128,256]{2,1,0:T(8,128)(2,1)} %get-tuple-element.14), channel_id=1, source_target_pairs={{0,256},{128,384},{256,0},{384,128},{1,257},{129,385},{257,1},{385... | collective-permute-start | bytes 1572872 | tf_op jit(solution)/shard_map/ppermute | solution.py:277
  122.4 26.7 %collective-permute-start.6 = (bf16[8,128,256]{2,1,0:T(8,128)(2,1)}, bf16[8,128,256]{2,1,0:T(8,128)(2,1)S(1)}, u32[]{:S(2)}, u32[]{:S(2)}) collective-permute-start(bf16[8,128,256]{2,1,0:T(8,128)(2,1)} %get-tuple-element.15), channel_id=1, source_target_pairs={{0,384},{128,0},{256,128},{384,256},{1,385},{129,1},{257,129},{385... | collective-permute-start | bytes 1572872 | tf_op jit(solution)/shard_map/ppermute | solution.py:277
  125.7 23.5 %collective-permute-start.7 = (bf16[8,128,256]{2,1,0:T(8,128)(2,1)}, bf16[8,128,256]{2,1,0:T(8,128)(2,1)S(1)}, u32[]{:S(2)}, u32[]{:S(2)}) collective-permute-start(bf16[8,128,256]{2,1,0:T(8,128)(2,1)} %get-tuple-element.16), channel_id=1, source_target_pairs={{0,128},{128,256},{256,384},{384,0},{1,129},{129,257},{257,385},{3... | collective-permute-start | bytes 1572872 | tf_op jit(solution)/shard_map/ppermute | solution.py:277
Sparse Core Ops, SparseCore 0:
  10.5 49.4 all-gather.2
  120.6 32.3 reduce-scatter.1

commit v4 on v3

--- a/solution.py
+++ b/solution.py
@@ -17,6 +17,7 @@
 NY = 8
 NZ = 8
 QPAD = 272
+KPAD = 144
 LOW = -1e30
 SCALE = 1.0 / math.sqrt(HD)
 LOG2E = 1.0 / math.log(2.0)
@@ -45,14 +46,12 @@
 
 
 def stats_kernel(
-    pairs_ref, count_ref, q_hbm, kv0, kv1, kv2, kv3, out_ref, q_ref, k_ref, m_ref, l_ref, sems
+    pairs_ref, count_ref, q_hbm, kv_hbm, out_ref, sent_hbm, q_ref, k_ref, m_ref, l_ref, sems
 ):
-    copies = [pltpu.make_async_copy(q_hbm.at[:, pl.ds(0, TILE), :], q_ref, sems.at[0])]
-    for n, piece in enumerate((kv0, kv1, kv2, kv3)):
-        source = piece.at[:, pl.ds(0, TILE), pl.ds(0, HD)]
-        copies.append(
-            pltpu.make_async_copy(source, k_ref.at[pl.ds(n * NY, NY)], sems.at[n + 1])
-        )
+    copies = (
+        pltpu.make_async_copy(q_hbm.at[:, pl.ds(0, TILE), :], q_ref, sems.at[0]),
+        pltpu.make_async_copy(kv_hbm.at[:, :, pl.ds(0, HD)], k_ref, sems.at[1]),
+    )
     for copy in copies:
         copy.start()
     m_ref[...] = jnp.full(m_ref.shape, LOW, jnp.float32)
@@ -79,6 +78,11 @@
     out_ref[...] = jnp.where(
         total > 0.0, m_ref[...][:NQ] + jnp.log2(jnp.maximum(total, 1e-30)), LOW
     )
+    copies = [pltpu.make_async_copy(out_ref, sent_hbm.at[n], sems.at[n]) for n in range(NQ)]
+    for copy in copies:
+        copy.start()
+    for copy in copies:
+        copy.wait()
 
 
 def weights_of(q_ref, kv_ref, total_ref, rq, jk):
@@ -89,23 +93,21 @@
     return probs, (probs * (grad_probs - delta)).astype(jnp.bfloat16)
 
 
-def load(q_hbm, pieces, q_ref, kv_ref, sems):
-    copies = [pltpu.make_async_copy(q_hbm, q_ref, sems.at[0])]
-    for n, piece in enumerate(pieces):
-        source = piece.at[:, pl.ds(0, TILE), :]
-        copies.append(
-            pltpu.make_async_copy(source, kv_ref.at[pl.ds(n * NY, NY)], sems.at[n + 1])
-        )
+def load(q_hbm, kv_hbm, q_ref, kv_ref, sems):
+    copies = (
+        pltpu.make_async_copy(q_hbm, q_ref, sems.at[0]),
+        pltpu.make_async_copy(kv_hbm, kv_ref, sems.at[1]),
+    )
     for copy in copies:
         copy.start()
     return copies
 
 
 def query_kernel(
-    pairs_ref, count_ref, core_ref, q_hbm, kv0, kv1, kv2, kv3, total_ref, kept_ref, sent_ref,
+    pairs_ref, count_ref, core_ref, q_hbm, kv_hbm, total_ref, kept_ref, sent_ref,
     q_ref, kv_ref, acc, ds_ref, sems,
 ):
-    copies = load(q_hbm, (kv0, kv1, kv2, kv3), q_ref, kv_ref, sems)
+    copies = load(q_hbm, kv_hbm, q_ref, kv_ref, sems)
     acc[...] = jnp.zeros(acc.shape, jnp.float32)
     for copy in copies:
         copy.wait()
@@ -127,17 +129,17 @@
 
 
 def key_kernel(
-    pairs_ref, count_ref, core_ref, q_hbm, kv0, kv1, kv2, kv3, total_ref, own_ref, far_ref,
+    pairs_ref, count_ref, core_ref, x_ref, q_hbm, kv_hbm, total_ref, own_ref, far_ref,
     kept_hbm, got_hbm, chip_hbm, out0, out1, out2, out3,
     q_ref, kv_ref, acc, p_ref, ds_ref, kept_ref, got_ref, chip_ref, sems,
 ):
     two = (
-        pltpu.make_async_copy(kept_hbm, kept_ref, sems.at[5]),
-        pltpu.make_async_copy(got_hbm, got_ref, sems.at[6]),
+        pltpu.make_async_copy(kept_hbm, kept_ref, sems.at[2]),
+        pltpu.make_async_copy(got_hbm, got_ref, sems.at[3]),
     )
     for copy in two:
         copy.start()
-    copies = load(q_hbm, (kv0, kv1, kv2, kv3), q_ref, kv_ref, sems)
+    copies = load(q_hbm, kv_hbm, q_ref, kv_ref, sems)
     acc[...] = jnp.zeros(acc.shape, jnp.float32)
     for copy in two:
         copy.wait()
@@ -148,7 +150,7 @@
         chip_ref[n] = (
             kept_ref[n].astype(jnp.float32) * own + got_ref[n].astype(jnp.float32) * far
         ).astype(jnp.bfloat16)
-    leave = pltpu.make_async_copy(chip_ref, chip_hbm, sems.at[7])
+    leave = pltpu.make_async_copy(chip_ref, chip_hbm, sems.at[4])
     leave.start()
     for copy in copies:
         copy.wait()
@@ -173,8 +175,39 @@
 
     lax.fori_loop(0, blocks_of(count_ref, STEP), visit, 0)
     for n, out_ref in enumerate((out0, out1, out2, out3)):
-        out_ref[...] = acc[n * NY : (n + 1) * NY].astype(jnp.bfloat16)
+        first = pl.multiple_of(((x_ref[0] + n) & 3) * NY, NY)
+        out_ref[...] = acc[pl.ds(first, NY)].astype(jnp.bfloat16)
     leave.wait()
+
+
+def prepare_kernel(q_in, g_in, o_in, k_in, v_in, mask_in, q_ref, kv_hbm, kv_ref, sems):
+    kv_ref[:TILE, :HD] = k_in[...]
+    kv_ref[:TILE, HD:] = v_in[...]
+    kv_ref[TILE:, :] = jnp.zeros((KPAD - TILE, 2 * HD), jnp.bfloat16)
+    kv_ref[TILE:, :NK] = mask_in[...].astype(jnp.float32).astype(jnp.bfloat16)
+    copies = [pltpu.make_async_copy(kv_ref, kv_hbm.at[n], sems.at[n]) for n in range(NY)]
+    for copy in copies:
+        copy.start()
+    q_ref[:TILE] = q_in[...]
+    q_ref[TILE : 2 * TILE] = g_in[...]
+    for h in range(HQ):
+        cols = slice(h * HD, (h + 1) * HD)
+        product = g_in[:, cols].astype(jnp.float32) * o_in[:, cols].astype(jnp.float32)
+        delta = jnp.sum(product.T, axis=0, keepdims=True).astype(jnp.bfloat16)
+        q_ref[2 * TILE :, cols] = jnp.broadcast_to(delta, (QPAD - 2 * TILE, HD))
+    for copy in copies:
+        copy.wait()
+
+
+def finish_kernel(dq_ref, over_y_ref, query_ref, key_ref, value_ref):
+    for h in range(HQ):
+        cols = slice(h * TILE, (h + 1) * TILE)
+        query_ref[:, cols] = (dq_ref[:, cols].astype(jnp.float32).T * SCALE).astype(jnp.bfloat16)
+    sums = over_y_ref[0].astype(jnp.float32)
+    for n in range(1, NY):
+        sums += over_y_ref[n].astype(jnp.float32)
+    key_ref[...] = (sums[:, :HD] * SCALE).astype(jnp.bfloat16)
+    value_ref[...] = sums[:, HD:].astype(jnp.bfloat16)
 
 
 def vmem():
@@ -190,7 +223,7 @@
 
 
 def params():
-    return pltpu.CompilerParams(vmem_limit_bytes=60 * 1024 * 1024)
+    return pltpu.CompilerParams(vmem_limit_bytes=50 * 1024 * 1024)
 
 
 def cost(mib):
@@ -204,23 +237,54 @@
     ]
 
 
+def call_prepare(q, g, o, k, v, mask):
+    return pl.pallas_call(
+        prepare_kernel,
+        out_shape=(
+            jax.ShapeDtypeStruct((QPAD, ROWS), jnp.bfloat16),
+            jax.ShapeDtypeStruct((NY, KPAD, 2 * HD), jnp.bfloat16),
+        ),
+        in_specs=[vmem()] * 6,
+        out_specs=(vmem(), anywhere()),
+        scratch_shapes=[
+            pltpu.VMEM((KPAD, 2 * HD), jnp.bfloat16),
+            pltpu.SemaphoreType.DMA((NY,)),
+        ],
+        name="prepare",
+    )(q, g, o, k, v, mask)
+
+
+def call_finish(dq, over_y):
+    tile = jax.ShapeDtypeStruct((TILE, HD), jnp.bfloat16)
+    return pl.pallas_call(
+        finish_kernel,
+        out_shape=(jax.ShapeDtypeStruct((TILE, ROWS), jnp.bfloat16), tile, tile),
+        in_specs=[vmem()] * 2,
+        out_specs=(vmem(),) * 3,
+        name="finish",
+    )(dq, over_y)
+
+
 def call_stats(pairs, count, q, kv):
     return pl.pallas_call(
         stats_kernel,
-        out_shape=jax.ShapeDtypeStruct((NQ, 1, ROWS), jnp.float32),
-        in_specs=[smem(), smem()] + [anywhere()] * 5,
-        out_specs=vmem(),
+        out_shape=(
+            jax.ShapeDtypeStruct((NQ, 1, ROWS), jnp.float32),
+            jax.ShapeDtypeStruct((NQ, NQ, 1, ROWS), jnp.float32),
+        ),
+        in_specs=[smem()] * 2 + [anywhere()] * 2,
+        out_specs=(vmem(), anywhere()),
         scratch_shapes=[
             pltpu.VMEM((NQ, TILE, ROWS), jnp.bfloat16),
             pltpu.VMEM((NK, TILE, HD), jnp.bfloat16),
             pltpu.VMEM((NQ + 1, 1, ROWS), jnp.float32),
             pltpu.VMEM((NQ + 1, 1, ROWS), jnp.float32),
-            pltpu.SemaphoreType.DMA((5,)),
+            pltpu.SemaphoreType.DMA((NQ,)),
         ],
         compiler_params=params(),
         cost_estimate=cost(4),
         name="row_statistics",
-    )(pairs, count, q, *kv)
+    )(pairs, count, q, kv)
 
 
 def call_query(pairs, count, core, q, kv, part):
@@ -228,27 +292,27 @@
     return pl.pallas_call(
         query_kernel,
         out_shape=(half, half),
-        in_specs=[smem()] * 3 + [anywhere()] * 5 + [vmem()],
+        in_specs=[smem()] * 3 + [anywhere()] * 2 + [vmem()],
         out_specs=(vmem(), vmem()),
         scratch_shapes=loaded()
         + [
             pltpu.VMEM((NQ + 1, HD, ROWS), jnp.float32),
             pltpu.VMEM((STEP, TILE, ROWS), jnp.bfloat16),
-            pltpu.SemaphoreType.DMA((5,)),
+            pltpu.SemaphoreType.DMA((2,)),
         ],
         compiler_params=params(),
         cost_estimate=cost(8),
         name="query_gradient",
-    )(pairs, count, core, q, *kv, part)
-
-
-def call_key(pairs, count, core, q, kv, total, own, far, kept, got):
+    )(pairs, count, core, q, kv, part)
+
+
+def call_key(pairs, count, core, x, q, kv, total, own, far, kept, got):
     quarter = jax.ShapeDtypeStruct((NY, TILE, 2 * HD), jnp.bfloat16)
     half = pltpu.VMEM((NZ, HD, ROWS), jnp.bfloat16)
     return pl.pallas_call(
         key_kernel,
         out_shape=(jax.ShapeDtypeStruct((NZ, HD, ROWS), jnp.bfloat16),) + (quarter,) * 4,
-        in_specs=[smem()] * 3 + [anywhere()] * 5 + [vmem()] * 3 + [anywhere()] * 2,
+        in_specs=[smem()] * 4 + [anywhere()] * 2 + [vmem()] * 3 + [anywhere()] * 2,
         out_specs=(anywhere(),) + (vmem(),) * 4,
         scratch_shapes=loaded()
         + [
@@ -258,12 +322,12 @@
             half,
             half,
             half,
-            pltpu.SemaphoreType.DMA((8,)),
+            pltpu.SemaphoreType.DMA((5,)),
         ],
         compiler_params=params(),
         cost_estimate=cost(8),
         name="key_gradient",
-    )(pairs, count, core, q, *kv, total, own, far, kept, got)
+    )(pairs, count, core, x, q, kv, total, own, far, kept, got)
 
 
 def to_everyone(value, axis):
@@ -300,21 +364,14 @@
     core = lax.axis_index("c")
     y_hi = lax.axis_index("yh")
     y_lo = lax.axis_index("yl")
-    product = out_grad.astype(jnp.float32) * forward_out.astype(jnp.float32)
-    delta = jnp.sum(product.reshape(TILE, HQ, HD), axis=2).astype(jnp.bfloat16)
-    delta_rows = jnp.pad(delta.T.reshape(1, ROWS), ((0, 15), (0, 0)))
-    q_own = jnp.concatenate([query_states, out_grad, delta_rows], axis=0)
+    q_own, kv_own = call_prepare(
+        query_states, out_grad, forward_out, key_states, value_states, block_mask
+    )
     q_all = lax.all_gather(q_own, ("c", "z"), axis=0, tiled=False)
-
-    mask_rows = jnp.pad(block_mask.astype(jnp.bfloat16).reshape(2, 2 * HD), ((0, 14), (0, 0)))
-    kv_own = jnp.concatenate(
-        [jnp.concatenate([key_states, value_states], axis=1), mask_rows], axis=0
-    )
-    kv_y = to_everyone(kv_own, Y)
-    kv_all = (kv_y, along_x(kv_y, 1), along_x(kv_y, -1), along_x(kv_y, 2))
-
-    mine = lax.dynamic_slice_in_dim(kv_y[:, TILE : TILE + 2], y_lo * 2, 2, 0)
-    mine = mine.reshape(2, 16, 32)
+    kv_y = lax.all_to_all(kv_own, Y, 0, 0, tiled=True)
+    kv_all = to_everyone(kv_y[:, :TILE], "x").reshape(NK, TILE, 2 * HD)
+
+    mine = lax.dynamic_slice_in_dim(kv_y[:, TILE:, :NK], y_lo * 2, 2, 0)
     other = swap_cores(mine)
     first = jnp.where(core == 0, mine, other)
     second = jnp.where(core == 0, other, mine)
@@ -322,13 +379,12 @@
     both = lax.dynamic_slice_in_dim(both, y_hi * 8, 8, 2)
     both = both.reshape(2, 2, 8, 16, 2)
     both = jnp.where(core == 0, both[..., 0], both[..., 1])
-    mask = both.transpose(0, 2, 3, 1).reshape(NQ, 4, NY)
-    turned = lax.dynamic_slice_in_dim(jnp.concatenate([mask, mask], 1), lax.axis_index("x"), 4, 1)
-    mask = jnp.concatenate([turned[:, :1], turned[:, 3:], turned[:, 1:3]], axis=1).reshape(NQ, NK)
+    mask = both.transpose(0, 2, 3, 1).reshape(NQ, NK)
     pairs, count = list_pairs(mask)
 
-    part = call_stats(pairs, count, q_all, kv_all)
-    parts = to_everyone(part.reshape(NQ * ROWS // HD, HD), ("c", "z"))
+    part, parts = call_stats(pairs, count, q_all, kv_all)
+    parts = parts.reshape(NQ, NQ * ROWS // HD, HD)
+    parts = lax.all_to_all(parts, ("c", "z"), 0, 0, tiled=True)
     kept, sent = call_query(pairs, count, core[None], q_all, kv_all, part)
     got = swap_cores(sent)
 
@@ -337,21 +393,16 @@
     total = total.reshape(NQ, 1, ROWS)
     far = lax.dynamic_index_in_dim(parts, (1 - core) * NZ + lax.axis_index("z"), 0, False)
     far = far.reshape(NQ, 1, ROWS)
-    chip, here, back, ahead, across = call_key(
-        pairs, count, core[None], q_all, kv_all, total, part, far, kept, got
+    x = lax.axis_index("x")
+    chip, here, ahead, across, back = call_key(
+        pairs, count, core[None], x[None], q_all, kv_all, total, part, far, kept, got
     )
 
     dq_own = lax.psum_scatter(chip, "z", scatter_dimension=0, tiled=True)[0]
-    dq_own = (dq_own.astype(jnp.float32) * SCALE).astype(jnp.bfloat16)
-    query_grad = dq_own.reshape(HD, HQ, TILE).transpose(2, 1, 0).reshape(TILE, HQ * HD)
-
     over_x = (here, along_x(across, 2), along_x(back, -1), along_x(ahead, 1))
     over_x = sum(p.astype(jnp.float32) for p in over_x).astype(jnp.bfloat16)
     over_y = lax.all_to_all(over_x, Y, 0, 0, tiled=True)
-    sums = over_y.astype(jnp.float32).sum(axis=0)
-    key_grad = (sums[:, :HD] * SCALE).astype(jnp.bfloat16)
-    value_grad = sums[:, HD:].astype(jnp.bfloat16)
-    return query_grad, key_grad, value_grad
+    return call_finish(dq_own, over_y)
 
 
 def solution(mesh):

time: 180 us -> 164 us (0.911)
  the two profiles are of different devices: /device:TPU:75 before, /device:TPU:9 now
where the time goes in v4:
time: 164 us
  waiting for transfers between devices  45.9 us (28%)
  blocking collectives  44.3 us (27%)
  starting transfers between devices  34.9 us (21%)
  Pallas kernels  20 us (12%)
  between operations  14.2 us (9%)
  other arithmetic  2.28 us (1%)
  local copies, waits for them, and re-layouts  2.2 us (1%)
    all_to_all x1, blocking collectives, body(): kv_y = lax.all_to_all(kv_own, Y, 0, 0, tiled=True)  23.4 us
    all_to_all x1, blocking collectives, body(): over_y = lax.all_to_all(over_x, Y, 0, 0, tiled=True)  21 us
    all_to_all x1, waiting for transfers between devices, to_everyone(): lax.all_to_all(jnp.broadcast_to(value[None], (peers, *value.shape)), axis...  19.1 us
    ppermute x3, waiting for transfers between devices, along_x(): return lax.ppermute(value, 'x', [(n, (n + by) % 4) for n in range(4)])  18.9 us
    all_to_all x1, starting transfers between devices, body(): parts = lax.all_to_all(parts, ('c', 'z'), 0, 0, tiled=True)  14.2 us
    ppermute x3, starting transfers between devices, along_x(): return lax.ppermute(value, 'x', [(n, (n + by) % 4) for n in range(4)])  9.58 us
    all_to_all x1, waiting for transfers between devices, body(): parts = lax.all_to_all(parts, ('c', 'z'), 0, 0, tiled=True)  7.09 us
    pallas_call x1, Pallas kernels, call_key(): pl.pallas_call(key_kernel, out_shape=(jax.ShapeDtypeStruct((NZ, HD, ROWS)...  6.09 us
  transfers between devices with their start and end apart: 9, of which 6 were waited for; matrix products, arithmetic and copies ran while one was open for 3% of the time, Pallas kernels for 3%

profile of v4, /device:TPU:9, one launch (start us, length us, event | category | flops | bytes accessed | tf_op | source)
XLA Modules:
  0.0 163.8 jit_solution(8549626665929708307)
XLA Ops:
  7.2 2.8 %prepare.1 = (bf16[272,512]{1,0:T(8,128)(2,1)}, bf16[8,144,256]{2,1,0:T(8,128)(2,1)}) custom-call(bf16[128,512]{1,0:T(8,128)(2,1)} %q_in.1, bf16[128,512]{1,0:T(8,128)(2,1)} %g_in.1, bf16[128,512]{1,0:T(8,128)(2,1)} %o_in.1, bf16[128,128]{1,0:T(8,128)(2,1)} %k_in.1, bf16[128,128]{1,0:T(8,128)(2,1)} %v_in.1, s32[16,32]{1,0:T(8,128)} %mask_in.1), custom_call_target="tpu_custom_call" | custom-call | tf_op jit(solution)/shard_map/prepare/pallas_call | solution.py:241
  10.0 23.4 %all_to_all.20 = bf16[8,144,256]{2,1,0:T(8,128)(2,1)S(1)} all-to-all(bf16[8,144,256]{2,1,0:T(8,128)(2,1)} %get-tuple-element.14), channel_id=1, replica_groups=mesh['x'=4,'yl'=4,'c'=2,'yh'=2,'z'=8] {'yl','yh'}, dimensions={0} | all-to-all | bytes 1179648 | tf_op jit(solution)/shard_map/all_to_all | solution.py:371
  33.4 1.6 broadcast_in_dim.55
  35.0 5.5 %all-to-all-start.1 = ((bf16[4,8,128,256]{3,2,1,0:T(8,128)(2,1)}), bf16[4,8,128,256]{3,2,1,0:T(8,128)(2,1)S(1)}, u32[]{:S(2)}, u32[]{:S(2)}) async-start(bf16[4,8,128,256]{3,2,1,0:T(8,128)(2,1)} %broadcast_in_dim.55), calls=%async_computation.1 | async-start | bytes 4194304 | tf_op jit(solution)/shard_map/all_to_all | solution.py:335
  40.5 3.0 %collective-permute-start = (bf16[2,16,32]{2,1,0:T(8,128)(2,1)S(1)}, bf16[2,16,32]{2,1,0:T(8,128)(2,1)S(1)}, u32[]{:S(2)}, u32[]{:S(2)}) collective-permute-start(bf16[2,16,32]{2,1,0:T(8,128)(2,1)S(1)} %constant_dynamic-slice_fusion.1), channel_id=1, source_target_pairs={{0,16},{16,0},{1,17},{17,1},{2,18},{18,2},{3,19},{19,3},{4,20},{20... | collective-permute-start | bytes 6152 | tf_op jit(solution)/shard_map/ppermute | solution.py:345
  43.5 0.8 collective-permute-done
  44.4 0.7 convert_reduce_fusion
  45.7 0.3 select_reduce_fusion
  46.0 0.7 select_add_fusion
  46.7 19.1 %all-to-all-done.1 = bf16[4,8,128,256]{3,2,1,0:T(8,128)(2,1)S(1)} async-done(((bf16[4,8,128,256]{3,2,1,0:T(8,128)(2,1)}), bf16[4,8,128,256]{3,2,1,0:T(8,128)(2,1)S(1)}, u32[]{:S(2)}, u32[]{:S(2)}) %all-to-all-start.1) | async-done | bytes 2097184 | tf_op jit(solution)/shard_map/all_to_all | solution.py:335
  65.8 4.2 %row_statistics.1 = (f32[16,1,512]{2,1,0:T(1,128)S(1)}, f32[16,16,1,512]{3,2,1,0:T(1,128)}) custom-call(s32[516]{0:T(1024)S(1)} %pad.4.pairs_ref, s32[1]{0:T(128)} %bitcast.6.count_ref, bf16[16,272,512]{2,1,0:T(8,128)(2,1)} %bitcast.27, bf16[32,128,256]{2,1,0:T(8,128)(2,1)S(1)} %bitcast.19), custom_call_target="tpu_custom_call" | custom-call | flops 10000000000 | bytes 4194304 | tf_op jit(solution)/shard_map/row_statistics/pallas_call | solution.py:269
  70.0 14.2 %all-to-all-start.2 = ((f32[16,64,128]{2,1,0:T(8,128)}), f32[16,64,128]{2,1,0:T(8,128)S(1)}, u32[]{:S(2)}, u32[]{:S(2)}) async-start(f32[16,64,128]{2,1,0:T(8,128)} %bitcast.11), calls=%async_computation.2 | async-start | bytes 1048576 | tf_op jit(solution)/shard_map/all_to_all | solution.py:387
  84.3 5.0 %query_gradient.1 = (bf16[8,128,512]{2,1,0:T(8,128)(2,1)S(1)}, bf16[8,128,512]{2,1,0:T(8,128)(2,1)S(1)}) custom-call(s32[516]{0:T(1024)S(1)} %pad.4.pairs_ref, s32[1]{0:T(128)} %bitcast.6.count_ref, s32[1]{0:T(128)} %bitcast.7.core_ref, bf16[16,272,512]{2,1,0:T(8,128)(2,1)} %bitcast.28, bf16[32,128,256]{2,1,0:T(8,128)(2,1)} %bitcast.20, ...), custom_call_target="tpu_custom_call" | custom-call | flops 10000000000 | bytes 8388608 | tf_op jit(solution)/shard_map/query_gradient/pallas_call | solution.py:292
  89.3 2.6 %collective-permute-start.1 = (bf16[8,128,512]{2,1,0:T(8,128)(2,1)S(1)}, bf16[8,128,512]{2,1,0:T(8,128)(2,1)}, u32[]{:S(2)}, u32[]{:S(2)}) collective-permute-start(bf16[8,128,512]{2,1,0:T(8,128)(2,1)S(1)} %get-tuple-element.19), channel_id=1, source_target_pairs={{0,16},{16,0},{1,17},{17,1},{2,18},{18,2},{3,19},{19,3},{4,20},{20... | collective-permute-start | bytes 3145736 | tf_op jit(solution)/shard_map/ppermute | solution.py:345
  91.9 7.1 %all-to-all-done.2 = f32[16,64,128]{2,1,0:T(8,128)S(1)} async-done(((f32[16,64,128]{2,1,0:T(8,128)}), f32[16,64,128]{2,1,0:T(8,128)S(1)}, u32[]{:S(2)}, u32[]{:S(2)}) %all-to-all-start.2) | async-done | bytes 524320 | tf_op jit(solution)/shard_map/all_to_all | solution.py:387
  99.2 6.1 %key_gradient.1 = (bf16[8,128,512]{2,1,0:T(8,128)(2,1)}, bf16[8,128,256]{2,1,0:T(8,128)(2,1)S(1)}, bf16[8,128,256]{2,1,0:T(8,128)(2,1)S(1)}, bf16[8,128,256]{2,1,0:T(8,128)(2,1)S(1)}, bf16[8,128,256]{2,1,0:T(8,128)(2,1)S(1)}) custom-call(s32[516]{0:T(1024)S(1)} %pad.4.pairs_ref, s32[1]{0:T(128)} %bitcast.6.count_ref, s32[1]{0:T(128)} %bitcast.7.core_ref, ...), custom_call_target="tpu_custom_call" | custom-call | flops 10000000000 | bytes 8388608 | tf_op jit(solution)/shard_map/key_gradient/pallas_call | solution.py:312
  105.3 2.7 %collective-permute-start.2 = (bf16[8,128,256]{2,1,0:T(8,128)(2,1)S(1)}, bf16[8,128,256]{2,1,0:T(8,128)(2,1)S(1)}, u32[]{:S(2)}, u32[]{:S(2)}) collective-permute-start(bf16[8,128,256]{2,1,0:T(8,128)(2,1)S(1)} %get-tuple-element.22), channel_id=1, source_target_pairs={{0,256},{128,384},{256,0},{384,128},{1,257},{129,385},{257,1},{385... | collective-permute-start | bytes 1572872 | tf_op jit(solution)/shard_map/ppermute | solution.py:341
  108.0 5.0 %collective-permute-start.3 = (bf16[8,128,256]{2,1,0:T(8,128)(2,1)S(1)}, bf16[8,128,256]{2,1,0:T(8,128)(2,1)S(1)}, u32[]{:S(2)}, u32[]{:S(2)}) collective-permute-start(bf16[8,128,256]{2,1,0:T(8,128)(2,1)S(1)} %get-tuple-element.23), channel_id=1, source_target_pairs={{0,384},{128,0},{256,128},{384,256},{1,385},{129,1},{257,129},{385... | collective-permute-start | bytes 1572872 | tf_op jit(solution)/shard_map/ppermute | solution.py:341
  113.0 1.9 %collective-permute-start.4 = (bf16[8,128,256]{2,1,0:T(8,128)(2,1)S(1)}, bf16[8,128,256]{2,1,0:T(8,128)(2,1)S(1)}, u32[]{:S(2)}, u32[]{:S(2)}) collective-permute-start(bf16[8,128,256]{2,1,0:T(8,128)(2,1)S(1)} %get-tuple-element.24), channel_id=1, source_target_pairs={{0,128},{128,256},{256,384},{384,0},{1,129},{129,257},{257,385},{3... | collective-permute-start | bytes 1572872 | tf_op jit(solution)/shard_map/ppermute | solution.py:341
  114.9 5.5 %collective-permute-done.2 = bf16[8,128,256]{2,1,0:T(8,128)(2,1)S(1)} collective-permute-done((bf16[8,128,256]{2,1,0:T(8,128)(2,1)S(1)}, bf16[8,128,256]{2,1,0:T(8,128)(2,1)S(1)}, u32[]{:S(2)}, u32[]{:S(2)}) %collective-permute-start.2) | collective-permute-done | bytes 524320 | tf_op jit(solution)/shard_map/ppermute | solution.py:341
  120.4 10.8 %collective-permute-done.3 = bf16[8,128,256]{2,1,0:T(8,128)(2,1)S(1)} collective-permute-done((bf16[8,128,256]{2,1,0:T(8,128)(2,1)S(1)}, bf16[8,128,256]{2,1,0:T(8,128)(2,1)S(1)}, u32[]{:S(2)}, u32[]{:S(2)}) %collective-permute-start.3) | collective-permute-done | bytes 524320 | tf_op jit(solution)/shard_map/ppermute | solution.py:341
  131.3 2.5 %collective-permute-done.4 = bf16[8,128,256]{2,1,0:T(8,128)(2,1)S(1)} collective-permute-done((bf16[8,128,256]{2,1,0:T(8,128)(2,1)S(1)}, bf16[8,128,256]{2,1,0:T(8,128)(2,1)S(1)}, u32[]{:S(2)}, u32[]{:S(2)}) %collective-permute-start.4) | collective-permute-done | bytes 524320 | tf_op jit(solution)/shard_map/ppermute | solution.py:341
  134.1 21.0 %all_to_all.21.over_y_ref = bf16[8,128,256]{2,1,0:T(8,128)(2,1)} all-to-all(bf16[8,128,256]{2,1,0:T(8,128)(2,1)S(1)} %add_convert_fusion), channel_id=1, replica_groups=mesh['x'=4,'yl'=4,'c'=2,'yh'=2,'z'=8] {'yl','yh'}, dimensions={0} | all-to-all | bytes 1048576 | tf_op jit(solution)/shard_map/all_to_all | solution.py:404
  155.0 1.9 %finish.1 = (bf16[128,512]{1,0:T(8,128)(2,1)}, bf16[128,128]{1,0:T(8,128)(2,1)}, bf16[128,128]{1,0:T(8,128)(2,1)}) custom-call(bf16[128,512]{1,0:T(8,128)(2,1)} %bitcast.25, bf16[8,128,256]{2,1,0:T(8,128)(2,1)} %all_to_all.21.over_y_ref), custom_call_target="tpu_custom_call" | custom-call | tf_op jit(solution)/shard_map/finish/pallas_call | solution.py:259
  (28 shorter events, 1.3 us)
Async XLA Ops:
  7.2 58.6 %all-gather.3.cloned.1.call-start = ((), (), s32[]{:S(2)}) async-start(), calls=%async_computation.6 | async-start | bytes 4734976 | tf_op jit(solution)/shard_map/all_gather | solution.py:370
  35.0 30.8 %all-to-all-start.1 = ((bf16[4,8,128,256]{3,2,1,0:T(8,128)(2,1)}), bf16[4,8,128,256]{3,2,1,0:T(8,128)(2,1)S(1)}, u32[]{:S(2)}, u32[]{:S(2)}) async-start(bf16[4,8,128,256]{3,2,1,0:T(8,128)(2,1)} %broadcast_in_dim.55), calls=%async_computation.1 | async-start | bytes 4194304 | tf_op jit(solution)/shard_map/all_to_all | solution.py:335
  40.5 3.8 %collective-permute-start = (bf16[2,16,32]{2,1,0:T(8,128)(2,1)S(1)}, bf16[2,16,32]{2,1,0:T(8,128)(2,1)S(1)}, u32[]{:S(2)}, u32[]{:S(2)}) collective-permute-start(bf16[2,16,32]{2,1,0:T(8,128)(2,1)S(1)} %constant_dynamic-slice_fusion.1), channel_id=1, source_target_pairs={{0,16},{16,0},{1,17},{17,1},{2,18},{18,2},{3,19},{19,3},{4,20},{20... | collective-permute-start | bytes 6152 | tf_op jit(solution)/shard_map/ppermute | solution.py:345
  65.8 4.2 %copy-start = (bf16[4,8,128,256]{3,2,1,0:T(8,128)(2,1)}, bf16[4,8,128,256]{3,2,1,0:T(8,128)(2,1)S(1)}, u32[]{:S(2)}) copy-start(bf16[4,8,128,256]{3,2,1,0:T(8,128)(2,1)S(1)} %all-to-all-done.1) | copy-start | bytes 6291460
  70.0 29.0 %all-to-all-start.2 = ((f32[16,64,128]{2,1,0:T(8,128)}), f32[16,64,128]{2,1,0:T(8,128)S(1)}, u32[]{:S(2)}, u32[]{:S(2)}) async-start(f32[16,64,128]{2,1,0:T(8,128)} %bitcast.11), calls=%async_computation.2 | async-start | bytes 1048576 | tf_op jit(solution)/shard_map/all_to_all | solution.py:387
  84.2 70.8 %reduce-scatter.2.cloned.1.call-start = ((), (), s32[]{:S(2)}) async-start(), calls=%async_computation.5 | async-start | bytes 1179648 | tf_op jit(solution)/shard_map/reduce_scatter | solution.py:401
  89.3 9.9 %copy-start.1 = (bf16[8,128,512]{2,1,0:T(8,128)(2,1)}, bf16[8,128,512]{2,1,0:T(8,128)(2,1)S(1)}, u32[]{:S(2)}) copy-start(bf16[8,128,512]{2,1,0:T(8,128)(2,1)S(1)} %get-tuple-element.18.kept_hbm) | copy-start | bytes 3145732
  89.3 9.9 %collective-permute-start.1 = (bf16[8,128,512]{2,1,0:T(8,128)(2,1)S(1)}, bf16[8,128,512]{2,1,0:T(8,128)(2,1)}, u32[]{:S(2)}, u32[]{:S(2)}) collective-permute-start(bf16[8,128,512]{2,1,0:T(8,128)(2,1)S(1)} %get-tuple-element.19), channel_id=1, source_target_pairs={{0,16},{16,0},{1,17},{17,1},{2,18},{18,2},{3,19},{19,3},{4,20},{20... | collective-permute-start | bytes 3145736 | tf_op jit(solution)/shard_map/ppermute | solution.py:345
  105.3 15.1 %collective-permute-start.2 = (bf16[8,128,256]{2,1,0:T(8,128)(2,1)S(1)}, bf16[8,128,256]{2,1,0:T(8,128)(2,1)S(1)}, u32[]{:S(2)}, u32[]{:S(2)}) collective-permute-start(bf16[8,128,256]{2,1,0:T(8,128)(2,1)S(1)} %get-tuple-element.22), channel_id=1, source_target_pairs={{0,256},{128,384},{256,0},{384,128},{1,257},{129,385},{257,1},{385... | collective-permute-start | bytes 1572872 | tf_op jit(solution)/shard_map/ppermute | solution.py:341
  108.0 23.3 %collective-permute-start.3 = (bf16[8,128,256]{2,1,0:T(8,128)(2,1)S(1)}, bf16[8,128,256]{2,1,0:T(8,128)(2,1)S(1)}, u32[]{:S(2)}, u32[]{:S(2)}) collective-permute-start(bf16[8,128,256]{2,1,0:T(8,128)(2,1)S(1)} %get-tuple-element.23), channel_id=1, source_target_pairs={{0,384},{128,0},{256,128},{384,256},{1,385},{129,1},{257,129},{385... | collective-permute-start | bytes 1572872 | tf_op jit(solution)/shard_map/ppermute | solution.py:341
  113.0 20.8 %collective-permute-start.4 = (bf16[8,128,256]{2,1,0:T(8,128)(2,1)S(1)}, bf16[8,128,256]{2,1,0:T(8,128)(2,1)S(1)}, u32[]{:S(2)}, u32[]{:S(2)}) collective-permute-start(bf16[8,128,256]{2,1,0:T(8,128)(2,1)S(1)} %get-tuple-element.24), channel_id=1, source_target_pairs={{0,128},{128,256},{256,384},{384,0},{1,129},{129,257},{257,385},{3... | collective-permute-start | bytes 1572872 | tf_op jit(solution)/shard_map/ppermute | solution.py:341
Sparse Core Ops, SparseCore 0:
  10.1 50.8 all-gather.2
  105.4 33.8 reduce-scatter.1

commit v5 on v4

--- a/solution.py
+++ b/solution.py
@@ -46,11 +46,11 @@
 
 
 def stats_kernel(
-    pairs_ref, count_ref, q_hbm, kv_hbm, out_ref, sent_hbm, q_ref, k_ref, m_ref, l_ref, sems
+    pairs_ref, count_ref, q_hbm, k_hbm, out_ref, sent_hbm, q_ref, k_ref, m_ref, l_ref, sems
 ):
     copies = (
         pltpu.make_async_copy(q_hbm.at[:, pl.ds(0, TILE), :], q_ref, sems.at[0]),
-        pltpu.make_async_copy(kv_hbm.at[:, :, pl.ds(0, HD)], k_ref, sems.at[1]),
+        pltpu.make_async_copy(k_hbm, k_ref, sems.at[1]),
     )
     for copy in copies:
         copy.start()
@@ -85,29 +85,35 @@
         copy.wait()
 
 
-def weights_of(q_ref, kv_ref, total_ref, rq, jk):
-    scores = dot(kv_ref[jk, :, :HD], heads(q_ref, rq, 0), ((1,), (1,))) * (SCALE * LOG2E)
+def weights_of(q_ref, k_ref, v_ref, total_ref, rq, jk):
+    scores = dot(k_ref[jk], heads(q_ref, rq, 0), ((1,), (1,))) * (SCALE * LOG2E)
     probs = jnp.exp2(scores - total_ref[rq])
-    grad_probs = dot(kv_ref[jk, :, HD:], heads(q_ref, rq, TILE), ((1,), (1,)))
+    grad_probs = dot(v_ref[jk], heads(q_ref, rq, TILE), ((1,), (1,)))
     delta = q_ref[rq, 2 * TILE : 2 * TILE + 16, :].astype(jnp.float32)[0:1, :]
     return probs, (probs * (grad_probs - delta)).astype(jnp.bfloat16)
 
 
-def load(q_hbm, kv_hbm, q_ref, kv_ref, sems):
-    copies = (
+def of_x(x_ref, by):
+    return pl.ds(pl.multiple_of(((x_ref[0] + by) & 3) * NY, NY), NY)
+
+
+def load(x_ref, q_hbm, k_hbm, values, q_ref, k_ref, v_ref, sems):
+    copies = [
         pltpu.make_async_copy(q_hbm, q_ref, sems.at[0]),
-        pltpu.make_async_copy(kv_hbm, kv_ref, sems.at[1]),
-    )
+        pltpu.make_async_copy(k_hbm, k_ref, sems.at[1]),
+    ]
+    for n, piece in enumerate(values):
+        copies.append(pltpu.make_async_copy(piece, v_ref.at[of_x(x_ref, n)], sems.at[2 + n]))
     for copy in copies:
         copy.start()
     return copies
 
 
 def query_kernel(
-    pairs_ref, count_ref, core_ref, q_hbm, kv_hbm, total_ref, kept_ref, sent_ref,
-    q_ref, kv_ref, acc, ds_ref, sems,
+    pairs_ref, count_ref, core_ref, x_ref, q_hbm, k_hbm, v0, v1, v2, v3, total_ref,
+    kept_ref, sent_ref, q_ref, k_ref, v_ref, acc, ds_ref, sems,
 ):
-    copies = load(q_hbm, kv_hbm, q_ref, kv_ref, sems)
+    copies = load(x_ref, q_hbm, k_hbm, (v0, v1, v2, v3), q_ref, k_ref, v_ref, sems)
     acc[...] = jnp.zeros(acc.shape, jnp.float32)
     for copy in copies:
         copy.wait()
@@ -115,8 +121,8 @@
     def visit(i, carry):
         where = [unpack(pairs_ref, i * STEP + u) for u in range(STEP)]
         for u, (_, _, rq, jk) in enumerate(where):
-            ds_ref[u] = weights_of(q_ref, kv_ref, total_ref, rq, jk)[1]
-        parts = [dot(kv_ref[w[3], :, :HD], ds_ref[u], ((0,), (0,))) for u, w in enumerate(where)]
+            ds_ref[u] = weights_of(q_ref, k_ref, v_ref, total_ref, rq, jk)[1]
+        parts = [dot(k_ref[w[3]], ds_ref[u], ((0,), (0,))) for u, w in enumerate(where)]
         for (r, _, _, _), part in zip(where, parts):
             acc[r] += part
         return carry
@@ -129,18 +135,19 @@
 
 
 def key_kernel(
-    pairs_ref, count_ref, core_ref, x_ref, q_hbm, kv_hbm, total_ref, own_ref, far_ref,
-    kept_hbm, got_hbm, chip_hbm, out0, out1, out2, out3,
-    q_ref, kv_ref, acc, p_ref, ds_ref, kept_ref, got_ref, chip_ref, sems,
+    pairs_ref, count_ref, core_ref, x_ref, q_hbm, k_hbm, v0, v1, v2, v3, total_ref, own_ref,
+    far_ref, kept_hbm, got_hbm, chip_hbm, dk0, dk1, dk2, dk3, dv0, dv1, dv2, dv3,
+    q_ref, k_ref, v_ref, k_acc, v_acc, p_ref, ds_ref, kept_ref, got_ref, chip_ref, sems,
 ):
     two = (
-        pltpu.make_async_copy(kept_hbm, kept_ref, sems.at[2]),
-        pltpu.make_async_copy(got_hbm, got_ref, sems.at[3]),
+        pltpu.make_async_copy(kept_hbm, kept_ref, sems.at[6]),
+        pltpu.make_async_copy(got_hbm, got_ref, sems.at[7]),
     )
     for copy in two:
         copy.start()
-    copies = load(q_hbm, kv_hbm, q_ref, kv_ref, sems)
-    acc[...] = jnp.zeros(acc.shape, jnp.float32)
+    copies = load(x_ref, q_hbm, k_hbm, (v0, v1, v2, v3), q_ref, k_ref, v_ref, sems)
+    k_acc[...] = jnp.zeros(k_acc.shape, jnp.float32)
+    v_acc[...] = jnp.zeros(v_acc.shape, jnp.float32)
     for copy in two:
         copy.wait()
     for n in range(NZ):
@@ -150,7 +157,7 @@
         chip_ref[n] = (
             kept_ref[n].astype(jnp.float32) * own + got_ref[n].astype(jnp.float32) * far
         ).astype(jnp.bfloat16)
-    leave = pltpu.make_async_copy(chip_ref, chip_hbm, sems.at[4])
+    leave = pltpu.make_async_copy(chip_ref, chip_hbm, sems.at[8])
     leave.start()
     for copy in copies:
         copy.wait()
@@ -158,7 +165,7 @@
     def visit(i, carry):
         where = [unpack(pairs_ref, i * STEP + u) for u in range(STEP)]
         for u, (_, _, rq, jk) in enumerate(where):
-            probs, grad_scores = weights_of(q_ref, kv_ref, total_ref, rq, jk)
+            probs, grad_scores = weights_of(q_ref, k_ref, v_ref, total_ref, rq, jk)
             p_ref[u] = probs.astype(jnp.bfloat16)
             ds_ref[u] = grad_scores
         parts = [
@@ -169,14 +176,14 @@
             for u, w in enumerate(where)
         ]
         for (_, j, _, _), (of_key, of_value) in zip(where, parts):
-            acc[j, :, :HD] += of_key
-            acc[j, :, HD:] += of_value
+            k_acc[j] += of_key
+            v_acc[j] += of_value
         return carry
 
     lax.fori_loop(0, blocks_of(count_ref, STEP), visit, 0)
-    for n, out_ref in enumerate((out0, out1, out2, out3)):
-        first = pl.multiple_of(((x_ref[0] + n) & 3) * NY, NY)
-        out_ref[...] = acc[pl.ds(first, NY)].astype(jnp.bfloat16)
+    for n, (dk_ref, dv_ref) in enumerate(((dk0, dv0), (dk1, dv1), (dk2, dv2), (dk3, dv3))):
+        dk_ref[...] = k_acc[of_x(x_ref, n)].astype(jnp.bfloat16)
+        dv_ref[...] = v_acc[of_x(x_ref, n)].astype(jnp.bfloat16)
     leave.wait()
 
 
@@ -199,15 +206,15 @@
         copy.wait()
 
 
-def finish_kernel(dq_ref, over_y_ref, query_ref, key_ref, value_ref):
+def finish_kernel(dq_ref, dk_ref, dv_ref, query_ref, key_ref, value_ref):
     for h in range(HQ):
         cols = slice(h * TILE, (h + 1) * TILE)
         query_ref[:, cols] = (dq_ref[:, cols].astype(jnp.float32).T * SCALE).astype(jnp.bfloat16)
-    sums = over_y_ref[0].astype(jnp.float32)
-    for n in range(1, NY):
-        sums += over_y_ref[n].astype(jnp.float32)
-    key_ref[...] = (sums[:, :HD] * SCALE).astype(jnp.bfloat16)
-    value_ref[...] = sums[:, HD:].astype(jnp.bfloat16)
+    for parts_ref, out_ref, scale in ((dk_ref, key_ref, SCALE), (dv_ref, value_ref, 1.0)):
+        total = parts_ref[0].astype(jnp.float32)
+        for n in range(1, NY):
+            total += parts_ref[n].astype(jnp.float32)
+        out_ref[...] = (total * scale).astype(jnp.bfloat16)
 
 
 def vmem():
@@ -233,7 +240,8 @@
 def loaded():
     return [
         pltpu.VMEM((NQ, QPAD, ROWS), jnp.bfloat16),
-        pltpu.VMEM((NK, TILE, 2 * HD), jnp.bfloat16),
+        pltpu.VMEM((NK, TILE, HD), jnp.bfloat16),
+        pltpu.VMEM((NK, TILE, HD), jnp.bfloat16),
     ]
 
 
@@ -254,18 +262,18 @@
     )(q, g, o, k, v, mask)
 
 
-def call_finish(dq, over_y):
+def call_finish(dq, dk, dv):
     tile = jax.ShapeDtypeStruct((TILE, HD), jnp.bfloat16)
     return pl.pallas_call(
         finish_kernel,
         out_shape=(jax.ShapeDtypeStruct((TILE, ROWS), jnp.bfloat16), tile, tile),
-        in_specs=[vmem()] * 2,
+        in_specs=[vmem()] * 3,
         out_specs=(vmem(),) * 3,
         name="finish",
-    )(dq, over_y)
-
-
-def call_stats(pairs, count, q, kv):
+    )(dq, dk, dv)
+
+
+def call_stats(pairs, count, q, k):
     return pl.pallas_call(
         stats_kernel,
         out_shape=(
@@ -284,50 +292,51 @@
         compiler_params=params(),
         cost_estimate=cost(4),
         name="row_statistics",
-    )(pairs, count, q, kv)
-
-
-def call_query(pairs, count, core, q, kv, part):
+    )(pairs, count, q, k)
+
+
+def call_query(pairs, count, core, x, q, k, values, part):
     half = jax.ShapeDtypeStruct((NZ, HD, ROWS), jnp.bfloat16)
     return pl.pallas_call(
         query_kernel,
         out_shape=(half, half),
-        in_specs=[smem()] * 3 + [anywhere()] * 2 + [vmem()],
+        in_specs=[smem()] * 4 + [anywhere()] * 6 + [vmem()],
         out_specs=(vmem(), vmem()),
         scratch_shapes=loaded()
         + [
             pltpu.VMEM((NQ + 1, HD, ROWS), jnp.float32),
             pltpu.VMEM((STEP, TILE, ROWS), jnp.bfloat16),
-            pltpu.SemaphoreType.DMA((2,)),
+            pltpu.SemaphoreType.DMA((6,)),
         ],
         compiler_params=params(),
         cost_estimate=cost(8),
         name="query_gradient",
-    )(pairs, count, core, q, kv, part)
-
-
-def call_key(pairs, count, core, x, q, kv, total, own, far, kept, got):
-    quarter = jax.ShapeDtypeStruct((NY, TILE, 2 * HD), jnp.bfloat16)
+    )(pairs, count, core, x, q, k, *values, part)
+
+
+def call_key(pairs, count, core, x, q, k, values, total, own, far, kept, got):
+    quarter = jax.ShapeDtypeStruct((NY, TILE, HD), jnp.bfloat16)
     half = pltpu.VMEM((NZ, HD, ROWS), jnp.bfloat16)
     return pl.pallas_call(
         key_kernel,
-        out_shape=(jax.ShapeDtypeStruct((NZ, HD, ROWS), jnp.bfloat16),) + (quarter,) * 4,
-        in_specs=[smem()] * 4 + [anywhere()] * 2 + [vmem()] * 3 + [anywhere()] * 2,
-        out_specs=(anywhere(),) + (vmem(),) * 4,
+        out_shape=(jax.ShapeDtypeStruct((NZ, HD, ROWS), jnp.bfloat16),) + (quarter,) * 8,
+        in_specs=[smem()] * 4 + [anywhere()] * 6 + [vmem()] * 3 + [anywhere()] * 2,
+        out_specs=(anywhere(),) + (vmem(),) * 8,
         scratch_shapes=loaded()
         + [
-            pltpu.VMEM((NK + 1, TILE, 2 * HD), jnp.float32),
+            pltpu.VMEM((NK + 1, TILE, HD), jnp.float32),
+            pltpu.VMEM((NK + 1, TILE, HD), jnp.float32),
             pltpu.VMEM((STEP, TILE, ROWS), jnp.bfloat16),
             pltpu.VMEM((STEP, TILE, ROWS), jnp.bfloat16),
             half,
             half,
             half,
-            pltpu.SemaphoreType.DMA((5,)),
+            pltpu.SemaphoreType.DMA((9,)),
         ],
         compiler_params=params(),
         cost_estimate=cost(8),
         name="key_gradient",
-    )(pairs, count, core, x, q, kv, total, own, far, kept, got)
+    )(pairs, count, core, x, q, k, *values, total, own, far, kept, got)
 
 
 def to_everyone(value, axis):
@@ -343,6 +352,12 @@
 
 def swap_cores(value):
     return lax.ppermute(value, "c", [(0, 1), (1, 0)])
+
+
+def sum_over_keys(here, ahead, across, back):
+    arrived = (here, along_x(across, 2), along_x(ahead, 1), along_x(back, -1))
+    over_x = sum(p.astype(jnp.float32) for p in arrived).astype(jnp.bfloat16)
+    return lax.all_to_all(over_x, Y, 0, 0, tiled=True)
 
 
 def list_pairs(tile_mask):
@@ -361,7 +376,7 @@
 
 
 def body(query_states, out_grad, forward_out, key_states, value_states, block_mask):
-    core = lax.axis_index("c")
+    core, x = lax.axis_index("c"), lax.axis_index("x")
     y_hi = lax.axis_index("yh")
     y_lo = lax.axis_index("yl")
     q_own, kv_own = call_prepare(
@@ -369,10 +384,11 @@
     )
     q_all = lax.all_gather(q_own, ("c", "z"), axis=0, tiled=False)
     kv_y = lax.all_to_all(kv_own, Y, 0, 0, tiled=True)
-    kv_all = to_everyone(kv_y[:, :TILE], "x").reshape(NK, TILE, 2 * HD)
-
+    k_all = to_everyone(kv_y[:, :TILE, :HD], "x").reshape(NK, TILE, HD)
     mine = lax.dynamic_slice_in_dim(kv_y[:, TILE:, :NK], y_lo * 2, 2, 0)
     other = swap_cores(mine)
+    v_y, other = lax.optimization_barrier((kv_y[:, :TILE, HD:], other))
+    v_all = (v_y, along_x(v_y, -1), along_x(v_y, 2), along_x(v_y, 1))
     first = jnp.where(core == 0, mine, other)
     second = jnp.where(core == 0, other, mine)
     both = jnp.stack([first, second])
@@ -382,10 +398,10 @@
     mask = both.transpose(0, 2, 3, 1).reshape(NQ, NK)
     pairs, count = list_pairs(mask)
 
-    part, parts = call_stats(pairs, count, q_all, kv_all)
+    part, parts = call_stats(pairs, count, q_all, k_all)
     parts = parts.reshape(NQ, NQ * ROWS // HD, HD)
     parts = lax.all_to_all(parts, ("c", "z"), 0, 0, tiled=True)
-    kept, sent = call_query(pairs, count, core[None], q_all, kv_all, part)
+    kept, sent = call_query(pairs, count, core[None], x[None], q_all, k_all, v_all, part)
     got = swap_cores(sent)
 
     top = jnp.max(parts, axis=0)
@@ -393,16 +409,12 @@
     total = total.reshape(NQ, 1, ROWS)
     far = lax.dynamic_index_in_dim(parts, (1 - core) * NZ + lax.axis_index("z"), 0, False)
     far = far.reshape(NQ, 1, ROWS)
-    x = lax.axis_index("x")
-    chip, here, ahead, across, back = call_key(
-        pairs, count, core[None], x[None], q_all, kv_all, total, part, far, kept, got
-    )
-
+    chip, *parts = call_key(
+        pairs, count, core[None], x[None], q_all, k_all, v_all, total, part, far, kept, got
+    )
     dq_own = lax.psum_scatter(chip, "z", scatter_dimension=0, tiled=True)[0]
-    over_x = (here, along_x(across, 2), along_x(back, -1), along_x(ahead, 1))
-    over_x = sum(p.astype(jnp.float32) for p in over_x).astype(jnp.bfloat16)
-    over_y = lax.all_to_all(over_x, Y, 0, 0, tiled=True)
-    return call_finish(dq_own, over_y)
+    dv_own, dk_own = sum_over_keys(*parts[4:]), sum_over_keys(*parts[:4])
+    return call_finish(dq_own, dk_own, dv_own)
 
 
 def solution(mesh):

time: 164 us -> 160 us (0.976)
  the two profiles are of different devices: /device:TPU:9 before, /device:TPU:14 now
where the time goes in v5:
time: 160 us; the launch traced here: 159 us
  starting transfers between devices  64.9 us (41%)
  waiting for transfers between devices  39 us (24%)
  Pallas kernels  22.9 us (14%)
  between operations  14.3 us (9%)
  blocking collectives  12 us (8%)
  other arithmetic  3 us (2%)
  local copies, waits for them, and re-layouts  2.92 us (2%)
    ppermute x9, starting transfers between devices, along_x(): return lax.ppermute(value, 'x', [(n, (n + by) % 4) for n in range(4)])  27.7 us
    all_to_all x1, waiting for transfers between devices, body(): kv_y = lax.all_to_all(kv_own, Y, 0, 0, tiled=True)  16.6 us
    all_to_all x1, starting transfers between devices, sum_over_keys(): return lax.all_to_all(over_x, Y, 0, 0, tiled=True)  12.5 us
    all_to_all x1, blocking collectives, sum_over_keys(): return lax.all_to_all(over_x, Y, 0, 0, tiled=True)  12 us
    all_to_all x1, waiting for transfers between devices, sum_over_keys(): return lax.all_to_all(over_x, Y, 0, 0, tiled=True)  8.72 us
    all_to_all x1, starting transfers between devices, body(): parts = lax.all_to_all(parts, ('c', 'z'), 0, 0, tiled=True)  8.03 us
    all_to_all x1, starting transfers between devices, body(): kv_y = lax.all_to_all(kv_own, Y, 0, 0, tiled=True)  7.56 us
    pallas_call x1, Pallas kernels, call_key(): pl.pallas_call(key_kernel, out_shape=(jax.ShapeDtypeStruct((NZ, HD, ROWS)...  7.21 us
  transfers between devices with their start and end apart: 17, of which 5 were waited for; matrix products, arithmetic and copies ran while one was open for 3% of the time, Pallas kernels for 7%

profile of v5, /device:TPU:14, one launch (start us, length us, event | category | flops | bytes accessed | tf_op | source)
XLA Modules:
  0.0 159.0 jit_solution(11881246270862489097)
XLA Ops:
  7.2 2.8 %prepare.1 = (bf16[272,512]{1,0:T(8,128)(2,1)}, bf16[8,144,256]{2,1,0:T(8,128)(2,1)}) custom-call(bf16[128,512]{1,0:T(8,128)(2,1)} %q_in.1, bf16[128,512]{1,0:T(8,128)(2,1)} %g_in.1, bf16[128,512]{1,0:T(8,128)(2,1)} %o_in.1, bf16[128,128]{1,0:T(8,128)(2,1)} %k_in.1, bf16[128,128]{1,0:T(8,128)(2,1)} %v_in.1, s32[16,32]{1,0:T(8,128)} %mask_in.1), custom_call_target="tpu_custom_call" | custom-call | tf_op jit(solution)/shard_map/prepare/pallas_call | solution.py:249
  10.0 7.6 %all-to-all-start = ((bf16[8,144,256]{2,1,0:T(8,128)(2,1)}), bf16[8,144,256]{2,1,0:T(8,128)(2,1)S(1)}, u32[]{:S(2)}, u32[]{:S(2)}) async-start(bf16[8,144,256]{2,1,0:T(8,128)(2,1)} %get-tuple-element.20), calls=%async_computation | async-start | bytes 1179648 | tf_op jit(solution)/shard_map/all_to_all | solution.py:386
  17.6 16.6 %all-to-all-done = bf16[8,144,256]{2,1,0:T(8,128)(2,1)S(1)} async-done(((bf16[8,144,256]{2,1,0:T(8,128)(2,1)}), bf16[8,144,256]{2,1,0:T(8,128)(2,1)S(1)}, u32[]{:S(2)}, u32[]{:S(2)}) %all-to-all-start) | async-done | bytes 589856 | tf_op jit(solution)/shard_map/all_to_all | solution.py:386
  34.2 1.9 %collective-permute-start = (bf16[2,16,32]{2,1,0:T(8,128)(2,1)S(1)}, bf16[2,16,32]{2,1,0:T(8,128)(2,1)S(1)}, u32[]{:S(2)}, u32[]{:S(2)}) collective-permute-start(bf16[2,16,32]{2,1,0:T(8,128)(2,1)S(1)} %constant_dynamic-slice_fusion.1), channel_id=1, source_target_pairs={{0,16},{16,0},{1,17},{17,1},{2,18},{18,2},{3,19},{19,3},{4,20},{20... | collective-permute-start | bytes 6152 | tf_op jit(solution)/shard_map/ppermute | solution.py:354
  37.6 4.8 %all-to-all-start.1 = ((bf16[4,8,128,128]{3,2,1,0:T(8,128)(2,1)}), bf16[4,8,128,128]{3,2,1,0:T(8,128)(2,1)S(1)}, u32[]{:S(2)}, u32[]{:S(2)}) async-start(bf16[4,8,128,128]{3,2,1,0:T(8,128)(2,1)} %broadcast_in_dim.56), calls=%async_computation.1 | async-start | bytes 2097152 | tf_op jit(solution)/shard_map/all_to_all | solution.py:344
  44.3 4.8 %collective-permute-start.2 = (bf16[8,128,128]{2,1,0:T(8,128)(2,1)S(1)}, bf16[8,128,128]{2,1,0:T(8,128)(2,1)S(1)}, u32[]{:S(2)}, u32[]{:S(2)}) collective-permute-start(bf16[8,128,128]{2,1,0:T(8,128)(2,1)S(1)} %get-tuple-element.23.v0), channel_id=1, source_target_pairs={{0,256},{128,384},{256,0},{384,128},{1,257},{129,385},{257,1},{385... | collective-permute-start | bytes 786440 | tf_op jit(solution)/shard_map/ppermute | solution.py:350
  49.1 1.9 %collective-permute-start.1 = (bf16[8,128,128]{2,1,0:T(8,128)(2,1)S(1)}, bf16[8,128,128]{2,1,0:T(8,128)(2,1)S(1)}, u32[]{:S(2)}, u32[]{:S(2)}) collective-permute-start(bf16[8,128,128]{2,1,0:T(8,128)(2,1)S(1)} %get-tuple-element.23.v0), channel_id=1, source_target_pairs={{0,384},{128,0},{256,128},{384,256},{1,385},{129,1},{257,129},{385... | collective-permute-start | bytes 786440 | tf_op jit(solution)/shard_map/ppermute | solution.py:350
  53.4 3.4 %all-to-all-done.1 = bf16[4,8,128,128]{3,2,1,0:T(8,128)(2,1)S(1)} async-done(((bf16[4,8,128,128]{3,2,1,0:T(8,128)(2,1)}), bf16[4,8,128,128]{3,2,1,0:T(8,128)(2,1)S(1)}, u32[]{:S(2)}, u32[]{:S(2)}) %all-to-all-start.1) | async-done | bytes 1048608 | tf_op jit(solution)/shard_map/all_to_all | solution.py:344
  56.8 3.8 %all-gather.3.cloned.1.call-done = bf16[4352,512]{1,0:T(8,128)(2,1)} async-done(((bf16[272,512]{1,0:T(8,128)(2,1)}), bf16[4352,512]{1,0:T(8,128)(2,1)}) %all-gather.3.cloned.1.call-update) | async-done | bytes 4456464 | tf_op jit(solution)/shard_map/all_gather | solution.py:385
  60.6 5.2 %row_statistics.1 = (f32[16,1,512]{2,1,0:T(1,128)S(1)}, f32[16,16,1,512]{3,2,1,0:T(1,128)}) custom-call(s32[516]{0:T(1024)S(1)} %pad.4.pairs_ref, s32[1]{0:T(128)} %bitcast.6.count_ref, bf16[16,272,512]{2,1,0:T(8,128)(2,1)} %bitcast.27, bf16[32,128,128]{2,1,0:T(8,128)(2,1)S(1)} %bitcast.19), custom_call_target="tpu_custom_call" | custom-call | flops 10000000000 | bytes 4194304 | tf_op jit(solution)/shard_map/row_statistics/pallas_call | solution.py:277
  65.8 8.0 %all-to-all-start.2 = ((f32[16,64,128]{2,1,0:T(8,128)}), f32[16,64,128]{2,1,0:T(8,128)S(1)}, u32[]{:S(2)}, u32[]{:S(2)}) async-start(f32[16,64,128]{2,1,0:T(8,128)} %bitcast.11), calls=%async_computation.2 | async-start | bytes 1048576 | tf_op jit(solution)/shard_map/all_to_all | solution.py:403
  73.9 5.9 %query_gradient.1 = (bf16[8,128,512]{2,1,0:T(8,128)(2,1)S(1)}, bf16[8,128,512]{2,1,0:T(8,128)(2,1)S(1)}) custom-call(s32[516]{0:T(1024)S(1)} %pad.4.pairs_ref, s32[1]{0:T(128)} %bitcast.6.count_ref, s32[1]{0:T(128)} %bitcast.7.core_ref, s32[1]{0:T(128)} %bitcast.8.x_ref, bf16[16,272,512]{2,1,0:T(8,128)(2,1)} %bitcast.28, bf16[32,128,128]{2,1,0:T(8,128)(2,1)} %bitcast.20, ...), custom_call_target="tpu_custom_call" | custom-call | flops 10000000000 | bytes 8388608 | tf_op jit(solution)/shard_map/query_gradient/pallas_call | solution.py:300
  80.8 2.3 %collective-permute-start.4 = (bf16[8,128,512]{2,1,0:T(8,128)(2,1)S(1)}, bf16[8,128,512]{2,1,0:T(8,128)(2,1)}, u32[]{:S(2)}, u32[]{:S(2)}) collective-permute-start(bf16[8,128,512]{2,1,0:T(8,128)(2,1)S(1)} %get-tuple-element.27), channel_id=1, source_target_pairs={{0,16},{16,0},{1,17},{17,1},{2,18},{18,2},{3,19},{19,3},{4,20},{20... | collective-permute-start | bytes 3145736 | tf_op jit(solution)/shard_map/ppermute | solution.py:354
  83.1 6.4 %all-to-all-done.2 = f32[16,64,128]{2,1,0:T(8,128)S(1)} async-done(((f32[16,64,128]{2,1,0:T(8,128)}), f32[16,64,128]{2,1,0:T(8,128)S(1)}, u32[]{:S(2)}, u32[]{:S(2)}) %all-to-all-start.2) | async-done | bytes 524320 | tf_op jit(solution)/shard_map/all_to_all | solution.py:403
  89.7 7.2 %key_gradient.1 = (bf16[8,128,512]{2,1,0:T(8,128)(2,1)}, bf16[8,128,128]{2,1,0:T(8,128)(2,1)S(1)}, bf16[8,128,128]{2,1,0:T(8,128)(2,1)S(1)}, bf16[8,128,128]{2,1...) custom-call(s32[516]{0:T(1024)S(1)} %pad.4.pairs_ref, ...), custom_call_target="tpu_custom_call" | custom-call | flops 10000000000 | bytes 8388608 | tf_op jit(solution)/shard_map/key_gradient/pallas_call | solution.py:320
  97.0 1.9 %collective-permute-start.5 = (bf16[8,128,128]{2,1,0:T(8,128)(2,1)S(1)}, bf16[8,128,128]{2,1,0:T(8,128)(2,1)S(1)}, u32[]{:S(2)}, u32[]{:S(2)}) collective-permute-start(bf16[8,128,128]{2,1,0:T(8,128)(2,1)S(1)} %get-tuple-element.30), channel_id=1, source_target_pairs={{0,256},{128,384},{256,0},{384,128},{1,257},{129,385},{257,1},{385... | collective-permute-start | bytes 786440 | tf_op jit(solution)/shard_map/ppermute | solution.py:350
  98.9 2.6 %collective-permute-start.6 = (bf16[8,128,128]{2,1,0:T(8,128)(2,1)S(1)}, bf16[8,128,128]{2,1,0:T(8,128)(2,1)S(1)}, u32[]{:S(2)}, u32[]{:S(2)}) collective-permute-start(bf16[8,128,128]{2,1,0:T(8,128)(2,1)S(1)} %get-tuple-element.31), channel_id=1, source_target_pairs={{0,128},{128,256},{256,384},{384,0},{1,129},{129,257},{257,385},{3... | collective-permute-start | bytes 786440 | tf_op jit(solution)/shard_map/ppermute | solution.py:350
  101.5 3.3 %collective-permute-start.7 = (bf16[8,128,128]{2,1,0:T(8,128)(2,1)S(1)}, bf16[8,128,128]{2,1,0:T(8,128)(2,1)S(1)}, u32[]{:S(2)}, u32[]{:S(2)}) collective-permute-start(bf16[8,128,128]{2,1,0:T(8,128)(2,1)S(1)} %get-tuple-element.32), channel_id=1, source_target_pairs={{0,384},{128,0},{256,128},{384,256},{1,385},{129,1},{257,129},{385... | collective-permute-start | bytes 786440 | tf_op jit(solution)/shard_map/ppermute | solution.py:350
  104.7 5.4 %collective-permute-start.8 = (bf16[8,128,128]{2,1,0:T(8,128)(2,1)S(1)}, bf16[8,128,128]{2,1,0:T(8,128)(2,1)S(1)}, u32[]{:S(2)}, u32[]{:S(2)}) collective-permute-start(bf16[8,128,128]{2,1,0:T(8,128)(2,1)S(1)} %get-tuple-element.34), channel_id=1, source_target_pairs={{0,256},{128,384},{256,0},{384,128},{1,257},{129,385},{257,1},{385... | collective-permute-start | bytes 786440 | tf_op jit(solution)/shard_map/ppermute | solution.py:350
  110.2 2.5 %collective-permute-start.9 = (bf16[8,128,128]{2,1,0:T(8,128)(2,1)S(1)}, bf16[8,128,128]{2,1,0:T(8,128)(2,1)S(1)}, u32[]{:S(2)}, u32[]{:S(2)}) collective-permute-start(bf16[8,128,128]{2,1,0:T(8,128)(2,1)S(1)} %get-tuple-element.35), channel_id=1, source_target_pairs={{0,128},{128,256},{256,384},{384,0},{1,129},{129,257},{257,385},{3... | collective-permute-start | bytes 786440 | tf_op jit(solution)/shard_map/ppermute | solution.py:350
  112.7 3.3 %collective-permute-start.10 = (bf16[8,128,128]{2,1,0:T(8,128)(2,1)S(1)}, bf16[8,128,128]{2,1,0:T(8,128)(2,1)S(1)}, u32[]{:S(2)}, u32[]{:S(2)}) collective-permute-start(bf16[8,128,128]{2,1,0:T(8,128)(2,1)S(1)} %get-tuple-element.36), channel_id=1, source_target_pairs={{0,384},{128,0},{256,128},{384,256},{1,385},{129,1},{257,129},{385... | collective-permute-start | bytes 786440 | tf_op jit(solution)/shard_map/ppermute | solution.py:350
  116.9 12.5 %all-to-all-start.3 = ((bf16[8,128,128]{2,1,0:T(8,128)(2,1)}), bf16[8,128,128]{2,1,0:T(8,128)(2,1)S(1)}, u32[]{:S(2)}, u32[]{:S(2)}) async-start(bf16[8,128,128]{2,1,0:T(8,128)(2,1)} %add_convert_fusion.1), calls=%async_computation.4 | async-start | bytes 524288 | tf_op jit(solution)/shard_map/all_to_all | solution.py:360
  129.6 8.7 %all-to-all-done.3.dk_ref = bf16[8,128,128]{2,1,0:T(8,128)(2,1)S(1)} async-done(((bf16[8,128,128]{2,1,0:T(8,128)(2,1)}), bf16[8,128,128]{2,1,0:T(8,128)(2,1)S(1)}, u32[]{:S(2)}, u32[]{:S(2)}) %all-to-all-start.3) | async-done | bytes 262176 | tf_op jit(solution)/shard_map/all_to_all | solution.py:360
  138.3 12.0 %all_to_all.25.dv_ref = bf16[8,128,128]{2,1,0:T(8,128)(2,1)} all-to-all(bf16[8,128,128]{2,1,0:T(8,128)(2,1)S(1)} %add_convert_fusion), channel_id=1, replica_groups=mesh['x'=4,'yl'=4,'c'=2,'yh'=2,'z'=8] {'yl','yh'}, dimensions={0} | all-to-all | bytes 524288 | tf_op jit(solution)/shard_map/all_to_all | solution.py:360
  (46 shorter events, 9.8 us)
Async XLA Ops:
  7.2 53.5 %all-gather.3.cloned.1.call-start = ((), (), s32[]{:S(2)}) async-start(), calls=%async_computation.7 | async-start | bytes 4734976 | tf_op jit(solution)/shard_map/all_gather | solution.py:385
  10.0 24.2 %all-to-all-start = ((bf16[8,144,256]{2,1,0:T(8,128)(2,1)}), bf16[8,144,256]{2,1,0:T(8,128)(2,1)S(1)}, u32[]{:S(2)}, u32[]{:S(2)}) async-start(bf16[8,144,256]{2,1,0:T(8,128)(2,1)} %get-tuple-element.20), calls=%async_computation | async-start | bytes 1179648 | tf_op jit(solution)/shard_map/all_to_all | solution.py:386
  34.2 8.1 %collective-permute-start = (bf16[2,16,32]{2,1,0:T(8,128)(2,1)S(1)}, bf16[2,16,32]{2,1,0:T(8,128)(2,1)S(1)}, u32[]{:S(2)}, u32[]{:S(2)}) collective-permute-start(bf16[2,16,32]{2,1,0:T(8,128)(2,1)S(1)} %constant_dynamic-slice_fusion.1), channel_id=1, source_target_pairs={{0,16},{16,0},{1,17},{17,1},{2,18},{18,2},{3,19},{19,3},{4,20},{20... | collective-permute-start | bytes 6152 | tf_op jit(solution)/shard_map/ppermute | solution.py:354
  37.6 19.3 %all-to-all-start.1 = ((bf16[4,8,128,128]{3,2,1,0:T(8,128)(2,1)}), bf16[4,8,128,128]{3,2,1,0:T(8,128)(2,1)S(1)}, u32[]{:S(2)}, u32[]{:S(2)}) async-start(bf16[4,8,128,128]{3,2,1,0:T(8,128)(2,1)} %broadcast_in_dim.56), calls=%async_computation.1 | async-start | bytes 2097152 | tf_op jit(solution)/shard_map/all_to_all | solution.py:344
  42.3 31.6 %collective-permute-start.3 = (bf16[8,128,128]{2,1,0:T(8,128)(2,1)S(1)}, bf16[8,128,128]{2,1,0:T(8,128)(2,1)S(1)}, u32[]{:S(2)}, u32[]{:S(2)}) collective-permute-start(bf16[8,128,128]{2,1,0:T(8,128)(2,1)S(1)} %get-tuple-element.23.v0), channel_id=1, source_target_pairs={{0,128},{128,256},{256,384},{384,0},{1,129},{129,257},{257,385},{3... | collective-permute-start | bytes 786440 | tf_op jit(solution)/shard_map/ppermute | solution.py:350
  44.3 29.7 %collective-permute-start.2 = (bf16[8,128,128]{2,1,0:T(8,128)(2,1)S(1)}, bf16[8,128,128]{2,1,0:T(8,128)(2,1)S(1)}, u32[]{:S(2)}, u32[]{:S(2)}) collective-permute-start(bf16[8,128,128]{2,1,0:T(8,128)(2,1)S(1)} %get-tuple-element.23.v0), channel_id=1, source_target_pairs={{0,256},{128,384},{256,0},{384,128},{1,257},{129,385},{257,1},{385... | collective-permute-start | bytes 786440 | tf_op jit(solution)/shard_map/ppermute | solution.py:350
  49.1 24.9 %collective-permute-start.1 = (bf16[8,128,128]{2,1,0:T(8,128)(2,1)S(1)}, bf16[8,128,128]{2,1,0:T(8,128)(2,1)S(1)}, u32[]{:S(2)}, u32[]{:S(2)}) collective-permute-start(bf16[8,128,128]{2,1,0:T(8,128)(2,1)S(1)} %get-tuple-element.23.v0), channel_id=1, source_target_pairs={{0,384},{128,0},{256,128},{384,256},{1,385},{129,1},{257,129},{385... | collective-permute-start | bytes 786440 | tf_op jit(solution)/shard_map/ppermute | solution.py:350
  56.8 9.0 %copy-start = (bf16[4,8,128,128]{3,2,1,0:T(8,128)(2,1)}, bf16[4,8,128,128]{3,2,1,0:T(8,128)(2,1)S(1)}, u32[]{:S(2)}) copy-start(bf16[4,8,128,128]{3,2,1,0:T(8,128)(2,1)S(1)} %all-to-all-done.1) | copy-start | bytes 3145732
  65.8 23.7 %all-to-all-start.2 = ((f32[16,64,128]{2,1,0:T(8,128)}), f32[16,64,128]{2,1,0:T(8,128)S(1)}, u32[]{:S(2)}, u32[]{:S(2)}) async-start(f32[16,64,128]{2,1,0:T(8,128)} %bitcast.11), calls=%async_computation.2 | async-start | bytes 1048576 | tf_op jit(solution)/shard_map/all_to_all | solution.py:403
  73.9 76.5 %reduce-scatter.2.cloned.1.call-start = ((), (), s32[]{:S(2)}) async-start(), calls=%async_computation.6 | async-start | bytes 1179648 | tf_op jit(solution)/shard_map/reduce_scatter | solution.py:415
  79.8 1.0 copy-start.1
  80.8 8.9 %collective-permute-start.4 = (bf16[8,128,512]{2,1,0:T(8,128)(2,1)S(1)}, bf16[8,128,512]{2,1,0:T(8,128)(2,1)}, u32[]{:S(2)}, u32[]{:S(2)}) collective-permute-start(bf16[8,128,512]{2,1,0:T(8,128)(2,1)S(1)} %get-tuple-element.27), channel_id=1, source_target_pairs={{0,16},{16,0},{1,17},{17,1},{2,18},{18,2},{3,19},{19,3},{4,20},{20... | collective-permute-start | bytes 3145736 | tf_op jit(solution)/shard_map/ppermute | solution.py:354
  97.0 15.8 %collective-permute-start.5 = (bf16[8,128,128]{2,1,0:T(8,128)(2,1)S(1)}, bf16[8,128,128]{2,1,0:T(8,128)(2,1)S(1)}, u32[]{:S(2)}, u32[]{:S(2)}) collective-permute-start(bf16[8,128,128]{2,1,0:T(8,128)(2,1)S(1)} %get-tuple-element.30), channel_id=1, source_target_pairs={{0,256},{128,384},{256,0},{384,128},{1,257},{129,385},{257,1},{385... | collective-permute-start | bytes 786440 | tf_op jit(solution)/shard_map/ppermute | solution.py:350
  98.9 17.2 %collective-permute-start.6 = (bf16[8,128,128]{2,1,0:T(8,128)(2,1)S(1)}, bf16[8,128,128]{2,1,0:T(8,128)(2,1)S(1)}, u32[]{:S(2)}, u32[]{:S(2)}) collective-permute-start(bf16[8,128,128]{2,1,0:T(8,128)(2,1)S(1)} %get-tuple-element.31), channel_id=1, source_target_pairs={{0,128},{128,256},{256,384},{384,0},{1,129},{129,257},{257,385},{3... | collective-permute-start | bytes 786440 | tf_op jit(solution)/shard_map/ppermute | solution.py:350
  101.5 14.6 %collective-permute-start.7 = (bf16[8,128,128]{2,1,0:T(8,128)(2,1)S(1)}, bf16[8,128,128]{2,1,0:T(8,128)(2,1)S(1)}, u32[]{:S(2)}, u32[]{:S(2)}) collective-permute-start(bf16[8,128,128]{2,1,0:T(8,128)(2,1)S(1)} %get-tuple-element.32), channel_id=1, source_target_pairs={{0,384},{128,0},{256,128},{384,256},{1,385},{129,1},{257,129},{385... | collective-permute-start | bytes 786440 | tf_op jit(solution)/shard_map/ppermute | solution.py:350
  104.7 24.7 %collective-permute-start.8 = (bf16[8,128,128]{2,1,0:T(8,128)(2,1)S(1)}, bf16[8,128,128]{2,1,0:T(8,128)(2,1)S(1)}, u32[]{:S(2)}, u32[]{:S(2)}) collective-permute-start(bf16[8,128,128]{2,1,0:T(8,128)(2,1)S(1)} %get-tuple-element.34), channel_id=1, source_target_pairs={{0,256},{128,384},{256,0},{384,128},{1,257},{129,385},{257,1},{385... | collective-permute-start | bytes 786440 | tf_op jit(solution)/shard_map/ppermute | solution.py:350
  110.2 19.3 %collective-permute-start.9 = (bf16[8,128,128]{2,1,0:T(8,128)(2,1)S(1)}, bf16[8,128,128]{2,1,0:T(8,128)(2,1)S(1)}, u32[]{:S(2)}, u32[]{:S(2)}) collective-permute-start(bf16[8,128,128]{2,1,0:T(8,128)(2,1)S(1)} %get-tuple-element.35), channel_id=1, source_target_pairs={{0,128},{128,256},{256,384},{384,0},{1,129},{129,257},{257,385},{3... | collective-permute-start | bytes 786440 | tf_op jit(solution)/shard_map/ppermute | solution.py:350
  112.7 16.7 %collective-permute-start.10 = (bf16[8,128,128]{2,1,0:T(8,128)(2,1)S(1)}, bf16[8,128,128]{2,1,0:T(8,128)(2,1)S(1)}, u32[]{:S(2)}, u32[]{:S(2)}) collective-permute-start(bf16[8,128,128]{2,1,0:T(8,128)(2,1)S(1)} %get-tuple-element.36), channel_id=1, source_target_pairs={{0,384},{128,0},{256,128},{384,256},{1,385},{129,1},{257,129},{385... | collective-permute-start | bytes 786440 | tf_op jit(solution)/shard_map/ppermute | solution.py:350
  116.9 21.4 %all-to-all-start.3 = ((bf16[8,128,128]{2,1,0:T(8,128)(2,1)}), bf16[8,128,128]{2,1,0:T(8,128)(2,1)S(1)}, u32[]{:S(2)}, u32[]{:S(2)}) async-start(bf16[8,128,128]{2,1,0:T(8,128)(2,1)} %add_convert_fusion.1), calls=%async_computation.4 | async-start | bytes 524288 | tf_op jit(solution)/shard_map/all_to_all | solution.py:360
  138.3 12.0 %copy-start.2 = (bf16[8,128,128]{2,1,0:T(8,128)(2,1)}, bf16[8,128,128]{2,1,0:T(8,128)(2,1)S(1)}, u32[]{:S(2)}) copy-start(bf16[8,128,128]{2,1,0:T(8,128)(2,1)S(1)} %all-to-all-done.3.dk_ref) | copy-start | bytes 786436
Sparse Core Ops, SparseCore 0:
  10.1 50.4 all-gather.2
  97.1 40.8 reduce-scatter.1

commit v6 on v5

--- a/solution.py
+++ b/solution.py
@@ -136,7 +136,7 @@
 
 def key_kernel(
     pairs_ref, count_ref, core_ref, x_ref, q_hbm, k_hbm, v0, v1, v2, v3, total_ref, own_ref,
-    far_ref, kept_hbm, got_hbm, chip_hbm, dk0, dk1, dk2, dk3, dv0, dv1, dv2, dv3,
+    far_ref, kept_hbm, got_hbm, chip_hbm, out0, out1, out2, out3,
     q_ref, k_ref, v_ref, k_acc, v_acc, p_ref, ds_ref, kept_ref, got_ref, chip_ref, sems,
 ):
     two = (
@@ -181,9 +181,9 @@
         return carry
 
     lax.fori_loop(0, blocks_of(count_ref, STEP), visit, 0)
-    for n, (dk_ref, dv_ref) in enumerate(((dk0, dv0), (dk1, dv1), (dk2, dv2), (dk3, dv3))):
-        dk_ref[...] = k_acc[of_x(x_ref, n)].astype(jnp.bfloat16)
-        dv_ref[...] = v_acc[of_x(x_ref, n)].astype(jnp.bfloat16)
+    for n, out_ref in enumerate((out0, out1, out2, out3)):
+        out_ref[:, :, :HD] = k_acc[of_x(x_ref, n)].astype(jnp.bfloat16)
+        out_ref[:, :, HD:] = v_acc[of_x(x_ref, n)].astype(jnp.bfloat16)
     leave.wait()
 
 
@@ -206,15 +206,18 @@
         copy.wait()
 
 
-def finish_kernel(dq_ref, dk_ref, dv_ref, query_ref, key_ref, value_ref):
+def finish_queries_kernel(dq_ref, query_ref):
     for h in range(HQ):
         cols = slice(h * TILE, (h + 1) * TILE)
         query_ref[:, cols] = (dq_ref[:, cols].astype(jnp.float32).T * SCALE).astype(jnp.bfloat16)
-    for parts_ref, out_ref, scale in ((dk_ref, key_ref, SCALE), (dv_ref, value_ref, 1.0)):
-        total = parts_ref[0].astype(jnp.float32)
-        for n in range(1, NY):
-            total += parts_ref[n].astype(jnp.float32)
-        out_ref[...] = (total * scale).astype(jnp.bfloat16)
+
+
+def finish_keys_kernel(over_y_ref, key_ref, value_ref):
+    sums = over_y_ref[0].astype(jnp.float32)
+    for n in range(1, NY):
+        sums += over_y_ref[n].astype(jnp.float32)
+    key_ref[...] = (sums[:, :HD] * SCALE).astype(jnp.bfloat16)
+    value_ref[...] = sums[:, HD:].astype(jnp.bfloat16)
 
 
 def vmem():
@@ -262,15 +265,25 @@
     )(q, g, o, k, v, mask)
 
 
-def call_finish(dq, dk, dv):
+def call_finish_queries(dq):
+    return pl.pallas_call(
+        finish_queries_kernel,
+        out_shape=jax.ShapeDtypeStruct((TILE, ROWS), jnp.bfloat16),
+        in_specs=[vmem()],
+        out_specs=vmem(),
+        name="finish_queries",
+    )(dq)
+
+
+def call_finish_keys(over_y):
     tile = jax.ShapeDtypeStruct((TILE, HD), jnp.bfloat16)
     return pl.pallas_call(
-        finish_kernel,
-        out_shape=(jax.ShapeDtypeStruct((TILE, ROWS), jnp.bfloat16), tile, tile),
-        in_specs=[vmem()] * 3,
-        out_specs=(vmem(),) * 3,
-        name="finish",
-    )(dq, dk, dv)
+        finish_keys_kernel,
+        out_shape=(tile, tile),
+        in_specs=[vmem()],
+        out_specs=(vmem(),) * 2,
+        name="finish_keys",
+    )(over_y)
 
 
 def call_stats(pairs, count, q, k):
@@ -315,13 +328,13 @@
 
 
 def call_key(pairs, count, core, x, q, k, values, total, own, far, kept, got):
-    quarter = jax.ShapeDtypeStruct((NY, TILE, HD), jnp.bfloat16)
+    quarter = jax.ShapeDtypeStruct((NY, TILE, 2 * HD), jnp.bfloat16)
     half = pltpu.VMEM((NZ, HD, ROWS), jnp.bfloat16)
     return pl.pallas_call(
         key_kernel,
-        out_shape=(jax.ShapeDtypeStruct((NZ, HD, ROWS), jnp.bfloat16),) + (quarter,) * 8,
+        out_shape=(jax.ShapeDtypeStruct((NZ, HD, ROWS), jnp.bfloat16),) + (quarter,) * 4,
         in_specs=[smem()] * 4 + [anywhere()] * 6 + [vmem()] * 3 + [anywhere()] * 2,
-        out_specs=(anywhere(),) + (vmem(),) * 8,
+        out_specs=(anywhere(),) + (vmem(),) * 4,
         scratch_shapes=loaded()
         + [
             pltpu.VMEM((NK + 1, TILE, HD), jnp.float32),
@@ -413,8 +426,10 @@
         pairs, count, core[None], x[None], q_all, k_all, v_all, total, part, far, kept, got
     )
     dq_own = lax.psum_scatter(chip, "z", scatter_dimension=0, tiled=True)[0]
-    dv_own, dk_own = sum_over_keys(*parts[4:]), sum_over_keys(*parts[:4])
-    return call_finish(dq_own, dk_own, dv_own)
+    query_grad, over_y = lax.optimization_barrier(
+        (call_finish_queries(dq_own), sum_over_keys(*parts))
+    )
+    return query_grad, *call_finish_keys(over_y)
 
 
 def solution(mesh):

time: 160 us -> 161 us (level)
  the two profiles are of different devices: /device:TPU:14 before, /device:TPU:9 now
where the time goes in v6:
time: 161 us
  waiting for transfers between devices  63.2 us (39%)
  starting transfers between devices  51.6 us (32%)
  Pallas kernels  22.7 us (14%)
  between operations  14.3 us (9%)
  other arithmetic  5.17 us (3%)
  local copies, waits for them, and re-layouts  3.51 us (2%)
    ppermute x6, starting transfers between devices, along_x(): return lax.ppermute(value, 'x', [(n, (n + by) % 4) for n in range(4)])  20.6 us
    ppermute x6, waiting for transfers between devices, along_x(): return lax.ppermute(value, 'x', [(n, (n + by) % 4) for n in range(4)])  18.6 us
    all_to_all x1, waiting for transfers between devices, body(): kv_y = lax.all_to_all(kv_own, Y, 0, 0, tiled=True)  17.4 us
    all_to_all x1, waiting for transfers between devices, sum_over_keys(): return lax.all_to_all(over_x, Y, 0, 0, tiled=True)  14.1 us
    all_to_all x1, starting transfers between devices, body(): parts = lax.all_to_all(parts, ('c', 'z'), 0, 0, tiled=True)  9.74 us
    all_to_all x1, waiting for transfers between devices, body(): parts = lax.all_to_all(parts, ('c', 'z'), 0, 0, tiled=True)  7.45 us
    all_to_all x1, starting transfers between devices, body(): kv_y = lax.all_to_all(kv_own, Y, 0, 0, tiled=True)  7.01 us
    pallas_call x1, Pallas kernels, call_key(): pl.pallas_call(key_kernel, out_shape=(jax.ShapeDtypeStruct((NZ, HD, ROWS)...  6.56 us
  transfers between devices with their start and end apart: 14, of which 7 were waited for; matrix products, arithmetic and copies ran while one was open for 5% of the time, Pallas kernels for 7%

profile of v6, /device:TPU:9, one launch (start us, length us, event | category | flops | bytes accessed | tf_op | source)
XLA Modules:
  0.0 160.5 jit_solution(13969981060344369733)
XLA Ops:
  7.2 2.8 %prepare.1 = (bf16[272,512]{1,0:T(8,128)(2,1)}, bf16[8,144,256]{2,1,0:T(8,128)(2,1)}) custom-call(bf16[128,512]{1,0:T(8,128)(2,1)} %q_in.1, bf16[128,512]{1,0:T(8,128)(2,1)} %g_in.1, bf16[128,512]{1,0:T(8,128)(2,1)} %o_in.1, bf16[128,128]{1,0:T(8,128)(2,1)} %k_in.1, bf16[128,128]{1,0:T(8,128)(2,1)} %v_in.1, s32[16,32]{1,0:T(8,128)} %mask_in.1), custom_call_target="tpu_custom_call" | custom-call | tf_op jit(solution)/shard_map/prepare/pallas_call | solution.py:252
  10.0 7.0 %all-to-all-start = ((bf16[8,144,256]{2,1,0:T(8,128)(2,1)}), bf16[8,144,256]{2,1,0:T(8,128)(2,1)S(1)}, u32[]{:S(2)}, u32[]{:S(2)}) async-start(bf16[8,144,256]{2,1,0:T(8,128)(2,1)} %get-tuple-element.20), calls=%async_computation | async-start | bytes 1179648 | tf_op jit(solution)/shard_map/all_to_all | solution.py:399
  17.0 17.4 %all-to-all-done = bf16[8,144,256]{2,1,0:T(8,128)(2,1)S(1)} async-done(((bf16[8,144,256]{2,1,0:T(8,128)(2,1)}), bf16[8,144,256]{2,1,0:T(8,128)(2,1)S(1)}, u32[]{:S(2)}, u32[]{:S(2)}) %all-to-all-start) | async-done | bytes 589856 | tf_op jit(solution)/shard_map/all_to_all | solution.py:399
  34.4 2.4 %collective-permute-start = (bf16[2,16,32]{2,1,0:T(8,128)(2,1)S(1)}, bf16[2,16,32]{2,1,0:T(8,128)(2,1)S(1)}, u32[]{:S(2)}, u32[]{:S(2)}) collective-permute-start(bf16[2,16,32]{2,1,0:T(8,128)(2,1)S(1)} %constant_dynamic-slice_fusion.1), channel_id=1, source_target_pairs={{0,16},{16,0},{1,17},{17,1},{2,18},{18,2},{3,19},{19,3},{4,20},{20... | collective-permute-start | bytes 6152 | tf_op jit(solution)/shard_map/ppermute | solution.py:367
  38.2 4.0 %all-to-all-start.1 = ((bf16[4,8,128,128]{3,2,1,0:T(8,128)(2,1)}), bf16[4,8,128,128]{3,2,1,0:T(8,128)(2,1)S(1)}, u32[]{:S(2)}, u32[]{:S(2)}) async-start(bf16[4,8,128,128]{3,2,1,0:T(8,128)(2,1)} %broadcast_in_dim.56), calls=%async_computation.1 | async-start | bytes 2097152 | tf_op jit(solution)/shard_map/all_to_all | solution.py:357
  42.2 3.4 %collective-permute-start.3 = (bf16[8,128,128]{2,1,0:T(8,128)(2,1)S(1)}, bf16[8,128,128]{2,1,0:T(8,128)(2,1)S(1)}, u32[]{:S(2)}, u32[]{:S(2)}) collective-permute-start(bf16[8,128,128]{2,1,0:T(8,128)(2,1)S(1)} %get-tuple-element.23.v0), channel_id=1, source_target_pairs={{0,128},{128,256},{256,384},{384,0},{1,129},{129,257},{257,385},{3... | collective-permute-start | bytes 786440 | tf_op jit(solution)/shard_map/ppermute | solution.py:363
  45.6 4.3 %collective-permute-start.2 = (bf16[8,128,128]{2,1,0:T(8,128)(2,1)S(1)}, bf16[8,128,128]{2,1,0:T(8,128)(2,1)S(1)}, u32[]{:S(2)}, u32[]{:S(2)}) collective-permute-start(bf16[8,128,128]{2,1,0:T(8,128)(2,1)S(1)} %get-tuple-element.23.v0), channel_id=1, source_target_pairs={{0,256},{128,384},{256,0},{384,128},{1,257},{129,385},{257,1},{385... | collective-permute-start | bytes 786440 | tf_op jit(solution)/shard_map/ppermute | solution.py:363
  49.9 3.1 %collective-permute-start.1 = (bf16[8,128,128]{2,1,0:T(8,128)(2,1)S(1)}, bf16[8,128,128]{2,1,0:T(8,128)(2,1)S(1)}, u32[]{:S(2)}, u32[]{:S(2)}) collective-permute-start(bf16[8,128,128]{2,1,0:T(8,128)(2,1)S(1)} %get-tuple-element.23.v0), channel_id=1, source_target_pairs={{0,384},{128,0},{256,128},{384,256},{1,385},{129,1},{257,129},{385... | collective-permute-start | bytes 786440 | tf_op jit(solution)/shard_map/ppermute | solution.py:363
  55.5 1.8 %all-to-all-done.1 = bf16[4,8,128,128]{3,2,1,0:T(8,128)(2,1)S(1)} async-done(((bf16[4,8,128,128]{3,2,1,0:T(8,128)(2,1)}), bf16[4,8,128,128]{3,2,1,0:T(8,128)(2,1)S(1)}, u32[]{:S(2)}, u32[]{:S(2)}) %all-to-all-start.1) | async-done | bytes 1048608 | tf_op jit(solution)/shard_map/all_to_all | solution.py:357
  57.2 3.8 %all-gather.3.cloned.1.call-done = bf16[4352,512]{1,0:T(8,128)(2,1)} async-done(((bf16[272,512]{1,0:T(8,128)(2,1)}), bf16[4352,512]{1,0:T(8,128)(2,1)}) %all-gather.3.cloned.1.call-update) | async-done | bytes 4456464 | tf_op jit(solution)/shard_map/all_gather | solution.py:398
  61.1 4.7 %row_statistics.1 = (f32[16,1,512]{2,1,0:T(1,128)S(1)}, f32[16,16,1,512]{3,2,1,0:T(1,128)}) custom-call(s32[516]{0:T(1024)S(1)} %pad.4.pairs_ref, s32[1]{0:T(128)} %bitcast.6.count_ref, bf16[16,272,512]{2,1,0:T(8,128)(2,1)} %bitcast.27, bf16[32,128,128]{2,1,0:T(8,128)(2,1)S(1)} %bitcast.19), custom_call_target="tpu_custom_call" | custom-call | flops 10000000000 | bytes 4194304 | tf_op jit(solution)/shard_map/row_statistics/pallas_call | solution.py:290
  65.8 9.7 %all-to-all-start.2 = ((f32[16,64,128]{2,1,0:T(8,128)}), f32[16,64,128]{2,1,0:T(8,128)}, u32[]{:S(2)}, u32[]{:S(2)}) async-start(f32[16,64,128]{2,1,0:T(8,128)} %bitcast.11), calls=%async_computation.2 | async-start | bytes 1048576 | tf_op jit(solution)/shard_map/all_to_all | solution.py:416
  75.6 5.3 %query_gradient.1 = (bf16[8,128,512]{2,1,0:T(8,128)(2,1)S(1)}, bf16[8,128,512]{2,1,0:T(8,128)(2,1)S(1)}) custom-call(s32[516]{0:T(1024)S(1)} %pad.4.pairs_ref, s32[1]{0:T(128)} %bitcast.6.count_ref, s32[1]{0:T(128)} %bitcast.7.core_ref, s32[1]{0:T(128)} %bitcast.8.x_ref, bf16[16,272,512]{2,1,0:T(8,128)(2,1)} %bitcast.28, bf16[32,128,128]{2,1,0:T(8,128)(2,1)} %bitcast.20, ...), custom_call_target="tpu_custom_call" | custom-call | flops 10000000000 | bytes 8388608 | tf_op jit(solution)/shard_map/query_gradient/pallas_call | solution.py:313
  80.9 2.1 %collective-permute-start.4 = (bf16[8,128,512]{2,1,0:T(8,128)(2,1)S(1)}, bf16[8,128,512]{2,1,0:T(8,128)(2,1)}, u32[]{:S(2)}, u32[]{:S(2)}) collective-permute-start(bf16[8,128,512]{2,1,0:T(8,128)(2,1)S(1)} %get-tuple-element.27), channel_id=1, source_target_pairs={{0,16},{16,0},{1,17},{17,1},{2,18},{18,2},{3,19},{19,3},{4,20},{20... | collective-permute-start | bytes 3145736 | tf_op jit(solution)/shard_map/ppermute | solution.py:367
  83.0 7.4 %all-to-all-done.2 = f32[16,64,128]{2,1,0:T(8,128)} async-done(((f32[16,64,128]{2,1,0:T(8,128)}), f32[16,64,128]{2,1,0:T(8,128)}, u32[]{:S(2)}, u32[]{:S(2)}) %all-to-all-start.2) | async-done | bytes 524320 | tf_op jit(solution)/shard_map/all_to_all | solution.py:416
  93.5 6.6 %key_gradient.1 = (bf16[8,128,512]{2,1,0:T(8,128)(2,1)}, bf16[8,128,256]{2,1,0:T(8,128)(2,1)S(1)}, bf16[8,128,256]{2,1,0:T(8,128)(2,1)S(1)}, bf16[8,128,256]{2,1,0:T(8,128)(2,1)S(1)}, bf16[8,128,256]{2,1,0:T(8,128)(2,1)S(1)}) custom-call(s32[516]{0:T(1024)S(1)} %pad.4.pairs_ref, s32[1]{0:T(128)} %bitcast.6.count_ref, s32[1]{0:T(128)} %bitcast.7.core_ref, ...), custom_call_target="tpu_custom_call" | custom-call | flops 10000000000 | bytes 8388608 | tf_op jit(solution)/shard_map/key_gradient/pallas_call | solution.py:333
  100.1 3.3 %collective-permute-start.5 = (bf16[8,128,256]{2,1,0:T(8,128)(2,1)S(1)}, bf16[8,128,256]{2,1,0:T(8,128)(2,1)S(1)}, u32[]{:S(2)}, u32[]{:S(2)}) collective-permute-start(bf16[8,128,256]{2,1,0:T(8,128)(2,1)S(1)} %get-tuple-element.30), channel_id=1, source_target_pairs={{0,256},{128,384},{256,0},{384,128},{1,257},{129,385},{257,1},{385... | collective-permute-start | bytes 1572872 | tf_op jit(solution)/shard_map/ppermute | solution.py:363
  103.4 2.5 %collective-permute-start.6 = (bf16[8,128,256]{2,1,0:T(8,128)(2,1)S(1)}, bf16[8,128,256]{2,1,0:T(8,128)(2,1)S(1)}, u32[]{:S(2)}, u32[]{:S(2)}) collective-permute-start(bf16[8,128,256]{2,1,0:T(8,128)(2,1)S(1)} %get-tuple-element.31), channel_id=1, source_target_pairs={{0,128},{128,256},{256,384},{384,0},{1,129},{129,257},{257,385},{3... | collective-permute-start | bytes 1572872 | tf_op jit(solution)/shard_map/ppermute | solution.py:363
  105.9 4.0 %collective-permute-start.7 = (bf16[8,128,256]{2,1,0:T(8,128)(2,1)S(1)}, bf16[8,128,256]{2,1,0:T(8,128)(2,1)S(1)}, u32[]{:S(2)}, u32[]{:S(2)}) collective-permute-start(bf16[8,128,256]{2,1,0:T(8,128)(2,1)S(1)} %get-tuple-element.32), channel_id=1, source_target_pairs={{0,384},{128,0},{256,128},{384,256},{1,385},{129,1},{257,129},{385... | collective-permute-start | bytes 1572872 | tf_op jit(solution)/shard_map/ppermute | solution.py:363
  109.9 6.0 %collective-permute-done.5 = bf16[8,128,256]{2,1,0:T(8,128)(2,1)S(1)} collective-permute-done((bf16[8,128,256]{2,1,0:T(8,128)(2,1)S(1)}, bf16[8,128,256]{2,1,0:T(8,128)(2,1)S(1)}, u32[]{:S(2)}, u32[]{:S(2)}) %collective-permute-start.5) | collective-permute-done | bytes 524320 | tf_op jit(solution)/shard_map/ppermute | solution.py:363
  115.9 12.6 %collective-permute-done.6 = bf16[8,128,256]{2,1,0:T(8,128)(2,1)S(1)} collective-permute-done((bf16[8,128,256]{2,1,0:T(8,128)(2,1)S(1)}, bf16[8,128,256]{2,1,0:T(8,128)(2,1)S(1)}, u32[]{:S(2)}, u32[]{:S(2)}) %collective-permute-start.6) | collective-permute-done | bytes 524320 | tf_op jit(solution)/shard_map/ppermute | solution.py:363
  129.6 5.8 %all-to-all-start.3 = ((bf16[8,128,256]{2,1,0:T(8,128)(2,1)}), bf16[8,128,256]{2,1,0:T(8,128)(2,1)S(1)}, u32[]{:S(2)}, u32[]{:S(2)}) async-start(bf16[8,128,256]{2,1,0:T(8,128)(2,1)} %add_convert_fusion), calls=%async_computation.4 | async-start | bytes 1048576 | tf_op jit(solution)/shard_map/all_to_all | solution.py:373
  137.1 14.1 %all-to-all-done.3.over_y_ref = bf16[8,128,256]{2,1,0:T(8,128)(2,1)S(1)} async-done(((bf16[8,128,256]{2,1,0:T(8,128)(2,1)}), bf16[8,128,256]{2,1,0:T(8,128)(2,1)S(1)}, u32[]{:S(2)}, u32[]{:S(2)}) %all-to-all-start.3) | async-done | bytes 524320 | tf_op jit(solution)/shard_map/all_to_all | solution.py:373
  152.0 1.7 %finish_keys.1 = (bf16[128,128]{1,0:T(8,128)(2,1)}, bf16[128,128]{1,0:T(8,128)(2,1)}) custom-call(bf16[8,128,256]{2,1,0:T(8,128)(2,1)} %copy-done.2), custom_call_target="tpu_custom_call" | custom-call | tf_op jit(solution)/shard_map/finish_keys/pallas_call | solution.py:280
  (39 shorter events, 10.5 us)
Async XLA Ops:
  7.2 53.9 %all-gather.3.cloned.1.call-start = ((), (), s32[]{:S(2)}) async-start(), calls=%async_computation.6 | async-start | bytes 4734976 | tf_op jit(solution)/shard_map/all_gather | solution.py:398
  10.0 24.4 %all-to-all-start = ((bf16[8,144,256]{2,1,0:T(8,128)(2,1)}), bf16[8,144,256]{2,1,0:T(8,128)(2,1)S(1)}, u32[]{:S(2)}, u32[]{:S(2)}) async-start(bf16[8,144,256]{2,1,0:T(8,128)(2,1)} %get-tuple-element.20), calls=%async_computation | async-start | bytes 1179648 | tf_op jit(solution)/shard_map/all_to_all | solution.py:399
  34.4 7.8 %collective-permute-start = (bf16[2,16,32]{2,1,0:T(8,128)(2,1)S(1)}, bf16[2,16,32]{2,1,0:T(8,128)(2,1)S(1)}, u32[]{:S(2)}, u32[]{:S(2)}) collective-permute-start(bf16[2,16,32]{2,1,0:T(8,128)(2,1)S(1)} %constant_dynamic-slice_fusion.1), channel_id=1, source_target_pairs={{0,16},{16,0},{1,17},{17,1},{2,18},{18,2},{3,19},{19,3},{4,20},{20... | collective-permute-start | bytes 6152 | tf_op jit(solution)/shard_map/ppermute | solution.py:367
  38.2 19.0 %all-to-all-start.1 = ((bf16[4,8,128,128]{3,2,1,0:T(8,128)(2,1)}), bf16[4,8,128,128]{3,2,1,0:T(8,128)(2,1)S(1)}, u32[]{:S(2)}, u32[]{:S(2)}) async-start(bf16[4,8,128,128]{3,2,1,0:T(8,128)(2,1)} %broadcast_in_dim.56), calls=%async_computation.1 | async-start | bytes 2097152 | tf_op jit(solution)/shard_map/all_to_all | solution.py:357
  42.2 33.4 %collective-permute-start.3 = (bf16[8,128,128]{2,1,0:T(8,128)(2,1)S(1)}, bf16[8,128,128]{2,1,0:T(8,128)(2,1)S(1)}, u32[]{:S(2)}, u32[]{:S(2)}) collective-permute-start(bf16[8,128,128]{2,1,0:T(8,128)(2,1)S(1)} %get-tuple-element.23.v0), channel_id=1, source_target_pairs={{0,128},{128,256},{256,384},{384,0},{1,129},{129,257},{257,385},{3... | collective-permute-start | bytes 786440 | tf_op jit(solution)/shard_map/ppermute | solution.py:363
  45.6 30.0 %collective-permute-start.2 = (bf16[8,128,128]{2,1,0:T(8,128)(2,1)S(1)}, bf16[8,128,128]{2,1,0:T(8,128)(2,1)S(1)}, u32[]{:S(2)}, u32[]{:S(2)}) collective-permute-start(bf16[8,128,128]{2,1,0:T(8,128)(2,1)S(1)} %get-tuple-element.23.v0), channel_id=1, source_target_pairs={{0,256},{128,384},{256,0},{384,128},{1,257},{129,385},{257,1},{385... | collective-permute-start | bytes 786440 | tf_op jit(solution)/shard_map/ppermute | solution.py:363
  49.9 25.7 %collective-permute-start.1 = (bf16[8,128,128]{2,1,0:T(8,128)(2,1)S(1)}, bf16[8,128,128]{2,1,0:T(8,128)(2,1)S(1)}, u32[]{:S(2)}, u32[]{:S(2)}) collective-permute-start(bf16[8,128,128]{2,1,0:T(8,128)(2,1)S(1)} %get-tuple-element.23.v0), channel_id=1, source_target_pairs={{0,384},{128,0},{256,128},{384,256},{1,385},{129,1},{257,129},{385... | collective-permute-start | bytes 786440 | tf_op jit(solution)/shard_map/ppermute | solution.py:363
  57.2 8.6 %copy-start = (bf16[4,8,128,128]{3,2,1,0:T(8,128)(2,1)}, bf16[4,8,128,128]{3,2,1,0:T(8,128)(2,1)S(1)}, u32[]{:S(2)}) copy-start(bf16[4,8,128,128]{3,2,1,0:T(8,128)(2,1)S(1)} %all-to-all-done.1) | copy-start | bytes 3145732
  65.8 24.6 %all-to-all-start.2 = ((f32[16,64,128]{2,1,0:T(8,128)}), f32[16,64,128]{2,1,0:T(8,128)}, u32[]{:S(2)}, u32[]{:S(2)}) async-start(f32[16,64,128]{2,1,0:T(8,128)} %bitcast.11), calls=%async_computation.2 | async-start | bytes 1048576 | tf_op jit(solution)/shard_map/all_to_all | solution.py:416
  75.6 59.8 %reduce-scatter.2.cloned.1.call-start = ((), (), s32[]{:S(2)}) async-start(), calls=%async_computation.5 | async-start | bytes 1179648 | tf_op jit(solution)/shard_map/reduce_scatter | solution.py:428
  80.9 12.6 %copy-start.1 = (bf16[8,128,512]{2,1,0:T(8,128)(2,1)}, bf16[8,128,512]{2,1,0:T(8,128)(2,1)S(1)}, u32[]{:S(2)}) copy-start(bf16[8,128,512]{2,1,0:T(8,128)(2,1)S(1)} %get-tuple-element.26.kept_hbm) | copy-start | bytes 3145732
  80.9 12.5 %collective-permute-start.4 = (bf16[8,128,512]{2,1,0:T(8,128)(2,1)S(1)}, bf16[8,128,512]{2,1,0:T(8,128)(2,1)}, u32[]{:S(2)}, u32[]{:S(2)}) collective-permute-start(bf16[8,128,512]{2,1,0:T(8,128)(2,1)S(1)} %get-tuple-element.27), channel_id=1, source_target_pairs={{0,16},{16,0},{1,17},{17,1},{2,18},{18,2},{3,19},{19,3},{4,20},{20... | collective-permute-start | bytes 3145736 | tf_op jit(solution)/shard_map/ppermute | solution.py:367
  100.1 15.9 %collective-permute-start.5 = (bf16[8,128,256]{2,1,0:T(8,128)(2,1)S(1)}, bf16[8,128,256]{2,1,0:T(8,128)(2,1)S(1)}, u32[]{:S(2)}, u32[]{:S(2)}) collective-permute-start(bf16[8,128,256]{2,1,0:T(8,128)(2,1)S(1)} %get-tuple-element.30), channel_id=1, source_target_pairs={{0,256},{128,384},{256,0},{384,128},{1,257},{129,385},{257,1},{385... | collective-permute-start | bytes 1572872 | tf_op jit(solution)/shard_map/ppermute | solution.py:363
  103.4 25.1 %collective-permute-start.6 = (bf16[8,128,256]{2,1,0:T(8,128)(2,1)S(1)}, bf16[8,128,256]{2,1,0:T(8,128)(2,1)S(1)}, u32[]{:S(2)}, u32[]{:S(2)}) collective-permute-start(bf16[8,128,256]{2,1,0:T(8,128)(2,1)S(1)} %get-tuple-element.31), channel_id=1, source_target_pairs={{0,128},{128,256},{256,384},{384,0},{1,129},{129,257},{257,385},{3... | collective-permute-start | bytes 1572872 | tf_op jit(solution)/shard_map/ppermute | solution.py:363
  105.9 22.7 %collective-permute-start.7 = (bf16[8,128,256]{2,1,0:T(8,128)(2,1)S(1)}, bf16[8,128,256]{2,1,0:T(8,128)(2,1)S(1)}, u32[]{:S(2)}, u32[]{:S(2)}) collective-permute-start(bf16[8,128,256]{2,1,0:T(8,128)(2,1)S(1)} %get-tuple-element.32), channel_id=1, source_target_pairs={{0,384},{128,0},{256,128},{384,256},{1,385},{129,1},{257,129},{385... | collective-permute-start | bytes 1572872 | tf_op jit(solution)/shard_map/ppermute | solution.py:363
  129.6 21.5 %all-to-all-start.3 = ((bf16[8,128,256]{2,1,0:T(8,128)(2,1)}), bf16[8,128,256]{2,1,0:T(8,128)(2,1)S(1)}, u32[]{:S(2)}, u32[]{:S(2)}) async-start(bf16[8,128,256]{2,1,0:T(8,128)(2,1)} %add_convert_fusion), calls=%async_computation.4 | async-start | bytes 1048576 | tf_op jit(solution)/shard_map/all_to_all | solution.py:373
  151.2 0.8 copy-start.2
Sparse Core Ops, SparseCore 0:
  10.1 50.8 all-gather.2
  100.2 34.5 reduce-scatter.1

commit v7 on v6

--- a/solution.py
+++ b/solution.py
@@ -46,7 +46,7 @@
 
 
 def stats_kernel(
-    pairs_ref, count_ref, q_hbm, k_hbm, out_ref, sent_hbm, q_ref, k_ref, m_ref, l_ref, sems
+    pairs_ref, count_ref, q_hbm, k_hbm, out_ref, sent_hbm, q_ref, k_ref, m_ref, l_ref, sent_ref, sems
 ):
     copies = (
         pltpu.make_async_copy(q_hbm.at[:, pl.ds(0, TILE), :], q_ref, sems.at[0]),
@@ -78,7 +78,9 @@
     out_ref[...] = jnp.where(
         total > 0.0, m_ref[...][:NQ] + jnp.log2(jnp.maximum(total, 1e-30)), LOW
     )
-    copies = [pltpu.make_async_copy(out_ref, sent_hbm.at[n], sems.at[n]) for n in range(NQ)]
+    for n in range(NQ * HQ):
+        sent_ref[n : n + 1] = out_ref[n // HQ, :, n % HQ * TILE : (n % HQ + 1) * TILE]
+    copies = [pltpu.make_async_copy(sent_ref, sent_hbm.at[n], sems.at[n]) for n in range(NQ)]
     for copy in copies:
         copy.start()
     for copy in copies:
@@ -135,9 +137,9 @@
 
 
 def key_kernel(
-    pairs_ref, count_ref, core_ref, x_ref, q_hbm, k_hbm, v0, v1, v2, v3, total_ref, own_ref,
-    far_ref, kept_hbm, got_hbm, chip_hbm, out0, out1, out2, out3,
-    q_ref, k_ref, v_ref, k_acc, v_acc, p_ref, ds_ref, kept_ref, got_ref, chip_ref, sems,
+    pairs_ref, count_ref, core_ref, x_ref, z_ref, q_hbm, k_hbm, v0, v1, v2, v3, parts_ref,
+    kept_hbm, got_hbm, chip_hbm, out0, out1, out2, out3, q_ref, k_ref, v_ref, k_acc, v_acc,
+    p_ref, ds_ref, kept_ref, got_ref, chip_ref, total_ref, own_ref, far_ref, sems,
 ):
     two = (
         pltpu.make_async_copy(kept_hbm, kept_ref, sems.at[6]),
@@ -148,15 +150,27 @@
     copies = load(x_ref, q_hbm, k_hbm, (v0, v1, v2, v3), q_ref, k_ref, v_ref, sems)
     k_acc[...] = jnp.zeros(k_acc.shape, jnp.float32)
     v_acc[...] = jnp.zeros(v_acc.shape, jnp.float32)
+    top = parts_ref[0]
+    for n in range(1, NQ):
+        top = jnp.maximum(top, parts_ref[n])
+    summed = jnp.exp2(parts_ref[0] - top)
+    for n in range(1, NQ):
+        summed += jnp.exp2(parts_ref[n] - top)
+    total = top + jnp.log2(summed)
+    for n in range(NQ * HQ):
+        total_ref[n // HQ, :, n % HQ * TILE : (n % HQ + 1) * TILE] = total[n : n + 1]
+    own_ref[...] = jnp.exp2(parts_ref[core_ref[0] * NZ + z_ref[0]] - total)
+    far_ref[...] = jnp.exp2(parts_ref[(1 - core_ref[0]) * NZ + z_ref[0]] - total)
     for copy in two:
         copy.wait()
     for n in range(NZ):
-        r = core_ref[0] * NZ + n
-        own = jnp.exp2(own_ref[r] - total_ref[r])
-        far = jnp.exp2(far_ref[r] - total_ref[r])
-        chip_ref[n] = (
-            kept_ref[n].astype(jnp.float32) * own + got_ref[n].astype(jnp.float32) * far
-        ).astype(jnp.bfloat16)
+        for h in range(HQ):
+            row = pl.ds((core_ref[0] * NZ + n) * HQ + h, 1)
+            cols = slice(h * TILE, (h + 1) * TILE)
+            chip_ref[n, :, cols] = (
+                kept_ref[n, :, cols].astype(jnp.float32) * own_ref[row]
+                + got_ref[n, :, cols].astype(jnp.float32) * far_ref[row]
+            ).astype(jnp.bfloat16)
     leave = pltpu.make_async_copy(chip_ref, chip_hbm, sems.at[8])
     leave.start()
     for copy in copies:
@@ -187,21 +201,29 @@
     leave.wait()
 
 
-def prepare_kernel(q_in, g_in, o_in, k_in, v_in, mask_in, q_ref, kv_hbm, kv_ref, sems):
+def prepare_kernel(
+    q_in, g_in, o_in, k_in, v_in, mask_in, q_hbm, kv_hbm, kv_ref, delta_ref, sems
+):
+    rows = (pl.ds(0, TILE), pl.ds(TILE, TILE), pl.ds(2 * TILE, QPAD - 2 * TILE))
+    copies = [
+        pltpu.make_async_copy(source, q_hbm.at[row], sems.at[NY + n])
+        for n, (source, row) in enumerate(zip((q_in, g_in, delta_ref), rows))
+    ]
+    copies[0].start()
+    copies[1].start()
     kv_ref[:TILE, :HD] = k_in[...]
     kv_ref[:TILE, HD:] = v_in[...]
     kv_ref[TILE:, :] = jnp.zeros((KPAD - TILE, 2 * HD), jnp.bfloat16)
     kv_ref[TILE:, :NK] = mask_in[...].astype(jnp.float32).astype(jnp.bfloat16)
-    copies = [pltpu.make_async_copy(kv_ref, kv_hbm.at[n], sems.at[n]) for n in range(NY)]
-    for copy in copies:
-        copy.start()
-    q_ref[:TILE] = q_in[...]
-    q_ref[TILE : 2 * TILE] = g_in[...]
+    for n in range(NY):
+        copies.append(pltpu.make_async_copy(kv_ref, kv_hbm.at[n], sems.at[n]))
+        copies[-1].start()
     for h in range(HQ):
         cols = slice(h * HD, (h + 1) * HD)
         product = g_in[:, cols].astype(jnp.float32) * o_in[:, cols].astype(jnp.float32)
         delta = jnp.sum(product.T, axis=0, keepdims=True).astype(jnp.bfloat16)
-        q_ref[2 * TILE :, cols] = jnp.broadcast_to(delta, (QPAD - 2 * TILE, HD))
+        delta_ref[:, cols] = jnp.broadcast_to(delta, (QPAD - 2 * TILE, HD))
+    copies[2].start()
     for copy in copies:
         copy.wait()
 
@@ -232,8 +254,8 @@
     return pl.BlockSpec(memory_space=pl.ANY)
 
 
-def params():
-    return pltpu.CompilerParams(vmem_limit_bytes=50 * 1024 * 1024)
+def params(mib=50):
+    return pltpu.CompilerParams(vmem_limit_bytes=mib * 1024 * 1024)
 
 
 def cost(mib):
@@ -256,11 +278,13 @@
             jax.ShapeDtypeStruct((NY, KPAD, 2 * HD), jnp.bfloat16),
         ),
         in_specs=[vmem()] * 6,
-        out_specs=(vmem(), anywhere()),
+        out_specs=(anywhere(), anywhere()),
         scratch_shapes=[
             pltpu.VMEM((KPAD, 2 * HD), jnp.bfloat16),
-            pltpu.SemaphoreType.DMA((NY,)),
+            pltpu.VMEM((QPAD - 2 * TILE, ROWS), jnp.bfloat16),
+            pltpu.SemaphoreType.DMA((NY + 3,)),
         ],
+        compiler_params=params(8),
         name="prepare",
     )(q, g, o, k, v, mask)
 
@@ -271,6 +295,7 @@
         out_shape=jax.ShapeDtypeStruct((TILE, ROWS), jnp.bfloat16),
         in_specs=[vmem()],
         out_specs=vmem(),
+        compiler_params=params(8),
         name="finish_queries",
     )(dq)
 
@@ -282,6 +307,7 @@
         out_shape=(tile, tile),
         in_specs=[vmem()],
         out_specs=(vmem(),) * 2,
+        compiler_params=params(8),
         name="finish_keys",
     )(over_y)
 
@@ -291,7 +317,7 @@
         stats_kernel,
         out_shape=(
             jax.ShapeDtypeStruct((NQ, 1, ROWS), jnp.float32),
-            jax.ShapeDtypeStruct((NQ, NQ, 1, ROWS), jnp.float32),
+            jax.ShapeDtypeStruct((NQ, NQ * HQ, TILE), jnp.float32),
         ),
         in_specs=[smem()] * 2 + [anywhere()] * 2,
         out_specs=(vmem(), anywhere()),
@@ -300,6 +326,7 @@
             pltpu.VMEM((NK, TILE, HD), jnp.bfloat16),
             pltpu.VMEM((NQ + 1, 1, ROWS), jnp.float32),
             pltpu.VMEM((NQ + 1, 1, ROWS), jnp.float32),
+            pltpu.VMEM((NQ * HQ, TILE), jnp.float32),
             pltpu.SemaphoreType.DMA((NQ,)),
         ],
         compiler_params=params(),
@@ -327,13 +354,13 @@
     )(pairs, count, core, x, q, k, *values, part)
 
 
-def call_key(pairs, count, core, x, q, k, values, total, own, far, kept, got):
+def call_key(pairs, count, core, x, z, q, k, values, parts, kept, got):
     quarter = jax.ShapeDtypeStruct((NY, TILE, 2 * HD), jnp.bfloat16)
     half = pltpu.VMEM((NZ, HD, ROWS), jnp.bfloat16)
     return pl.pallas_call(
         key_kernel,
         out_shape=(jax.ShapeDtypeStruct((NZ, HD, ROWS), jnp.bfloat16),) + (quarter,) * 4,
-        in_specs=[smem()] * 4 + [anywhere()] * 6 + [vmem()] * 3 + [anywhere()] * 2,
+        in_specs=[smem()] * 5 + [anywhere()] * 6 + [vmem()] + [anywhere()] * 2,
         out_specs=(anywhere(),) + (vmem(),) * 4,
         scratch_shapes=loaded()
         + [
@@ -344,12 +371,15 @@
             half,
             half,
             half,
+            pltpu.VMEM((NQ, 1, ROWS), jnp.float32),
+            pltpu.VMEM((NQ * HQ, TILE), jnp.float32),
+            pltpu.VMEM((NQ * HQ, TILE), jnp.float32),
             pltpu.SemaphoreType.DMA((9,)),
         ],
         compiler_params=params(),
         cost_estimate=cost(8),
         name="key_gradient",
-    )(pairs, count, core, x, q, k, *values, total, own, far, kept, got)
+    )(pairs, count, core, x, z, q, k, *values, parts, kept, got)
 
 
 def to_everyone(value, axis):
@@ -389,7 +419,7 @@
 
 
 def body(query_states, out_grad, forward_out, key_states, value_states, block_mask):
-    core, x = lax.axis_index("c"), lax.axis_index("x")
+    core, x, z = (lax.axis_index(a) for a in ("c", "x", "z"))
     y_hi = lax.axis_index("yh")
     y_lo = lax.axis_index("yl")
     q_own, kv_own = call_prepare(
@@ -412,18 +442,13 @@
     pairs, count = list_pairs(mask)
 
     part, parts = call_stats(pairs, count, q_all, k_all)
-    parts = parts.reshape(NQ, NQ * ROWS // HD, HD)
     parts = lax.all_to_all(parts, ("c", "z"), 0, 0, tiled=True)
     kept, sent = call_query(pairs, count, core[None], x[None], q_all, k_all, v_all, part)
     got = swap_cores(sent)
 
-    top = jnp.max(parts, axis=0)
-    total = top + jnp.log2(jnp.sum(jnp.exp2(parts - top[None]), axis=0))
-    total = total.reshape(NQ, 1, ROWS)
-    far = lax.dynamic_index_in_dim(parts, (1 - core) * NZ + lax.axis_index("z"), 0, False)
-    far = far.reshape(NQ, 1, ROWS)
+    parts = jnp.maximum(parts, LOW)
     chip, *parts = call_key(
-        pairs, count, core[None], x[None], q_all, k_all, v_all, total, part, far, kept, got
+        pairs, count, core[None], x[None], z[None], q_all, k_all, v_all, parts, kept, got
     )
     dq_own = lax.psum_scatter(chip, "z", scatter_dimension=0, tiled=True)[0]
     query_grad, over_y = lax.optimization_barrier(

time: 161 us -> 161 us (level)
  the two profiles are of different devices: /device:TPU:9 before, /device:TPU:75 now
where the time goes in v7:
time: 161 us; the launch traced here: 160 us
  waiting for transfers between devices  62.8 us (39%)
  starting transfers between devices  50.4 us (31%)
  Pallas kernels  20.8 us (13%)
  between operations  14.3 us (9%)
  local copies, waits for them, and re-layouts  7.75 us (5%)
  other arithmetic  4.04 us (3%)
    ppermute x6, starting transfers between devices, along_x(): return lax.ppermute(value, 'x', [(n, (n + by) % 4) for n in range(4)])  20 us
    ppermute x6, waiting for transfers between devices, along_x(): return lax.ppermute(value, 'x', [(n, (n + by) % 4) for n in range(4)])  18.7 us
    all_to_all x1, waiting for transfers between devices, body(): kv_y = lax.all_to_all(kv_own, Y, 0, 0, tiled=True)  17.3 us
    all_to_all x1, waiting for transfers between devices, sum_over_keys(): return lax.all_to_all(over_x, Y, 0, 0, tiled=True)  14.3 us
    all_to_all x1, starting transfers between devices, body(): parts = lax.all_to_all(parts, ('c', 'z'), 0, 0, tiled=True)  8.64 us
    all_to_all x1, waiting for transfers between devices, body(): parts = lax.all_to_all(parts, ('c', 'z'), 0, 0, tiled=True)  7.37 us
    pallas_call x1, Pallas kernels, call_key(): pl.pallas_call(key_kernel, out_shape=(jax.ShapeDtypeStruct((NZ, HD, ROWS)...  7.27 us
    all_to_all x1, starting transfers between devices, body(): kv_y = lax.all_to_all(kv_own, Y, 0, 0, tiled=True)  7 us
  transfers between devices with their start and end apart: 14, of which 7 were waited for; matrix products, arithmetic and copies ran while one was open for 4% of the time, Pallas kernels for 7%

profile of v7, /device:TPU:75, one launch (start us, length us, event | category | flops | bytes accessed | tf_op | source)
XLA Modules:
  0.0 160.1 jit_solution(15269523898786439517)
XLA Ops:
  13.2 7.0 %all-to-all-start = ((bf16[8,144,256]{2,1,0:T(8,128)(2,1)}), bf16[8,144,256]{2,1,0:T(8,128)(2,1)S(1)}, u32[]{:S(2)}, u32[]{:S(2)}) async-start(bf16[8,144,256]{2,1,0:T(8,128)(2,1)} %get-tuple-element.20), calls=%async_computation | async-start | bytes 1179648 | tf_op jit(solution)/shard_map/all_to_all | solution.py:429
  20.2 17.3 %all-to-all-done = bf16[8,144,256]{2,1,0:T(8,128)(2,1)S(1)} async-done(((bf16[8,144,256]{2,1,0:T(8,128)(2,1)}), bf16[8,144,256]{2,1,0:T(8,128)(2,1)S(1)}, u32[]{:S(2)}, u32[]{:S(2)}) %all-to-all-start) | async-done | bytes 589856 | tf_op jit(solution)/shard_map/all_to_all | solution.py:429
  37.5 2.5 %collective-permute-start = (bf16[2,16,32]{2,1,0:T(8,128)(2,1)S(1)}, bf16[2,16,32]{2,1,0:T(8,128)(2,1)S(1)}, u32[]{:S(2)}, u32[]{:S(2)}) collective-permute-start(bf16[2,16,32]{2,1,0:T(8,128)(2,1)S(1)} %constant_dynamic-slice_fusion), channel_id=1, source_target_pairs={{0,16},{16,0},{1,17},{17,1},{2,18},{18,2},{3,19},{19,3},{4,20},{20... | collective-permute-start | bytes 6152 | tf_op jit(solution)/shard_map/ppermute | solution.py:397
  40.1 1.2 broadcast_in_dim.59
  41.4 4.3 %all-to-all-start.1 = ((bf16[4,8,128,128]{3,2,1,0:T(8,128)(2,1)}), bf16[4,8,128,128]{3,2,1,0:T(8,128)(2,1)S(1)}, u32[]{:S(2)}, u32[]{:S(2)}) async-start(bf16[4,8,128,128]{3,2,1,0:T(8,128)(2,1)} %broadcast_in_dim.59), calls=%async_computation.1 | async-start | bytes 2097152 | tf_op jit(solution)/shard_map/all_to_all | solution.py:387
  45.6 3.1 %collective-permute-start.3 = (bf16[8,128,128]{2,1,0:T(8,128)(2,1)S(1)}, bf16[8,128,128]{2,1,0:T(8,128)(2,1)S(1)}, u32[]{:S(2)}, u32[]{:S(2)}) collective-permute-start(bf16[8,128,128]{2,1,0:T(8,128)(2,1)S(1)} %get-tuple-element.23.v0), channel_id=1, source_target_pairs={{0,128},{128,256},{256,384},{384,0},{1,129},{129,257},{257,385},{3... | collective-permute-start | bytes 786440 | tf_op jit(solution)/shard_map/ppermute | solution.py:393
  48.7 2.5 %collective-permute-start.2 = (bf16[8,128,128]{2,1,0:T(8,128)(2,1)S(1)}, bf16[8,128,128]{2,1,0:T(8,128)(2,1)S(1)}, u32[]{:S(2)}, u32[]{:S(2)}) collective-permute-start(bf16[8,128,128]{2,1,0:T(8,128)(2,1)S(1)} %get-tuple-element.23.v0), channel_id=1, source_target_pairs={{0,256},{128,384},{256,0},{384,128},{1,257},{129,385},{257,1},{385... | collective-permute-start | bytes 786440 | tf_op jit(solution)/shard_map/ppermute | solution.py:393
  51.3 4.0 %collective-permute-start.1 = (bf16[8,128,128]{2,1,0:T(8,128)(2,1)S(1)}, bf16[8,128,128]{2,1,0:T(8,128)(2,1)S(1)}, u32[]{:S(2)}, u32[]{:S(2)}) collective-permute-start(bf16[8,128,128]{2,1,0:T(8,128)(2,1)S(1)} %get-tuple-element.23.v0), channel_id=1, source_target_pairs={{0,384},{128,0},{256,128},{384,256},{1,385},{129,1},{257,129},{385... | collective-permute-start | bytes 786440 | tf_op jit(solution)/shard_map/ppermute | solution.py:393
  57.7 1.8 %all-to-all-done.1 = bf16[4,8,128,128]{3,2,1,0:T(8,128)(2,1)S(1)} async-done(((bf16[4,8,128,128]{3,2,1,0:T(8,128)(2,1)}), bf16[4,8,128,128]{3,2,1,0:T(8,128)(2,1)S(1)}, u32[]{:S(2)}, u32[]{:S(2)}) %all-to-all-start.1) | async-done | bytes 1048608 | tf_op jit(solution)/shard_map/all_to_all | solution.py:387
  59.5 3.3 %all-gather.3.cloned.1.call-done = bf16[4352,512]{1,0:T(8,128)(2,1)} async-done(((bf16[272,512]{1,0:T(8,128)(2,1)}), bf16[4352,512]{1,0:T(8,128)(2,1)}) %all-gather.3.cloned.1.call-update) | async-done | bytes 4456464 | tf_op jit(solution)/shard_map/all_gather | solution.py:428
  62.8 5.2 %row_statistics.1 = (f32[16,1,512]{2,1,0:T(1,128)S(1)}, f32[16,64,128]{2,1,0:T(8,128)}) custom-call(s32[516]{0:T(1024)S(1)} %pad.4.pairs_ref, s32[1]{0:T(128)} %bitcast.6.count_ref, bf16[16,272,512]{2,1,0:T(8,128)(2,1)} %bitcast.23, bf16[32,128,128]{2,1,0:T(8,128)(2,1)S(1)} %bitcast.17), custom_call_target="tpu_custom_call" | custom-call | flops 10000000000 | bytes 4194304 | tf_op jit(solution)/shard_map/row_statistics/pallas_call | solution.py:316
  68.0 8.6 %all-to-all-start.2 = ((f32[16,64,128]{2,1,0:T(8,128)}), f32[16,64,128]{2,1,0:T(8,128)}, u32[]{:S(2)}, u32[]{:S(2)}) async-start(f32[16,64,128]{2,1,0:T(8,128)} %get-tuple-element.24), calls=%async_computation.2 | async-start | bytes 1048576 | tf_op jit(solution)/shard_map/all_to_all | solution.py:445
  76.7 5.9 %query_gradient.1 = (bf16[8,128,512]{2,1,0:T(8,128)(2,1)S(1)}, bf16[8,128,512]{2,1,0:T(8,128)(2,1)S(1)}) custom-call(s32[516]{0:T(1024)S(1)} %pad.4.pairs_ref, s32[1]{0:T(128)} %bitcast.6.count_ref, s32[1]{0:T(128)} %bitcast.7.core_ref, s32[1]{0:T(128)} %bitcast.8.x_ref, bf16[16,272,512]{2,1,0:T(8,128)(2,1)} %bitcast.24, bf16[32,128,128]{2,1,0:T(8,128)(2,1)} %bitcast.18, ...), custom_call_target="tpu_custom_call" | custom-call | flops 10000000000 | bytes 8388608 | tf_op jit(solution)/shard_map/query_gradient/pallas_call | solution.py:340
  82.6 1.9 %collective-permute-start.4 = (bf16[8,128,512]{2,1,0:T(8,128)(2,1)S(1)}, bf16[8,128,512]{2,1,0:T(8,128)(2,1)}, u32[]{:S(2)}, u32[]{:S(2)}) collective-permute-start(bf16[8,128,512]{2,1,0:T(8,128)(2,1)S(1)} %get-tuple-element.27), channel_id=1, source_target_pairs={{0,16},{16,0},{1,17},{17,1},{2,18},{18,2},{3,19},{19,3},{4,20},{20... | collective-permute-start | bytes 3145736 | tf_op jit(solution)/shard_map/ppermute | solution.py:397
  84.5 7.4 %all-to-all-done.2 = f32[16,64,128]{2,1,0:T(8,128)} async-done(((f32[16,64,128]{2,1,0:T(8,128)}), f32[16,64,128]{2,1,0:T(8,128)}, u32[]{:S(2)}, u32[]{:S(2)}) %all-to-all-start.2) | async-done | bytes 524320 | tf_op jit(solution)/shard_map/all_to_all | solution.py:445
  91.9 1.1 broadcast_maximum_fusion.parts_ref
  93.0 7.3 %key_gradient.1 = (bf16[8,128,512]{2,1,0:T(8,128)(2,1)}, bf16[8,128,256]{2,1,0:T(8,128)(2,1)S(1)}, bf16[8,128,256]{2,1,0:T(8,128)(2,1)S(1)}, bf16[8,128,256]{2,1,0:T(8,128)(2,1)S(1)}, bf16[8,128,256]{2,1,0:T(8,128)(2,1)S(1)}) custom-call(s32[516]{0:T(1024)S(1)} %pad.4.pairs_ref, s32[1]{0:T(128)} %bitcast.6.count_ref, s32[1]{0:T(128)} %bitcast.7.core_ref, ...), custom_call_target="tpu_custom_call" | custom-call | flops 10000000000 | bytes 8388608 | tf_op jit(solution)/shard_map/key_gradient/pallas_call | solution.py:360
  100.3 4.3 %collective-permute-start.5 = (bf16[8,128,256]{2,1,0:T(8,128)(2,1)S(1)}, bf16[8,128,256]{2,1,0:T(8,128)(2,1)S(1)}, u32[]{:S(2)}, u32[]{:S(2)}) collective-permute-start(bf16[8,128,256]{2,1,0:T(8,128)(2,1)S(1)} %get-tuple-element.30), channel_id=1, source_target_pairs={{0,256},{128,384},{256,0},{384,128},{1,257},{129,385},{257,1},{385... | collective-permute-start | bytes 1572872 | tf_op jit(solution)/shard_map/ppermute | solution.py:393
  104.6 4.0 %collective-permute-start.6 = (bf16[8,128,256]{2,1,0:T(8,128)(2,1)S(1)}, bf16[8,128,256]{2,1,0:T(8,128)(2,1)S(1)}, u32[]{:S(2)}, u32[]{:S(2)}) collective-permute-start(bf16[8,128,256]{2,1,0:T(8,128)(2,1)S(1)} %get-tuple-element.31), channel_id=1, source_target_pairs={{0,128},{128,256},{256,384},{384,0},{1,129},{129,257},{257,385},{3... | collective-permute-start | bytes 1572872 | tf_op jit(solution)/shard_map/ppermute | solution.py:393
  108.6 2.2 %collective-permute-start.7 = (bf16[8,128,256]{2,1,0:T(8,128)(2,1)S(1)}, bf16[8,128,256]{2,1,0:T(8,128)(2,1)S(1)}, u32[]{:S(2)}, u32[]{:S(2)}) collective-permute-start(bf16[8,128,256]{2,1,0:T(8,128)(2,1)S(1)} %get-tuple-element.32), channel_id=1, source_target_pairs={{0,384},{128,0},{256,128},{384,256},{1,385},{129,1},{257,129},{385... | collective-permute-start | bytes 1572872 | tf_op jit(solution)/shard_map/ppermute | solution.py:393
  110.8 5.5 %collective-permute-done.5 = bf16[8,128,256]{2,1,0:T(8,128)(2,1)S(1)} collective-permute-done((bf16[8,128,256]{2,1,0:T(8,128)(2,1)S(1)}, bf16[8,128,256]{2,1,0:T(8,128)(2,1)S(1)}, u32[]{:S(2)}, u32[]{:S(2)}) %collective-permute-start.5) | collective-permute-done | bytes 524320 | tf_op jit(solution)/shard_map/ppermute | solution.py:393
  116.3 13.2 %collective-permute-done.6 = bf16[8,128,256]{2,1,0:T(8,128)(2,1)S(1)} collective-permute-done((bf16[8,128,256]{2,1,0:T(8,128)(2,1)S(1)}, bf16[8,128,256]{2,1,0:T(8,128)(2,1)S(1)}, u32[]{:S(2)}, u32[]{:S(2)}) %collective-permute-start.6) | collective-permute-done | bytes 524320 | tf_op jit(solution)/shard_map/ppermute | solution.py:393
  130.6 6.0 %all-to-all-start.3 = ((bf16[8,128,256]{2,1,0:T(8,128)(2,1)}), bf16[8,128,256]{2,1,0:T(8,128)(2,1)S(1)}, u32[]{:S(2)}, u32[]{:S(2)}) async-start(bf16[8,128,256]{2,1,0:T(8,128)(2,1)} %add_convert_fusion), calls=%async_computation.4 | async-start | bytes 1048576 | tf_op jit(solution)/shard_map/all_to_all | solution.py:403
  138.3 14.3 %all-to-all-done.3.over_y_ref = bf16[8,128,256]{2,1,0:T(8,128)(2,1)S(1)} async-done(((bf16[8,128,256]{2,1,0:T(8,128)(2,1)}), bf16[8,128,256]{2,1,0:T(8,128)(2,1)S(1)}, u32[]{:S(2)}, u32[]{:S(2)}) %all-to-all-start.3) | async-done | bytes 524320 | tf_op jit(solution)/shard_map/all_to_all | solution.py:403
  (48 shorter events, 12.1 us)
Async XLA Ops:
  7.2 55.6 %all-gather.3.cloned.1.call-start = ((), (), s32[]{:S(2)}) async-start(), calls=%async_computation.6 | async-start | bytes 4734976 | tf_op jit(solution)/shard_map/all_gather | solution.py:428
  7.2 0.9 copy-start.1
  8.1 0.9 copy-start.2
  9.0 0.9 copy-start.3
  9.9 0.8 copy-start.5
  10.7 0.8 copy-start.6
  11.4 0.7 copy-start.7
  13.2 24.3 %all-to-all-start = ((bf16[8,144,256]{2,1,0:T(8,128)(2,1)}), bf16[8,144,256]{2,1,0:T(8,128)(2,1)S(1)}, u32[]{:S(2)}, u32[]{:S(2)}) async-start(bf16[8,144,256]{2,1,0:T(8,128)(2,1)} %get-tuple-element.20), calls=%async_computation | async-start | bytes 1179648 | tf_op jit(solution)/shard_map/all_to_all | solution.py:429
  37.5 8.1 %collective-permute-start = (bf16[2,16,32]{2,1,0:T(8,128)(2,1)S(1)}, bf16[2,16,32]{2,1,0:T(8,128)(2,1)S(1)}, u32[]{:S(2)}, u32[]{:S(2)}) collective-permute-start(bf16[2,16,32]{2,1,0:T(8,128)(2,1)S(1)} %constant_dynamic-slice_fusion), channel_id=1, source_target_pairs={{0,16},{16,0},{1,17},{17,1},{2,18},{18,2},{3,19},{19,3},{4,20},{20... | collective-permute-start | bytes 6152 | tf_op jit(solution)/shard_map/ppermute | solution.py:397
  41.4 18.1 %all-to-all-start.1 = ((bf16[4,8,128,128]{3,2,1,0:T(8,128)(2,1)}), bf16[4,8,128,128]{3,2,1,0:T(8,128)(2,1)S(1)}, u32[]{:S(2)}, u32[]{:S(2)}) async-start(bf16[4,8,128,128]{3,2,1,0:T(8,128)(2,1)} %broadcast_in_dim.59), calls=%async_computation.1 | async-start | bytes 2097152 | tf_op jit(solution)/shard_map/all_to_all | solution.py:387
  45.6 31.0 %collective-permute-start.3 = (bf16[8,128,128]{2,1,0:T(8,128)(2,1)S(1)}, bf16[8,128,128]{2,1,0:T(8,128)(2,1)S(1)}, u32[]{:S(2)}, u32[]{:S(2)}) collective-permute-start(bf16[8,128,128]{2,1,0:T(8,128)(2,1)S(1)} %get-tuple-element.23.v0), channel_id=1, source_target_pairs={{0,128},{128,256},{256,384},{384,0},{1,129},{129,257},{257,385},{3... | collective-permute-start | bytes 786440 | tf_op jit(solution)/shard_map/ppermute | solution.py:393
  48.7 28.0 %collective-permute-start.2 = (bf16[8,128,128]{2,1,0:T(8,128)(2,1)S(1)}, bf16[8,128,128]{2,1,0:T(8,128)(2,1)S(1)}, u32[]{:S(2)}, u32[]{:S(2)}) collective-permute-start(bf16[8,128,128]{2,1,0:T(8,128)(2,1)S(1)} %get-tuple-element.23.v0), channel_id=1, source_target_pairs={{0,256},{128,384},{256,0},{384,128},{1,257},{129,385},{257,1},{385... | collective-permute-start | bytes 786440 | tf_op jit(solution)/shard_map/ppermute | solution.py:393
  51.3 25.4 %collective-permute-start.1 = (bf16[8,128,128]{2,1,0:T(8,128)(2,1)S(1)}, bf16[8,128,128]{2,1,0:T(8,128)(2,1)S(1)}, u32[]{:S(2)}, u32[]{:S(2)}) collective-permute-start(bf16[8,128,128]{2,1,0:T(8,128)(2,1)S(1)} %get-tuple-element.23.v0), channel_id=1, source_target_pairs={{0,384},{128,0},{256,128},{384,256},{1,385},{129,1},{257,129},{385... | collective-permute-start | bytes 786440 | tf_op jit(solution)/shard_map/ppermute | solution.py:393
  59.4 8.5 %copy-start = (bf16[4,8,128,128]{3,2,1,0:T(8,128)(2,1)}, bf16[4,8,128,128]{3,2,1,0:T(8,128)(2,1)S(1)}, u32[]{:S(2)}) copy-start(bf16[4,8,128,128]{3,2,1,0:T(8,128)(2,1)S(1)} %all-to-all-done.1) | copy-start | bytes 3145732
  68.0 23.9 %all-to-all-start.2 = ((f32[16,64,128]{2,1,0:T(8,128)}), f32[16,64,128]{2,1,0:T(8,128)}, u32[]{:S(2)}, u32[]{:S(2)}) async-start(f32[16,64,128]{2,1,0:T(8,128)} %get-tuple-element.24), calls=%async_computation.2 | async-start | bytes 1048576 | tf_op jit(solution)/shard_map/all_to_all | solution.py:445
  76.6 60.0 %reduce-scatter.2.cloned.1.call-start = ((), (), s32[]{:S(2)}) async-start(), calls=%async_computation.5 | async-start | bytes 1179648 | tf_op jit(solution)/shard_map/reduce_scatter | solution.py:453
  82.6 10.4 %copy-start.8 = (bf16[8,128,512]{2,1,0:T(8,128)(2,1)}, bf16[8,128,512]{2,1,0:T(8,128)(2,1)S(1)}, u32[]{:S(2)}) copy-start(bf16[8,128,512]{2,1,0:T(8,128)(2,1)S(1)} %get-tuple-element.26.kept_hbm) | copy-start | bytes 3145732
  82.6 10.4 %collective-permute-start.4 = (bf16[8,128,512]{2,1,0:T(8,128)(2,1)S(1)}, bf16[8,128,512]{2,1,0:T(8,128)(2,1)}, u32[]{:S(2)}, u32[]{:S(2)}) collective-permute-start(bf16[8,128,512]{2,1,0:T(8,128)(2,1)S(1)} %get-tuple-element.27), channel_id=1, source_target_pairs={{0,16},{16,0},{1,17},{17,1},{2,18},{18,2},{3,19},{19,3},{4,20},{20... | collective-permute-start | bytes 3145736 | tf_op jit(solution)/shard_map/ppermute | solution.py:397
  100.3 16.0 %collective-permute-start.5 = (bf16[8,128,256]{2,1,0:T(8,128)(2,1)S(1)}, bf16[8,128,256]{2,1,0:T(8,128)(2,1)S(1)}, u32[]{:S(2)}, u32[]{:S(2)}) collective-permute-start(bf16[8,128,256]{2,1,0:T(8,128)(2,1)S(1)} %get-tuple-element.30), channel_id=1, source_target_pairs={{0,256},{128,384},{256,0},{384,128},{1,257},{129,385},{257,1},{385... | collective-permute-start | bytes 1572872 | tf_op jit(solution)/shard_map/ppermute | solution.py:393
  104.6 24.9 %collective-permute-start.6 = (bf16[8,128,256]{2,1,0:T(8,128)(2,1)S(1)}, bf16[8,128,256]{2,1,0:T(8,128)(2,1)S(1)}, u32[]{:S(2)}, u32[]{:S(2)}) collective-permute-start(bf16[8,128,256]{2,1,0:T(8,128)(2,1)S(1)} %get-tuple-element.31), channel_id=1, source_target_pairs={{0,128},{128,256},{256,384},{384,0},{1,129},{129,257},{257,385},{3... | collective-permute-start | bytes 1572872 | tf_op jit(solution)/shard_map/ppermute | solution.py:393
  108.6 20.9 %collective-permute-start.7 = (bf16[8,128,256]{2,1,0:T(8,128)(2,1)S(1)}, bf16[8,128,256]{2,1,0:T(8,128)(2,1)S(1)}, u32[]{:S(2)}, u32[]{:S(2)}) collective-permute-start(bf16[8,128,256]{2,1,0:T(8,128)(2,1)S(1)} %get-tuple-element.32), channel_id=1, source_target_pairs={{0,384},{128,0},{256,128},{384,256},{1,385},{129,1},{257,129},{385... | collective-permute-start | bytes 1572872 | tf_op jit(solution)/shard_map/ppermute | solution.py:393
  130.6 21.9 %all-to-all-start.3 = ((bf16[8,128,256]{2,1,0:T(8,128)(2,1)}), bf16[8,128,256]{2,1,0:T(8,128)(2,1)S(1)}, u32[]{:S(2)}, u32[]{:S(2)}) async-start(bf16[8,128,256]{2,1,0:T(8,128)(2,1)} %add_convert_fusion), calls=%async_computation.4 | async-start | bytes 1048576 | tf_op jit(solution)/shard_map/all_to_all | solution.py:403
  136.6 0.9 copy-start.4
Sparse Core Ops, SparseCore 0:
  13.3 49.4 all-gather.2
  100.4 34.6 reduce-scatter.1

commit v8 on v7

--- a/solution.py
+++ b/solution.py
@@ -22,6 +22,7 @@
 SCALE = 1.0 / math.sqrt(HD)
 LOG2E = 1.0 / math.log(2.0)
 Y = ("yl", "yh")
+SCALARS = 4
 STEP = 4
 
 
@@ -35,18 +36,18 @@
     )
 
 
-def unpack(pairs_ref, s):
-    pair = pairs_ref[s]
+def unpack(info_ref, s):
+    pair = info_ref[SCALARS + s]
     r, j = pair >> 6, pair & 63
     return r, j, jnp.minimum(r, NQ - 1), jnp.minimum(j, NK - 1)
 
 
-def blocks_of(count_ref, per_step):
-    return (count_ref[0] + (per_step - 1)) // per_step
+def steps_of(info_ref):
+    return (info_ref[0] + (STEP - 1)) // STEP
 
 
 def stats_kernel(
-    pairs_ref, count_ref, q_hbm, k_hbm, out_ref, sent_hbm, q_ref, k_ref, m_ref, l_ref, sent_ref, sems
+    info_ref, q_hbm, k_hbm, out_ref, sent_hbm, q_ref, k_ref, m_ref, l_ref, sent_ref, sems
 ):
     copies = (
         pltpu.make_async_copy(q_hbm.at[:, pl.ds(0, TILE), :], q_ref, sems.at[0]),
@@ -62,7 +63,7 @@
     def visit(i, carry):
         found = []
         for u in range(STEP):
-            r, _, rq, jk = unpack(pairs_ref, i * STEP + u)
+            r, _, rq, jk = unpack(info_ref, i * STEP + u)
             scores = dot(k_ref[jk], heads(q_ref, rq, 0), ((1,), (1,))) * (SCALE * LOG2E)
             top = jnp.max(scores, axis=0, keepdims=True)
             found.append((r, top, jnp.sum(jnp.exp2(scores - top), axis=0, keepdims=True)))
@@ -73,7 +74,7 @@
             l_ref[r] = l_ref[r] * jnp.exp2(old - new) + total * jnp.exp2(top - new)
         return carry
 
-    lax.fori_loop(0, blocks_of(count_ref, STEP), visit, 0)
+    lax.fori_loop(0, steps_of(info_ref), visit, 0)
     total = l_ref[...][:NQ]
     out_ref[...] = jnp.where(
         total > 0.0, m_ref[...][:NQ] + jnp.log2(jnp.maximum(total, 1e-30)), LOW
@@ -95,33 +96,33 @@
     return probs, (probs * (grad_probs - delta)).astype(jnp.bfloat16)
 
 
-def of_x(x_ref, by):
-    return pl.ds(pl.multiple_of(((x_ref[0] + by) & 3) * NY, NY), NY)
-
-
-def load(x_ref, q_hbm, k_hbm, values, q_ref, k_ref, v_ref, sems):
+def of_x(info_ref, by):
+    return pl.ds(pl.multiple_of(((info_ref[2] + by) & 3) * NY, NY), NY)
+
+
+def load(info_ref, q_hbm, k_hbm, values, q_ref, k_ref, v_ref, sems):
     copies = [
         pltpu.make_async_copy(q_hbm, q_ref, sems.at[0]),
         pltpu.make_async_copy(k_hbm, k_ref, sems.at[1]),
     ]
     for n, piece in enumerate(values):
-        copies.append(pltpu.make_async_copy(piece, v_ref.at[of_x(x_ref, n)], sems.at[2 + n]))
+        copies.append(pltpu.make_async_copy(piece, v_ref.at[of_x(info_ref, n)], sems.at[2 + n]))
     for copy in copies:
         copy.start()
     return copies
 
 
 def query_kernel(
-    pairs_ref, count_ref, core_ref, x_ref, q_hbm, k_hbm, v0, v1, v2, v3, total_ref,
+    info_ref, q_hbm, k_hbm, v0, v1, v2, v3, total_ref,
     kept_ref, sent_ref, q_ref, k_ref, v_ref, acc, ds_ref, sems,
 ):
-    copies = load(x_ref, q_hbm, k_hbm, (v0, v1, v2, v3), q_ref, k_ref, v_ref, sems)
+    copies = load(info_ref, q_hbm, k_hbm, (v0, v1, v2, v3), q_ref, k_ref, v_ref, sems)
     acc[...] = jnp.zeros(acc.shape, jnp.float32)
     for copy in copies:
         copy.wait()
 
     def visit(i, carry):
-        where = [unpack(pairs_ref, i * STEP + u) for u in range(STEP)]
+        where = [unpack(info_ref, i * STEP + u) for u in range(STEP)]
         for u, (_, _, rq, jk) in enumerate(where):
             ds_ref[u] = weights_of(q_ref, k_ref, v_ref, total_ref, rq, jk)[1]
         parts = [dot(k_ref[w[3]], ds_ref[u], ((0,), (0,))) for u, w in enumerate(where)]
@@ -129,15 +130,15 @@
             acc[r] += part
         return carry
 
-    lax.fori_loop(0, blocks_of(count_ref, STEP), visit, 0)
-    mine = core_ref[0] * NZ
+    lax.fori_loop(0, steps_of(info_ref), visit, 0)
+    mine = info_ref[1] * NZ
     for n in range(NZ):
         kept_ref[n] = acc[mine + n].astype(jnp.bfloat16)
         sent_ref[n] = acc[NZ - mine + n].astype(jnp.bfloat16)
 
 
 def key_kernel(
-    pairs_ref, count_ref, core_ref, x_ref, z_ref, q_hbm, k_hbm, v0, v1, v2, v3, parts_ref,
+    info_ref, q_hbm, k_hbm, v0, v1, v2, v3, parts_ref,
     kept_hbm, got_hbm, chip_hbm, out0, out1, out2, out3, q_ref, k_ref, v_ref, k_acc, v_acc,
     p_ref, ds_ref, kept_ref, got_ref, chip_ref, total_ref, own_ref, far_ref, sems,
 ):
@@ -147,7 +148,7 @@
     )
     for copy in two:
         copy.start()
-    copies = load(x_ref, q_hbm, k_hbm, (v0, v1, v2, v3), q_ref, k_ref, v_ref, sems)
+    copies = load(info_ref, q_hbm, k_hbm, (v0, v1, v2, v3), q_ref, k_ref, v_ref, sems)
     k_acc[...] = jnp.zeros(k_acc.shape, jnp.float32)
     v_acc[...] = jnp.zeros(v_acc.shape, jnp.float32)
     top = parts_ref[0]
@@ -159,13 +160,13 @@
     total = top + jnp.log2(summed)
     for n in range(NQ * HQ):
         total_ref[n // HQ, :, n % HQ * TILE : (n % HQ + 1) * TILE] = total[n : n + 1]
-    own_ref[...] = jnp.exp2(parts_ref[core_ref[0] * NZ + z_ref[0]] - total)
-    far_ref[...] = jnp.exp2(parts_ref[(1 - core_ref[0]) * NZ + z_ref[0]] - total)
+    own_ref[...] = jnp.exp2(parts_ref[info_ref[1] * NZ + info_ref[3]] - total)
+    far_ref[...] = jnp.exp2(parts_ref[(1 - info_ref[1]) * NZ + info_ref[3]] - total)
     for copy in two:
         copy.wait()
     for n in range(NZ):
         for h in range(HQ):
-            row = pl.ds((core_ref[0] * NZ + n) * HQ + h, 1)
+            row = pl.ds((info_ref[1] * NZ + n) * HQ + h, 1)
             cols = slice(h * TILE, (h + 1) * TILE)
             chip_ref[n, :, cols] = (
                 kept_ref[n, :, cols].astype(jnp.float32) * own_ref[row]
@@ -177,7 +178,7 @@
         copy.wait()
 
     def visit(i, carry):
-        where = [unpack(pairs_ref, i * STEP + u) for u in range(STEP)]
+        where = [unpack(info_ref, i * STEP + u) for u in range(STEP)]
         for u, (_, _, rq, jk) in enumerate(where):
             probs, grad_scores = weights_of(q_ref, k_ref, v_ref, total_ref, rq, jk)
             p_ref[u] = probs.astype(jnp.bfloat16)
@@ -194,37 +195,51 @@
             v_acc[j] += of_value
         return carry
 
-    lax.fori_loop(0, blocks_of(count_ref, STEP), visit, 0)
+    lax.fori_loop(0, steps_of(info_ref), visit, 0)
     for n, out_ref in enumerate((out0, out1, out2, out3)):
-        out_ref[:, :, :HD] = k_acc[of_x(x_ref, n)].astype(jnp.bfloat16)
-        out_ref[:, :, HD:] = v_acc[of_x(x_ref, n)].astype(jnp.bfloat16)
+        out_ref[:, :, :HD] = k_acc[of_x(info_ref, n)].astype(jnp.bfloat16)
+        out_ref[:, :, HD:] = v_acc[of_x(info_ref, n)].astype(jnp.bfloat16)
     leave.wait()
 
 
 def prepare_kernel(
-    q_in, g_in, o_in, k_in, v_in, mask_in, q_hbm, kv_hbm, kv_ref, delta_ref, sems
+    q_in, g_in, o_in, k_in, v_in, mask_in, q_hbm, kv_hbm,
+    q_ref, g_ref, o_ref, mask_ref, kv_ref, delta_ref, sems,
 ):
+    k_part, v_part = (kv_ref.at[pl.ds(0, TILE), pl.ds(n * HD, HD)] for n in range(2))
+    ends = (q_ref, g_ref, o_ref, k_part, v_part, mask_ref)
+    starts = (q_in, g_in, o_in, k_in, v_in, mask_in)
+    q_get, g_get, o_get, k_get, v_get, mask_get = (
+        pltpu.make_async_copy(start, end, sems.at[n])
+        for n, (start, end) in enumerate(zip(starts, ends))
+    )
+    for copy in (g_get, o_get, q_get, k_get, v_get, mask_get):
+        copy.start()
+    kv_ref[TILE:, :] = jnp.zeros((KPAD - TILE, 2 * HD), jnp.bfloat16)
     rows = (pl.ds(0, TILE), pl.ds(TILE, TILE), pl.ds(2 * TILE, QPAD - 2 * TILE))
-    copies = [
-        pltpu.make_async_copy(source, q_hbm.at[row], sems.at[NY + n])
-        for n, (source, row) in enumerate(zip((q_in, g_in, delta_ref), rows))
-    ]
-    copies[0].start()
-    copies[1].start()
-    kv_ref[:TILE, :HD] = k_in[...]
-    kv_ref[:TILE, HD:] = v_in[...]
-    kv_ref[TILE:, :] = jnp.zeros((KPAD - TILE, 2 * HD), jnp.bfloat16)
-    kv_ref[TILE:, :NK] = mask_in[...].astype(jnp.float32).astype(jnp.bfloat16)
-    for n in range(NY):
-        copies.append(pltpu.make_async_copy(kv_ref, kv_hbm.at[n], sems.at[n]))
-        copies[-1].start()
+    q_put, g_put, delta_put = (
+        pltpu.make_async_copy(start, q_hbm.at[row], sems.at[6 + n])
+        for n, (start, row) in enumerate(zip((q_ref, g_ref, delta_ref), rows))
+    )
+    g_get.wait()
+    g_put.start()
+    o_get.wait()
     for h in range(HQ):
         cols = slice(h * HD, (h + 1) * HD)
-        product = g_in[:, cols].astype(jnp.float32) * o_in[:, cols].astype(jnp.float32)
+        product = g_ref[:, cols].astype(jnp.float32) * o_ref[:, cols].astype(jnp.float32)
         delta = jnp.sum(product.T, axis=0, keepdims=True).astype(jnp.bfloat16)
         delta_ref[:, cols] = jnp.broadcast_to(delta, (QPAD - 2 * TILE, HD))
-    copies[2].start()
-    for copy in copies:
+    delta_put.start()
+    q_get.wait()
+    q_put.start()
+    k_get.wait()
+    v_get.wait()
+    mask_get.wait()
+    kv_ref[TILE:, :NK] = mask_ref[...].astype(jnp.float32).astype(jnp.bfloat16)
+    puts = [pltpu.make_async_copy(kv_ref, kv_hbm.at[n], sems.at[9 + n]) for n in range(NY)]
+    for copy in puts:
+        copy.start()
+    for copy in (g_put, q_put, delta_put, *puts):
         copy.wait()
 
 
@@ -277,14 +292,18 @@
             jax.ShapeDtypeStruct((QPAD, ROWS), jnp.bfloat16),
             jax.ShapeDtypeStruct((NY, KPAD, 2 * HD), jnp.bfloat16),
         ),
-        in_specs=[vmem()] * 6,
+        in_specs=[anywhere()] * 6,
         out_specs=(anywhere(), anywhere()),
         scratch_shapes=[
+            pltpu.VMEM((TILE, ROWS), jnp.bfloat16),
+            pltpu.VMEM((TILE, ROWS), jnp.bfloat16),
+            pltpu.VMEM((TILE, ROWS), jnp.bfloat16),
+            pltpu.VMEM((2 * NZ, NK), jnp.int32),
             pltpu.VMEM((KPAD, 2 * HD), jnp.bfloat16),
             pltpu.VMEM((QPAD - 2 * TILE, ROWS), jnp.bfloat16),
-            pltpu.SemaphoreType.DMA((NY + 3,)),
+            pltpu.SemaphoreType.DMA((9 + NY,)),
         ],
-        compiler_params=params(8),
+        compiler_params=params(60),
         name="prepare",
     )(q, g, o, k, v, mask)
 
@@ -312,14 +331,14 @@
     )(over_y)
 
 
-def call_stats(pairs, count, q, k):
+def call_stats(info, q, k):
     return pl.pallas_call(
         stats_kernel,
         out_shape=(
             jax.ShapeDtypeStruct((NQ, 1, ROWS), jnp.float32),
             jax.ShapeDtypeStruct((NQ, NQ * HQ, TILE), jnp.float32),
         ),
-        in_specs=[smem()] * 2 + [anywhere()] * 2,
+        in_specs=[smem()] + [anywhere()] * 2,
         out_specs=(vmem(), anywhere()),
         scratch_shapes=[
             pltpu.VMEM((NQ, TILE, ROWS), jnp.bfloat16),
@@ -332,15 +351,15 @@
         compiler_params=params(),
         cost_estimate=cost(4),
         name="row_statistics",
-    )(pairs, count, q, k)
-
-
-def call_query(pairs, count, core, x, q, k, values, part):
+    )(info, q, k)
+
+
+def call_query(info, q, k, values, part):
     half = jax.ShapeDtypeStruct((NZ, HD, ROWS), jnp.bfloat16)
     return pl.pallas_call(
         query_kernel,
         out_shape=(half, half),
-        in_specs=[smem()] * 4 + [anywhere()] * 6 + [vmem()],
+        in_specs=[smem()] + [anywhere()] * 6 + [vmem()],
         out_specs=(vmem(), vmem()),
         scratch_shapes=loaded()
         + [
@@ -351,16 +370,16 @@
         compiler_params=params(),
         cost_estimate=cost(8),
         name="query_gradient",
-    )(pairs, count, core, x, q, k, *values, part)
-
-
-def call_key(pairs, count, core, x, z, q, k, values, parts, kept, got):
+    )(info, q, k, *values, part)
+
+
+def call_key(info, q, k, values, parts, kept, got):
     quarter = jax.ShapeDtypeStruct((NY, TILE, 2 * HD), jnp.bfloat16)
     half = pltpu.VMEM((NZ, HD, ROWS), jnp.bfloat16)
     return pl.pallas_call(
         key_kernel,
         out_shape=(jax.ShapeDtypeStruct((NZ, HD, ROWS), jnp.bfloat16),) + (quarter,) * 4,
-        in_specs=[smem()] * 5 + [anywhere()] * 6 + [vmem()] + [anywhere()] * 2,
+        in_specs=[smem()] + [anywhere()] * 6 + [vmem()] + [anywhere()] * 2,
         out_specs=(anywhere(),) + (vmem(),) * 4,
         scratch_shapes=loaded()
         + [
@@ -379,7 +398,7 @@
         compiler_params=params(),
         cost_estimate=cost(8),
         name="key_gradient",
-    )(pairs, count, core, x, z, q, k, *values, parts, kept, got)
+    )(info, q, k, *values, parts, kept, got)
 
 
 def to_everyone(value, axis):
@@ -415,7 +434,7 @@
     spare = jnp.where(place < jnp.sum(ones), 0, NQ * 64 + NK)
     code = place // NK * 64 + place % NK
     pairs = jnp.sum(jnp.where(here, code[None, :], 0), axis=1) + spare
-    return jnp.pad(pairs, (0, STEP), constant_values=NQ * 64 + NK), jnp.sum(ones)[None]
+    return jnp.pad(pairs, (0, STEP), constant_values=NQ * 64 + NK), jnp.sum(ones)
 
 
 def body(query_states, out_grad, forward_out, key_states, value_states, block_mask):
@@ -440,15 +459,16 @@
     both = jnp.where(core == 0, both[..., 0], both[..., 1])
     mask = both.transpose(0, 2, 3, 1).reshape(NQ, NK)
     pairs, count = list_pairs(mask)
-
-    part, parts = call_stats(pairs, count, q_all, k_all)
+    info = jnp.concatenate([jnp.stack([count, core, x, z]), pairs])
+
+    part, parts = call_stats(info, q_all, k_all)
     parts = lax.all_to_all(parts, ("c", "z"), 0, 0, tiled=True)
-    kept, sent = call_query(pairs, count, core[None], x[None], q_all, k_all, v_all, part)
+    kept, sent = call_query(info, q_all, k_all, v_all, part)
     got = swap_cores(sent)
 
     parts = jnp.maximum(parts, LOW)
     chip, *parts = call_key(
-        pairs, count, core[None], x[None], z[None], q_all, k_all, v_all, parts, kept, got
+        info, q_all, k_all, v_all, parts, kept, got
     )
     dq_own = lax.psum_scatter(chip, "z", scatter_dimension=0, tiled=True)[0]
     query_grad, over_y = lax.optimization_barrier(

time: 161 us -> 156 us (0.969)
  the two profiles are of different devices: /device:TPU:75 before, /device:TPU:13 now
where the time goes in v8:
time: 156 us
  waiting for transfers between devices  66.4 us (43%)
  starting transfers between devices  47.2 us (30%)
  Pallas kernels  20 us (13%)
  between operations  14.3 us (9%)
  other arithmetic  4.03 us (3%)
  local copies, waits for them, and re-layouts  3.59 us (2%)
    ppermute x6, waiting for transfers between devices, along_x(): return lax.ppermute(value, 'x', [(n, (n + by) % 4) for n in range(4)])  19.2 us
    ppermute x6, starting transfers between devices, along_x(): return lax.ppermute(value, 'x', [(n, (n + by) % 4) for n in range(4)])  17.7 us
    all_to_all x1, waiting for transfers between devices, body(): kv_y = lax.all_to_all(kv_own, Y, 0, 0, tiled=True)  17.3 us
    all_to_all x1, waiting for transfers between devices, sum_over_keys(): return lax.all_to_all(over_x, Y, 0, 0, tiled=True)  14.1 us
    all_to_all x1, starting transfers between devices, sum_over_keys(): return lax.all_to_all(over_x, Y, 0, 0, tiled=True)  8.11 us
    all_to_all x1, waiting for transfers between devices, body(): parts = lax.all_to_all(parts, ('c', 'z'), 0, 0, tiled=True)  7.63 us
    all_to_all x1, starting transfers between devices, body(): kv_y = lax.all_to_all(kv_own, Y, 0, 0, tiled=True)  7 us
    all_gather x1, waiting for transfers between devices, body(): q_all = lax.all_gather(q_own, ('c', 'z'), axis=0, tiled=False)  6.71 us
  transfers between devices with their start and end apart: 14, of which 8 were waited for; matrix products, arithmetic and copies ran while one was open for 4% of the time, Pallas kernels for 7%

profile of v8, /device:TPU:13, one launch (start us, length us, event | category | flops | bytes accessed | tf_op | source)
XLA Modules:
  0.0 155.5 jit_solution(626062496520504476)
XLA Ops:
  7.2 2.1 %prepare.1 = (bf16[272,512]{1,0:T(8,128)(2,1)}, bf16[8,144,256]{2,1,0:T(8,128)(2,1)}) custom-call(bf16[128,512]{1,0:T(8,128)(2,1)} %q_in.1, bf16[128,512]{1,0:T(8,128)(2,1)} %g_in.1, bf16[128,512]{1,0:T(8,128)(2,1)} %o_in.1, bf16[128,128]{1,0:T(8,128)(2,1)} %k_in.1, bf16[128,128]{1,0:T(8,128)(2,1)} %v_in.1, s32[16,32]{1,0:T(8,128)} %mask_in.1), custom_call_target="tpu_custom_call" | custom-call | tf_op jit(solution)/shard_map/prepare/pallas_call | solution.py:289
  9.4 7.0 %all-to-all-start = ((bf16[8,144,256]{2,1,0:T(8,128)(2,1)}), bf16[8,144,256]{2,1,0:T(8,128)(2,1)S(1)}, u32[]{:S(2)}, u32[]{:S(2)}) async-start(bf16[8,144,256]{2,1,0:T(8,128)(2,1)} %get-tuple-element.20), calls=%async_computation | async-start | bytes 1179648 | tf_op jit(solution)/shard_map/all_to_all | solution.py:448
  16.4 17.3 %all-to-all-done = bf16[8,144,256]{2,1,0:T(8,128)(2,1)S(1)} async-done(((bf16[8,144,256]{2,1,0:T(8,128)(2,1)}), bf16[8,144,256]{2,1,0:T(8,128)(2,1)S(1)}, u32[]{:S(2)}, u32[]{:S(2)}) %all-to-all-start) | async-done | bytes 589856 | tf_op jit(solution)/shard_map/all_to_all | solution.py:448
  33.7 2.5 %collective-permute-start = (bf16[2,16,32]{2,1,0:T(8,128)(2,1)S(1)}, bf16[2,16,32]{2,1,0:T(8,128)(2,1)S(1)}, u32[]{:S(2)}, u32[]{:S(2)}) collective-permute-start(bf16[2,16,32]{2,1,0:T(8,128)(2,1)S(1)} %constant_dynamic-slice_fusion), channel_id=1, source_target_pairs={{0,16},{16,0},{1,17},{17,1},{2,18},{18,2},{3,19},{19,3},{4,20},{20... | collective-permute-start | bytes 6152 | tf_op jit(solution)/shard_map/ppermute | solution.py:416
  36.3 1.3 broadcast_in_dim.41
  37.6 4.2 %all-to-all-start.1 = ((bf16[4,8,128,128]{3,2,1,0:T(8,128)(2,1)}), bf16[4,8,128,128]{3,2,1,0:T(8,128)(2,1)S(1)}, u32[]{:S(2)}, u32[]{:S(2)}) async-start(bf16[4,8,128,128]{3,2,1,0:T(8,128)(2,1)} %broadcast_in_dim.41), calls=%async_computation.1 | async-start | bytes 2097152 | tf_op jit(solution)/shard_map/all_to_all | solution.py:406
  41.8 2.8 %collective-permute-start.3 = (bf16[8,128,128]{2,1,0:T(8,128)(2,1)S(1)}, bf16[8,128,128]{2,1,0:T(8,128)(2,1)S(1)}, u32[]{:S(2)}, u32[]{:S(2)}) collective-permute-start(bf16[8,128,128]{2,1,0:T(8,128)(2,1)S(1)} %get-tuple-element.23.v0), channel_id=1, source_target_pairs={{0,128},{128,256},{256,384},{384,0},{1,129},{129,257},{257,385},{3... | collective-permute-start | bytes 786440 | tf_op jit(solution)/shard_map/ppermute | solution.py:412
  44.6 2.5 %collective-permute-start.2 = (bf16[8,128,128]{2,1,0:T(8,128)(2,1)S(1)}, bf16[8,128,128]{2,1,0:T(8,128)(2,1)S(1)}, u32[]{:S(2)}, u32[]{:S(2)}) collective-permute-start(bf16[8,128,128]{2,1,0:T(8,128)(2,1)S(1)} %get-tuple-element.23.v0), channel_id=1, source_target_pairs={{0,256},{128,384},{256,0},{384,128},{1,257},{129,385},{257,1},{385... | collective-permute-start | bytes 786440 | tf_op jit(solution)/shard_map/ppermute | solution.py:412
  47.1 2.5 %collective-permute-start.1 = (bf16[8,128,128]{2,1,0:T(8,128)(2,1)S(1)}, bf16[8,128,128]{2,1,0:T(8,128)(2,1)S(1)}, u32[]{:S(2)}, u32[]{:S(2)}) collective-permute-start(bf16[8,128,128]{2,1,0:T(8,128)(2,1)S(1)} %get-tuple-element.23.v0), channel_id=1, source_target_pairs={{0,384},{128,0},{256,128},{384,256},{1,385},{129,1},{257,129},{385... | collective-permute-start | bytes 786440 | tf_op jit(solution)/shard_map/ppermute | solution.py:412
  52.8 1.4 all-to-all-done.1
  54.3 6.7 %all-gather.3.cloned.1.call-done = bf16[4352,512]{1,0:T(8,128)(2,1)} async-done(((bf16[272,512]{1,0:T(8,128)(2,1)}), bf16[4352,512]{1,0:T(8,128)(2,1)}) %all-gather.3.cloned.1.call-update) | async-done | bytes 4456464 | tf_op jit(solution)/shard_map/all_gather | solution.py:447
  61.0 4.6 %row_statistics.1 = (f32[16,1,512]{2,1,0:T(1,128)S(1)}, f32[16,64,128]{2,1,0:T(8,128)}) custom-call(s32[520]{0:T(1024)S(1)} %concatenate.3.info_ref, bf16[16,272,512]{2,1,0:T(8,128)(2,1)} %bitcast.23, bf16[32,128,128]{2,1,0:T(8,128)(2,1)S(1)} %bitcast.17), custom_call_target="tpu_custom_call" | custom-call | flops 10000000000 | bytes 4194304 | tf_op jit(solution)/shard_map/row_statistics/pallas_call | solution.py:335
  65.6 5.7 %all-to-all-start.2 = ((f32[16,64,128]{2,1,0:T(8,128)}), f32[16,64,128]{2,1,0:T(8,128)}, u32[]{:S(2)}, u32[]{:S(2)}) async-start(f32[16,64,128]{2,1,0:T(8,128)} %get-tuple-element.24), calls=%async_computation.2 | async-start | bytes 1048576 | tf_op jit(solution)/shard_map/all_to_all | solution.py:465
  71.4 5.2 %query_gradient.1 = (bf16[8,128,512]{2,1,0:T(8,128)(2,1)S(1)}, bf16[8,128,512]{2,1,0:T(8,128)(2,1)S(1)}) custom-call(s32[520]{0:T(1024)S(1)} %concatenate.3.info_ref, bf16[16,272,512]{2,1,0:T(8,128)(2,1)} %bitcast.24, bf16[32,128,128]{2,1,0:T(8,128)(2,1)} %bitcast.18, bf16[8,128,128]{2,1,0:T(8,128)(2,1)S(1)} %get-tuple-element.23.v0, ...), custom_call_target="tpu_custom_call" | custom-call | flops 10000000000 | bytes 8388608 | tf_op jit(solution)/shard_map/query_gradient/pallas_call | solution.py:359
  76.6 1.9 %collective-permute-start.4 = (bf16[8,128,512]{2,1,0:T(8,128)(2,1)S(1)}, bf16[8,128,512]{2,1,0:T(8,128)(2,1)}, u32[]{:S(2)}, u32[]{:S(2)}) collective-permute-start(bf16[8,128,512]{2,1,0:T(8,128)(2,1)S(1)} %get-tuple-element.27), channel_id=1, source_target_pairs={{0,16},{16,0},{1,17},{17,1},{2,18},{18,2},{3,19},{19,3},{4,20},{20... | collective-permute-start | bytes 3145736 | tf_op jit(solution)/shard_map/ppermute | solution.py:416
  78.6 7.6 %all-to-all-done.2 = f32[16,64,128]{2,1,0:T(8,128)} async-done(((f32[16,64,128]{2,1,0:T(8,128)}), f32[16,64,128]{2,1,0:T(8,128)}, u32[]{:S(2)}, u32[]{:S(2)}) %all-to-all-start.2) | async-done | bytes 524320 | tf_op jit(solution)/shard_map/all_to_all | solution.py:465
  87.3 6.6 %key_gradient.1 = (bf16[8,128,512]{2,1,0:T(8,128)(2,1)}, bf16[8,128,256]{2,1,0:T(8,128)(2,1)S(1)}, bf16[8,128,256]{2,1,0:T(8,128)(2,1)S(1)}, bf16[8,128,256]{2,1,0:T(8,128)(2,1)S(1)}, bf16[8,128,256]{2,1,0:T(8,128)(2,1)S(1)}) custom-call(s32[520]{0:T(1024)S(1)} %concatenate.3.info_ref, bf16[16,272,512]{2,1,0:T(8,128)(2,1)} %bitcast.25, ...), custom_call_target="tpu_custom_call" | custom-call | flops 10000000000 | bytes 8388608 | tf_op jit(solution)/shard_map/key_gradient/pallas_call | solution.py:379
  94.0 4.4 %collective-permute-start.5 = (bf16[8,128,256]{2,1,0:T(8,128)(2,1)S(1)}, bf16[8,128,256]{2,1,0:T(8,128)(2,1)S(1)}, u32[]{:S(2)}, u32[]{:S(2)}) collective-permute-start(bf16[8,128,256]{2,1,0:T(8,128)(2,1)S(1)} %get-tuple-element.30), channel_id=1, source_target_pairs={{0,256},{128,384},{256,0},{384,128},{1,257},{129,385},{257,1},{385... | collective-permute-start | bytes 1572872 | tf_op jit(solution)/shard_map/ppermute | solution.py:412
  98.4 3.5 %collective-permute-start.6 = (bf16[8,128,256]{2,1,0:T(8,128)(2,1)S(1)}, bf16[8,128,256]{2,1,0:T(8,128)(2,1)S(1)}, u32[]{:S(2)}, u32[]{:S(2)}) collective-permute-start(bf16[8,128,256]{2,1,0:T(8,128)(2,1)S(1)} %get-tuple-element.31), channel_id=1, source_target_pairs={{0,128},{128,256},{256,384},{384,0},{1,129},{129,257},{257,385},{3... | collective-permute-start | bytes 1572872 | tf_op jit(solution)/shard_map/ppermute | solution.py:412
  101.9 1.9 %collective-permute-start.7 = (bf16[8,128,256]{2,1,0:T(8,128)(2,1)S(1)}, bf16[8,128,256]{2,1,0:T(8,128)(2,1)S(1)}, u32[]{:S(2)}, u32[]{:S(2)}) collective-permute-start(bf16[8,128,256]{2,1,0:T(8,128)(2,1)S(1)} %get-tuple-element.32), channel_id=1, source_target_pairs={{0,384},{128,0},{256,128},{384,256},{1,385},{129,1},{257,129},{385... | collective-permute-start | bytes 1572872 | tf_op jit(solution)/shard_map/ppermute | solution.py:412
  103.9 6.8 %collective-permute-done.5 = bf16[8,128,256]{2,1,0:T(8,128)(2,1)S(1)} collective-permute-done((bf16[8,128,256]{2,1,0:T(8,128)(2,1)S(1)}, bf16[8,128,256]{2,1,0:T(8,128)(2,1)S(1)}, u32[]{:S(2)}, u32[]{:S(2)}) %collective-permute-start.5) | collective-permute-done | bytes 524320 | tf_op jit(solution)/shard_map/ppermute | solution.py:412
  110.6 11.8 %collective-permute-done.6 = bf16[8,128,256]{2,1,0:T(8,128)(2,1)S(1)} collective-permute-done((bf16[8,128,256]{2,1,0:T(8,128)(2,1)S(1)}, bf16[8,128,256]{2,1,0:T(8,128)(2,1)S(1)}, u32[]{:S(2)}, u32[]{:S(2)}) %collective-permute-start.6) | collective-permute-done | bytes 524320 | tf_op jit(solution)/shard_map/ppermute | solution.py:412
  124.1 8.1 %all-to-all-start.3 = ((bf16[8,128,256]{2,1,0:T(8,128)(2,1)}), bf16[8,128,256]{2,1,0:T(8,128)(2,1)S(1)}, u32[]{:S(2)}, u32[]{:S(2)}) async-start(bf16[8,128,256]{2,1,0:T(8,128)(2,1)} %add_convert_fusion), calls=%async_computation.4 | async-start | bytes 1048576 | tf_op jit(solution)/shard_map/all_to_all | solution.py:422
  133.9 14.1 %all-to-all-done.3.over_y_ref = bf16[8,128,256]{2,1,0:T(8,128)(2,1)S(1)} async-done(((bf16[8,128,256]{2,1,0:T(8,128)(2,1)}), bf16[8,128,256]{2,1,0:T(8,128)(2,1)S(1)}, u32[]{:S(2)}, u32[]{:S(2)}) %all-to-all-start.3) | async-done | bytes 524320 | tf_op jit(solution)/shard_map/all_to_all | solution.py:422
  (37 shorter events, 8.5 us)
Async XLA Ops:
  7.2 53.8 %all-gather.3.cloned.1.call-start = ((), (), s32[]{:S(2)}) async-start(), calls=%async_computation.6 | async-start | bytes 4734976 | tf_op jit(solution)/shard_map/all_gather | solution.py:447
  9.4 24.3 %all-to-all-start = ((bf16[8,144,256]{2,1,0:T(8,128)(2,1)}), bf16[8,144,256]{2,1,0:T(8,128)(2,1)S(1)}, u32[]{:S(2)}, u32[]{:S(2)}) async-start(bf16[8,144,256]{2,1,0:T(8,128)(2,1)} %get-tuple-element.20), calls=%async_computation | async-start | bytes 1179648 | tf_op jit(solution)/shard_map/all_to_all | solution.py:448
  33.7 8.2 %collective-permute-start = (bf16[2,16,32]{2,1,0:T(8,128)(2,1)S(1)}, bf16[2,16,32]{2,1,0:T(8,128)(2,1)S(1)}, u32[]{:S(2)}, u32[]{:S(2)}) collective-permute-start(bf16[2,16,32]{2,1,0:T(8,128)(2,1)S(1)} %constant_dynamic-slice_fusion), channel_id=1, source_target_pairs={{0,16},{16,0},{1,17},{17,1},{2,18},{18,2},{3,19},{19,3},{4,20},{20... | collective-permute-start | bytes 6152 | tf_op jit(solution)/shard_map/ppermute | solution.py:416
  37.6 16.7 %all-to-all-start.1 = ((bf16[4,8,128,128]{3,2,1,0:T(8,128)(2,1)}), bf16[4,8,128,128]{3,2,1,0:T(8,128)(2,1)S(1)}, u32[]{:S(2)}, u32[]{:S(2)}) async-start(bf16[4,8,128,128]{3,2,1,0:T(8,128)(2,1)} %broadcast_in_dim.41), calls=%async_computation.1 | async-start | bytes 2097152 | tf_op jit(solution)/shard_map/all_to_all | solution.py:406
  41.8 29.5 %collective-permute-start.3 = (bf16[8,128,128]{2,1,0:T(8,128)(2,1)S(1)}, bf16[8,128,128]{2,1,0:T(8,128)(2,1)S(1)}, u32[]{:S(2)}, u32[]{:S(2)}) collective-permute-start(bf16[8,128,128]{2,1,0:T(8,128)(2,1)S(1)} %get-tuple-element.23.v0), channel_id=1, source_target_pairs={{0,128},{128,256},{256,384},{384,0},{1,129},{129,257},{257,385},{3... | collective-permute-start | bytes 786440 | tf_op jit(solution)/shard_map/ppermute | solution.py:412
  44.6 26.7 %collective-permute-start.2 = (bf16[8,128,128]{2,1,0:T(8,128)(2,1)S(1)}, bf16[8,128,128]{2,1,0:T(8,128)(2,1)S(1)}, u32[]{:S(2)}, u32[]{:S(2)}) collective-permute-start(bf16[8,128,128]{2,1,0:T(8,128)(2,1)S(1)} %get-tuple-element.23.v0), channel_id=1, source_target_pairs={{0,256},{128,384},{256,0},{384,128},{1,257},{129,385},{257,1},{385... | collective-permute-start | bytes 786440 | tf_op jit(solution)/shard_map/ppermute | solution.py:412
  47.1 24.3 %collective-permute-start.1 = (bf16[8,128,128]{2,1,0:T(8,128)(2,1)S(1)}, bf16[8,128,128]{2,1,0:T(8,128)(2,1)S(1)}, u32[]{:S(2)}, u32[]{:S(2)}) collective-permute-start(bf16[8,128,128]{2,1,0:T(8,128)(2,1)S(1)} %get-tuple-element.23.v0), channel_id=1, source_target_pairs={{0,384},{128,0},{256,128},{384,256},{1,385},{129,1},{257,129},{385... | collective-permute-start | bytes 786440 | tf_op jit(solution)/shard_map/ppermute | solution.py:412
  54.3 11.3 %copy-start = (bf16[4,8,128,128]{3,2,1,0:T(8,128)(2,1)}, bf16[4,8,128,128]{3,2,1,0:T(8,128)(2,1)S(1)}, u32[]{:S(2)}) copy-start(bf16[4,8,128,128]{3,2,1,0:T(8,128)(2,1)S(1)} %all-to-all-done.1) | copy-start | bytes 3145732
  65.6 20.6 %all-to-all-start.2 = ((f32[16,64,128]{2,1,0:T(8,128)}), f32[16,64,128]{2,1,0:T(8,128)}, u32[]{:S(2)}, u32[]{:S(2)}) async-start(f32[16,64,128]{2,1,0:T(8,128)} %get-tuple-element.24), calls=%async_computation.2 | async-start | bytes 1048576 | tf_op jit(solution)/shard_map/all_to_all | solution.py:465
  71.3 60.9 %reduce-scatter.2.cloned.1.call-start = ((), (), s32[]{:S(2)}) async-start(), calls=%async_computation.5 | async-start | bytes 1179648 | tf_op jit(solution)/shard_map/reduce_scatter | solution.py:473
  76.6 10.7 %copy-start.2 = (bf16[8,128,512]{2,1,0:T(8,128)(2,1)}, bf16[8,128,512]{2,1,0:T(8,128)(2,1)S(1)}, u32[]{:S(2)}) copy-start(bf16[8,128,512]{2,1,0:T(8,128)(2,1)S(1)} %get-tuple-element.26.kept_hbm) | copy-start | bytes 3145732
  76.6 10.7 %collective-permute-start.4 = (bf16[8,128,512]{2,1,0:T(8,128)(2,1)S(1)}, bf16[8,128,512]{2,1,0:T(8,128)(2,1)}, u32[]{:S(2)}, u32[]{:S(2)}) collective-permute-start(bf16[8,128,512]{2,1,0:T(8,128)(2,1)S(1)} %get-tuple-element.27), channel_id=1, source_target_pairs={{0,16},{16,0},{1,17},{17,1},{2,18},{18,2},{3,19},{19,3},{4,20},{20... | collective-permute-start | bytes 3145736 | tf_op jit(solution)/shard_map/ppermute | solution.py:416
  94.0 16.7 %collective-permute-start.5 = (bf16[8,128,256]{2,1,0:T(8,128)(2,1)S(1)}, bf16[8,128,256]{2,1,0:T(8,128)(2,1)S(1)}, u32[]{:S(2)}, u32[]{:S(2)}) collective-permute-start(bf16[8,128,256]{2,1,0:T(8,128)(2,1)S(1)} %get-tuple-element.30), channel_id=1, source_target_pairs={{0,256},{128,384},{256,0},{384,128},{1,257},{129,385},{257,1},{385... | collective-permute-start | bytes 1572872 | tf_op jit(solution)/shard_map/ppermute | solution.py:412
  98.4 24.0 %collective-permute-start.6 = (bf16[8,128,256]{2,1,0:T(8,128)(2,1)S(1)}, bf16[8,128,256]{2,1,0:T(8,128)(2,1)S(1)}, u32[]{:S(2)}, u32[]{:S(2)}) collective-permute-start(bf16[8,128,256]{2,1,0:T(8,128)(2,1)S(1)} %get-tuple-element.31), channel_id=1, source_target_pairs={{0,128},{128,256},{256,384},{384,0},{1,129},{129,257},{257,385},{3... | collective-permute-start | bytes 1572872 | tf_op jit(solution)/shard_map/ppermute | solution.py:412
  101.9 21.1 %collective-permute-start.7 = (bf16[8,128,256]{2,1,0:T(8,128)(2,1)S(1)}, bf16[8,128,256]{2,1,0:T(8,128)(2,1)S(1)}, u32[]{:S(2)}, u32[]{:S(2)}) collective-permute-start(bf16[8,128,256]{2,1,0:T(8,128)(2,1)S(1)} %get-tuple-element.32), channel_id=1, source_target_pairs={{0,384},{128,0},{256,128},{384,256},{1,385},{129,1},{257,129},{385... | collective-permute-start | bytes 1572872 | tf_op jit(solution)/shard_map/ppermute | solution.py:412
  124.1 23.9 %all-to-all-start.3 = ((bf16[8,128,256]{2,1,0:T(8,128)(2,1)}), bf16[8,128,256]{2,1,0:T(8,128)(2,1)S(1)}, u32[]{:S(2)}, u32[]{:S(2)}) async-start(bf16[8,128,256]{2,1,0:T(8,128)(2,1)} %add_convert_fusion), calls=%async_computation.4 | async-start | bytes 1048576 | tf_op jit(solution)/shard_map/all_to_all | solution.py:422
  132.2 0.9 copy-start.1
Sparse Core Ops, SparseCore 0:
  10.1 50.8 all-gather.2
  94.1 37.8 reduce-scatter.1

commit v9 on v8

--- a/solution.py
+++ b/solution.py
@@ -137,20 +137,7 @@
         sent_ref[n] = acc[NZ - mine + n].astype(jnp.bfloat16)
 
 
-def key_kernel(
-    info_ref, q_hbm, k_hbm, v0, v1, v2, v3, parts_ref,
-    kept_hbm, got_hbm, chip_hbm, out0, out1, out2, out3, q_ref, k_ref, v_ref, k_acc, v_acc,
-    p_ref, ds_ref, kept_ref, got_ref, chip_ref, total_ref, own_ref, far_ref, sems,
-):
-    two = (
-        pltpu.make_async_copy(kept_hbm, kept_ref, sems.at[6]),
-        pltpu.make_async_copy(got_hbm, got_ref, sems.at[7]),
-    )
-    for copy in two:
-        copy.start()
-    copies = load(info_ref, q_hbm, k_hbm, (v0, v1, v2, v3), q_ref, k_ref, v_ref, sems)
-    k_acc[...] = jnp.zeros(k_acc.shape, jnp.float32)
-    v_acc[...] = jnp.zeros(v_acc.shape, jnp.float32)
+def combine_kernel(info_ref, parts_ref, total_ref, own_ref, far_ref):
     top = parts_ref[0]
     for n in range(1, NQ):
         top = jnp.maximum(top, parts_ref[n])
@@ -162,8 +149,9 @@
         total_ref[n // HQ, :, n % HQ * TILE : (n % HQ + 1) * TILE] = total[n : n + 1]
     own_ref[...] = jnp.exp2(parts_ref[info_ref[1] * NZ + info_ref[3]] - total)
     far_ref[...] = jnp.exp2(parts_ref[(1 - info_ref[1]) * NZ + info_ref[3]] - total)
-    for copy in two:
-        copy.wait()
+
+
+def weigh_kernel(info_ref, own_ref, far_ref, kept_ref, got_ref, chip_ref):
     for n in range(NZ):
         for h in range(HQ):
             row = pl.ds((info_ref[1] * NZ + n) * HQ + h, 1)
@@ -172,8 +160,15 @@
                 kept_ref[n, :, cols].astype(jnp.float32) * own_ref[row]
                 + got_ref[n, :, cols].astype(jnp.float32) * far_ref[row]
             ).astype(jnp.bfloat16)
-    leave = pltpu.make_async_copy(chip_ref, chip_hbm, sems.at[8])
-    leave.start()
+
+
+def key_kernel(
+    info_ref, q_hbm, k_hbm, v0, v1, v2, v3, total_ref, out0, out1, out2, out3,
+    q_ref, k_ref, v_ref, k_acc, v_acc, p_ref, ds_ref, sems,
+):
+    copies = load(info_ref, q_hbm, k_hbm, (v0, v1, v2, v3), q_ref, k_ref, v_ref, sems)
+    k_acc[...] = jnp.zeros(k_acc.shape, jnp.float32)
+    v_acc[...] = jnp.zeros(v_acc.shape, jnp.float32)
     for copy in copies:
         copy.wait()
 
@@ -199,7 +194,6 @@
     for n, out_ref in enumerate((out0, out1, out2, out3)):
         out_ref[:, :, :HD] = k_acc[of_x(info_ref, n)].astype(jnp.bfloat16)
         out_ref[:, :, HD:] = v_acc[of_x(info_ref, n)].astype(jnp.bfloat16)
-    leave.wait()
 
 
 def prepare_kernel(
@@ -373,32 +367,49 @@
     )(info, q, k, *values, part)
 
 
-def call_key(info, q, k, values, parts, kept, got):
+def call_combine(info, parts):
+    rows = jax.ShapeDtypeStruct((NQ * HQ, TILE), jnp.float32)
+    return pl.pallas_call(
+        combine_kernel,
+        out_shape=(jax.ShapeDtypeStruct((NQ, 1, ROWS), jnp.float32), rows, rows),
+        in_specs=[smem(), vmem()],
+        out_specs=(vmem(),) * 3,
+        compiler_params=params(8),
+        cost_estimate=cost(8),
+        name="combine_statistics",
+    )(info, parts)
+
+
+def call_weigh(info, own, far, kept, got):
+    return pl.pallas_call(
+        weigh_kernel,
+        out_shape=jax.ShapeDtypeStruct((NZ, HD, ROWS), jnp.bfloat16),
+        in_specs=[smem()] + [vmem()] * 4,
+        out_specs=vmem(),
+        compiler_params=params(8),
+        name="weigh_queries",
+    )(info, own, far, kept, got)
+
+
+def call_key(info, q, k, values, total):
     quarter = jax.ShapeDtypeStruct((NY, TILE, 2 * HD), jnp.bfloat16)
-    half = pltpu.VMEM((NZ, HD, ROWS), jnp.bfloat16)
     return pl.pallas_call(
         key_kernel,
-        out_shape=(jax.ShapeDtypeStruct((NZ, HD, ROWS), jnp.bfloat16),) + (quarter,) * 4,
-        in_specs=[smem()] + [anywhere()] * 6 + [vmem()] + [anywhere()] * 2,
-        out_specs=(anywhere(),) + (vmem(),) * 4,
-        scratch_shapes=loaded()
-        + [
+        out_shape=(quarter,) * 4,
+        in_specs=[smem()] + [anywhere()] * 6 + [vmem()],
+        out_specs=(vmem(),) * 4,
+        scratch_shapes=[
+            *loaded(),
             pltpu.VMEM((NK + 1, TILE, HD), jnp.float32),
             pltpu.VMEM((NK + 1, TILE, HD), jnp.float32),
             pltpu.VMEM((STEP, TILE, ROWS), jnp.bfloat16),
             pltpu.VMEM((STEP, TILE, ROWS), jnp.bfloat16),
-            half,
-            half,
-            half,
-            pltpu.VMEM((NQ, 1, ROWS), jnp.float32),
-            pltpu.VMEM((NQ * HQ, TILE), jnp.float32),
-            pltpu.VMEM((NQ * HQ, TILE), jnp.float32),
-            pltpu.SemaphoreType.DMA((9,)),
+            pltpu.SemaphoreType.DMA((6,)),
         ],
         compiler_params=params(),
         cost_estimate=cost(8),
         name="key_gradient",
-    )(info, q, k, *values, parts, kept, got)
+    )(info, q, k, *values, total)
 
 
 def to_everyone(value, axis):
@@ -466,10 +477,10 @@
     kept, sent = call_query(info, q_all, k_all, v_all, part)
     got = swap_cores(sent)
 
-    parts = jnp.maximum(parts, LOW)
-    chip, *parts = call_key(
-        info, q_all, k_all, v_all, parts, kept, got
-    )
+    total, own, far = call_combine(info, parts)
+    chip = call_weigh(info, own, far, kept, got)
+    parts = call_key(info, q_all, k_all, v_all, total)
+
     dq_own = lax.psum_scatter(chip, "z", scatter_dimension=0, tiled=True)[0]
     query_grad, over_y = lax.optimization_barrier(
         (call_finish_queries(dq_own), sum_over_keys(*parts))

time: 156 us -> 159 us (1.019)
  starting transfers between devices: 47.2 us -> 49.2 us
    all_to_all x1, starting transfers between devices: 5.73 us -> 11.2 us  [body(): parts = lax.all_to_all(parts, ('c', 'z'), 0, 0, tiled=True)]
    all_to_all x1, starting transfers between devices: 8.11 us -> 5.61 us  [sum_over_keys(): return lax.all_to_all(over_x, Y, 0, 0, tiled=True)]
    ppermute x6, waiting for transfers between devices: 19.2 us -> 20.9 us  [along_x(): return lax.ppermute(value, 'x', [(n, (n + by) % 4) for n in range(4)])]
    ppermute x6, starting transfers between devices: 17.7 us -> 16 us  [along_x(): return lax.ppermute(value, 'x', [(n, (n + by) % 4) for n in range(4)])]
    pallas_call x1 -> x3, Pallas kernels: 6.62 us -> 7.62 us  [the longest x1 4.93 us: call_key(): pl.pallas_call(key_kernel, out_shape=(quarter,) * 4, in_specs=[smem()] +...]
  transfers between devices with their start and end apart: 14 -> 14, of which waited for: 8 -> 7; matrix products, arithmetic and copies ran while one was open for 4% -> 4% of each run, Pallas kernels for 7% -> 10%
where the time goes in v9:
time: 159 us; the launch traced here: 158 us
  waiting for transfers between devices  66.5 us (42%)
  starting transfers between devices  49.2 us (31%)
  Pallas kernels  20.9 us (13%)
  between operations  14.3 us (9%)
  local copies, waits for them, and re-layouts  4.52 us (3%)
  other arithmetic  2.95 us (2%)
    ppermute x6, waiting for transfers between devices, along_x(): return lax.ppermute(value, 'x', [(n, (n + by) % 4) for n in range(4)])  20.9 us
    all_to_all x1, waiting for transfers between devices, body(): kv_y = lax.all_to_all(kv_own, Y, 0, 0, tiled=True)  17.3 us
    ppermute x6, starting transfers between devices, along_x(): return lax.ppermute(value, 'x', [(n, (n + by) % 4) for n in range(4)])  16 us
    all_to_all x1, waiting for transfers between devices, sum_over_keys(): return lax.all_to_all(over_x, Y, 0, 0, tiled=True)  14.2 us
    all_to_all x1, starting transfers between devices, body(): parts = lax.all_to_all(parts, ('c', 'z'), 0, 0, tiled=True)  11.2 us
    all_to_all x1, starting transfers between devices, body(): kv_y = lax.all_to_all(kv_own, Y, 0, 0, tiled=True)  7 us
    all_gather x1, waiting for transfers between devices, body(): q_all = lax.all_gather(q_own, ('c', 'z'), axis=0, tiled=False)  6.69 us
    all_to_all x1, waiting for transfers between devices, body(): parts = lax.all_to_all(parts, ('c', 'z'), 0, 0, tiled=True)  6.42 us
  transfers between devices with their start and end apart: 14, of which 7 were waited for; matrix products, arithmetic and copies ran while one was open for 4% of the time, Pallas kernels for 10%

profile of v9, /device:TPU:13, one launch (start us, length us, event | category | flops | bytes accessed | tf_op | source)
XLA Modules:
  0.0 158.3 jit_solution(15964909482331938020)
XLA Ops:
  7.2 2.2 %prepare.1 = (bf16[272,512]{1,0:T(8,128)(2,1)}, bf16[8,144,256]{2,1,0:T(8,128)(2,1)}) custom-call(bf16[128,512]{1,0:T(8,128)(2,1)} %q_in.1, bf16[128,512]{1,0:T(8,128)(2,1)} %g_in.1, bf16[128,512]{1,0:T(8,128)(2,1)} %o_in.1, bf16[128,128]{1,0:T(8,128)(2,1)} %k_in.1, bf16[128,128]{1,0:T(8,128)(2,1)} %v_in.1, s32[16,32]{1,0:T(8,128)} %mask_in.1), custom_call_target="tpu_custom_call" | custom-call | tf_op jit(solution)/shard_map/prepare/pallas_call | solution.py:283
  9.4 7.0 %all-to-all-start = ((bf16[8,144,256]{2,1,0:T(8,128)(2,1)}), bf16[8,144,256]{2,1,0:T(8,128)(2,1)S(1)}, u32[]{:S(2)}, u32[]{:S(2)}) async-start(bf16[8,144,256]{2,1,0:T(8,128)(2,1)} %get-tuple-element.22), calls=%async_computation | async-start | bytes 1179648 | tf_op jit(solution)/shard_map/all_to_all | solution.py:459
  16.4 17.3 %all-to-all-done = bf16[8,144,256]{2,1,0:T(8,128)(2,1)S(1)} async-done(((bf16[8,144,256]{2,1,0:T(8,128)(2,1)}), bf16[8,144,256]{2,1,0:T(8,128)(2,1)S(1)}, u32[]{:S(2)}, u32[]{:S(2)}) %all-to-all-start) | async-done | bytes 589856 | tf_op jit(solution)/shard_map/all_to_all | solution.py:459
  33.7 2.5 %collective-permute-start = (bf16[2,16,32]{2,1,0:T(8,128)(2,1)S(1)}, bf16[2,16,32]{2,1,0:T(8,128)(2,1)S(1)}, u32[]{:S(2)}, u32[]{:S(2)}) collective-permute-start(bf16[2,16,32]{2,1,0:T(8,128)(2,1)S(1)} %constant_dynamic-slice_fusion), channel_id=1, source_target_pairs={{0,16},{16,0},{1,17},{17,1},{2,18},{18,2},{3,19},{19,3},{4,20},{20... | collective-permute-start | bytes 6152 | tf_op jit(solution)/shard_map/ppermute | solution.py:427
  36.4 1.3 broadcast_in_dim.41
  37.6 4.2 %all-to-all-start.1 = ((bf16[4,8,128,128]{3,2,1,0:T(8,128)(2,1)}), bf16[4,8,128,128]{3,2,1,0:T(8,128)(2,1)S(1)}, u32[]{:S(2)}, u32[]{:S(2)}) async-start(bf16[4,8,128,128]{3,2,1,0:T(8,128)(2,1)} %broadcast_in_dim.41), calls=%async_computation.1 | async-start | bytes 2097152 | tf_op jit(solution)/shard_map/all_to_all | solution.py:417
  41.9 2.2 %collective-permute-start.1 = (bf16[8,128,128]{2,1,0:T(8,128)(2,1)S(1)}, bf16[8,128,128]{2,1,0:T(8,128)(2,1)S(1)}, u32[]{:S(2)}, u32[]{:S(2)}) collective-permute-start(bf16[8,128,128]{2,1,0:T(8,128)(2,1)S(1)} %get-tuple-element.28.v0), channel_id=1, source_target_pairs={{0,384},{128,0},{256,128},{384,256},{1,385},{129,1},{257,129},{385... | collective-permute-start | bytes 786440 | tf_op jit(solution)/shard_map/ppermute | solution.py:423
  44.0 4.3 %collective-permute-start.2 = (bf16[8,128,128]{2,1,0:T(8,128)(2,1)S(1)}, bf16[8,128,128]{2,1,0:T(8,128)(2,1)S(1)}, u32[]{:S(2)}, u32[]{:S(2)}) collective-permute-start(bf16[8,128,128]{2,1,0:T(8,128)(2,1)S(1)} %get-tuple-element.28.v0), channel_id=1, source_target_pairs={{0,256},{128,384},{256,0},{384,128},{1,257},{129,385},{257,1},{385... | collective-permute-start | bytes 786440 | tf_op jit(solution)/shard_map/ppermute | solution.py:423
  48.4 1.9 %collective-permute-start.3 = (bf16[8,128,128]{2,1,0:T(8,128)(2,1)S(1)}, bf16[8,128,128]{2,1,0:T(8,128)(2,1)S(1)}, u32[]{:S(2)}, u32[]{:S(2)}) collective-permute-start(bf16[8,128,128]{2,1,0:T(8,128)(2,1)S(1)} %get-tuple-element.28.v0), channel_id=1, source_target_pairs={{0,128},{128,256},{256,384},{384,0},{1,129},{129,257},{257,385},{3... | collective-permute-start | bytes 786440 | tf_op jit(solution)/shard_map/ppermute | solution.py:423
  54.3 6.7 %all-gather.3.cloned.1.call-done = bf16[4352,512]{1,0:T(8,128)(2,1)} async-done(((bf16[272,512]{1,0:T(8,128)(2,1)}), bf16[4352,512]{1,0:T(8,128)(2,1)}) %all-gather.3.cloned.1.call-update) | async-done | bytes 4456464 | tf_op jit(solution)/shard_map/all_gather | solution.py:458
  61.0 4.1 %row_statistics.1 = (f32[16,1,512]{2,1,0:T(1,128)S(1)}, f32[16,64,128]{2,1,0:T(8,128)}) custom-call(s32[520]{0:T(1024)S(1)} %concatenate.3.info_ref, bf16[16,272,512]{2,1,0:T(8,128)(2,1)} %bitcast.23, bf16[32,128,128]{2,1,0:T(8,128)(2,1)S(1)} %bitcast.17), custom_call_target="tpu_custom_call" | custom-call | flops 10000000000 | bytes 4194304 | tf_op jit(solution)/shard_map/row_statistics/pallas_call | solution.py:329
  65.1 11.2 %all-to-all-start.2 = ((f32[16,64,128]{2,1,0:T(8,128)}), f32[16,64,128]{2,1,0:T(8,128)S(1)}, u32[]{:S(2)}, u32[]{:S(2)}) async-start(f32[16,64,128]{2,1,0:T(8,128)} %get-tuple-element.25), calls=%async_computation.2 | async-start | bytes 1048576 | tf_op jit(solution)/shard_map/all_to_all | solution.py:476
  76.3 5.6 %query_gradient.1 = (bf16[8,128,512]{2,1,0:T(8,128)(2,1)S(1)}, bf16[8,128,512]{2,1,0:T(8,128)(2,1)}) custom-call(s32[520]{0:T(1024)S(1)} %concatenate.3.info_ref, bf16[16,272,512]{2,1,0:T(8,128)(2,1)} %bitcast.24, bf16[32,128,128]{2,1,0:T(8,128)(2,1)} %bitcast.18, bf16[8,128,128]{2,1,0:T(8,128)(2,1)S(1)} %get-tuple-element.28.v0, ...), custom_call_target="tpu_custom_call" | custom-call | flops 10000000000 | bytes 8388608 | tf_op jit(solution)/shard_map/query_gradient/pallas_call | solution.py:353
  82.0 2.6 %collective-permute-start.4 = (bf16[8,128,512]{2,1,0:T(8,128)(2,1)}, bf16[8,128,512]{2,1,0:T(8,128)(2,1)S(1)}, u32[]{:S(2)}, u32[]{:S(2)}) collective-permute-start(bf16[8,128,512]{2,1,0:T(8,128)(2,1)} %get-tuple-element.31), channel_id=1, source_target_pairs={{0,16},{16,0},{1,17},{17,1},{2,18},{18,2},{3,19},{19,3},{4,20},{20... | collective-permute-start | bytes 3145736 | tf_op jit(solution)/shard_map/ppermute | solution.py:427
  84.6 6.4 %all-to-all-done.2.parts_ref = f32[16,64,128]{2,1,0:T(8,128)S(1)} async-done(((f32[16,64,128]{2,1,0:T(8,128)}), f32[16,64,128]{2,1,0:T(8,128)S(1)}, u32[]{:S(2)}, u32[]{:S(2)}) %all-to-all-start.2) | async-done | bytes 524320 | tf_op jit(solution)/shard_map/all_to_all | solution.py:476
  91.7 2.0 %weigh_queries.1 = bf16[8,128,512]{2,1,0:T(8,128)(2,1)} custom-call(s32[520]{0:T(1024)S(1)} %concatenate.3.info_ref, f32[64,128]{1,0:T(8,128)S(1)} %get-tuple-element.26.own_ref, f32[64,128]{1,0:T(8,128)S(1)} %get-tuple-element.27.far_ref, bf16[8,128,512]{2,1,0:T(8,128)(2,1)S(1)} %get-tuple-element.30.kept_ref, ...), custom_call_target="tpu_custom_call" | custom-call | tf_op jit(solution)/shard_map/weigh_queries/pallas_call | solution.py:384
  94.7 4.9 %key_gradient.1 = (bf16[8,128,256]{2,1,0:T(8,128)(2,1)S(1)}, bf16[8,128,256]{2,1,0:T(8,128)(2,1)S(1)}, bf16[8,128,256]{2,1,0:T(8,128)(2,1)S(1)}, bf16[8,128,256]{2,1,0:T(8,128)(2,1)S(1)}) custom-call(s32[520]{0:T(1024)S(1)} %concatenate.3.info_ref, bf16[16,272,512]{2,1,0:T(8,128)(2,1)} %bitcast.25, bf16[32,128,128]{2,1,0:T(8,128)(2,1)} %bitcast.19, ...), custom_call_target="tpu_custom_call" | custom-call | flops 10000000000 | bytes 8388608 | tf_op jit(solution)/shard_map/key_gradient/pallas_call | solution.py:396
  99.6 1.9 %collective-permute-start.5 = (bf16[8,128,256]{2,1,0:T(8,128)(2,1)S(1)}, bf16[8,128,256]{2,1,0:T(8,128)(2,1)S(1)}, u32[]{:S(2)}, u32[]{:S(2)}) collective-permute-start(bf16[8,128,256]{2,1,0:T(8,128)(2,1)S(1)} %get-tuple-element.34), channel_id=1, source_target_pairs={{0,256},{128,384},{256,0},{384,128},{1,257},{129,385},{257,1},{385... | collective-permute-start | bytes 1572872 | tf_op jit(solution)/shard_map/ppermute | solution.py:423
  101.6 3.8 %collective-permute-start.6 = (bf16[8,128,256]{2,1,0:T(8,128)(2,1)S(1)}, bf16[8,128,256]{2,1,0:T(8,128)(2,1)S(1)}, u32[]{:S(2)}, u32[]{:S(2)}) collective-permute-start(bf16[8,128,256]{2,1,0:T(8,128)(2,1)S(1)} %get-tuple-element.35), channel_id=1, source_target_pairs={{0,128},{128,256},{256,384},{384,0},{1,129},{129,257},{257,385},{3... | collective-permute-start | bytes 1572872 | tf_op jit(solution)/shard_map/ppermute | solution.py:423
  105.4 1.9 %collective-permute-start.7 = (bf16[8,128,256]{2,1,0:T(8,128)(2,1)S(1)}, bf16[8,128,256]{2,1,0:T(8,128)(2,1)S(1)}, u32[]{:S(2)}, u32[]{:S(2)}) collective-permute-start(bf16[8,128,256]{2,1,0:T(8,128)(2,1)S(1)} %get-tuple-element.36), channel_id=1, source_target_pairs={{0,384},{128,0},{256,128},{384,256},{1,385},{129,1},{257,129},{385... | collective-permute-start | bytes 1572872 | tf_op jit(solution)/shard_map/ppermute | solution.py:423
  107.3 7.5 %collective-permute-done.5 = bf16[8,128,256]{2,1,0:T(8,128)(2,1)S(1)} collective-permute-done((bf16[8,128,256]{2,1,0:T(8,128)(2,1)S(1)}, bf16[8,128,256]{2,1,0:T(8,128)(2,1)S(1)}, u32[]{:S(2)}, u32[]{:S(2)}) %collective-permute-start.5) | collective-permute-done | bytes 524320 | tf_op jit(solution)/shard_map/ppermute | solution.py:423
  114.8 13.4 %collective-permute-done.6 = bf16[8,128,256]{2,1,0:T(8,128)(2,1)S(1)} collective-permute-done((bf16[8,128,256]{2,1,0:T(8,128)(2,1)S(1)}, bf16[8,128,256]{2,1,0:T(8,128)(2,1)S(1)}, u32[]{:S(2)}, u32[]{:S(2)}) %collective-permute-start.6) | collective-permute-done | bytes 524320 | tf_op jit(solution)/shard_map/ppermute | solution.py:423
  129.3 5.6 %all-to-all-start.3 = ((bf16[8,128,256]{2,1,0:T(8,128)(2,1)}), bf16[8,128,256]{2,1,0:T(8,128)(2,1)S(1)}, u32[]{:S(2)}, u32[]{:S(2)}) async-start(bf16[8,128,256]{2,1,0:T(8,128)(2,1)} %add_convert_fusion), calls=%async_computation.4 | async-start | bytes 1048576 | tf_op jit(solution)/shard_map/all_to_all | solution.py:433
  136.6 14.2 %all-to-all-done.3.over_y_ref = bf16[8,128,256]{2,1,0:T(8,128)(2,1)S(1)} async-done(((bf16[8,128,256]{2,1,0:T(8,128)(2,1)}), bf16[8,128,256]{2,1,0:T(8,128)(2,1)S(1)}, u32[]{:S(2)}, u32[]{:S(2)}) %all-to-all-start.3) | async-done | bytes 524320 | tf_op jit(solution)/shard_map/all_to_all | solution.py:433
  (40 shorter events, 9.3 us)
Async XLA Ops:
  7.2 53.8 %all-gather.3.cloned.1.call-start = ((), (), s32[]{:S(2)}) async-start(), calls=%async_computation.6 | async-start | bytes 4734976 | tf_op jit(solution)/shard_map/all_gather | solution.py:458
  9.4 24.3 %all-to-all-start = ((bf16[8,144,256]{2,1,0:T(8,128)(2,1)}), bf16[8,144,256]{2,1,0:T(8,128)(2,1)S(1)}, u32[]{:S(2)}, u32[]{:S(2)}) async-start(bf16[8,144,256]{2,1,0:T(8,128)(2,1)} %get-tuple-element.22), calls=%async_computation | async-start | bytes 1179648 | tf_op jit(solution)/shard_map/all_to_all | solution.py:459
  33.7 8.1 %collective-permute-start = (bf16[2,16,32]{2,1,0:T(8,128)(2,1)S(1)}, bf16[2,16,32]{2,1,0:T(8,128)(2,1)S(1)}, u32[]{:S(2)}, u32[]{:S(2)}) collective-permute-start(bf16[2,16,32]{2,1,0:T(8,128)(2,1)S(1)} %constant_dynamic-slice_fusion), channel_id=1, source_target_pairs={{0,16},{16,0},{1,17},{17,1},{2,18},{18,2},{3,19},{19,3},{4,20},{20... | collective-permute-start | bytes 6152 | tf_op jit(solution)/shard_map/ppermute | solution.py:427
  37.6 16.7 %all-to-all-start.1 = ((bf16[4,8,128,128]{3,2,1,0:T(8,128)(2,1)}), bf16[4,8,128,128]{3,2,1,0:T(8,128)(2,1)S(1)}, u32[]{:S(2)}, u32[]{:S(2)}) async-start(bf16[4,8,128,128]{3,2,1,0:T(8,128)(2,1)} %broadcast_in_dim.41), calls=%async_computation.1 | async-start | bytes 2097152 | tf_op jit(solution)/shard_map/all_to_all | solution.py:417
  41.9 34.4 %collective-permute-start.1 = (bf16[8,128,128]{2,1,0:T(8,128)(2,1)S(1)}, bf16[8,128,128]{2,1,0:T(8,128)(2,1)S(1)}, u32[]{:S(2)}, u32[]{:S(2)}) collective-permute-start(bf16[8,128,128]{2,1,0:T(8,128)(2,1)S(1)} %get-tuple-element.28.v0), channel_id=1, source_target_pairs={{0,384},{128,0},{256,128},{384,256},{1,385},{129,1},{257,129},{385... | collective-permute-start | bytes 786440 | tf_op jit(solution)/shard_map/ppermute | solution.py:423
  44.0 32.3 %collective-permute-start.2 = (bf16[8,128,128]{2,1,0:T(8,128)(2,1)S(1)}, bf16[8,128,128]{2,1,0:T(8,128)(2,1)S(1)}, u32[]{:S(2)}, u32[]{:S(2)}) collective-permute-start(bf16[8,128,128]{2,1,0:T(8,128)(2,1)S(1)} %get-tuple-element.28.v0), channel_id=1, source_target_pairs={{0,256},{128,384},{256,0},{384,128},{1,257},{129,385},{257,1},{385... | collective-permute-start | bytes 786440 | tf_op jit(solution)/shard_map/ppermute | solution.py:423
  48.4 28.0 %collective-permute-start.3 = (bf16[8,128,128]{2,1,0:T(8,128)(2,1)S(1)}, bf16[8,128,128]{2,1,0:T(8,128)(2,1)S(1)}, u32[]{:S(2)}, u32[]{:S(2)}) collective-permute-start(bf16[8,128,128]{2,1,0:T(8,128)(2,1)S(1)} %get-tuple-element.28.v0), channel_id=1, source_target_pairs={{0,128},{128,256},{256,384},{384,0},{1,129},{129,257},{257,385},{3... | collective-permute-start | bytes 786440 | tf_op jit(solution)/shard_map/ppermute | solution.py:423
  54.3 10.8 %copy-start = (bf16[4,8,128,128]{3,2,1,0:T(8,128)(2,1)}, bf16[4,8,128,128]{3,2,1,0:T(8,128)(2,1)S(1)}, u32[]{:S(2)}) copy-start(bf16[4,8,128,128]{3,2,1,0:T(8,128)(2,1)S(1)} %all-to-all-done.1) | copy-start | bytes 3145732
  65.1 25.9 %all-to-all-start.2 = ((f32[16,64,128]{2,1,0:T(8,128)}), f32[16,64,128]{2,1,0:T(8,128)S(1)}, u32[]{:S(2)}, u32[]{:S(2)}) async-start(f32[16,64,128]{2,1,0:T(8,128)} %get-tuple-element.25), calls=%async_computation.2 | async-start | bytes 1048576 | tf_op jit(solution)/shard_map/all_to_all | solution.py:476
  76.2 58.7 %reduce-scatter.2.cloned.1.call-start = ((), (), s32[]{:S(2)}) async-start(), calls=%async_computation.5 | async-start | bytes 1179648 | tf_op jit(solution)/shard_map/reduce_scatter | solution.py:484
  76.3 5.6 %copy-start.2 = (bf16[8,128,128]{2,1,0:T(8,128)(2,1)}, bf16[8,128,128]{2,1,0:T(8,128)(2,1)S(1)}, u32[]{:S(2)}) copy-start(bf16[8,128,128]{2,1,0:T(8,128)(2,1)S(1)} %collective-permute-done.3.v3) | copy-start | bytes 786436
  82.0 9.7 %collective-permute-start.4 = (bf16[8,128,512]{2,1,0:T(8,128)(2,1)}, bf16[8,128,512]{2,1,0:T(8,128)(2,1)S(1)}, u32[]{:S(2)}, u32[]{:S(2)}) collective-permute-start(bf16[8,128,512]{2,1,0:T(8,128)(2,1)} %get-tuple-element.31), channel_id=1, source_target_pairs={{0,16},{16,0},{1,17},{17,1},{2,18},{18,2},{3,19},{19,3},{4,20},{20... | collective-permute-start | bytes 3145736 | tf_op jit(solution)/shard_map/ppermute | solution.py:427
  93.7 1.0 copy-start.3
  99.6 15.2 %collective-permute-start.5 = (bf16[8,128,256]{2,1,0:T(8,128)(2,1)S(1)}, bf16[8,128,256]{2,1,0:T(8,128)(2,1)S(1)}, u32[]{:S(2)}, u32[]{:S(2)}) collective-permute-start(bf16[8,128,256]{2,1,0:T(8,128)(2,1)S(1)} %get-tuple-element.34), channel_id=1, source_target_pairs={{0,256},{128,384},{256,0},{384,128},{1,257},{129,385},{257,1},{385... | collective-permute-start | bytes 1572872 | tf_op jit(solution)/shard_map/ppermute | solution.py:423
  101.6 26.7 %collective-permute-start.6 = (bf16[8,128,256]{2,1,0:T(8,128)(2,1)S(1)}, bf16[8,128,256]{2,1,0:T(8,128)(2,1)S(1)}, u32[]{:S(2)}, u32[]{:S(2)}) collective-permute-start(bf16[8,128,256]{2,1,0:T(8,128)(2,1)S(1)} %get-tuple-element.35), channel_id=1, source_target_pairs={{0,128},{128,256},{256,384},{384,0},{1,129},{129,257},{257,385},{3... | collective-permute-start | bytes 1572872 | tf_op jit(solution)/shard_map/ppermute | solution.py:423
  105.4 22.9 %collective-permute-start.7 = (bf16[8,128,256]{2,1,0:T(8,128)(2,1)S(1)}, bf16[8,128,256]{2,1,0:T(8,128)(2,1)S(1)}, u32[]{:S(2)}, u32[]{:S(2)}) collective-permute-start(bf16[8,128,256]{2,1,0:T(8,128)(2,1)S(1)} %get-tuple-element.36), channel_id=1, source_target_pairs={{0,384},{128,0},{256,128},{384,256},{1,385},{129,1},{257,129},{385... | collective-permute-start | bytes 1572872 | tf_op jit(solution)/shard_map/ppermute | solution.py:423
  129.3 21.5 %all-to-all-start.3 = ((bf16[8,128,256]{2,1,0:T(8,128)(2,1)}), bf16[8,128,256]{2,1,0:T(8,128)(2,1)S(1)}, u32[]{:S(2)}, u32[]{:S(2)}) async-start(bf16[8,128,256]{2,1,0:T(8,128)(2,1)} %add_convert_fusion), calls=%async_computation.4 | async-start | bytes 1048576 | tf_op jit(solution)/shard_map/all_to_all | solution.py:433
  134.9 0.9 copy-start.1
Sparse Core Ops, SparseCore 0:
  10.1 50.8 all-gather.2
  93.9 34.5 reduce-scatter.1

commit v10 on v9

--- a/solution.py
+++ b/solution.py
@@ -151,7 +151,22 @@
     far_ref[...] = jnp.exp2(parts_ref[(1 - info_ref[1]) * NZ + info_ref[3]] - total)
 
 
-def weigh_kernel(info_ref, own_ref, far_ref, kept_ref, got_ref, chip_ref):
+def key_kernel(
+    info_ref, q_hbm, k_hbm, v0, v1, v2, v3, total_ref, own_ref, far_ref, kept_hbm, got_hbm,
+    chip_hbm, out0, out1, out2, out3,
+    q_ref, k_ref, v_ref, k_acc, v_acc, p_ref, ds_ref, kept_ref, got_ref, chip_ref, sems,
+):
+    two = (
+        pltpu.make_async_copy(kept_hbm, kept_ref, sems.at[6]),
+        pltpu.make_async_copy(got_hbm, got_ref, sems.at[7]),
+    )
+    for copy in two:
+        copy.start()
+    copies = load(info_ref, q_hbm, k_hbm, (v0, v1, v2, v3), q_ref, k_ref, v_ref, sems)
+    k_acc[...] = jnp.zeros(k_acc.shape, jnp.float32)
+    v_acc[...] = jnp.zeros(v_acc.shape, jnp.float32)
+    for copy in two:
+        copy.wait()
     for n in range(NZ):
         for h in range(HQ):
             row = pl.ds((info_ref[1] * NZ + n) * HQ + h, 1)
@@ -160,15 +175,8 @@
                 kept_ref[n, :, cols].astype(jnp.float32) * own_ref[row]
                 + got_ref[n, :, cols].astype(jnp.float32) * far_ref[row]
             ).astype(jnp.bfloat16)
-
-
-def key_kernel(
-    info_ref, q_hbm, k_hbm, v0, v1, v2, v3, total_ref, out0, out1, out2, out3,
-    q_ref, k_ref, v_ref, k_acc, v_acc, p_ref, ds_ref, sems,
-):
-    copies = load(info_ref, q_hbm, k_hbm, (v0, v1, v2, v3), q_ref, k_ref, v_ref, sems)
-    k_acc[...] = jnp.zeros(k_acc.shape, jnp.float32)
-    v_acc[...] = jnp.zeros(v_acc.shape, jnp.float32)
+    leave = pltpu.make_async_copy(chip_ref, chip_hbm, sems.at[8])
+    leave.start()
     for copy in copies:
         copy.wait()
 
@@ -194,6 +202,7 @@
     for n, out_ref in enumerate((out0, out1, out2, out3)):
         out_ref[:, :, :HD] = k_acc[of_x(info_ref, n)].astype(jnp.bfloat16)
         out_ref[:, :, HD:] = v_acc[of_x(info_ref, n)].astype(jnp.bfloat16)
+    leave.wait()
 
 
 def prepare_kernel(
@@ -380,36 +389,29 @@
     )(info, parts)
 
 
-def call_weigh(info, own, far, kept, got):
-    return pl.pallas_call(
-        weigh_kernel,
-        out_shape=jax.ShapeDtypeStruct((NZ, HD, ROWS), jnp.bfloat16),
-        in_specs=[smem()] + [vmem()] * 4,
-        out_specs=vmem(),
-        compiler_params=params(8),
-        name="weigh_queries",
-    )(info, own, far, kept, got)
-
-
-def call_key(info, q, k, values, total):
+def call_key(info, q, k, values, statistics, kept, got):
     quarter = jax.ShapeDtypeStruct((NY, TILE, 2 * HD), jnp.bfloat16)
+    half = pltpu.VMEM((NZ, HD, ROWS), jnp.bfloat16)
     return pl.pallas_call(
         key_kernel,
-        out_shape=(quarter,) * 4,
-        in_specs=[smem()] + [anywhere()] * 6 + [vmem()],
-        out_specs=(vmem(),) * 4,
+        out_shape=(jax.ShapeDtypeStruct((NZ, HD, ROWS), jnp.bfloat16),) + (quarter,) * 4,
+        in_specs=[smem()] + [anywhere()] * 6 + [vmem()] * 3 + [anywhere()] * 2,
+        out_specs=(anywhere(),) + (vmem(),) * 4,
         scratch_shapes=[
             *loaded(),
             pltpu.VMEM((NK + 1, TILE, HD), jnp.float32),
             pltpu.VMEM((NK + 1, TILE, HD), jnp.float32),
             pltpu.VMEM((STEP, TILE, ROWS), jnp.bfloat16),
             pltpu.VMEM((STEP, TILE, ROWS), jnp.bfloat16),
-            pltpu.SemaphoreType.DMA((6,)),
+            half,
+            half,
+            half,
+            pltpu.SemaphoreType.DMA((9,)),
         ],
         compiler_params=params(),
         cost_estimate=cost(8),
         name="key_gradient",
-    )(info, q, k, *values, total)
+    )(info, q, k, *values, *statistics, kept, got)
 
 
 def to_everyone(value, axis):
@@ -477,9 +479,8 @@
     kept, sent = call_query(info, q_all, k_all, v_all, part)
     got = swap_cores(sent)
 
-    total, own, far = call_combine(info, parts)
-    chip = call_weigh(info, own, far, kept, got)
-    parts = call_key(info, q_all, k_all, v_all, total)
+    statistics = call_combine(info, parts)
+    chip, *parts = call_key(info, q_all, k_all, v_all, statistics, kept, got)
 
     dq_own = lax.psum_scatter(chip, "z", scatter_dimension=0, tiled=True)[0]
     query_grad, over_y = lax.optimization_barrier(

time: 159 us -> 155 us (0.975)
  the two profiles are of different devices: /device:TPU:13 before, /device:TPU:11 now
where the time goes in v10:
time: 155 us; the launch traced here: 154 us
  waiting for transfers between devices  64.4 us (42%)
  starting transfers between devices  45.3 us (29%)
  Pallas kernels  22.5 us (15%)
  between operations  14.2 us (9%)
  local copies, waits for them, and re-layouts  4.54 us (3%)
  other arithmetic  2.94 us (2%)
    ppermute x6, waiting for transfers between devices, along_x(): return lax.ppermute(value, 'x', [(n, (n + by) % 4) for n in range(4)])  20.6 us
    ppermute x6, starting transfers between devices, along_x(): return lax.ppermute(value, 'x', [(n, (n + by) % 4) for n in range(4)])  17.4 us
    all_to_all x1, waiting for transfers between devices, body(): kv_y = lax.all_to_all(kv_own, Y, 0, 0, tiled=True)  17.3 us
    all_to_all x1, waiting for transfers between devices, sum_over_keys(): return lax.all_to_all(over_x, Y, 0, 0, tiled=True)  14.2 us
    pallas_call x1, Pallas kernels, call_key(): pl.pallas_call(key_kernel, out_shape=(jax.ShapeDtypeStruct((NZ, HD, ROWS)...  7.36 us
    all_to_all x1, starting transfers between devices, body(): kv_y = lax.all_to_all(kv_own, Y, 0, 0, tiled=True)  7 us
    all_to_all x1, starting transfers between devices, body(): parts = lax.all_to_all(parts, ('c', 'z'), 0, 0, tiled=True)  6.89 us
    all_to_all x1, waiting for transfers between devices, body(): parts = lax.all_to_all(parts, ('c', 'z'), 0, 0, tiled=True)  5.87 us
  transfers between devices with their start and end apart: 14, of which 8 were waited for; matrix products, arithmetic and copies ran while one was open for 4% of the time, Pallas kernels for 8%

profile of v10, /device:TPU:11, one launch (start us, length us, event | category | flops | bytes accessed | tf_op | source)
XLA Modules:
  0.0 154.0 jit_solution(9732353907709874192)
XLA Ops:
  7.2 2.1 %prepare.1 = (bf16[272,512]{1,0:T(8,128)(2,1)}, bf16[8,144,256]{2,1,0:T(8,128)(2,1)}) custom-call(bf16[128,512]{1,0:T(8,128)(2,1)} %q_in.1, bf16[128,512]{1,0:T(8,128)(2,1)} %g_in.1, bf16[128,512]{1,0:T(8,128)(2,1)} %o_in.1, bf16[128,128]{1,0:T(8,128)(2,1)} %k_in.1, bf16[128,128]{1,0:T(8,128)(2,1)} %v_in.1, s32[16,32]{1,0:T(8,128)} %mask_in.1), custom_call_target="tpu_custom_call" | custom-call | tf_op jit(solution)/shard_map/prepare/pallas_call | solution.py:292
  9.4 7.0 %all-to-all-start = ((bf16[8,144,256]{2,1,0:T(8,128)(2,1)}), bf16[8,144,256]{2,1,0:T(8,128)(2,1)S(1)}, u32[]{:S(2)}, u32[]{:S(2)}) async-start(bf16[8,144,256]{2,1,0:T(8,128)(2,1)} %get-tuple-element.23), calls=%async_computation | async-start | bytes 1179648 | tf_op jit(solution)/shard_map/all_to_all | solution.py:461
  16.4 17.3 %all-to-all-done = bf16[8,144,256]{2,1,0:T(8,128)(2,1)S(1)} async-done(((bf16[8,144,256]{2,1,0:T(8,128)(2,1)}), bf16[8,144,256]{2,1,0:T(8,128)(2,1)S(1)}, u32[]{:S(2)}, u32[]{:S(2)}) %all-to-all-start) | async-done | bytes 589856 | tf_op jit(solution)/shard_map/all_to_all | solution.py:461
  33.7 2.5 %collective-permute-start = (bf16[2,16,32]{2,1,0:T(8,128)(2,1)S(1)}, bf16[2,16,32]{2,1,0:T(8,128)(2,1)S(1)}, u32[]{:S(2)}, u32[]{:S(2)}) collective-permute-start(bf16[2,16,32]{2,1,0:T(8,128)(2,1)S(1)} %constant_dynamic-slice_fusion), channel_id=1, source_target_pairs={{0,16},{16,0},{1,17},{17,1},{2,18},{18,2},{3,19},{19,3},{4,20},{20... | collective-permute-start | bytes 6152 | tf_op jit(solution)/shard_map/ppermute | solution.py:429
  36.3 1.3 broadcast_in_dim.41
  37.6 4.3 %all-to-all-start.1 = ((bf16[4,8,128,128]{3,2,1,0:T(8,128)(2,1)}), bf16[4,8,128,128]{3,2,1,0:T(8,128)(2,1)S(1)}, u32[]{:S(2)}, u32[]{:S(2)}) async-start(bf16[4,8,128,128]{3,2,1,0:T(8,128)(2,1)} %broadcast_in_dim.41), calls=%async_computation.1 | async-start | bytes 2097152 | tf_op jit(solution)/shard_map/all_to_all | solution.py:419
  41.9 3.1 %collective-permute-start.3 = (bf16[8,128,128]{2,1,0:T(8,128)(2,1)S(1)}, bf16[8,128,128]{2,1,0:T(8,128)(2,1)S(1)}, u32[]{:S(2)}, u32[]{:S(2)}) collective-permute-start(bf16[8,128,128]{2,1,0:T(8,128)(2,1)S(1)} %get-tuple-element.26.v0), channel_id=1, source_target_pairs={{0,128},{128,256},{256,384},{384,0},{1,129},{129,257},{257,385},{3... | collective-permute-start | bytes 786440 | tf_op jit(solution)/shard_map/ppermute | solution.py:425
  45.0 2.5 %collective-permute-start.2 = (bf16[8,128,128]{2,1,0:T(8,128)(2,1)S(1)}, bf16[8,128,128]{2,1,0:T(8,128)(2,1)S(1)}, u32[]{:S(2)}, u32[]{:S(2)}) collective-permute-start(bf16[8,128,128]{2,1,0:T(8,128)(2,1)S(1)} %get-tuple-element.26.v0), channel_id=1, source_target_pairs={{0,256},{128,384},{256,0},{384,128},{1,257},{129,385},{257,1},{385... | collective-permute-start | bytes 786440 | tf_op jit(solution)/shard_map/ppermute | solution.py:425
  47.5 4.0 %collective-permute-start.1 = (bf16[8,128,128]{2,1,0:T(8,128)(2,1)S(1)}, bf16[8,128,128]{2,1,0:T(8,128)(2,1)S(1)}, u32[]{:S(2)}, u32[]{:S(2)}) collective-permute-start(bf16[8,128,128]{2,1,0:T(8,128)(2,1)S(1)} %get-tuple-element.26.v0), channel_id=1, source_target_pairs={{0,384},{128,0},{256,128},{384,256},{1,385},{129,1},{257,129},{385... | collective-permute-start | bytes 786440 | tf_op jit(solution)/shard_map/ppermute | solution.py:425
  55.7 5.3 %all-gather.3.cloned.1.call-done = bf16[4352,512]{1,0:T(8,128)(2,1)} async-done(((bf16[272,512]{1,0:T(8,128)(2,1)}), bf16[4352,512]{1,0:T(8,128)(2,1)}) %all-gather.3.cloned.1.call-update) | async-done | bytes 4456464 | tf_op jit(solution)/shard_map/all_gather | solution.py:460
  61.0 5.0 %row_statistics.1 = (f32[16,1,512]{2,1,0:T(1,128)S(1)}, f32[16,64,128]{2,1,0:T(8,128)}) custom-call(s32[520]{0:T(1024)S(1)} %concatenate.3.info_ref, bf16[16,272,512]{2,1,0:T(8,128)(2,1)} %bitcast.23, bf16[32,128,128]{2,1,0:T(8,128)(2,1)S(1)} %bitcast.17), custom_call_target="tpu_custom_call" | custom-call | flops 10000000000 | bytes 4194304 | tf_op jit(solution)/shard_map/row_statistics/pallas_call | solution.py:338
  66.0 6.9 %all-to-all-start.2 = ((f32[16,64,128]{2,1,0:T(8,128)}), f32[16,64,128]{2,1,0:T(8,128)S(1)}, u32[]{:S(2)}, u32[]{:S(2)}) async-start(f32[16,64,128]{2,1,0:T(8,128)} %get-tuple-element.27), calls=%async_computation.2 | async-start | bytes 1048576 | tf_op jit(solution)/shard_map/all_to_all | solution.py:478
  73.0 5.8 %query_gradient.1 = (bf16[8,128,512]{2,1,0:T(8,128)(2,1)S(1)}, bf16[8,128,512]{2,1,0:T(8,128)(2,1)S(1)}) custom-call(s32[520]{0:T(1024)S(1)} %concatenate.3.info_ref, bf16[16,272,512]{2,1,0:T(8,128)(2,1)} %bitcast.24, bf16[32,128,128]{2,1,0:T(8,128)(2,1)} %bitcast.18, bf16[8,128,128]{2,1,0:T(8,128)(2,1)S(1)} %get-tuple-element.26.v0, ...), custom_call_target="tpu_custom_call" | custom-call | flops 10000000000 | bytes 8388608 | tf_op jit(solution)/shard_map/query_gradient/pallas_call | solution.py:362
  79.8 2.0 %collective-permute-start.4 = (bf16[8,128,512]{2,1,0:T(8,128)(2,1)S(1)}, bf16[8,128,512]{2,1,0:T(8,128)(2,1)}, u32[]{:S(2)}, u32[]{:S(2)}) collective-permute-start(bf16[8,128,512]{2,1,0:T(8,128)(2,1)S(1)} %get-tuple-element.33), channel_id=1, source_target_pairs={{0,16},{16,0},{1,17},{17,1},{2,18},{18,2},{3,19},{19,3},{4,20},{20... | collective-permute-start | bytes 3145736 | tf_op jit(solution)/shard_map/ppermute | solution.py:429
  81.8 5.9 %all-to-all-done.2.parts_ref = f32[16,64,128]{2,1,0:T(8,128)S(1)} async-done(((f32[16,64,128]{2,1,0:T(8,128)}), f32[16,64,128]{2,1,0:T(8,128)S(1)}, u32[]{:S(2)}, u32[]{:S(2)}) %all-to-all-start.2) | async-done | bytes 524320 | tf_op jit(solution)/shard_map/all_to_all | solution.py:478
  88.4 7.4 %key_gradient.1 = (bf16[8,128,512]{2,1,0:T(8,128)(2,1)}, bf16[8,128,256]{2,1,0:T(8,128)(2,1)S(1)}, bf16[8,128,256]{2,1,0:T(8,128)(2,1)S(1)}, bf16[8,128,256]{2,1,0:T(8,128)(2,1)S(1)}, bf16[8,128,256]{2,1,0:T(8,128)(2,1)S(1)}) custom-call(s32[520]{0:T(1024)S(1)} %concatenate.3.info_ref, bf16[16,272,512]{2,1,0:T(8,128)(2,1)} %bitcast.25, ...), custom_call_target="tpu_custom_call" | custom-call | flops 10000000000 | bytes 8388608 | tf_op jit(solution)/shard_map/key_gradient/pallas_call | solution.py:395
  95.8 2.6 %collective-permute-start.5 = (bf16[8,128,256]{2,1,0:T(8,128)(2,1)S(1)}, bf16[8,128,256]{2,1,0:T(8,128)(2,1)S(1)}, u32[]{:S(2)}, u32[]{:S(2)}) collective-permute-start(bf16[8,128,256]{2,1,0:T(8,128)(2,1)S(1)} %get-tuple-element.36), channel_id=1, source_target_pairs={{0,256},{128,384},{256,0},{384,128},{1,257},{129,385},{257,1},{385... | collective-permute-start | bytes 1572872 | tf_op jit(solution)/shard_map/ppermute | solution.py:425
  98.4 1.9 %collective-permute-start.6 = (bf16[8,128,256]{2,1,0:T(8,128)(2,1)S(1)}, bf16[8,128,256]{2,1,0:T(8,128)(2,1)S(1)}, u32[]{:S(2)}, u32[]{:S(2)}) collective-permute-start(bf16[8,128,256]{2,1,0:T(8,128)(2,1)S(1)} %get-tuple-element.37), channel_id=1, source_target_pairs={{0,128},{128,256},{256,384},{384,0},{1,129},{129,257},{257,385},{3... | collective-permute-start | bytes 1572872 | tf_op jit(solution)/shard_map/ppermute | solution.py:425
  100.3 3.4 %collective-permute-start.7 = (bf16[8,128,256]{2,1,0:T(8,128)(2,1)S(1)}, bf16[8,128,256]{2,1,0:T(8,128)(2,1)S(1)}, u32[]{:S(2)}, u32[]{:S(2)}) collective-permute-start(bf16[8,128,256]{2,1,0:T(8,128)(2,1)S(1)} %get-tuple-element.38), channel_id=1, source_target_pairs={{0,384},{128,0},{256,128},{384,256},{1,385},{129,1},{257,129},{385... | collective-permute-start | bytes 1572872 | tf_op jit(solution)/shard_map/ppermute | solution.py:425
  103.7 8.0 %collective-permute-done.5 = bf16[8,128,256]{2,1,0:T(8,128)(2,1)S(1)} collective-permute-done((bf16[8,128,256]{2,1,0:T(8,128)(2,1)S(1)}, bf16[8,128,256]{2,1,0:T(8,128)(2,1)S(1)}, u32[]{:S(2)}, u32[]{:S(2)}) %collective-permute-start.5) | collective-permute-done | bytes 524320 | tf_op jit(solution)/shard_map/ppermute | solution.py:425
  111.7 8.7 %collective-permute-done.6 = bf16[8,128,256]{2,1,0:T(8,128)(2,1)S(1)} collective-permute-done((bf16[8,128,256]{2,1,0:T(8,128)(2,1)S(1)}, bf16[8,128,256]{2,1,0:T(8,128)(2,1)S(1)}, u32[]{:S(2)}, u32[]{:S(2)}) %collective-permute-start.6) | collective-permute-done | bytes 524320 | tf_op jit(solution)/shard_map/ppermute | solution.py:425
  120.4 3.9 %collective-permute-done.7 = bf16[8,128,256]{2,1,0:T(8,128)(2,1)S(1)} collective-permute-done((bf16[8,128,256]{2,1,0:T(8,128)(2,1)S(1)}, bf16[8,128,256]{2,1,0:T(8,128)(2,1)S(1)}, u32[]{:S(2)}, u32[]{:S(2)}) %collective-permute-start.7) | collective-permute-done | bytes 524320 | tf_op jit(solution)/shard_map/ppermute | solution.py:425
  125.3 5.2 %all-to-all-start.3 = ((bf16[8,128,256]{2,1,0:T(8,128)(2,1)}), bf16[8,128,256]{2,1,0:T(8,128)(2,1)S(1)}, u32[]{:S(2)}, u32[]{:S(2)}) async-start(bf16[8,128,256]{2,1,0:T(8,128)(2,1)} %add_convert_fusion), calls=%async_computation.4 | async-start | bytes 1048576 | tf_op jit(solution)/shard_map/all_to_all | solution.py:435
  132.2 14.2 %all-to-all-done.3.over_y_ref = bf16[8,128,256]{2,1,0:T(8,128)(2,1)S(1)} async-done(((bf16[8,128,256]{2,1,0:T(8,128)(2,1)}), bf16[8,128,256]{2,1,0:T(8,128)(2,1)S(1)}, u32[]{:S(2)}, u32[]{:S(2)}) %all-to-all-start.3) | async-done | bytes 524320 | tf_op jit(solution)/shard_map/all_to_all | solution.py:435
  (37 shorter events, 9.5 us)
Async XLA Ops:
  7.2 53.8 %all-gather.3.cloned.1.call-start = ((), (), s32[]{:S(2)}) async-start(), calls=%async_computation.6 | async-start | bytes 4734976 | tf_op jit(solution)/shard_map/all_gather | solution.py:460
  9.4 24.3 %all-to-all-start = ((bf16[8,144,256]{2,1,0:T(8,128)(2,1)}), bf16[8,144,256]{2,1,0:T(8,128)(2,1)S(1)}, u32[]{:S(2)}, u32[]{:S(2)}) async-start(bf16[8,144,256]{2,1,0:T(8,128)(2,1)} %get-tuple-element.23), calls=%async_computation | async-start | bytes 1179648 | tf_op jit(solution)/shard_map/all_to_all | solution.py:461
  33.7 8.2 %collective-permute-start = (bf16[2,16,32]{2,1,0:T(8,128)(2,1)S(1)}, bf16[2,16,32]{2,1,0:T(8,128)(2,1)S(1)}, u32[]{:S(2)}, u32[]{:S(2)}) collective-permute-start(bf16[2,16,32]{2,1,0:T(8,128)(2,1)S(1)} %constant_dynamic-slice_fusion), channel_id=1, source_target_pairs={{0,16},{16,0},{1,17},{17,1},{2,18},{18,2},{3,19},{19,3},{4,20},{20... | collective-permute-start | bytes 6152 | tf_op jit(solution)/shard_map/ppermute | solution.py:429
  37.6 18.1 %all-to-all-start.1 = ((bf16[4,8,128,128]{3,2,1,0:T(8,128)(2,1)}), bf16[4,8,128,128]{3,2,1,0:T(8,128)(2,1)S(1)}, u32[]{:S(2)}, u32[]{:S(2)}) async-start(bf16[4,8,128,128]{3,2,1,0:T(8,128)(2,1)} %broadcast_in_dim.41), calls=%async_computation.1 | async-start | bytes 2097152 | tf_op jit(solution)/shard_map/all_to_all | solution.py:419
  41.9 31.1 %collective-permute-start.3 = (bf16[8,128,128]{2,1,0:T(8,128)(2,1)S(1)}, bf16[8,128,128]{2,1,0:T(8,128)(2,1)S(1)}, u32[]{:S(2)}, u32[]{:S(2)}) collective-permute-start(bf16[8,128,128]{2,1,0:T(8,128)(2,1)S(1)} %get-tuple-element.26.v0), channel_id=1, source_target_pairs={{0,128},{128,256},{256,384},{384,0},{1,129},{129,257},{257,385},{3... | collective-permute-start | bytes 786440 | tf_op jit(solution)/shard_map/ppermute | solution.py:425
  45.0 28.0 %collective-permute-start.2 = (bf16[8,128,128]{2,1,0:T(8,128)(2,1)S(1)}, bf16[8,128,128]{2,1,0:T(8,128)(2,1)S(1)}, u32[]{:S(2)}, u32[]{:S(2)}) collective-permute-start(bf16[8,128,128]{2,1,0:T(8,128)(2,1)S(1)} %get-tuple-element.26.v0), channel_id=1, source_target_pairs={{0,256},{128,384},{256,0},{384,128},{1,257},{129,385},{257,1},{385... | collective-permute-start | bytes 786440 | tf_op jit(solution)/shard_map/ppermute | solution.py:425
  47.5 25.5 %collective-permute-start.1 = (bf16[8,128,128]{2,1,0:T(8,128)(2,1)S(1)}, bf16[8,128,128]{2,1,0:T(8,128)(2,1)S(1)}, u32[]{:S(2)}, u32[]{:S(2)}) collective-permute-start(bf16[8,128,128]{2,1,0:T(8,128)(2,1)S(1)} %get-tuple-element.26.v0), channel_id=1, source_target_pairs={{0,384},{128,0},{256,128},{384,256},{1,385},{129,1},{257,129},{385... | collective-permute-start | bytes 786440 | tf_op jit(solution)/shard_map/ppermute | solution.py:425
  55.7 10.3 %copy-start = (bf16[4,8,128,128]{3,2,1,0:T(8,128)(2,1)}, bf16[4,8,128,128]{3,2,1,0:T(8,128)(2,1)S(1)}, u32[]{:S(2)}) copy-start(bf16[4,8,128,128]{3,2,1,0:T(8,128)(2,1)S(1)} %all-to-all-done.1) | copy-start | bytes 3145732
  66.0 21.7 %all-to-all-start.2 = ((f32[16,64,128]{2,1,0:T(8,128)}), f32[16,64,128]{2,1,0:T(8,128)S(1)}, u32[]{:S(2)}, u32[]{:S(2)}) async-start(f32[16,64,128]{2,1,0:T(8,128)} %get-tuple-element.27), calls=%async_computation.2 | async-start | bytes 1048576 | tf_op jit(solution)/shard_map/all_to_all | solution.py:478
  72.9 57.6 %reduce-scatter.2.cloned.1.call-start = ((), (), s32[]{:S(2)}) async-start(), calls=%async_computation.5 | async-start | bytes 1179648 | tf_op jit(solution)/shard_map/reduce_scatter | solution.py:485
  78.8 1.0 copy-start.2
  79.8 8.6 %collective-permute-start.4 = (bf16[8,128,512]{2,1,0:T(8,128)(2,1)S(1)}, bf16[8,128,512]{2,1,0:T(8,128)(2,1)}, u32[]{:S(2)}, u32[]{:S(2)}) collective-permute-start(bf16[8,128,512]{2,1,0:T(8,128)(2,1)S(1)} %get-tuple-element.33), channel_id=1, source_target_pairs={{0,16},{16,0},{1,17},{17,1},{2,18},{18,2},{3,19},{19,3},{4,20},{20... | collective-permute-start | bytes 3145736 | tf_op jit(solution)/shard_map/ppermute | solution.py:429
  95.8 15.9 %collective-permute-start.5 = (bf16[8,128,256]{2,1,0:T(8,128)(2,1)S(1)}, bf16[8,128,256]{2,1,0:T(8,128)(2,1)S(1)}, u32[]{:S(2)}, u32[]{:S(2)}) collective-permute-start(bf16[8,128,256]{2,1,0:T(8,128)(2,1)S(1)} %get-tuple-element.36), channel_id=1, source_target_pairs={{0,256},{128,384},{256,0},{384,128},{1,257},{129,385},{257,1},{385... | collective-permute-start | bytes 1572872 | tf_op jit(solution)/shard_map/ppermute | solution.py:425
  98.4 22.0 %collective-permute-start.6 = (bf16[8,128,256]{2,1,0:T(8,128)(2,1)S(1)}, bf16[8,128,256]{2,1,0:T(8,128)(2,1)S(1)}, u32[]{:S(2)}, u32[]{:S(2)}) collective-permute-start(bf16[8,128,256]{2,1,0:T(8,128)(2,1)S(1)} %get-tuple-element.37), channel_id=1, source_target_pairs={{0,128},{128,256},{256,384},{384,0},{1,129},{129,257},{257,385},{3... | collective-permute-start | bytes 1572872 | tf_op jit(solution)/shard_map/ppermute | solution.py:425
  100.3 24.0 %collective-permute-start.7 = (bf16[8,128,256]{2,1,0:T(8,128)(2,1)S(1)}, bf16[8,128,256]{2,1,0:T(8,128)(2,1)S(1)}, u32[]{:S(2)}, u32[]{:S(2)}) collective-permute-start(bf16[8,128,256]{2,1,0:T(8,128)(2,1)S(1)} %get-tuple-element.38), channel_id=1, source_target_pairs={{0,384},{128,0},{256,128},{384,256},{1,385},{129,1},{257,129},{385... | collective-permute-start | bytes 1572872 | tf_op jit(solution)/shard_map/ppermute | solution.py:425
  125.3 21.1 %all-to-all-start.3 = ((bf16[8,128,256]{2,1,0:T(8,128)(2,1)}), bf16[8,128,256]{2,1,0:T(8,128)(2,1)S(1)}, u32[]{:S(2)}, u32[]{:S(2)}) async-start(bf16[8,128,256]{2,1,0:T(8,128)(2,1)} %add_convert_fusion), calls=%async_computation.4 | async-start | bytes 1048576 | tf_op jit(solution)/shard_map/all_to_all | solution.py:435
  130.5 0.9 copy-start.1
Sparse Core Ops, SparseCore 0:
  10.1 50.8 all-gather.2
  95.9 34.5 reduce-scatter.1

commit v11 on v10

--- a/solution.py
+++ b/solution.py
@@ -47,7 +47,7 @@
 
 
 def stats_kernel(
-    info_ref, q_hbm, k_hbm, out_ref, sent_hbm, q_ref, k_ref, m_ref, l_ref, sent_ref, sems
+    info_ref, q_hbm, k_hbm, sent_hbm, q_ref, k_ref, m_ref, l_ref, sent_ref, sems
 ):
     copies = (
         pltpu.make_async_copy(q_hbm.at[:, pl.ds(0, TILE), :], q_ref, sems.at[0]),
@@ -76,11 +76,11 @@
 
     lax.fori_loop(0, steps_of(info_ref), visit, 0)
     total = l_ref[...][:NQ]
-    out_ref[...] = jnp.where(
+    part = jnp.where(
         total > 0.0, m_ref[...][:NQ] + jnp.log2(jnp.maximum(total, 1e-30)), LOW
     )
     for n in range(NQ * HQ):
-        sent_ref[n : n + 1] = out_ref[n // HQ, :, n % HQ * TILE : (n % HQ + 1) * TILE]
+        sent_ref[n : n + 1] = part[n // HQ, :, n % HQ * TILE : (n % HQ + 1) * TILE]
     copies = [pltpu.make_async_copy(sent_ref, sent_hbm.at[n], sems.at[n]) for n in range(NQ)]
     for copy in copies:
         copy.start()
@@ -113,13 +113,17 @@
 
 
 def query_kernel(
-    info_ref, q_hbm, k_hbm, v0, v1, v2, v3, total_ref,
-    kept_ref, sent_ref, q_ref, k_ref, v_ref, acc, ds_ref, sems,
+    info_ref, q_hbm, k_hbm, v0, v1, v2, v3, parts_hbm,
+    kept_ref, sent_ref, q_ref, k_ref, v_ref, acc, ds_ref, part_ref, total_ref, sems,
 ):
     copies = load(info_ref, q_hbm, k_hbm, (v0, v1, v2, v3), q_ref, k_ref, v_ref, sems)
+    copies.append(pltpu.make_async_copy(parts_hbm.at[0], part_ref, sems.at[6]))
+    copies[-1].start()
     acc[...] = jnp.zeros(acc.shape, jnp.float32)
     for copy in copies:
         copy.wait()
+    for n in range(NQ * HQ):
+        total_ref[n // HQ, :, n % HQ * TILE : (n % HQ + 1) * TILE] = part_ref[n : n + 1]
 
     def visit(i, carry):
         where = [unpack(info_ref, i * STEP + u) for u in range(STEP)]
@@ -243,6 +247,17 @@
     for copy in puts:
         copy.start()
     for copy in (g_put, q_put, delta_put, *puts):
+        copy.wait()
+
+
+def split_kernel(kv_ref, k_hbm, v_hbm, sems):
+    keys = kv_ref.at[:, pl.ds(0, TILE), pl.ds(0, HD)]
+    values = kv_ref.at[:, pl.ds(0, TILE), pl.ds(HD, HD)]
+    copies = [pltpu.make_async_copy(keys, k_hbm.at[n], sems.at[n]) for n in range(4)]
+    copies.append(pltpu.make_async_copy(values, v_hbm, sems.at[4]))
+    for copy in copies:
+        copy.start()
+    for copy in copies:
         copy.wait()
 
 
@@ -311,6 +326,21 @@
     )(q, g, o, k, v, mask)
 
 
+def call_split(kv):
+    return pl.pallas_call(
+        split_kernel,
+        out_shape=(
+            jax.ShapeDtypeStruct((4, NY, TILE, HD), jnp.bfloat16),
+            jax.ShapeDtypeStruct((NY, TILE, HD), jnp.bfloat16),
+        ),
+        in_specs=[vmem()],
+        out_specs=(anywhere(), anywhere()),
+        scratch_shapes=[pltpu.SemaphoreType.DMA((5,))],
+        compiler_params=params(8),
+        name="split_keys",
+    )(kv)
+
+
 def call_finish_queries(dq):
     return pl.pallas_call(
         finish_queries_kernel,
@@ -337,12 +367,9 @@
 def call_stats(info, q, k):
     return pl.pallas_call(
         stats_kernel,
-        out_shape=(
-            jax.ShapeDtypeStruct((NQ, 1, ROWS), jnp.float32),
-            jax.ShapeDtypeStruct((NQ, NQ * HQ, TILE), jnp.float32),
-        ),
+        out_shape=jax.ShapeDtypeStruct((NQ, NQ * HQ, TILE), jnp.float32),
         in_specs=[smem()] + [anywhere()] * 2,
-        out_specs=(vmem(), anywhere()),
+        out_specs=anywhere(),
         scratch_shapes=[
             pltpu.VMEM((NQ, TILE, ROWS), jnp.bfloat16),
             pltpu.VMEM((NK, TILE, HD), jnp.bfloat16),
@@ -357,23 +384,25 @@
     )(info, q, k)
 
 
-def call_query(info, q, k, values, part):
+def call_query(info, q, k, values, parts):
     half = jax.ShapeDtypeStruct((NZ, HD, ROWS), jnp.bfloat16)
     return pl.pallas_call(
         query_kernel,
         out_shape=(half, half),
-        in_specs=[smem()] + [anywhere()] * 6 + [vmem()],
+        in_specs=[smem()] + [anywhere()] * 7,
         out_specs=(vmem(), vmem()),
         scratch_shapes=loaded()
         + [
             pltpu.VMEM((NQ + 1, HD, ROWS), jnp.float32),
             pltpu.VMEM((STEP, TILE, ROWS), jnp.bfloat16),
-            pltpu.SemaphoreType.DMA((6,)),
+            pltpu.VMEM((NQ * HQ, TILE), jnp.float32),
+            pltpu.VMEM((NQ, 1, ROWS), jnp.float32),
+            pltpu.SemaphoreType.DMA((7,)),
         ],
         compiler_params=params(),
         cost_estimate=cost(8),
         name="query_gradient",
-    )(info, q, k, *values, part)
+    )(info, q, k, *values, parts)
 
 
 def call_combine(info, parts):
@@ -414,13 +443,6 @@
     )(info, q, k, *values, *statistics, kept, got)
 
 
-def to_everyone(value, axis):
-    peers = lax.axis_size(axis)
-    return lax.all_to_all(
-        jnp.broadcast_to(value[None], (peers, *value.shape)), axis, 0, 0, tiled=True
-    )
-
-
 def along_x(value, by):
     return lax.ppermute(value, "x", [(n, (n + by) % 4) for n in range(4)])
 
@@ -459,10 +481,12 @@
     )
     q_all = lax.all_gather(q_own, ("c", "z"), axis=0, tiled=False)
     kv_y = lax.all_to_all(kv_own, Y, 0, 0, tiled=True)
-    k_all = to_everyone(kv_y[:, :TILE, :HD], "x").reshape(NK, TILE, HD)
+    k_copies, v_y = call_split(kv_y)
+    k_all = lax.all_to_all(k_copies, "x", 0, 0, tiled=True).reshape(NK, TILE, HD)
     mine = lax.dynamic_slice_in_dim(kv_y[:, TILE:, :NK], y_lo * 2, 2, 0)
+    v_y, mine = lax.optimization_barrier((v_y, mine))
     other = swap_cores(mine)
-    v_y, other = lax.optimization_barrier((kv_y[:, :TILE, HD:], other))
+    v_y, other = lax.optimization_barrier((v_y, other))
     v_all = (v_y, along_x(v_y, -1), along_x(v_y, 2), along_x(v_y, 1))
     first = jnp.where(core == 0, mine, other)
     second = jnp.where(core == 0, other, mine)
@@ -474,9 +498,9 @@
     pairs, count = list_pairs(mask)
     info = jnp.concatenate([jnp.stack([count, core, x, z]), pairs])
 
-    part, parts = call_stats(info, q_all, k_all)
-    parts = lax.all_to_all(parts, ("c", "z"), 0, 0, tiled=True)
-    kept, sent = call_query(info, q_all, k_all, v_all, part)
+    sent_parts = call_stats(info, q_all, k_all)
+    parts = lax.all_to_all(sent_parts, ("c", "z"), 0, 0, tiled=True)
+    kept, sent = call_query(info, q_all, k_all, v_all, sent_parts)
     got = swap_cores(sent)
 
     statistics = call_combine(info, parts)

time: 155 us -> 155 us (level)
  the two profiles are of different devices: /device:TPU:11 before, /device:TPU:13 now
where the time goes in v11:
time: 155 us; the launch traced here: 154 us
  waiting for transfers between devices  66.1 us (43%)
  starting transfers between devices  45.7 us (29%)
  Pallas kernels  21.8 us (14%)
  between operations  14.3 us (9%)
  local copies, waits for them, and re-layouts  3.14 us (2%)
  other arithmetic  2.94 us (2%)
    ppermute x6, waiting for transfers between devices, along_x(): return lax.ppermute(value, 'x', [(n, (n + by) % 4) for n in range(4)])  19.5 us
    all_to_all x1, waiting for transfers between devices, body(): kv_y = lax.all_to_all(kv_own, Y, 0, 0, tiled=True)  17.3 us
    ppermute x6, starting transfers between devices, along_x(): return lax.ppermute(value, 'x', [(n, (n + by) % 4) for n in range(4)])  16.8 us
    all_to_all x1, waiting for transfers between devices, sum_over_keys(): return lax.all_to_all(over_x, Y, 0, 0, tiled=True)  12.8 us
    all_to_all x1, starting transfers between devices, body(): kv_y = lax.all_to_all(kv_own, Y, 0, 0, tiled=True)  7 us
    all_gather x1, waiting for transfers between devices, body(): q_all = lax.all_gather(q_own, ('c', 'z'), axis=0, tiled=False)  6.99 us
    all_to_all x1, starting transfers between devices, body(): parts = lax.all_to_all(sent_parts, ('c', 'z'), 0, 0, tiled=True)  6.86 us
    pallas_call x1, Pallas kernels, call_key(): pl.pallas_call(key_kernel, out_shape=(jax.ShapeDtypeStruct((NZ, HD, ROWS)...  6.63 us
  transfers between devices with their start and end apart: 14, of which 8 were waited for; matrix products, arithmetic and copies ran while one was open for 3% of the time, Pallas kernels for 8%

profile of v11, /device:TPU:13, one launch (start us, length us, event | category | flops | bytes accessed | tf_op | source)
XLA Modules:
  0.0 153.9 jit_solution(13661066525490317853)
XLA Ops:
  7.2 2.1 %prepare.1 = (bf16[272,512]{1,0:T(8,128)(2,1)}, bf16[8,144,256]{2,1,0:T(8,128)(2,1)}) custom-call(bf16[128,512]{1,0:T(8,128)(2,1)} %q_in.1, bf16[128,512]{1,0:T(8,128)(2,1)} %g_in.1, bf16[128,512]{1,0:T(8,128)(2,1)} %o_in.1, bf16[128,128]{1,0:T(8,128)(2,1)} %k_in.1, bf16[128,128]{1,0:T(8,128)(2,1)} %v_in.1, s32[16,32]{1,0:T(8,128)} %mask_in.1), custom_call_target="tpu_custom_call" | custom-call | tf_op jit(solution)/shard_map/prepare/pallas_call | solution.py:307
  9.4 7.0 %all-to-all-start = ((bf16[8,144,256]{2,1,0:T(8,128)(2,1)}), bf16[8,144,256]{2,1,0:T(8,128)(2,1)S(1)}, u32[]{:S(2)}, u32[]{:S(2)}) async-start(bf16[8,144,256]{2,1,0:T(8,128)(2,1)} %get-tuple-element.25), calls=%async_computation | async-start | bytes 1179648 | tf_op jit(solution)/shard_map/all_to_all | solution.py:483
  16.4 17.3 %all-to-all-done.kv_ref = bf16[8,144,256]{2,1,0:T(8,128)(2,1)S(1)} async-done(((bf16[8,144,256]{2,1,0:T(8,128)(2,1)}), bf16[8,144,256]{2,1,0:T(8,128)(2,1)S(1)}, u32[]{:S(2)}, u32[]{:S(2)}) %all-to-all-start) | async-done | bytes 589856 | tf_op jit(solution)/shard_map/all_to_all | solution.py:483
  34.8 2.5 %collective-permute-start = (bf16[2,16,32]{2,1,0:T(8,128)(2,1)S(1)}, bf16[2,16,32]{2,1,0:T(8,128)(2,1)S(1)}, u32[]{:S(2)}, u32[]{:S(2)}) collective-permute-start(bf16[2,16,32]{2,1,0:T(8,128)(2,1)S(1)} %constant_dynamic-slice_fusion), channel_id=1, source_target_pairs={{0,16},{16,0},{1,17},{17,1},{2,18},{18,2},{3,19},{19,3},{4,20},{20... | collective-permute-start | bytes 6152 | tf_op jit(solution)/shard_map/ppermute | solution.py:451
  37.3 4.2 %all-to-all-start.1 = ((bf16[4,8,128,128]{3,2,1,0:T(8,128)(2,1)}), bf16[4,8,128,128]{3,2,1,0:T(8,128)(2,1)S(1)}, u32[]{:S(2)}, u32[]{:S(2)}) async-start(bf16[4,8,128,128]{3,2,1,0:T(8,128)(2,1)} %get-tuple-element.31), calls=%async_computation.1 | async-start | bytes 2097152 | tf_op jit(solution)/shard_map/all_to_all | solution.py:485
  41.6 2.8 %collective-permute-start.3 = (bf16[8,128,128]{2,1,0:T(8,128)(2,1)S(1)}, bf16[8,128,128]{2,1,0:T(8,128)(2,1)S(1)}, u32[]{:S(2)}, u32[]{:S(2)}) collective-permute-start(bf16[8,128,128]{2,1,0:T(8,128)(2,1)S(1)} %get-tuple-element.32.v0), channel_id=1, source_target_pairs={{0,128},{128,256},{256,384},{384,0},{1,129},{129,257},{257,385},{3... | collective-permute-start | bytes 786440 | tf_op jit(solution)/shard_map/ppermute | solution.py:447
  44.3 2.5 %collective-permute-start.2 = (bf16[8,128,128]{2,1,0:T(8,128)(2,1)S(1)}, bf16[8,128,128]{2,1,0:T(8,128)(2,1)S(1)}, u32[]{:S(2)}, u32[]{:S(2)}) collective-permute-start(bf16[8,128,128]{2,1,0:T(8,128)(2,1)S(1)} %get-tuple-element.32.v0), channel_id=1, source_target_pairs={{0,256},{128,384},{256,0},{384,128},{1,257},{129,385},{257,1},{385... | collective-permute-start | bytes 786440 | tf_op jit(solution)/shard_map/ppermute | solution.py:447
  46.8 2.5 %collective-permute-start.1 = (bf16[8,128,128]{2,1,0:T(8,128)(2,1)S(1)}, bf16[8,128,128]{2,1,0:T(8,128)(2,1)S(1)}, u32[]{:S(2)}, u32[]{:S(2)}) collective-permute-start(bf16[8,128,128]{2,1,0:T(8,128)(2,1)S(1)} %get-tuple-element.32.v0), channel_id=1, source_target_pairs={{0,384},{128,0},{256,128},{384,256},{1,385},{129,1},{257,129},{385... | collective-permute-start | bytes 786440 | tf_op jit(solution)/shard_map/ppermute | solution.py:447
  52.5 1.4 all-to-all-done.1
  54.0 7.0 %all-gather.3.cloned.1.call-done = bf16[4352,512]{1,0:T(8,128)(2,1)} async-done(((bf16[272,512]{1,0:T(8,128)(2,1)}), bf16[4352,512]{1,0:T(8,128)(2,1)}) %all-gather.3.cloned.1.call-update) | async-done | bytes 4456464 | tf_op jit(solution)/shard_map/all_gather | solution.py:482
  61.0 4.5 %row_statistics.1.parts_hbm = f32[16,64,128]{2,1,0:T(8,128)} custom-call(s32[520]{0:T(1024)S(1)} %concatenate.3.info_ref, bf16[16,272,512]{2,1,0:T(8,128)(2,1)} %bitcast.23, bf16[32,128,128]{2,1,0:T(8,128)(2,1)S(1)} %bitcast.17), custom_call_target="tpu_custom_call" | custom-call | flops 10000000000 | bytes 4194304 | tf_op jit(solution)/shard_map/row_statistics/pallas_call | solution.py:368
  65.5 6.9 %all-to-all-start.2 = ((f32[16,64,128]{2,1,0:T(8,128)}), f32[16,64,128]{2,1,0:T(8,128)S(1)}, u32[]{:S(2)}, u32[]{:S(2)}) async-start(f32[16,64,128]{2,1,0:T(8,128)} %row_statistics.1.parts_hbm), calls=%async_computation.2 | async-start | bytes 1048576 | tf_op jit(solution)/shard_map/all_to_all | solution.py:502
  72.5 5.3 %query_gradient.1 = (bf16[8,128,512]{2,1,0:T(8,128)(2,1)S(1)}, bf16[8,128,512]{2,1,0:T(8,128)(2,1)S(1)}) custom-call(s32[520]{0:T(1024)S(1)} %concatenate.3.info_ref, bf16[16,272,512]{2,1,0:T(8,128)(2,1)} %bitcast.24, bf16[32,128,128]{2,1,0:T(8,128)(2,1)} %bitcast.18, bf16[8,128,128]{2,1,0:T(8,128)(2,1)S(1)} %get-tuple-element.32.v0, ...), custom_call_target="tpu_custom_call" | custom-call | flops 10000000000 | bytes 8388608 | tf_op jit(solution)/shard_map/query_gradient/pallas_call | solution.py:389
  78.7 1.9 %collective-permute-start.4 = (bf16[8,128,512]{2,1,0:T(8,128)(2,1)S(1)}, bf16[8,128,512]{2,1,0:T(8,128)(2,1)}, u32[]{:S(2)}, u32[]{:S(2)}) collective-permute-start(bf16[8,128,512]{2,1,0:T(8,128)(2,1)S(1)} %get-tuple-element.37), channel_id=1, source_target_pairs={{0,16},{16,0},{1,17},{17,1},{2,18},{18,2},{3,19},{19,3},{4,20},{20... | collective-permute-start | bytes 3145736 | tf_op jit(solution)/shard_map/ppermute | solution.py:451
  80.6 6.6 %all-to-all-done.2.parts_ref = f32[16,64,128]{2,1,0:T(8,128)S(1)} async-done(((f32[16,64,128]{2,1,0:T(8,128)}), f32[16,64,128]{2,1,0:T(8,128)S(1)}, u32[]{:S(2)}, u32[]{:S(2)}) %all-to-all-start.2) | async-done | bytes 524320 | tf_op jit(solution)/shard_map/all_to_all | solution.py:502
  87.9 6.6 %key_gradient.1 = (bf16[8,128,512]{2,1,0:T(8,128)(2,1)}, bf16[8,128,256]{2,1,0:T(8,128)(2,1)S(1)}, bf16[8,128,256]{2,1,0:T(8,128)(2,1)S(1)}, bf16[8,128,256]{2,1,0:T(8,128)(2,1)S(1)}, bf16[8,128,256]{2,1,0:T(8,128)(2,1)S(1)}) custom-call(s32[520]{0:T(1024)S(1)} %concatenate.3.info_ref, bf16[16,272,512]{2,1,0:T(8,128)(2,1)} %bitcast.25, ...), custom_call_target="tpu_custom_call" | custom-call | flops 10000000000 | bytes 8388608 | tf_op jit(solution)/shard_map/key_gradient/pallas_call | solution.py:424
  94.5 3.7 %collective-permute-start.5 = (bf16[8,128,256]{2,1,0:T(8,128)(2,1)S(1)}, bf16[8,128,256]{2,1,0:T(8,128)(2,1)S(1)}, u32[]{:S(2)}, u32[]{:S(2)}) collective-permute-start(bf16[8,128,256]{2,1,0:T(8,128)(2,1)S(1)} %get-tuple-element.40), channel_id=1, source_target_pairs={{0,256},{128,384},{256,0},{384,128},{1,257},{129,385},{257,1},{385... | collective-permute-start | bytes 1572872 | tf_op jit(solution)/shard_map/ppermute | solution.py:447
  98.2 2.6 %collective-permute-start.6 = (bf16[8,128,256]{2,1,0:T(8,128)(2,1)S(1)}, bf16[8,128,256]{2,1,0:T(8,128)(2,1)S(1)}, u32[]{:S(2)}, u32[]{:S(2)}) collective-permute-start(bf16[8,128,256]{2,1,0:T(8,128)(2,1)S(1)} %get-tuple-element.41), channel_id=1, source_target_pairs={{0,128},{128,256},{256,384},{384,0},{1,129},{129,257},{257,385},{3... | collective-permute-start | bytes 1572872 | tf_op jit(solution)/shard_map/ppermute | solution.py:447
  100.8 2.7 %collective-permute-start.7 = (bf16[8,128,256]{2,1,0:T(8,128)(2,1)S(1)}, bf16[8,128,256]{2,1,0:T(8,128)(2,1)S(1)}, u32[]{:S(2)}, u32[]{:S(2)}) collective-permute-start(bf16[8,128,256]{2,1,0:T(8,128)(2,1)S(1)} %get-tuple-element.42), channel_id=1, source_target_pairs={{0,384},{128,0},{256,128},{384,256},{1,385},{129,1},{257,129},{385... | collective-permute-start | bytes 1572872 | tf_op jit(solution)/shard_map/ppermute | solution.py:447
  103.5 7.7 %collective-permute-done.5 = bf16[8,128,256]{2,1,0:T(8,128)(2,1)S(1)} collective-permute-done((bf16[8,128,256]{2,1,0:T(8,128)(2,1)S(1)}, bf16[8,128,256]{2,1,0:T(8,128)(2,1)S(1)}, u32[]{:S(2)}, u32[]{:S(2)}) %collective-permute-start.5) | collective-permute-done | bytes 524320 | tf_op jit(solution)/shard_map/ppermute | solution.py:447
  111.2 11.8 %collective-permute-done.6 = bf16[8,128,256]{2,1,0:T(8,128)(2,1)S(1)} collective-permute-done((bf16[8,128,256]{2,1,0:T(8,128)(2,1)S(1)}, bf16[8,128,256]{2,1,0:T(8,128)(2,1)S(1)}, u32[]{:S(2)}, u32[]{:S(2)}) %collective-permute-start.6) | collective-permute-done | bytes 524320 | tf_op jit(solution)/shard_map/ppermute | solution.py:447
  124.1 6.3 %all-to-all-start.3 = ((bf16[8,128,256]{2,1,0:T(8,128)(2,1)}), bf16[8,128,256]{2,1,0:T(8,128)(2,1)S(1)}, u32[]{:S(2)}, u32[]{:S(2)}) async-start(bf16[8,128,256]{2,1,0:T(8,128)(2,1)} %add_convert_fusion), calls=%async_computation.4 | async-start | bytes 1048576 | tf_op jit(solution)/shard_map/all_to_all | solution.py:457
  130.4 1.5 reduce-scatter.2.cloned.1.call-done
  133.6 12.8 %all-to-all-done.3.over_y_ref = bf16[8,128,256]{2,1,0:T(8,128)(2,1)S(1)} async-done(((bf16[8,128,256]{2,1,0:T(8,128)(2,1)}), bf16[8,128,256]{2,1,0:T(8,128)(2,1)S(1)}, u32[]{:S(2)}, u32[]{:S(2)}) %all-to-all-start.3) | async-done | bytes 524320 | tf_op jit(solution)/shard_map/all_to_all | solution.py:457
  (36 shorter events, 9.4 us)
Async XLA Ops:
  7.2 53.8 %all-gather.3.cloned.1.call-start = ((), (), s32[]{:S(2)}) async-start(), calls=%async_computation.6 | async-start | bytes 4734976 | tf_op jit(solution)/shard_map/all_gather | solution.py:482
  9.4 24.3 %all-to-all-start = ((bf16[8,144,256]{2,1,0:T(8,128)(2,1)}), bf16[8,144,256]{2,1,0:T(8,128)(2,1)S(1)}, u32[]{:S(2)}, u32[]{:S(2)}) async-start(bf16[8,144,256]{2,1,0:T(8,128)(2,1)} %get-tuple-element.25), calls=%async_computation | async-start | bytes 1179648 | tf_op jit(solution)/shard_map/all_to_all | solution.py:483
  34.8 6.8 %collective-permute-start = (bf16[2,16,32]{2,1,0:T(8,128)(2,1)S(1)}, bf16[2,16,32]{2,1,0:T(8,128)(2,1)S(1)}, u32[]{:S(2)}, u32[]{:S(2)}) collective-permute-start(bf16[2,16,32]{2,1,0:T(8,128)(2,1)S(1)} %constant_dynamic-slice_fusion), channel_id=1, source_target_pairs={{0,16},{16,0},{1,17},{17,1},{2,18},{18,2},{3,19},{19,3},{4,20},{20... | collective-permute-start | bytes 6152 | tf_op jit(solution)/shard_map/ppermute | solution.py:451
  37.3 16.7 %all-to-all-start.1 = ((bf16[4,8,128,128]{3,2,1,0:T(8,128)(2,1)}), bf16[4,8,128,128]{3,2,1,0:T(8,128)(2,1)S(1)}, u32[]{:S(2)}, u32[]{:S(2)}) async-start(bf16[4,8,128,128]{3,2,1,0:T(8,128)(2,1)} %get-tuple-element.31), calls=%async_computation.1 | async-start | bytes 2097152 | tf_op jit(solution)/shard_map/all_to_all | solution.py:485
  41.6 30.9 %collective-permute-start.3 = (bf16[8,128,128]{2,1,0:T(8,128)(2,1)S(1)}, bf16[8,128,128]{2,1,0:T(8,128)(2,1)S(1)}, u32[]{:S(2)}, u32[]{:S(2)}) collective-permute-start(bf16[8,128,128]{2,1,0:T(8,128)(2,1)S(1)} %get-tuple-element.32.v0), channel_id=1, source_target_pairs={{0,128},{128,256},{256,384},{384,0},{1,129},{129,257},{257,385},{3... | collective-permute-start | bytes 786440 | tf_op jit(solution)/shard_map/ppermute | solution.py:447
  44.3 28.1 %collective-permute-start.2 = (bf16[8,128,128]{2,1,0:T(8,128)(2,1)S(1)}, bf16[8,128,128]{2,1,0:T(8,128)(2,1)S(1)}, u32[]{:S(2)}, u32[]{:S(2)}) collective-permute-start(bf16[8,128,128]{2,1,0:T(8,128)(2,1)S(1)} %get-tuple-element.32.v0), channel_id=1, source_target_pairs={{0,256},{128,384},{256,0},{384,128},{1,257},{129,385},{257,1},{385... | collective-permute-start | bytes 786440 | tf_op jit(solution)/shard_map/ppermute | solution.py:447
  46.8 25.6 %collective-permute-start.1 = (bf16[8,128,128]{2,1,0:T(8,128)(2,1)S(1)}, bf16[8,128,128]{2,1,0:T(8,128)(2,1)S(1)}, u32[]{:S(2)}, u32[]{:S(2)}) collective-permute-start(bf16[8,128,128]{2,1,0:T(8,128)(2,1)S(1)} %get-tuple-element.32.v0), channel_id=1, source_target_pairs={{0,384},{128,0},{256,128},{384,256},{1,385},{129,1},{257,129},{385... | collective-permute-start | bytes 786440 | tf_op jit(solution)/shard_map/ppermute | solution.py:447
  54.0 11.5 %copy-start = (bf16[4,8,128,128]{3,2,1,0:T(8,128)(2,1)}, bf16[4,8,128,128]{3,2,1,0:T(8,128)(2,1)S(1)}, u32[]{:S(2)}) copy-start(bf16[4,8,128,128]{3,2,1,0:T(8,128)(2,1)S(1)} %all-to-all-done.1) | copy-start | bytes 3145732
  65.5 21.6 %all-to-all-start.2 = ((f32[16,64,128]{2,1,0:T(8,128)}), f32[16,64,128]{2,1,0:T(8,128)S(1)}, u32[]{:S(2)}, u32[]{:S(2)}) async-start(f32[16,64,128]{2,1,0:T(8,128)} %row_statistics.1.parts_hbm), calls=%async_computation.2 | async-start | bytes 1048576 | tf_op jit(solution)/shard_map/all_to_all | solution.py:502
  72.4 59.5 %reduce-scatter.2.cloned.1.call-start = ((), (), s32[]{:S(2)}) async-start(), calls=%async_computation.5 | async-start | bytes 1179648 | tf_op jit(solution)/shard_map/reduce_scatter | solution.py:509
  77.7 1.0 copy-start.2
  78.7 9.2 %collective-permute-start.4 = (bf16[8,128,512]{2,1,0:T(8,128)(2,1)S(1)}, bf16[8,128,512]{2,1,0:T(8,128)(2,1)}, u32[]{:S(2)}, u32[]{:S(2)}) collective-permute-start(bf16[8,128,512]{2,1,0:T(8,128)(2,1)S(1)} %get-tuple-element.37), channel_id=1, source_target_pairs={{0,16},{16,0},{1,17},{17,1},{2,18},{18,2},{3,19},{19,3},{4,20},{20... | collective-permute-start | bytes 3145736 | tf_op jit(solution)/shard_map/ppermute | solution.py:451
  94.5 16.7 %collective-permute-start.5 = (bf16[8,128,256]{2,1,0:T(8,128)(2,1)S(1)}, bf16[8,128,256]{2,1,0:T(8,128)(2,1)S(1)}, u32[]{:S(2)}, u32[]{:S(2)}) collective-permute-start(bf16[8,128,256]{2,1,0:T(8,128)(2,1)S(1)} %get-tuple-element.40), channel_id=1, source_target_pairs={{0,256},{128,384},{256,0},{384,128},{1,257},{129,385},{257,1},{385... | collective-permute-start | bytes 1572872 | tf_op jit(solution)/shard_map/ppermute | solution.py:447
  98.2 24.8 %collective-permute-start.6 = (bf16[8,128,256]{2,1,0:T(8,128)(2,1)S(1)}, bf16[8,128,256]{2,1,0:T(8,128)(2,1)S(1)}, u32[]{:S(2)}, u32[]{:S(2)}) collective-permute-start(bf16[8,128,256]{2,1,0:T(8,128)(2,1)S(1)} %get-tuple-element.41), channel_id=1, source_target_pairs={{0,128},{128,256},{256,384},{384,0},{1,129},{129,257},{257,385},{3... | collective-permute-start | bytes 1572872 | tf_op jit(solution)/shard_map/ppermute | solution.py:447
  100.8 22.2 %collective-permute-start.7 = (bf16[8,128,256]{2,1,0:T(8,128)(2,1)S(1)}, bf16[8,128,256]{2,1,0:T(8,128)(2,1)S(1)}, u32[]{:S(2)}, u32[]{:S(2)}) collective-permute-start(bf16[8,128,256]{2,1,0:T(8,128)(2,1)S(1)} %get-tuple-element.42), channel_id=1, source_target_pairs={{0,384},{128,0},{256,128},{384,256},{1,385},{129,1},{257,129},{385... | collective-permute-start | bytes 1572872 | tf_op jit(solution)/shard_map/ppermute | solution.py:447
  124.1 22.3 %all-to-all-start.3 = ((bf16[8,128,256]{2,1,0:T(8,128)(2,1)}), bf16[8,128,256]{2,1,0:T(8,128)(2,1)S(1)}, u32[]{:S(2)}, u32[]{:S(2)}) async-start(bf16[8,128,256]{2,1,0:T(8,128)(2,1)} %add_convert_fusion), calls=%async_computation.4 | async-start | bytes 1048576 | tf_op jit(solution)/shard_map/all_to_all | solution.py:457
  131.9 0.9 copy-start.1
Sparse Core Ops, SparseCore 0:
  10.1 50.8 all-gather.2
  94.6 37.2 reduce-scatter.1

commit v12 on v11

--- a/solution.py
+++ b/solution.py
@@ -23,7 +23,7 @@
 LOG2E = 1.0 / math.log(2.0)
 Y = ("yl", "yh")
 SCALARS = 4
-STEP = 4
+STEP = 6
 
 
 def dot(a, b, dims):

time: 155 us -> 155 us (level)
  the two profiles are of different devices: /device:TPU:13 before, /device:TPU:16 now
where the time goes in v12:
time: 155 us; the launch traced here: 154 us
  waiting for transfers between devices  59.7 us (39%)
  starting transfers between devices  54.9 us (35%)
  Pallas kernels  18.8 us (12%)
  between operations  14.3 us (9%)
  local copies, waits for them, and re-layouts  3.14 us (2%)
  other arithmetic  2.94 us (2%)
    ppermute x6, starting transfers between devices, along_x(): return lax.ppermute(value, 'x', [(n, (n + by) % 4) for n in range(4)])  21.7 us
    ppermute x6, waiting for transfers between devices, along_x(): return lax.ppermute(value, 'x', [(n, (n + by) % 4) for n in range(4)])  19.1 us
    all_to_all x1, waiting for transfers between devices, body(): kv_y = lax.all_to_all(kv_own, Y, 0, 0, tiled=True)  14.9 us
    all_to_all x1, starting transfers between devices, body(): parts = lax.all_to_all(sent_parts, ('c', 'z'), 0, 0, tiled=True)  9.57 us
    all_to_all x1, starting transfers between devices, body(): kv_y = lax.all_to_all(kv_own, Y, 0, 0, tiled=True)  9.18 us
    all_to_all x1, waiting for transfers between devices, sum_over_keys(): return lax.all_to_all(over_x, Y, 0, 0, tiled=True)  9.17 us
    all_to_all x1, waiting for transfers between devices, body(): parts = lax.all_to_all(sent_parts, ('c', 'z'), 0, 0, tiled=True)  7.29 us
    pallas_call x1, Pallas kernels, call_key(): pl.pallas_call(key_kernel, out_shape=(jax.ShapeDtypeStruct((NZ, HD, ROWS)...  5.46 us
  transfers between devices with their start and end apart: 14, of which 8 were waited for; matrix products, arithmetic and copies ran while one was open for 3% of the time, Pallas kernels for 7%

profile of v12, /device:TPU:16, one launch (start us, length us, event | category | flops | bytes accessed | tf_op | source)
XLA Modules:
  0.0 153.7 jit_solution(18170172724814254205)
XLA Ops:
  7.2 2.1 %prepare.1 = (bf16[272,512]{1,0:T(8,128)(2,1)}, bf16[8,144,256]{2,1,0:T(8,128)(2,1)}) custom-call(bf16[128,512]{1,0:T(8,128)(2,1)} %q_in.1, bf16[128,512]{1,0:T(8,128)(2,1)} %g_in.1, bf16[128,512]{1,0:T(8,128)(2,1)} %o_in.1, bf16[128,128]{1,0:T(8,128)(2,1)} %k_in.1, bf16[128,128]{1,0:T(8,128)(2,1)} %v_in.1, s32[16,32]{1,0:T(8,128)} %mask_in.1), custom_call_target="tpu_custom_call" | custom-call | tf_op jit(solution)/shard_map/prepare/pallas_call | solution.py:307
  9.4 9.2 %all-to-all-start = ((bf16[8,144,256]{2,1,0:T(8,128)(2,1)}), bf16[8,144,256]{2,1,0:T(8,128)(2,1)S(1)}, u32[]{:S(2)}, u32[]{:S(2)}) async-start(bf16[8,144,256]{2,1,0:T(8,128)(2,1)} %get-tuple-element.25), calls=%async_computation | async-start | bytes 1179648 | tf_op jit(solution)/shard_map/all_to_all | solution.py:483
  18.6 14.9 %all-to-all-done.kv_ref = bf16[8,144,256]{2,1,0:T(8,128)(2,1)S(1)} async-done(((bf16[8,144,256]{2,1,0:T(8,128)(2,1)}), bf16[8,144,256]{2,1,0:T(8,128)(2,1)S(1)}, u32[]{:S(2)}, u32[]{:S(2)}) %all-to-all-start) | async-done | bytes 589856 | tf_op jit(solution)/shard_map/all_to_all | solution.py:483
  34.5 1.9 %collective-permute-start = (bf16[2,16,32]{2,1,0:T(8,128)(2,1)S(1)}, bf16[2,16,32]{2,1,0:T(8,128)(2,1)S(1)}, u32[]{:S(2)}, u32[]{:S(2)}) collective-permute-start(bf16[2,16,32]{2,1,0:T(8,128)(2,1)S(1)} %constant_dynamic-slice_fusion), channel_id=1, source_target_pairs={{0,16},{16,0},{1,17},{17,1},{2,18},{18,2},{3,19},{19,3},{4,20},{20... | collective-permute-start | bytes 6152 | tf_op jit(solution)/shard_map/ppermute | solution.py:451
  36.5 4.3 %all-to-all-start.1 = ((bf16[4,8,128,128]{3,2,1,0:T(8,128)(2,1)}), bf16[4,8,128,128]{3,2,1,0:T(8,128)(2,1)S(1)}, u32[]{:S(2)}, u32[]{:S(2)}) async-start(bf16[4,8,128,128]{3,2,1,0:T(8,128)(2,1)} %get-tuple-element.31), calls=%async_computation.1 | async-start | bytes 2097152 | tf_op jit(solution)/shard_map/all_to_all | solution.py:485
  40.8 3.9 %collective-permute-start.3 = (bf16[8,128,128]{2,1,0:T(8,128)(2,1)S(1)}, bf16[8,128,128]{2,1,0:T(8,128)(2,1)S(1)}, u32[]{:S(2)}, u32[]{:S(2)}) collective-permute-start(bf16[8,128,128]{2,1,0:T(8,128)(2,1)S(1)} %get-tuple-element.32.v0), channel_id=1, source_target_pairs={{0,128},{128,256},{256,384},{384,0},{1,129},{129,257},{257,385},{3... | collective-permute-start | bytes 786440 | tf_op jit(solution)/shard_map/ppermute | solution.py:447
  44.7 4.6 %collective-permute-start.2 = (bf16[8,128,128]{2,1,0:T(8,128)(2,1)S(1)}, bf16[8,128,128]{2,1,0:T(8,128)(2,1)S(1)}, u32[]{:S(2)}, u32[]{:S(2)}) collective-permute-start(bf16[8,128,128]{2,1,0:T(8,128)(2,1)S(1)} %get-tuple-element.32.v0), channel_id=1, source_target_pairs={{0,256},{128,384},{256,0},{384,128},{1,257},{129,385},{257,1},{385... | collective-permute-start | bytes 786440 | tf_op jit(solution)/shard_map/ppermute | solution.py:447
  49.3 3.4 %collective-permute-start.1 = (bf16[8,128,128]{2,1,0:T(8,128)(2,1)S(1)}, bf16[8,128,128]{2,1,0:T(8,128)(2,1)S(1)}, u32[]{:S(2)}, u32[]{:S(2)}) collective-permute-start(bf16[8,128,128]{2,1,0:T(8,128)(2,1)S(1)} %get-tuple-element.32.v0), channel_id=1, source_target_pairs={{0,384},{128,0},{256,128},{384,256},{1,385},{129,1},{257,129},{385... | collective-permute-start | bytes 786440 | tf_op jit(solution)/shard_map/ppermute | solution.py:447
  55.8 1.4 all-to-all-done.1
  57.3 3.2 %all-gather.3.cloned.1.call-done = bf16[4352,512]{1,0:T(8,128)(2,1)} async-done(((bf16[272,512]{1,0:T(8,128)(2,1)}), bf16[4352,512]{1,0:T(8,128)(2,1)}) %all-gather.3.cloned.1.call-update) | async-done | bytes 4456464 | tf_op jit(solution)/shard_map/all_gather | solution.py:482
  60.5 3.7 %row_statistics.1.parts_hbm = f32[16,64,128]{2,1,0:T(8,128)} custom-call(s32[522]{0:T(1024)S(1)} %concatenate.3.info_ref, bf16[16,272,512]{2,1,0:T(8,128)(2,1)} %bitcast.23, bf16[32,128,128]{2,1,0:T(8,128)(2,1)S(1)} %bitcast.17), custom_call_target="tpu_custom_call" | custom-call | flops 10000000000 | bytes 4194304 | tf_op jit(solution)/shard_map/row_statistics/pallas_call | solution.py:368
  64.3 9.6 %all-to-all-start.2 = ((f32[16,64,128]{2,1,0:T(8,128)}), f32[16,64,128]{2,1,0:T(8,128)S(1)}, u32[]{:S(2)}, u32[]{:S(2)}) async-start(f32[16,64,128]{2,1,0:T(8,128)} %row_statistics.1.parts_hbm), calls=%async_computation.2 | async-start | bytes 1048576 | tf_op jit(solution)/shard_map/all_to_all | solution.py:502
  73.9 4.2 %query_gradient.1 = (bf16[8,128,512]{2,1,0:T(8,128)(2,1)S(1)}, bf16[8,128,512]{2,1,0:T(8,128)(2,1)S(1)}) custom-call(s32[522]{0:T(1024)S(1)} %concatenate.3.info_ref, bf16[16,272,512]{2,1,0:T(8,128)(2,1)} %bitcast.24, bf16[32,128,128]{2,1,0:T(8,128)(2,1)} %bitcast.18, bf16[8,128,128]{2,1,0:T(8,128)(2,1)S(1)} %get-tuple-element.32.v0, ...), custom_call_target="tpu_custom_call" | custom-call | flops 10000000000 | bytes 8388608 | tf_op jit(solution)/shard_map/query_gradient/pallas_call | solution.py:389
  79.1 3.1 %collective-permute-start.4 = (bf16[8,128,512]{2,1,0:T(8,128)(2,1)S(1)}, bf16[8,128,512]{2,1,0:T(8,128)(2,1)}, u32[]{:S(2)}, u32[]{:S(2)}) collective-permute-start(bf16[8,128,512]{2,1,0:T(8,128)(2,1)S(1)} %get-tuple-element.37), channel_id=1, source_target_pairs={{0,16},{16,0},{1,17},{17,1},{2,18},{18,2},{3,19},{19,3},{4,20},{20... | collective-permute-start | bytes 3145736 | tf_op jit(solution)/shard_map/ppermute | solution.py:451
  82.2 7.3 %all-to-all-done.2.parts_ref = f32[16,64,128]{2,1,0:T(8,128)S(1)} async-done(((f32[16,64,128]{2,1,0:T(8,128)}), f32[16,64,128]{2,1,0:T(8,128)S(1)}, u32[]{:S(2)}, u32[]{:S(2)}) %all-to-all-start.2) | async-done | bytes 524320 | tf_op jit(solution)/shard_map/all_to_all | solution.py:502
  90.2 5.5 %key_gradient.1 = (bf16[8,128,512]{2,1,0:T(8,128)(2,1)}, bf16[8,128,256]{2,1,0:T(8,128)(2,1)S(1)}, bf16[8,128,256]{2,1,0:T(8,128)(2,1)S(1)}, bf16[8,128,256]{2,1,0:T(8,128)(2,1)S(1)}, bf16[8,128,256]{2,1,0:T(8,128)(2,1)S(1)}) custom-call(s32[522]{0:T(1024)S(1)} %concatenate.3.info_ref, bf16[16,272,512]{2,1,0:T(8,128)(2,1)} %bitcast.25, ...), custom_call_target="tpu_custom_call" | custom-call | flops 10000000000 | bytes 8388608 | tf_op jit(solution)/shard_map/key_gradient/pallas_call | solution.py:424
  95.7 1.9 %collective-permute-start.5 = (bf16[8,128,256]{2,1,0:T(8,128)(2,1)S(1)}, bf16[8,128,256]{2,1,0:T(8,128)(2,1)S(1)}, u32[]{:S(2)}, u32[]{:S(2)}) collective-permute-start(bf16[8,128,256]{2,1,0:T(8,128)(2,1)S(1)} %get-tuple-element.40), channel_id=1, source_target_pairs={{0,256},{128,384},{256,0},{384,128},{1,257},{129,385},{257,1},{385... | collective-permute-start | bytes 1572872 | tf_op jit(solution)/shard_map/ppermute | solution.py:447
  97.6 5.4 %collective-permute-start.6 = (bf16[8,128,256]{2,1,0:T(8,128)(2,1)S(1)}, bf16[8,128,256]{2,1,0:T(8,128)(2,1)S(1)}, u32[]{:S(2)}, u32[]{:S(2)}) collective-permute-start(bf16[8,128,256]{2,1,0:T(8,128)(2,1)S(1)} %get-tuple-element.41), channel_id=1, source_target_pairs={{0,128},{128,256},{256,384},{384,0},{1,129},{129,257},{257,385},{3... | collective-permute-start | bytes 1572872 | tf_op jit(solution)/shard_map/ppermute | solution.py:447
  103.0 2.6 %collective-permute-start.7 = (bf16[8,128,256]{2,1,0:T(8,128)(2,1)S(1)}, bf16[8,128,256]{2,1,0:T(8,128)(2,1)S(1)}, u32[]{:S(2)}, u32[]{:S(2)}) collective-permute-start(bf16[8,128,256]{2,1,0:T(8,128)(2,1)S(1)} %get-tuple-element.42), channel_id=1, source_target_pairs={{0,384},{128,0},{256,128},{384,256},{1,385},{129,1},{257,129},{385... | collective-permute-start | bytes 1572872 | tf_op jit(solution)/shard_map/ppermute | solution.py:447
  105.6 8.3 %collective-permute-done.5 = bf16[8,128,256]{2,1,0:T(8,128)(2,1)S(1)} collective-permute-done((bf16[8,128,256]{2,1,0:T(8,128)(2,1)S(1)}, bf16[8,128,256]{2,1,0:T(8,128)(2,1)S(1)}, u32[]{:S(2)}, u32[]{:S(2)}) %collective-permute-start.5) | collective-permute-done | bytes 524320 | tf_op jit(solution)/shard_map/ppermute | solution.py:447
  113.9 10.8 %collective-permute-done.6 = bf16[8,128,256]{2,1,0:T(8,128)(2,1)S(1)} collective-permute-done((bf16[8,128,256]{2,1,0:T(8,128)(2,1)S(1)}, bf16[8,128,256]{2,1,0:T(8,128)(2,1)S(1)}, u32[]{:S(2)}, u32[]{:S(2)}) %collective-permute-start.6) | collective-permute-done | bytes 524320 | tf_op jit(solution)/shard_map/ppermute | solution.py:447
  125.8 5.0 %all-to-all-start.3 = ((bf16[8,128,256]{2,1,0:T(8,128)(2,1)}), bf16[8,128,256]{2,1,0:T(8,128)(2,1)S(1)}, u32[]{:S(2)}, u32[]{:S(2)}) async-start(bf16[8,128,256]{2,1,0:T(8,128)(2,1)} %add_convert_fusion), calls=%async_computation.4 | async-start | bytes 1048576 | tf_op jit(solution)/shard_map/all_to_all | solution.py:457
  130.7 4.6 %reduce-scatter.2.cloned.1.call-done = bf16[1,128,512]{2,1,0:T(8,128)(2,1)} async-done(((bf16[8,128,512]{2,1,0:T(8,128)(2,1)}), bf16[1,128,512]{2,1,0:T(8,128)(2,1)}) %reduce-scatter.2.cloned.1.call-update) | async-done | bytes 131088 | tf_op jit(solution)/shard_map/reduce_scatter | solution.py:509
  137.0 9.2 %all-to-all-done.3.over_y_ref = bf16[8,128,256]{2,1,0:T(8,128)(2,1)S(1)} async-done(((bf16[8,128,256]{2,1,0:T(8,128)(2,1)}), bf16[8,128,256]{2,1,0:T(8,128)(2,1)S(1)}, u32[]{:S(2)}, u32[]{:S(2)}) %all-to-all-start.3) | async-done | bytes 524320 | tf_op jit(solution)/shard_map/all_to_all | solution.py:457
  (36 shorter events, 9.4 us)
Async XLA Ops:
  7.2 53.4 %all-gather.3.cloned.1.call-start = ((), (), s32[]{:S(2)}) async-start(), calls=%async_computation.6 | async-start | bytes 4734976 | tf_op jit(solution)/shard_map/all_gather | solution.py:482
  9.4 24.0 %all-to-all-start = ((bf16[8,144,256]{2,1,0:T(8,128)(2,1)}), bf16[8,144,256]{2,1,0:T(8,128)(2,1)S(1)}, u32[]{:S(2)}, u32[]{:S(2)}) async-start(bf16[8,144,256]{2,1,0:T(8,128)(2,1)} %get-tuple-element.25), calls=%async_computation | async-start | bytes 1179648 | tf_op jit(solution)/shard_map/all_to_all | solution.py:483
  34.5 6.3 %collective-permute-start = (bf16[2,16,32]{2,1,0:T(8,128)(2,1)S(1)}, bf16[2,16,32]{2,1,0:T(8,128)(2,1)S(1)}, u32[]{:S(2)}, u32[]{:S(2)}) collective-permute-start(bf16[2,16,32]{2,1,0:T(8,128)(2,1)S(1)} %constant_dynamic-slice_fusion), channel_id=1, source_target_pairs={{0,16},{16,0},{1,17},{17,1},{2,18},{18,2},{3,19},{19,3},{4,20},{20... | collective-permute-start | bytes 6152 | tf_op jit(solution)/shard_map/ppermute | solution.py:451
  36.5 20.8 %all-to-all-start.1 = ((bf16[4,8,128,128]{3,2,1,0:T(8,128)(2,1)}), bf16[4,8,128,128]{3,2,1,0:T(8,128)(2,1)S(1)}, u32[]{:S(2)}, u32[]{:S(2)}) async-start(bf16[4,8,128,128]{3,2,1,0:T(8,128)(2,1)} %get-tuple-element.31), calls=%async_computation.1 | async-start | bytes 2097152 | tf_op jit(solution)/shard_map/all_to_all | solution.py:485
  40.8 33.1 %collective-permute-start.3 = (bf16[8,128,128]{2,1,0:T(8,128)(2,1)S(1)}, bf16[8,128,128]{2,1,0:T(8,128)(2,1)S(1)}, u32[]{:S(2)}, u32[]{:S(2)}) collective-permute-start(bf16[8,128,128]{2,1,0:T(8,128)(2,1)S(1)} %get-tuple-element.32.v0), channel_id=1, source_target_pairs={{0,128},{128,256},{256,384},{384,0},{1,129},{129,257},{257,385},{3... | collective-permute-start | bytes 786440 | tf_op jit(solution)/shard_map/ppermute | solution.py:447
  44.7 29.2 %collective-permute-start.2 = (bf16[8,128,128]{2,1,0:T(8,128)(2,1)S(1)}, bf16[8,128,128]{2,1,0:T(8,128)(2,1)S(1)}, u32[]{:S(2)}, u32[]{:S(2)}) collective-permute-start(bf16[8,128,128]{2,1,0:T(8,128)(2,1)S(1)} %get-tuple-element.32.v0), channel_id=1, source_target_pairs={{0,256},{128,384},{256,0},{384,128},{1,257},{129,385},{257,1},{385... | collective-permute-start | bytes 786440 | tf_op jit(solution)/shard_map/ppermute | solution.py:447
  49.3 24.6 %collective-permute-start.1 = (bf16[8,128,128]{2,1,0:T(8,128)(2,1)S(1)}, bf16[8,128,128]{2,1,0:T(8,128)(2,1)S(1)}, u32[]{:S(2)}, u32[]{:S(2)}) collective-permute-start(bf16[8,128,128]{2,1,0:T(8,128)(2,1)S(1)} %get-tuple-element.32.v0), channel_id=1, source_target_pairs={{0,384},{128,0},{256,128},{384,256},{1,385},{129,1},{257,129},{385... | collective-permute-start | bytes 786440 | tf_op jit(solution)/shard_map/ppermute | solution.py:447
  57.3 7.0 %copy-start = (bf16[4,8,128,128]{3,2,1,0:T(8,128)(2,1)}, bf16[4,8,128,128]{3,2,1,0:T(8,128)(2,1)S(1)}, u32[]{:S(2)}) copy-start(bf16[4,8,128,128]{3,2,1,0:T(8,128)(2,1)S(1)} %all-to-all-done.1) | copy-start | bytes 3145732
  64.3 25.2 %all-to-all-start.2 = ((f32[16,64,128]{2,1,0:T(8,128)}), f32[16,64,128]{2,1,0:T(8,128)S(1)}, u32[]{:S(2)}, u32[]{:S(2)}) async-start(f32[16,64,128]{2,1,0:T(8,128)} %row_statistics.1.parts_hbm), calls=%async_computation.2 | async-start | bytes 1048576 | tf_op jit(solution)/shard_map/all_to_all | solution.py:502
  73.8 61.5 %reduce-scatter.2.cloned.1.call-start = ((), (), s32[]{:S(2)}) async-start(), calls=%async_computation.5 | async-start | bytes 1179648 | tf_op jit(solution)/shard_map/reduce_scatter | solution.py:509
  78.2 1.0 copy-start.2
  79.1 11.1 %collective-permute-start.4 = (bf16[8,128,512]{2,1,0:T(8,128)(2,1)S(1)}, bf16[8,128,512]{2,1,0:T(8,128)(2,1)}, u32[]{:S(2)}, u32[]{:S(2)}) collective-permute-start(bf16[8,128,512]{2,1,0:T(8,128)(2,1)S(1)} %get-tuple-element.37), channel_id=1, source_target_pairs={{0,16},{16,0},{1,17},{17,1},{2,18},{18,2},{3,19},{19,3},{4,20},{20... | collective-permute-start | bytes 3145736 | tf_op jit(solution)/shard_map/ppermute | solution.py:451
  95.7 18.2 %collective-permute-start.5 = (bf16[8,128,256]{2,1,0:T(8,128)(2,1)S(1)}, bf16[8,128,256]{2,1,0:T(8,128)(2,1)S(1)}, u32[]{:S(2)}, u32[]{:S(2)}) collective-permute-start(bf16[8,128,256]{2,1,0:T(8,128)(2,1)S(1)} %get-tuple-element.40), channel_id=1, source_target_pairs={{0,256},{128,384},{256,0},{384,128},{1,257},{129,385},{257,1},{385... | collective-permute-start | bytes 1572872 | tf_op jit(solution)/shard_map/ppermute | solution.py:447
  97.6 27.1 %collective-permute-start.6 = (bf16[8,128,256]{2,1,0:T(8,128)(2,1)S(1)}, bf16[8,128,256]{2,1,0:T(8,128)(2,1)S(1)}, u32[]{:S(2)}, u32[]{:S(2)}) collective-permute-start(bf16[8,128,256]{2,1,0:T(8,128)(2,1)S(1)} %get-tuple-element.41), channel_id=1, source_target_pairs={{0,128},{128,256},{256,384},{384,0},{1,129},{129,257},{257,385},{3... | collective-permute-start | bytes 1572872 | tf_op jit(solution)/shard_map/ppermute | solution.py:447
  103.0 21.7 %collective-permute-start.7 = (bf16[8,128,256]{2,1,0:T(8,128)(2,1)S(1)}, bf16[8,128,256]{2,1,0:T(8,128)(2,1)S(1)}, u32[]{:S(2)}, u32[]{:S(2)}) collective-permute-start(bf16[8,128,256]{2,1,0:T(8,128)(2,1)S(1)} %get-tuple-element.42), channel_id=1, source_target_pairs={{0,384},{128,0},{256,128},{384,256},{1,385},{129,1},{257,129},{385... | collective-permute-start | bytes 1572872 | tf_op jit(solution)/shard_map/ppermute | solution.py:447
  125.8 20.4 %all-to-all-start.3 = ((bf16[8,128,256]{2,1,0:T(8,128)(2,1)}), bf16[8,128,256]{2,1,0:T(8,128)(2,1)S(1)}, u32[]{:S(2)}, u32[]{:S(2)}) async-start(bf16[8,128,256]{2,1,0:T(8,128)(2,1)} %add_convert_fusion), calls=%async_computation.4 | async-start | bytes 1048576 | tf_op jit(solution)/shard_map/all_to_all | solution.py:457
  135.4 0.9 copy-start.1
Sparse Core Ops, SparseCore 0:
  10.1 50.3 all-gather.2
  95.8 39.4 reduce-scatter.1
